TPU v7x, 32 devices: a whole 2x2x4 slice. The times are simulated.
32 devices in a mesh: dp: 4 (over z), grad: 8 (over y, x, core).
Axes of the slice: x: 2, y: 2, z: 4, core: 2. Of those that a mesh axis runs over, the one named last changes fastest.
Arguments:
- factor_inputs: bfloat16 [512, 4, 1024], P('dp', None, 'grad'), may hold values from -6 to 6
- gradients: bfloat16 [4, 6144, 1024], P('dp', 'grad'), may hold values from -6 to 6
Outputs:
- preconditioned: bfloat16 [4, 6144, 1024], P('dp', 'grad')
All inputs are finite; a program needn't handle non-finite values. Where the computation divides by a largest or mean magnitude, that divisor is 1e-20 or more.
Results may differ from a plain program's by a relative error of at most 0.0065.
Values may be sent and summed in bfloat16 or wider, within the bound.
No kernel may reach another device: no remote copies, remote signals or barrier semaphores. Data moves between devices by JAX's collectives and lax.ppermute only.
A program may use at most 64 MiB of HBM per device.

v0:
```python
import jax
import jax.numpy as jnp
from jax import lax
from jax.sharding import PartitionSpec as P

ITERS = 4


DAMPING = 0.01


def local(factor_inputs, gradients):
    rows = factor_inputs.shape[2]
    width = rows * lax.axis_size("grad")
    tokens = factor_inputs.shape[0] * lax.axis_size("dp")
    partial_value = jnp.einsum(
        "tfr,tfc->frc",
        factor_inputs,
        lax.all_gather(factor_inputs, "grad", axis=2, tiled=True),
        preferred_element_type=jnp.float32,
    )
    summed = lax.psum_scatter(partial_value, "dp", scatter_dimension=0, tiled=True)
    covariance = summed[0] * (1.0 / tokens)
    first_row = lax.axis_index("grad") * rows
    col_ids = lax.broadcasted_iota(jnp.int32, (rows, width), 1)
    row_ids = lax.broadcasted_iota(jnp.int32, (rows, width), 0) + first_row
    eye_rows = (col_ids == row_ids).astype(jnp.float32)
    damped = covariance + DAMPING * eye_rows
    bound = lax.pmax(jnp.max(jnp.sum(jnp.abs(damped), axis=1)), "grad")
    iterate = (eye_rows * (1.0 / bound)).astype(jnp.bfloat16)
    lowered = damped.astype(jnp.bfloat16)
    first_step = 0
    for step in range(first_step, ITERS):
        whole = lax.all_gather(iterate, "grad", axis=0, tiled=True)
        image = jnp.dot(lowered, whole, preferred_element_type=jnp.float32).astype(jnp.bfloat16)
        product = jnp.dot(image, whole, preferred_element_type=jnp.float32)
        iterate = (2.0 * iterate.astype(jnp.float32) - product).astype(jnp.bfloat16)
    tile = gradients[0]
    result = jnp.dot(
        tile,
        lax.all_gather(iterate, "grad", axis=0, tiled=True),
        preferred_element_type=jnp.float32,
    )
    return result.astype(jnp.bfloat16)[None]


def solution(mesh):
    placed = (P("dp", None, "grad"), P("dp", "grad", None))
    return jax.shard_map(
        local, mesh=mesh, in_specs=placed, out_specs=P("dp", "grad", None), check_vma=False
    )
```

profile of v0, /device:TPU:0, one launch (start us, length us, event | category | flops | bytes accessed | tf_op | source)
XLA Modules:
  0.0 265.0 jit_solution(12561840499732702003)
XLA Ops:
  6.5 1.7 copy.3
  8.2 0.0 all-gather.7.cloned.1.call-update
  8.3 0.0 reduce-scatter.2.cloned.1.call-start
  8.3 27.2 %all-gather.7.cloned.1.call-done = bf16[128,4,1024]{2,0,1:T(8,128)(2,1)} async-done(((bf16[128,4,128]{2,0,1:T(8,128)(2,1)}), bf16[128,4,1024]{2,0,1:T(8,128)(2,1)}) %all-gather.7.cloned.1.call-update) | async-done | bytes 1048592 | tf_op jit(solution)/shard_map/all_gather | solution.py:19
  35.5 3.1 %fusion.9 = f32[4,128,1024]{2,1,0:T(8,128)} fusion(bf16[128,4,1024]{2,0,1:T(8,128)(2,1)} %all-gather.7.cloned.1.call-done, bf16[128,4,128]{2,1,0:T(4,128)(2,1)} %param.2), kind=kOutput, calls=%fused_computation.21 | convolution fusion | flops 134217728 | bytes 3276800 | tf_op jit(solution)/shard_map/tfr,tfc->frc/dot_general | solution.py:16
  38.7 0.0 reduce-scatter.2.cloned.1.call-update
  38.7 0.0 all-gather.9.cloned.1.call-start
  38.7 43.9 %reduce-scatter.2.cloned.1.call-done = f32[1,128,1024]{2,1,0:T(8,128)} async-done(((f32[4,128,1024]{2,1,0:T(8,128)}), f32[1,128,1024]{2,1,0:T(8,128)}) %reduce-scatter.2.cloned.1.call-update) | async-done | bytes 524304 | tf_op jit(solution)/shard_map/reduce_scatter | solution.py:22
  82.7 1.3 fusion.8
  84.0 0.6 reduce_max.9
  84.6 14.1 %pmax.7 = f32[]{:T(128)} all-reduce(f32[]{:T(128)} %reduce_max.9), channel_id=1, replica_groups=mesh['dp'=4,'grad'=8] {'grad'}, use_global_device_ids=true, to_apply=%region_3.0 | all-reduce | flops 1 | bytes 8 | tf_op jit(solution)/shard_map/pmax | solution.py:29
  99.4 0.8 select_convert_fusion
  100.2 0.0 all-gather.9.cloned.1.call-update
  100.2 0.0 all-gather.11.cloned.1.call-start
  100.2 25.7 %all-gather.9.cloned.1.call-done = bf16[1024,1024]{1,0:T(8,128)(2,1)} async-done(((bf16[128,1024]{1,0:T(8,128)(2,1)}), bf16[1024,1024]{1,0:T(8,128)(2,1)}) %all-gather.9.cloned.1.call-update) | async-done | bytes 2097168 | tf_op jit(solution)/shard_map/all_gather | solution.py:34
  126.0 3.7 %fusion.4 = bf16[128,1024]{1,0:T(8,128)(2,1)} fusion(bf16[1024,1024]{1,0:T(8,128)(2,1)} %all-gather.9.cloned.1.call-done, bf16[128,1024]{1,0:T(8,128)(2,1)S(1)} %get-tuple-element.5, bf16[]{:T(256)S(6)} %div.3, s32[128]{0:T(128)S(1)} %iota_add_fusion), kind=kOutput, calls=%fused_computation.11 | convolution fusion | flops 537788416 | bytes 2621954 | tf_op jit(solution)/shard_map/dot_general | solution.py:36
  129.7 0.0 all-gather.11.cloned.1.call-update
  129.7 0.0 all-gather.13.cloned.1.call-start
  129.7 28.0 %all-gather.11.cloned.1.call-done = bf16[1024,1024]{1,0:T(8,128)(2,1)} async-done(((bf16[128,1024]{1,0:T(8,128)(2,1)}), bf16[1024,1024]{1,0:T(8,128)(2,1)}) %all-gather.11.cloned.1.call-update) | async-done | bytes 2097168 | tf_op jit(solution)/shard_map/all_gather | solution.py:34
  157.7 3.7 %fusion.5 = bf16[128,1024]{1,0:T(8,128)(2,1)} fusion(bf16[1024,1024]{1,0:T(8,128)(2,1)} %all-gather.11.cloned.1.call-done, bf16[128,1024]{1,0:T(8,128)(2,1)S(1)} %get-tuple-element.5, bf16[128,1024]{1,0:T(8,128)(2,1)} %fusion.4), kind=kOutput, calls=%fused_computation.12 | convolution fusion | flops 537526272 | bytes 2883584 | tf_op jit(solution)/shard_map/dot_general | solution.py:36
  161.4 0.0 all-gather.13.cloned.1.call-update
  161.5 0.0 all-gather.15.cloned.1.call-start
  161.5 28.0 %all-gather.13.cloned.1.call-done = bf16[1024,1024]{1,0:T(8,128)(2,1)} async-done(((bf16[128,1024]{1,0:T(8,128)(2,1)}), bf16[1024,1024]{1,0:T(8,128)(2,1)}) %all-gather.13.cloned.1.call-update) | async-done | bytes 2097168 | tf_op jit(solution)/shard_map/all_gather | solution.py:34
  189.5 3.7 %fusion.6 = bf16[128,1024]{1,0:T(8,128)(2,1)} fusion(bf16[1024,1024]{1,0:T(8,128)(2,1)} %all-gather.13.cloned.1.call-done, bf16[128,1024]{1,0:T(8,128)(2,1)S(1)} %get-tuple-element.5, bf16[128,1024]{1,0:T(8,128)(2,1)} %fusion.5), kind=kOutput, calls=%fused_computation.13 | convolution fusion | flops 537526272 | bytes 2883584 | tf_op jit(solution)/shard_map/dot_general | solution.py:36
  193.2 0.0 all-gather.15.cloned.1.call-update
  193.2 0.0 all-gather.17.cloned.1.call-start
  193.3 28.0 %all-gather.15.cloned.1.call-done = bf16[1024,1024]{1,0:T(8,128)(2,1)} async-done(((bf16[128,1024]{1,0:T(8,128)(2,1)}), bf16[1024,1024]{1,0:T(8,128)(2,1)}) %all-gather.15.cloned.1.call-update) | async-done | bytes 2097168 | tf_op jit(solution)/shard_map/all_gather | solution.py:34
  221.3 3.7 %fusion.7 = bf16[128,1024]{1,0:T(8,128)(2,1)} fusion(bf16[1024,1024]{1,0:T(8,128)(2,1)} %all-gather.15.cloned.1.call-done, bf16[128,1024]{1,0:T(8,128)(2,1)S(1)} %get-tuple-element.5, bf16[128,1024]{1,0:T(8,128)(2,1)} %fusion.6), kind=kOutput, calls=%fused_computation.14 | convolution fusion | flops 537526272 | bytes 2883584 | tf_op jit(solution)/shard_map/dot_general | solution.py:36
  225.0 0.0 all-gather.17.cloned.1.call-update
  225.0 28.1 %all-gather.17.cloned.1.call-done = bf16[1024,1024]{1,0:T(8,128)(2,1)} async-done(((bf16[128,1024]{1,0:T(8,128)(2,1)}), bf16[1024,1024]{1,0:T(8,128)(2,1)}) %all-gather.17.cloned.1.call-update) | async-done | bytes 2097168 | tf_op jit(solution)/shard_map/all_gather | solution.py:41
  253.0 3.4 %fusion.1 = bf16[1,768,1024]{1,2,0:T(8,128)(2,1)S(1)} fusion(bf16[1024,1024]{1,0:T(8,128)(2,1)} %all-gather.17.cloned.1.call-done, bf16[1,768,1024]{2,1,0:T(8,128)(2,1)S(1)} %copy-done), kind=kOutput, calls=%fused_computation.2 | convolution fusion | flops 1611399168 | bytes 5242880 | tf_op jit(solution)/shard_map/dot_general | solution.py:39
  256.5 1.6 copy.5
  (4 shorter events, 0.0 us)
Async XLA Ops:
  6.5 246.5 %copy-start = (bf16[1,768,1024]{2,1,0:T(8,128)(2,1)S(1)}, bf16[1,768,1024]{2,1,0:T(8,128)(2,1)}, u32[]{:S(2)}) copy-start(bf16[1,768,1024]{2,1,0:T(8,128)(2,1)} %param.3) | copy-start | bytes 4718596
  6.5 29.0 %all-gather.7.cloned.1.call-start = ((), (), s32[]{:S(2)}) async-start(), calls=%async_computation.1 | async-start | bytes 1179648 | tf_op jit(solution)/shard_map/all_gather | solution.py:19
  8.3 74.4 %reduce-scatter.2.cloned.1.call-start = ((), (), s32[]{:S(2)}) async-start(), calls=%async_computation.2 | async-start | bytes 2621440 | tf_op jit(solution)/shard_map/reduce_scatter | solution.py:22
  38.7 87.3 %all-gather.9.cloned.1.call-start = ((), (), s32[]{:S(2)}) async-start(), calls=%async_computation.3 | async-start | bytes 2359296 | tf_op jit(solution)/shard_map/all_gather | solution.py:34
  100.2 57.6 %all-gather.11.cloned.1.call-start = ((), (), s32[]{:S(2)}) async-start(), calls=%async_computation.4 | async-start | bytes 2359296 | tf_op jit(solution)/shard_map/all_gather | solution.py:34
  129.7 59.8 %all-gather.13.cloned.1.call-start = ((), (), s32[]{:S(2)}) async-start(), calls=%async_computation.5 | async-start | bytes 2359296 | tf_op jit(solution)/shard_map/all_gather | solution.py:34
  161.5 59.8 %all-gather.15.cloned.1.call-start = ((), (), s32[]{:S(2)}) async-start(), calls=%async_computation.6 | async-start | bytes 2359296 | tf_op jit(solution)/shard_map/all_gather | solution.py:34
  193.2 59.8 %all-gather.17.cloned.1.call-start = ((), (), s32[]{:S(2)}) async-start(), calls=%async_computation.7 | async-start | bytes 2359296 | tf_op jit(solution)/shard_map/all_gather | solution.py:41
Sparse Core Ops, SparseCore 0:
  9.2 26.2 all-gather.6
  38.8 43.8 reduce-scatter.1
  100.3 25.6 all-gather.8
  129.8 27.8 all-gather.10
  161.6 27.8 all-gather.12
  193.3 27.8 all-gather.14
  225.1 27.8 all-gather.16
where the time goes:
time: 265 us
  waiting for transfers between devices  209 us (79%)
  matrix products  21.3 us (8%)
  between operations  14.2 us (5%)
  blocking collectives  14.1 us (5%)
  local copies, waits for them, and re-layouts  3.33 us (1%)
  other arithmetic  2.73 us (1%)
    all_gather x4, waiting for transfers between devices, local(): whole = lax.all_gather(iterate, 'grad', axis=0, tiled=True)  110 us
    reduce_scatter x1, waiting for transfers between devices, local(): lax.psum_scatter(partial_value, 'dp', scatter_dimension=0, tiled=True)  43.9 us
    all_gather x1, waiting for transfers between devices, local(): lax.all_gather(iterate, 'grad', axis=0, tiled=True)  28.1 us
    all_gather x1, waiting for transfers between devices, local(): lax.all_gather(factor_inputs, 'grad', axis=2, tiled=True)  27.2 us
    dot_general x4, matrix products, local(): product = jnp.dot(image, whole, preferred_element_type=jnp.float32)  14.8 us
    pmax x1, blocking collectives, local(): bound = lax.pmax(jnp.max(jnp.sum(jnp.abs(damped), axis=1)), 'grad')  14.1 us
  transfers between devices with their start and end apart: 7, of which 7 were waited for; matrix products, arithmetic and copies ran while one was open for 0% of the time, Pallas kernels for 0%

commit v1 on v0

v1 whole, which is shorter than its diff:
```python
import jax
import jax.numpy as jnp
from jax import lax
from jax.sharding import PartitionSpec as P

ITERS = 4
DAMPING = 0.01
TERMS = 2**ITERS


def gather_block(factor_inputs):
    pieces = jnp.transpose(factor_inputs, (1, 0, 2))
    piece = lax.all_to_all(pieces, "dp", split_axis=0, concat_axis=1, tiled=True)[0]
    return lax.all_gather(piece, "grad", axis=1, tiled=True)


def gather_block_by_steps(factor_inputs):
    replicas, members = lax.axis_size("dp"), lax.axis_size("grad")
    here, member = lax.axis_index("dp"), lax.axis_index("grad")
    pieces = jnp.transpose(factor_inputs, (1, 0, 2))
    parts = []
    for step in range(replicas):
        there = lax.rem(here + step, replicas)
        part = lax.dynamic_index_in_dim(pieces, there, 0, keepdims=False)
        if step:
            part = lax.ppermute(part, "dp", [(i, (i + step) % replicas) for i in range(replicas)])
        parts.append(part)
    held = [jnp.concatenate(parts, axis=0)]
    for far in range(2, members, 2):
        held.append(lax.ppermute(held[0], "grad", [(i, i ^ far) for i in range(members)]))
    near = [lax.ppermute(one, "grad", [(i, i ^ 1) for i in range(members)]) for one in held]
    stacked = jnp.stack([one for pair in zip(held, near) for one in pair])
    ordered = stacked[jnp.arange(members) ^ member]
    return jnp.transpose(ordered, (1, 0, 2)).reshape(ordered.shape[1], -1)


def largest_row(columns, tokens):
    covariance = jnp.einsum("tr,tc->rc", columns, columns, preferred_element_type=jnp.float32)
    return jnp.max(jnp.sum(jnp.abs(covariance), axis=1)) * (1.0 / tokens) + DAMPING


def times(a, b):
    product = jnp.dot(a[1].astype(jnp.bfloat16), b[1].astype(jnp.bfloat16), preferred_element_type=jnp.float32)
    return a[0] * b[0], a[0] * b[1] + b[0] * a[1] + product


def by_tokens(columns, tile):
    tokens = columns.shape[0]
    scale = 1.0 / largest_row(columns, tokens)
    gram = jnp.einsum("sc,tc->st", columns, columns, preferred_element_type=jnp.float32)
    image = jnp.einsum("rc,tc->rt", tile, columns, preferred_element_type=jnp.float32).astype(jnp.bfloat16)
    eps = 1.0 - scale * DAMPING
    sums = [jnp.float32(1.0)]
    for _ in range(TERMS - 1):
        sums.append(sums[-1] * eps + 1.0)
    powers = [(jnp.float32(1.0), None), (eps, gram * (-scale / tokens))]
    powers.append(times(powers[1], powers[1]))
    powers.append(times(powers[2], powers[1]))
    fourth = times(powers[2], powers[2])

    def block(i):
        shift, rest = sums[14 - 4 * i], 0.0
        for j in range(1, 4):
            if 4 * i + j < TERMS - 1:
                weight = sums[14 - 4 * i - j]
                shift, rest = shift + weight * powers[j][0], rest + weight * powers[j][1]
        return shift, rest

    total = block(3)
    for i in (2, 1, 0):
        product, own = times(total, fourth), block(i)
        total = product[0] + own[0], product[1] + own[1]
    mixed = jnp.dot(image, total[1].astype(jnp.bfloat16), preferred_element_type=jnp.float32)
    mixed = (mixed + total[0] * image.astype(jnp.float32)) * (-scale * scale / tokens)
    moved = jnp.dot(mixed.astype(jnp.bfloat16), columns, preferred_element_type=jnp.float32)
    return scale * sums[TERMS - 1] * tile.astype(jnp.float32) + moved


def by_features(columns, tile):
    tokens, width = columns.shape
    scale = 1.0 / largest_row(columns, tokens)
    covariance = jnp.einsum("tr,tc->rc", columns, columns, preferred_element_type=jnp.float32) * (1.0 / tokens)
    image = scale * (covariance + DAMPING * jnp.eye(width, dtype=jnp.float32))
    result = scale * tile.astype(jnp.float32)
    for step in range(ITERS):
        low = image.astype(jnp.bfloat16)
        result = 2.0 * result - jnp.dot(result.astype(jnp.bfloat16), low, preferred_element_type=jnp.float32)
        if step < ITERS - 1:
            image = 2.0 * image - jnp.dot(low, low, preferred_element_type=jnp.float32)
    return result


def local(factor_inputs, gradients):
    rows, members = factor_inputs.shape[2], lax.axis_size("grad")
    tokens = factor_inputs.shape[0] * lax.axis_size("dp")
    tile = gradients[0]
    if tokens < rows * members:
        result = by_tokens(gather_block_by_steps(factor_inputs), tile)
    else:
        result = by_features(gather_block(factor_inputs), tile)
    return result.astype(jnp.bfloat16)[None]


def solution(mesh):
    placed = (P("dp", None, "grad"), P("dp", "grad", None))
    return jax.shard_map(
        local, mesh=mesh, in_specs=placed, out_specs=P("dp", "grad", None), check_vma=False
    )
```

time: 265 us -> 42.2 us (0.16)
  waiting for transfers between devices: 209 us -> 9.76 us
  blocking collectives: 14.1 us -> 0 us
  between operations: 14.2 us -> 0.98 us
  starting transfers between devices: 0.25 us -> 11.2 us
  matrix products: 21.3 us -> 16.3 us
    all_gather x6 -> x0, waiting for transfers between devices: 165 us -> none  [the longest x4 110 us: local(): whole = lax.all_gather(iterate, 'grad', axis=0, tiled=True)]
    reduce_scatter x1 -> x0, waiting for transfers between devices: 43.9 us -> none  [local(): lax.psum_scatter(partial_value, 'dp', scatter_dimension=0, tiled=True)]
    pmax x1 -> x0, blocking collectives: 14.1 us -> none  [local(): bound = lax.pmax(jnp.max(jnp.sum(jnp.abs(damped), axis=1)), 'grad')]
    ppermute x0 -> x10, starting transfers between devices: none -> 11.2 us  [the longest x3 7.01 us: gather_block_by_steps(): lax.ppermute(part, 'dp', [(i, (i + step) % replicas) for i in range(repli...]
    ppermute x0 -> x10, waiting for transfers between devices: none -> 9.76 us  [the longest x3 6.36 us: gather_block_by_steps(): lax.ppermute(held[0], 'grad', [(i, i ^ far) for i in range(members)])]
    dot_general x6 -> x10, matrix products: 21.3 us -> 16.3 us  [the longest x1 4.49 us: by_tokens(): jnp.dot(image, total[1].astype(jnp.bfloat16), preferred_element_type=jnp....]
  transfers between devices with their start and end apart: 7 -> 10, of which waited for: 7 -> 6; matrix products, arithmetic and copies ran while one was open for 0% -> 0% of each run, Pallas kernels for 0% -> 0%
where the time goes in v1:
time: 42.2 us; the launch traced here: 42 us
  matrix products  16.3 us (39%)
  starting transfers between devices  11.2 us (27%)
  waiting for transfers between devices  9.76 us (23%)
  local copies, waits for them, and re-layouts  3.17 us (8%)
  between operations  0.98 us (2%)
  other arithmetic  0.63 us (1%)
    ppermute x3, starting transfers between devices, gather_block_by_steps(): lax.ppermute(part, 'dp', [(i, (i + step) % replicas) for i in range(repli...  7.01 us
    ppermute x3, waiting for transfers between devices, gather_block_by_steps(): lax.ppermute(held[0], 'grad', [(i, i ^ far) for i in range(members)])  6.36 us
    dot_general x1, matrix products, by_tokens(): jnp.dot(image, total[1].astype(jnp.bfloat16), preferred_element_type=jnp....  4.49 us
    dot_general x1, matrix products, by_tokens(): jnp.dot(mixed.astype(jnp.bfloat16), columns, preferred_element_type=jnp.f...  4.14 us
    dot_general x5, matrix products, times(): jnp.dot(a[1].astype(jnp.bfloat16), b[1].astype(jnp.bfloat16), preferred_e...  3.71 us
    ppermute x3, starting transfers between devices, gather_block_by_steps(): lax.ppermute(held[0], 'grad', [(i, i ^ far) for i in range(members)])  3.55 us
    ppermute x3, waiting for transfers between devices, gather_block_by_steps(): lax.ppermute(part, 'dp', [(i, (i + step) % replicas) for i in range(repli...  2.54 us
    dot_general x1, matrix products, by_tokens(): jnp.einsum('rc,tc->rt', tile, columns, preferred_element_type=jnp.float32)  1.93 us
  transfers between devices with their start and end apart: 10, of which 6 were waited for; matrix products, arithmetic and copies ran while one was open for 0% of the time, Pallas kernels for 0%

profile of v1, /device:TPU:0, one launch (start us, length us, event | category | flops | bytes accessed | tf_op | source)
XLA Modules:
  0.0 42.0 jit_solution(7813290677083671489)
XLA Ops:
  0.0 1.5 %constant_dynamic-slice_fusion.3 = (bf16[128,1,128]{2,1,0:T(2,128)(2,1)S(1)}, bf16[128,1,128]{2,1,0:T(2,128)(2,1)S(1)}, bf16[128,1,128]{2,1,0:T(2,128)(2,1)S(1)}, bf16[128,1,128]{2,1,0:T(2,128)(2,1)S(1)}) fusion(bf16[128,4,128]{2,1,0:T(4,128)(2,1)} %param.2, s32[]{:T(128)S(6)} %select_n.23, s32[]{:T(128)S(6)} %select_n.25, s32[]{:T(128)S(6)} %select_n.24, ...), kind=kLoop, calls=%fused_computation.62 | loop fusion | bytes 262160 | tf_op jit(solution)/shard_map/dynamic-slice
  1.5 3.1 %collective-permute-start = (bf16[128,128]{1,0:T(8,128)(2,1)S(1)}, bf16[128,128]{1,0:T(8,128)(2,1)S(1)}, u32[]{:S(2)}, u32[]{:S(2)}) collective-permute-start(bf16[128,128]{1,0:T(8,128)(2,1)S(1)} %bitcast.66), channel_id=1, source_target_pairs={{0,8},{8,16},{16,24},{24,0},{1,9},{9,17},{17,25},{25,1},{2,10},{10... | collective-permute-start | bytes 98312 | tf_op jit(solution)/shard_map/ppermute | solution.py:26
  4.6 2.6 %collective-permute-start.1 = (bf16[128,128]{1,0:T(8,128)(2,1)S(1)}, bf16[128,128]{1,0:T(8,128)(2,1)S(1)}, u32[]{:S(2)}, u32[]{:S(2)}) collective-permute-start(bf16[128,128]{1,0:T(8,128)(2,1)S(1)} %bitcast.67), channel_id=1, source_target_pairs={{0,16},{8,24},{16,0},{24,8},{1,17},{9,25},{17,1},{25,9},{2,18},{10... | collective-permute-start | bytes 98312 | tf_op jit(solution)/shard_map/ppermute | solution.py:26
  7.2 1.3 %collective-permute-start.2 = (bf16[128,128]{1,0:T(8,128)(2,1)S(1)}, bf16[128,128]{1,0:T(8,128)(2,1)S(1)}, u32[]{:S(2)}, u32[]{:S(2)}) collective-permute-start(bf16[128,128]{1,0:T(8,128)(2,1)S(1)} %bitcast.68), channel_id=1, source_target_pairs={{0,24},{8,0},{16,8},{24,16},{1,25},{9,1},{17,9},{25,17},{2,26},{10... | collective-permute-start | bytes 98312 | tf_op jit(solution)/shard_map/ppermute | solution.py:26
  8.6 1.2 %collective-permute-done.1 = bf16[128,128]{1,0:T(8,128)(2,1)S(1)} collective-permute-done((bf16[128,128]{1,0:T(8,128)(2,1)S(1)}, bf16[128,128]{1,0:T(8,128)(2,1)S(1)}, u32[]{:S(2)}, u32[]{:S(2)}) %collective-permute-start.1) | collective-permute-done | bytes 32800 | tf_op jit(solution)/shard_map/ppermute | solution.py:26
  9.8 1.3 %collective-permute-done.2 = bf16[128,128]{1,0:T(8,128)(2,1)S(1)} collective-permute-done((bf16[128,128]{1,0:T(8,128)(2,1)S(1)}, bf16[128,128]{1,0:T(8,128)(2,1)S(1)}, u32[]{:S(2)}, u32[]{:S(2)}) %collective-permute-start.2) | collective-permute-done | bytes 32800 | tf_op jit(solution)/shard_map/ppermute | solution.py:26
  11.1 0.1 collective-permute-start.3
  11.2 1.6 %collective-permute-start.4 = (bf16[512,128]{1,0:T(8,128)(2,1)S(1)}, bf16[512,128]{1,0:T(8,128)(2,1)S(1)}, u32[]{:S(2)}, u32[]{:S(2)}) collective-permute-start(bf16[512,128]{1,0:T(8,128)(2,1)S(1)} %pad_maximum_fusion), channel_id=1, source_target_pairs={{0,2},{1,3},{2,0},{3,1},{4,6},{5,7},{6,4},{7,5},{8,10},{9,11},{10,... | collective-permute-start | bytes 393224 | tf_op jit(solution)/shard_map/ppermute | solution.py:30
  12.8 1.5 %collective-permute-start.6 = (bf16[512,128]{1,0:T(8,128)(2,1)S(1)}, bf16[512,128]{1,0:T(8,128)(2,1)S(1)}, u32[]{:S(2)}, u32[]{:S(2)}) collective-permute-start(bf16[512,128]{1,0:T(8,128)(2,1)S(1)} %pad_maximum_fusion), channel_id=1, source_target_pairs={{0,4},{1,5},{2,6},{3,7},{4,0},{5,1},{6,2},{7,3},{8,12},{9,13},{10,... | collective-permute-start | bytes 393224 | tf_op jit(solution)/shard_map/ppermute | solution.py:30
  14.3 0.5 %collective-permute-start.8 = (bf16[512,128]{1,0:T(8,128)(2,1)S(1)}, bf16[512,128]{1,0:T(8,128)(2,1)S(1)}, u32[]{:S(2)}, u32[]{:S(2)}) collective-permute-start(bf16[512,128]{1,0:T(8,128)(2,1)S(1)} %pad_maximum_fusion), channel_id=1, source_target_pairs={{0,6},{1,7},{2,4},{3,5},{4,2},{5,3},{6,0},{7,1},{8,14},{9,15},{10,... | collective-permute-start | bytes 393224 | tf_op jit(solution)/shard_map/ppermute | solution.py:30
  14.8 2.7 %collective-permute-done.4 = bf16[512,128]{1,0:T(8,128)(2,1)S(1)} collective-permute-done((bf16[512,128]{1,0:T(8,128)(2,1)S(1)}, bf16[512,128]{1,0:T(8,128)(2,1)S(1)}, u32[]{:S(2)}, u32[]{:S(2)}) %collective-permute-start.4) | collective-permute-done | bytes 131104 | tf_op jit(solution)/shard_map/ppermute | solution.py:30
  17.5 0.0 collective-permute-start.5
  17.5 3.7 %collective-permute-done.6 = bf16[512,128]{1,0:T(8,128)(2,1)S(1)} collective-permute-done((bf16[512,128]{1,0:T(8,128)(2,1)S(1)}, bf16[512,128]{1,0:T(8,128)(2,1)S(1)}, u32[]{:S(2)}, u32[]{:S(2)}) %collective-permute-start.6) | collective-permute-done | bytes 131104 | tf_op jit(solution)/shard_map/ppermute | solution.py:30
  21.2 0.5 %collective-permute-start.9 = (bf16[512,128]{1,0:T(8,128)(2,1)S(1)}, bf16[512,128]{1,0:T(8,128)(2,1)S(1)}, u32[]{:S(2)}, u32[]{:S(2)}) collective-permute-start(bf16[512,128]{1,0:T(8,128)(2,1)S(1)} %collective-permute-done.8), channel_id=1, source_target_pairs={{0,1},{1,0},{2,3},{3,2},{4,5},{5,4},{6,7},{7,6},{8,9},{9,8},{10,11... | collective-permute-start | bytes 393224 | tf_op jit(solution)/shard_map/ppermute | solution.py:31
  21.8 0.7 %collective-permute-done.7 = bf16[512,128]{1,0:T(8,128)(2,1)S(1)} collective-permute-done((bf16[512,128]{1,0:T(8,128)(2,1)S(1)}, bf16[512,128]{1,0:T(8,128)(2,1)S(1)}, u32[]{:S(2)}, u32[]{:S(2)}) %collective-permute-start.7) | collective-permute-done | bytes 131104 | tf_op jit(solution)/shard_map/ppermute | solution.py:31
  22.5 0.1 collective-permute-done.9
  22.7 0.7 %gather_fusion = bf16[8,512,128]{2,1,0:T(8,128)(2,1)S(1)} fusion(bf16[8,512,128]{2,1,0:T(8,128)(2,1)S(1)} %bitcast_dynamic-update-slice_fusion, s32[1024]{0:T(1024)S(1)} %pad_clamp_fusion), kind=kCustom, calls=%fused_computation | custom fusion | bytes 2097184 | tf_op jit(solution)/shard_map/gather | solution.py:33
  23.5 0.5 %copy.7 = bf16[512,8,128]{0,2,1:T(8,128)(2,1)S(1)} copy(bf16[512,8,128]{2,0,1:T(8,128)(2,1)S(1)} %bitcast.60) | data formatting | bytes 2097152 | tf_op jit(solution)/shard_map/transpose | solution.py:34
  24.0 1.3 %abs_reduce_fusion = f32[1024]{0:T(1024)S(1)} fusion(bf16[512,1024]{0,1:T(8,128)(2,1)S(1)} %bitcast.61), kind=kOutput, calls=%fused_computation.1 | convolution fusion | flops 1075837952 | bytes 1052672 | tf_op jit(solution)/shard_map/tr,tc->rc/dot_general | solution.py:38
  25.3 0.6 %reduce_max.9 = f32[]{:T(128)} reduce(f32[1024]{0:T(1024)S(1)} %abs_reduce_fusion, f32[]{:T(128)} %constant.49.clone.1), dimensions={0}, to_apply=%region_1.2 | reduce | flops 1023 | bytes 4104 | tf_op jit(solution)/shard_map/reduce_max | solution.py:39
  26.7 0.7 %fusion.11 = f32[512,512]{1,0:T(8,128)S(1)} fusion(f32[]{:T(128)S(6)} %div.10, bf16[8,512,128]{2,1,0:T(8,128)(2,1)S(1)} %gather_fusion), kind=kOutput, calls=%fused_computation.20 | convolution fusion | flops 537133056 | bytes 2097156 | tf_op jit(solution)/shard_map/sc,tc->st/dot_general | solution.py:50
  27.4 0.4 %convolution_add_fusion.5 = f32[512,512]{1,0:T(8,128)S(1)} fusion(f32[512,512]{1,0:T(8,128)S(1)} %fusion.11, f32[]{:T(128)S(6)} %add.260), kind=kOutput, calls=%fused_computation.18 | convolution fusion | flops 269221888 | bytes 2097156 | tf_op jit(solution)/shard_map/dot_general | solution.py:43
  27.9 0.4 %convolution_add_fusion.2 = f32[512,512]{1,0:T(8,128)S(1)} fusion(f32[512,512]{1,0:T(8,128)S(1)} %convolution_add_fusion.5, f32[512,512]{1,0:T(8,128)S(1)} %fusion.11, f32[]{:T(128)S(6)} %sub.3, f32[]{:T(128)S(6)} %mul.256), kind=kOutput, calls=%fused_computation.14 | convolution fusion | flops 270008320 | bytes 3145736 | tf_op jit(solution)/shard_map/dot_general | solution.py:43
  28.3 0.0 copy-start
  28.4 0.4 %convolution_add_fusion.4 = f32[512,512]{1,0:T(8,128)S(1)} fusion(f32[512,512]{1,0:T(8,128)S(1)} %convolution_add_fusion.5, f32[]{:T(128)S(6)} %add.259), kind=kOutput, calls=%fused_computation.17 | convolution fusion | flops 269221888 | bytes 2097156 | tf_op jit(solution)/shard_map/dot_general | solution.py:43
  28.8 0.7 %fusion.10 = f32[512,512]{1,0:T(8,128)S(1)} fusion(f32[512,512]{1,0:T(8,128)S(1)} %convolution_add_fusion.2, f32[512,512]{1,0:T(8,128)S(1)} %convolution_add_fusion.5, f32[512,512]{1,0:T(8,128)S(1)} %fusion.11, f32[512,512]{1,0:T(8,128)S(1)} %convolution_add_fusion.4, f32[]{:T(128)S(6)} %add.206, f32[]{:T(128)S(6)} %add.207, f32[]{:T(128)S(6)} %add.208, ...), kind=kOutput, calls=%fused_computation.16 | convolution fusion | flops 272629760 | bytes 5242904 | tf_op jit(solution)/shard_map/dot_general | solution.py:43
  29.5 0.0 copy-start.3
  29.5 1.7 %fusion.9 = f32[512,512]{1,0:T(8,128)} fusion(f32[512,512]{1,0:T(8,128)S(1)} %convolution_add_fusion.2, f32[512,512]{1,0:T(8,128)S(1)} %convolution_add_fusion.5, f32[512,512]{1,0:T(8,128)S(1)} %fusion.11, f32[512,512]{1,0:T(8,128)S(1)} %fusion.10, f32[512,512]{1,0:T(8,128)S(1)} %convolution_add_fusion.4, f32[]{:T(128)S(6)} %add.210, f32[]{:T(128)S(6)} %add.211, ...), kind=kOutput, calls=%fused_computation.13 | convolution fusion | flops 271581184 | bytes 6291476 | tf_op jit(solution)/shard_map/dot_general | solution.py:43
  31.2 0.2 copy-done.3
  31.4 1.9 %fusion.5 = bf16[512,768]{1,0:T(8,128)(2,1)} fusion(bf16[512,1024]{0,1:T(8,128)(2,1)S(1)} %bitcast.63, bf16[1,768,1024]{2,1,0:T(8,128)(2,1)S(1)} %copy-done.3), kind=kOutput, calls=%fused_computation.9 | convolution fusion | flops 805699584 | bytes 3407872 | tf_op jit(solution)/shard_map/rc,tc->rt/dot_general | solution.py:51
  33.4 4.5 %fusion.1 = bf16[768,512]{0,1:T(8,128)(2,1)} fusion(bf16[512,768]{1,0:T(8,128)(2,1)} %fusion.5, f32[512,512]{1,0:T(8,128)} %copy-done, f32[512,512]{1,0:T(8,128)S(1)} %convolution_add_fusion.5, f32[512,512]{1,0:T(8,128)S(1)} %fusion.11, f32[512,512]{1,0:T(8,128)} %fusion.9, f32[512,512]{1,0:T(8,128)S(1)} %convolution_add_fusion.4, f32[]{:T(128)S(6)} %div.11, ...), kind=kOutput, calls=%fused_computation.5 | convolution fusion | flops 676462592 | bytes 6815772 | tf_op jit(solution)/shard_map/dot_general | solution.py:73
  37.8 4.1 %fusion.4 = bf16[1,768,1024]{2,1,0:T(8,128)(2,1)} fusion(bf16[768,512]{0,1:T(8,128)(2,1)} %fusion.1, bf16[512,1024]{0,1:T(8,128)(2,1)} %bitcast.62, bf16[1,768,1024]{2,1,0:T(8,128)(2,1)} %param.3, f32[]{:T(128)S(6)} %mul.253), kind=kOutput, calls=%fused_computation.8 | convolution fusion | flops 808452096 | bytes 4980740 | tf_op jit(solution)/shard_map/dot_general | solution.py:75
  (25 shorter events, 0.2 us)
Async XLA Ops:
  1.5 7.0 %collective-permute-start = (bf16[128,128]{1,0:T(8,128)(2,1)S(1)}, bf16[128,128]{1,0:T(8,128)(2,1)S(1)}, u32[]{:S(2)}, u32[]{:S(2)}) collective-permute-start(bf16[128,128]{1,0:T(8,128)(2,1)S(1)} %bitcast.66), channel_id=1, source_target_pairs={{0,8},{8,16},{16,24},{24,0},{1,9},{9,17},{17,25},{25,1},{2,10},{10... | collective-permute-start | bytes 98312 | tf_op jit(solution)/shard_map/ppermute | solution.py:26
  4.6 5.2 %collective-permute-start.1 = (bf16[128,128]{1,0:T(8,128)(2,1)S(1)}, bf16[128,128]{1,0:T(8,128)(2,1)S(1)}, u32[]{:S(2)}, u32[]{:S(2)}) collective-permute-start(bf16[128,128]{1,0:T(8,128)(2,1)S(1)} %bitcast.67), channel_id=1, source_target_pairs={{0,16},{8,24},{16,0},{24,8},{1,17},{9,25},{17,1},{25,9},{2,18},{10... | collective-permute-start | bytes 98312 | tf_op jit(solution)/shard_map/ppermute | solution.py:26
  7.2 3.9 %collective-permute-start.2 = (bf16[128,128]{1,0:T(8,128)(2,1)S(1)}, bf16[128,128]{1,0:T(8,128)(2,1)S(1)}, u32[]{:S(2)}, u32[]{:S(2)}) collective-permute-start(bf16[128,128]{1,0:T(8,128)(2,1)S(1)} %bitcast.68), channel_id=1, source_target_pairs={{0,24},{8,0},{16,8},{24,16},{1,25},{9,1},{17,9},{25,17},{2,26},{10... | collective-permute-start | bytes 98312 | tf_op jit(solution)/shard_map/ppermute | solution.py:26
  11.1 10.5 %collective-permute-start.3 = (bf16[512,128]{1,0:T(8,128)(2,1)S(1)}, bf16[512,128]{1,0:T(8,128)(2,1)S(1)}, u32[]{:S(2)}, u32[]{:S(2)}) collective-permute-start(bf16[512,128]{1,0:T(8,128)(2,1)S(1)} %pad_maximum_fusion), channel_id=1, source_target_pairs={{0,1},{1,0},{2,3},{3,2},{4,5},{5,4},{6,7},{7,6},{8,9},{9,8},{10,11... | collective-permute-start | bytes 393224 | tf_op jit(solution)/shard_map/ppermute | solution.py:31
  11.2 6.3 %collective-permute-start.4 = (bf16[512,128]{1,0:T(8,128)(2,1)S(1)}, bf16[512,128]{1,0:T(8,128)(2,1)S(1)}, u32[]{:S(2)}, u32[]{:S(2)}) collective-permute-start(bf16[512,128]{1,0:T(8,128)(2,1)S(1)} %pad_maximum_fusion), channel_id=1, source_target_pairs={{0,2},{1,3},{2,0},{3,1},{4,6},{5,7},{6,4},{7,5},{8,10},{9,11},{10,... | collective-permute-start | bytes 393224 | tf_op jit(solution)/shard_map/ppermute | solution.py:30
  12.8 8.4 %collective-permute-start.6 = (bf16[512,128]{1,0:T(8,128)(2,1)S(1)}, bf16[512,128]{1,0:T(8,128)(2,1)S(1)}, u32[]{:S(2)}, u32[]{:S(2)}) collective-permute-start(bf16[512,128]{1,0:T(8,128)(2,1)S(1)} %pad_maximum_fusion), channel_id=1, source_target_pairs={{0,4},{1,5},{2,6},{3,7},{4,0},{5,1},{6,2},{7,3},{8,12},{9,13},{10,... | collective-permute-start | bytes 393224 | tf_op jit(solution)/shard_map/ppermute | solution.py:30
  14.3 6.9 %collective-permute-start.8 = (bf16[512,128]{1,0:T(8,128)(2,1)S(1)}, bf16[512,128]{1,0:T(8,128)(2,1)S(1)}, u32[]{:S(2)}, u32[]{:S(2)}) collective-permute-start(bf16[512,128]{1,0:T(8,128)(2,1)S(1)} %pad_maximum_fusion), channel_id=1, source_target_pairs={{0,6},{1,7},{2,4},{3,5},{4,2},{5,3},{6,0},{7,1},{8,14},{9,15},{10,... | collective-permute-start | bytes 393224 | tf_op jit(solution)/shard_map/ppermute | solution.py:30
  17.5 4.2 %collective-permute-start.5 = (bf16[512,128]{1,0:T(8,128)(2,1)S(1)}, bf16[512,128]{1,0:T(8,128)(2,1)S(1)}, u32[]{:S(2)}, u32[]{:S(2)}) collective-permute-start(bf16[512,128]{1,0:T(8,128)(2,1)S(1)} %collective-permute-done.4), channel_id=1, source_target_pairs={{0,1},{1,0},{2,3},{3,2},{4,5},{5,4},{6,7},{7,6},{8,9},{9,8},{10,11... | collective-permute-start | bytes 393224 | tf_op jit(solution)/shard_map/ppermute | solution.py:31
  21.1 1.3 %collective-permute-start.7 = (bf16[512,128]{1,0:T(8,128)(2,1)S(1)}, bf16[512,128]{1,0:T(8,128)(2,1)S(1)}, u32[]{:S(2)}, u32[]{:S(2)}) collective-permute-start(bf16[512,128]{1,0:T(8,128)(2,1)S(1)} %collective-permute-done.6), channel_id=1, source_target_pairs={{0,1},{1,0},{2,3},{3,2},{4,5},{5,4},{6,7},{7,6},{8,9},{9,8},{10,11... | collective-permute-start | bytes 393224 | tf_op jit(solution)/shard_map/ppermute | solution.py:31
  21.2 1.5 %collective-permute-start.9 = (bf16[512,128]{1,0:T(8,128)(2,1)S(1)}, bf16[512,128]{1,0:T(8,128)(2,1)S(1)}, u32[]{:S(2)}, u32[]{:S(2)}) collective-permute-start(bf16[512,128]{1,0:T(8,128)(2,1)S(1)} %collective-permute-done.8), channel_id=1, source_target_pairs={{0,1},{1,0},{2,3},{3,2},{4,5},{5,4},{6,7},{7,6},{8,9},{9,8},{10,11... | collective-permute-start | bytes 393224 | tf_op jit(solution)/shard_map/ppermute | solution.py:31
  24.0 1.3 %copy-start.1 = (bf16[512,8,128]{0,2,1:T(8,128)(2,1)}, bf16[512,8,128]{0,2,1:T(8,128)(2,1)S(1)}, u32[]{:S(2)}) copy-start(bf16[512,8,128]{0,2,1:T(8,128)(2,1)S(1)} %copy.7) | copy-start | bytes 3145732
  28.3 1.1 %copy-start = (f32[512,512]{1,0:T(8,128)}, f32[512,512]{1,0:T(8,128)S(1)}, u32[]{:S(2)}) copy-start(f32[512,512]{1,0:T(8,128)S(1)} %convolution_add_fusion.2) | copy-start | bytes 3145732
  29.5 1.7 %copy-start.2 = (bf16[512,8,128]{0,2,1:T(8,128)(2,1)S(1)}, bf16[512,8,128]{0,2,1:T(8,128)(2,1)}, u32[]{:S(2)}) copy-start(bf16[512,8,128]{0,2,1:T(8,128)(2,1)} %copy-done.1) | copy-start | bytes 3145732
  29.5 1.9 %copy-start.3 = (bf16[1,768,1024]{2,1,0:T(8,128)(2,1)S(1)}, bf16[1,768,1024]{2,1,0:T(8,128)(2,1)}, u32[]{:S(2)}) copy-start(bf16[1,768,1024]{2,1,0:T(8,128)(2,1)} %param.3) | copy-start | bytes 4718596

commit v2 on v0

v2 whole, which is shorter than its diff:
```python
import functools

import jax
import jax.numpy as jnp
from jax import lax
from jax.experimental import pallas as pl
from jax.experimental.pallas import tpu as pltpu
from jax.sharding import PartitionSpec as P

ITERS = 4
DAMPING = 0.01
WHOLE = pl.BlockSpec(memory_space=pltpu.VMEM)
ANYWHERE = pl.BlockSpec(memory_space=pl.ANY)


def dot(a, b):
    return jnp.dot(a, b, preferred_element_type=jnp.float32)


def gather_block(factor_inputs):
    pieces = jnp.transpose(factor_inputs, (1, 0, 2))
    piece = lax.all_to_all(pieces, "dp", split_axis=0, concat_axis=1, tiled=True)[0]
    return lax.all_gather(piece, "grad", axis=1, tiled=True)


def by_features(columns, tile):
    tokens, width = columns.shape
    covariance = jnp.einsum("tr,tc->rc", columns, columns, preferred_element_type=jnp.float32) * (1.0 / tokens)
    damped = covariance + DAMPING * jnp.eye(width, dtype=jnp.float32)
    scale = 1.0 / jnp.max(jnp.sum(jnp.abs(damped), axis=1))
    image = scale * damped
    result = scale * tile.astype(jnp.float32)
    for step in range(ITERS):
        low = image.astype(jnp.bfloat16)
        result = 2.0 * result - dot(result.astype(jnp.bfloat16), low)
        if step < ITERS - 1:
            image = 2.0 * image - dot(low, low)
    return result


def split_blocks(factor_inputs):
    tokens, blocks, features = factor_inputs.shape

    def kernel(x_ref, out_ref):
        for block in range(blocks):
            out_ref[block] = x_ref[:, block, :]

    return pl.pallas_call(
        kernel,
        out_shape=jax.ShapeDtypeStruct((blocks, tokens, features), factor_inputs.dtype),
        in_specs=[WHOLE],
        out_specs=WHOLE,
    )(factor_inputs)


def block_kernel(count, *refs):
    pieces = refs[:count]
    tile_hbm, out_hbm = refs[count : count + 2]
    x, xt, tile, image, out, sems = refs[count + 2 :]
    tokens, width = x.shape
    rows = tile.shape[0]
    step = rows // 3
    features = width // count
    member = lax.axis_index("grad")
    load = pltpu.make_async_copy(tile_hbm, tile, sems.at[0])
    load.start()
    for far in range(count):
        at = pl.multiple_of((member ^ far) * features, features)
        piece = pieces[far][...]
        x[:, pl.ds(at, features)] = piece
        xt[pl.ds(at, features), :] = piece.T
    gram = dot(x[...], xt[...]) * (1.0 / tokens)
    low = gram.astype(jnp.bfloat16)
    second = dot(low, low)
    low2 = second.astype(jnp.bfloat16)
    largest = jnp.zeros((1, 1), jnp.float32)
    for at in range(0, width, 256):
        sums = jnp.sum(jnp.abs(dot(xt[...], x[:, at : at + 256])), axis=0, keepdims=True)
        largest = jnp.maximum(largest, jnp.max(sums, axis=1, keepdims=True))
    third, fourth = dot(low2, low), dot(low2, low2)
    load.wait()
    for at in range(0, rows, step):
        image[at : at + step, :] = dot(tile[at : at + step, :], xt[...]).astype(jnp.bfloat16)

    c = 1.0 / (largest * (1.0 / tokens) + DAMPING)
    eps = 1.0 - c * DAMPING
    eps2 = eps * eps
    eps3 = eps2 * eps
    eps4 = eps2 * eps2
    c2 = c * c
    c3 = c2 * c
    rows_id = lax.broadcasted_iota(jnp.int32, (tokens, tokens), 0)
    cols_id = lax.broadcasted_iota(jnp.int32, (tokens, tokens), 1)
    eye = (rows_id == cols_id).astype(jnp.float32)
    e1 = -c * gram
    e2 = -2.0 * eps * c * gram + c2 * second
    e3 = -3.0 * eps2 * c * gram + 3.0 * eps * c2 * second - c3 * third
    e4 = -4.0 * eps3 * c * gram + 6.0 * eps2 * c2 * second - 4.0 * eps * c3 * third + c2 * c2 * fourth
    u_m, u_n = 1.0 + eps + eps2 + eps3, e1 + e2 + e3
    w_m, w_n = 4.0 * eps3, eps2 * e1 + eps * e2 + e3
    a_m, a_n = u_m * w_m, u_m * w_n + w_m * u_n + dot(u_n.astype(jnp.bfloat16), w_n.astype(jnp.bfloat16))
    low4 = e4.astype(jnp.bfloat16)
    y_m = 1.0 + 2.0 * eps4 + 3.0 * eps4 * eps4
    y_n = (1.0 + 3.0 * eps4) * e4 + dot(low4, low4)
    q_m, q_n = a_m * y_m, a_m * y_n + y_m * a_n + dot(a_n.astype(jnp.bfloat16), y_n.astype(jnp.bfloat16))
    v = (1.0 + eps4) * (1.0 + eps4 * eps4)
    q_m = q_m + v * (1.0 + 2.0 * eps + 3.0 * eps2)
    q_n = q_n + v * ((1.0 + eps) * e1 + e2)
    q = ((q_m * eye + q_n) * (-c2 * (1.0 / tokens))).astype(jnp.bfloat16)
    p = c * (1.0 + eps) * (1.0 + eps2) * v
    stores = []
    for k, at in enumerate(range(0, rows, step)):
        mixed = dot(image[at : at + step, :], q).astype(jnp.bfloat16)
        moved = dot(mixed, x[...])
        out[at : at + step, :] = (p * tile[at : at + step, :].astype(jnp.float32) + moved).astype(jnp.bfloat16)
        store = pltpu.make_async_copy(out.at[pl.ds(at, step), :], out_hbm.at[pl.ds(at, step), :], sems.at[1 + k])
        store.start()
        stores.append(store)
    for store in stores:
        store.wait()


def by_tokens(pieces, tile):
    rows, width = tile.shape
    tokens = pieces[0].shape[0]
    return pl.pallas_call(
        functools.partial(block_kernel, len(pieces)),
        out_shape=jax.ShapeDtypeStruct((rows, width), jnp.bfloat16),
        in_specs=[WHOLE] * len(pieces) + [ANYWHERE],
        out_specs=ANYWHERE,
        scratch_shapes=[
            pltpu.VMEM((tokens, width), jnp.bfloat16),
            pltpu.VMEM((width, tokens), jnp.bfloat16),
            pltpu.VMEM((rows, width), jnp.bfloat16),
            pltpu.VMEM((rows, tokens), jnp.bfloat16),
            pltpu.VMEM((rows, width), jnp.bfloat16),
            pltpu.SemaphoreType.DMA((4,)),
        ],
        compiler_params=pltpu.CompilerParams(vmem_limit_bytes=40 * 2**20),
        name="whole_block",
    )(*pieces, tile)


def gather_pieces(factor_inputs):
    members = lax.axis_size("grad")
    parts = lax.all_to_all(split_blocks(factor_inputs), "dp", split_axis=0, concat_axis=0, tiled=True)
    held = [parts.reshape(-1, parts.shape[2])]
    for far in range(2, members, 2):
        held.append(lax.ppermute(held[0], "grad", [(i, i ^ far) for i in range(members)]))
    near = [lax.ppermute(one, "grad", [(i, i ^ 1) for i in range(members)]) for one in held]
    return [one for pair in zip(held, near) for one in pair]


def local(factor_inputs, gradients):
    features, members = factor_inputs.shape[2], lax.axis_size("grad")
    tokens = factor_inputs.shape[0] * lax.axis_size("dp")
    tile = gradients[0]
    if tokens < features * members and features % 128 == 0 and members & (members - 1) == 0:
        result = by_tokens(gather_pieces(factor_inputs), tile)
    else:
        result = by_features(gather_block(factor_inputs), tile)
    return result.astype(jnp.bfloat16)[None]


def solution(mesh):
    placed = (P("dp", None, "grad"), P("dp", "grad", None))
    return jax.shard_map(
        local, mesh=mesh, in_specs=placed, out_specs=P("dp", "grad", None), check_vma=False
    )
```

time: 265 us -> 34.2 us (0.13)
  waiting for transfers between devices: 209 us -> 5.57 us
  matrix products: 21.3 us -> 0 us
  between operations: 14.2 us -> 0.01 us
  Pallas kernels: 0 us -> 10.5 us
  starting transfers between devices: 0.25 us -> 4 us
  other arithmetic: 2.73 us -> 0 us
    all_gather x6 -> x0, waiting for transfers between devices: 165 us -> none  [the longest x4 110 us: local(): whole = lax.all_gather(iterate, 'grad', axis=0, tiled=True)]
    reduce_scatter x1 -> x0, waiting for transfers between devices: 43.9 us -> none  [local(): lax.psum_scatter(partial_value, 'dp', scatter_dimension=0, tiled=True)]
    dot_general x6 -> x0, matrix products: 21.3 us -> none  [the longest x4 14.8 us: local(): product = jnp.dot(image, whole, preferred_element_type=jnp.float32)]
    pmax x1 -> x0, blocking collectives: 14.1 us -> none  [local(): bound = lax.pmax(jnp.max(jnp.sum(jnp.abs(damped), axis=1)), 'grad')]
    all_to_all x0 -> x1, blocking collectives: none -> 12.4 us  [gather_pieces(): lax.all_to_all(split_blocks(factor_inputs), 'dp', split_axis=0, concat_ax...]
    pallas_call x0 -> x2, Pallas kernels: none -> 10.5 us  [the longest x1 8.65 us: by_tokens(): pl.pallas_call(functools.partial(block_kernel, len(pieces)), out_shape=ja...]
    ppermute x0 -> x7, waiting for transfers between devices: none -> 5.57 us  [the longest x3 4.55 us: gather_pieces(): lax.ppermute(held[0], 'grad', [(i, i ^ far) for i in range(members)])]
    ppermute x0 -> x7, starting transfers between devices: none -> 4 us  [the longest x3 3.49 us: gather_pieces(): lax.ppermute(held[0], 'grad', [(i, i ^ far) for i in range(members)])]
  transfers between devices with their start and end apart: 7 -> 7, of which waited for: 7 -> 4; matrix products, arithmetic and copies ran while one was open for 0% -> 0% of each run, Pallas kernels for 0% -> 0%
where the time goes in v2:
time: 34.2 us; the launch traced here: 33.9 us
  blocking collectives  12.4 us (36%)
  Pallas kernels  10.5 us (31%)
  waiting for transfers between devices  5.57 us (16%)
  starting transfers between devices  4 us (12%)
  local copies, waits for them, and re-layouts  1.41 us (4%)
    all_to_all x1, blocking collectives, gather_pieces(): lax.all_to_all(split_blocks(factor_inputs), 'dp', split_axis=0, concat_ax...  12.4 us
    pallas_call x1, Pallas kernels, by_tokens(): pl.pallas_call(functools.partial(block_kernel, len(pieces)), out_shape=ja...  8.65 us
    ppermute x3, waiting for transfers between devices, gather_pieces(): lax.ppermute(held[0], 'grad', [(i, i ^ far) for i in range(members)])  4.55 us
    ppermute x3, starting transfers between devices, gather_pieces(): lax.ppermute(held[0], 'grad', [(i, i ^ far) for i in range(members)])  3.49 us
    pallas_call x1, Pallas kernels, split_blocks(): pl.pallas_call(kernel, out_shape=jax.ShapeDtypeStruct((blocks, tokens, fe...  1.87 us
    unnamed x2, local copies, waits for them, and re-layouts  1.41 us
    ppermute x4, waiting for transfers between devices, gather_pieces(): lax.ppermute(one, 'grad', [(i, i ^ 1) for i in range(members)])  1.02 us
  transfers between devices with their start and end apart: 7, of which 4 were waited for; matrix products, arithmetic and copies ran while one was open for 0% of the time, Pallas kernels for 0%

profile of v2, /device:TPU:0, one launch (start us, length us, event | category | flops | bytes accessed | tf_op | source)
XLA Modules:
  0.0 33.9 jit_solution(13680461652536293619)
XLA Ops:
  0.0 1.9 %shard_map.28 = bf16[4,128,128]{2,1,0:T(8,128)(2,1)} custom-call(bf16[128,4,128]{2,1,0:T(4,128)(2,1)} %x_ref.1), custom_call_target="tpu_custom_call" | custom-call | tf_op jit(solution)/shard_map/pallas_call | solution.py:48
  1.9 12.4 %all_to_all.5 = bf16[4,128,128]{2,1,0:T(8,128)(2,1)S(1)} all-to-all(bf16[4,128,128]{2,1,0:T(8,128)(2,1)} %shard_map.28), channel_id=1, replica_groups=mesh['dp'=4,'grad'=8] {'dp'}, dimensions={0} | all-to-all | bytes 262144 | tf_op jit(solution)/shard_map/all_to_all | solution.py:146
  14.3 2.4 %collective-permute-start.5 = (bf16[512,128]{1,0:T(8,128)(2,1)S(1)}, bf16[512,128]{1,0:T(8,128)(2,1)S(1)}, u32[]{:S(2)}, u32[]{:S(2)}) collective-permute-start(bf16[512,128]{1,0:T(8,128)(2,1)S(1)} %bitcast.4), channel_id=1, source_target_pairs={{0,6},{1,7},{2,4},{3,5},{4,2},{5,3},{6,0},{7,1},{8,14},{9,15},{10,... | collective-permute-start | bytes 393224 | tf_op jit(solution)/shard_map/ppermute | solution.py:149
  16.7 0.5 %collective-permute-start.3 = (bf16[512,128]{1,0:T(8,128)(2,1)S(1)}, bf16[512,128]{1,0:T(8,128)(2,1)S(1)}, u32[]{:S(2)}, u32[]{:S(2)}) collective-permute-start(bf16[512,128]{1,0:T(8,128)(2,1)S(1)} %bitcast.5), channel_id=1, source_target_pairs={{0,4},{1,5},{2,6},{3,7},{4,0},{5,1},{6,2},{7,3},{8,12},{9,13},{10,... | collective-permute-start | bytes 393224 | tf_op jit(solution)/shard_map/ppermute | solution.py:149
  17.2 0.5 %collective-permute-start.1 = (bf16[512,128]{1,0:T(8,128)(2,1)S(1)}, bf16[512,128]{1,0:T(8,128)(2,1)S(1)}, u32[]{:S(2)}, u32[]{:S(2)}) collective-permute-start(bf16[512,128]{1,0:T(8,128)(2,1)S(1)} %bitcast.6), channel_id=1, source_target_pairs={{0,2},{1,3},{2,0},{3,1},{4,6},{5,7},{6,4},{7,5},{8,10},{9,11},{10,... | collective-permute-start | bytes 393224 | tf_op jit(solution)/shard_map/ppermute | solution.py:149
  17.8 0.0 collective-permute-start
  17.8 3.7 %collective-permute-done.5.refs_6_ = bf16[512,128]{1,0:T(8,128)(2,1)S(1)} collective-permute-done((bf16[512,128]{1,0:T(8,128)(2,1)S(1)}, bf16[512,128]{1,0:T(8,128)(2,1)S(1)}, u32[]{:S(2)}, u32[]{:S(2)}) %collective-permute-start.5) | collective-permute-done | bytes 131104 | tf_op jit(solution)/shard_map/ppermute | solution.py:149
  21.4 0.0 collective-permute-start.6
  21.4 0.9 %collective-permute-done.3.refs_4_ = bf16[512,128]{1,0:T(8,128)(2,1)S(1)} collective-permute-done((bf16[512,128]{1,0:T(8,128)(2,1)S(1)}, bf16[512,128]{1,0:T(8,128)(2,1)S(1)}, u32[]{:S(2)}, u32[]{:S(2)}) %collective-permute-start.3) | collective-permute-done | bytes 131104 | tf_op jit(solution)/shard_map/ppermute | solution.py:149
  22.3 0.0 collective-permute-start.4
  22.3 0.0 collective-permute-done.1.refs_2_
  22.3 0.5 %collective-permute-start.2 = (bf16[512,128]{1,0:T(8,128)(2,1)S(1)}, bf16[512,128]{1,0:T(8,128)(2,1)S(1)}, u32[]{:S(2)}, u32[]{:S(2)}) collective-permute-start(bf16[512,128]{1,0:T(8,128)(2,1)S(1)} %collective-permute-done.1.refs_2_), channel_id=1, source_target_pairs={{0,1},{1,0},{2,3},{3,2},{4,5},{5,4},{6,7},{7,6},{8,9},{9,8},{10,11... | collective-permute-start | bytes 393224 | tf_op jit(solution)/shard_map/ppermute | solution.py:150
  22.8 0.0 collective-permute-done.refs_1_
  22.8 0.0 collective-permute-done.6.refs_7_
  22.8 0.8 %collective-permute-done.4.refs_5_ = bf16[512,128]{1,0:T(8,128)(2,1)S(1)} collective-permute-done((bf16[512,128]{1,0:T(8,128)(2,1)S(1)}, bf16[512,128]{1,0:T(8,128)(2,1)S(1)}, u32[]{:S(2)}, u32[]{:S(2)}) %collective-permute-start.4) | collective-permute-done | bytes 131104 | tf_op jit(solution)/shard_map/ppermute | solution.py:150
  23.7 0.2 collective-permute-done.2.refs_3_
  23.8 0.0 copy-start
  23.8 1.4 %copy-done = bf16[1,768,1024]{2,1,0:T(8,128)(2,1)S(1)} copy-done((bf16[1,768,1024]{2,1,0:T(8,128)(2,1)S(1)}, bf16[1,768,1024]{2,1,0:T(8,128)(2,1)}, u32[]{:S(2)}) %copy-start) | copy-done | bytes 1572888
  25.3 8.6 %whole_block.1 = bf16[768,1024]{1,0:T(8,128)(2,1)} custom-call(bf16[512,128]{1,0:T(8,128)(2,1)S(1)} %bitcast.8, bf16[512,128]{1,0:T(8,128)(2,1)S(1)} %collective-permute-done.refs_1_, bf16[512,128]{1,0:T(8,128)(2,1)S(1)} %collective-permute-done.1.refs_2_, bf16[512,128]{1,0:T(8,128)(2,1)S(1)} %collective-permute-done.2.refs_3_, ...), custom_call_target="tpu_custom_call" | custom-call | tf_op jit(solution)/shard_map/whole_block/pallas_call | solution.py:126
Async XLA Ops:
  14.3 7.2 %collective-permute-start.5 = (bf16[512,128]{1,0:T(8,128)(2,1)S(1)}, bf16[512,128]{1,0:T(8,128)(2,1)S(1)}, u32[]{:S(2)}, u32[]{:S(2)}) collective-permute-start(bf16[512,128]{1,0:T(8,128)(2,1)S(1)} %bitcast.4), channel_id=1, source_target_pairs={{0,6},{1,7},{2,4},{3,5},{4,2},{5,3},{6,0},{7,1},{8,14},{9,15},{10,... | collective-permute-start | bytes 393224 | tf_op jit(solution)/shard_map/ppermute | solution.py:149
  16.7 5.6 %collective-permute-start.3 = (bf16[512,128]{1,0:T(8,128)(2,1)S(1)}, bf16[512,128]{1,0:T(8,128)(2,1)S(1)}, u32[]{:S(2)}, u32[]{:S(2)}) collective-permute-start(bf16[512,128]{1,0:T(8,128)(2,1)S(1)} %bitcast.5), channel_id=1, source_target_pairs={{0,4},{1,5},{2,6},{3,7},{4,0},{5,1},{6,2},{7,3},{8,12},{9,13},{10,... | collective-permute-start | bytes 393224 | tf_op jit(solution)/shard_map/ppermute | solution.py:149
  17.2 5.1 %collective-permute-start.1 = (bf16[512,128]{1,0:T(8,128)(2,1)S(1)}, bf16[512,128]{1,0:T(8,128)(2,1)S(1)}, u32[]{:S(2)}, u32[]{:S(2)}) collective-permute-start(bf16[512,128]{1,0:T(8,128)(2,1)S(1)} %bitcast.6), channel_id=1, source_target_pairs={{0,2},{1,3},{2,0},{3,1},{4,6},{5,7},{6,4},{7,5},{8,10},{9,11},{10,... | collective-permute-start | bytes 393224 | tf_op jit(solution)/shard_map/ppermute | solution.py:149
  17.8 5.1 %collective-permute-start = (bf16[512,128]{1,0:T(8,128)(2,1)S(1)}, bf16[512,128]{1,0:T(8,128)(2,1)S(1)}, u32[]{:S(2)}, u32[]{:S(2)}) collective-permute-start(bf16[512,128]{1,0:T(8,128)(2,1)S(1)} %bitcast.7), channel_id=1, source_target_pairs={{0,1},{1,0},{2,3},{3,2},{4,5},{5,4},{6,7},{7,6},{8,9},{9,8},{10,11... | collective-permute-start | bytes 393224 | tf_op jit(solution)/shard_map/ppermute | solution.py:150
  21.4 1.4 %collective-permute-start.6 = (bf16[512,128]{1,0:T(8,128)(2,1)S(1)}, bf16[512,128]{1,0:T(8,128)(2,1)S(1)}, u32[]{:S(2)}, u32[]{:S(2)}) collective-permute-start(bf16[512,128]{1,0:T(8,128)(2,1)S(1)} %collective-permute-done.5.refs_6_), channel_id=1, source_target_pairs={{0,1},{1,0},{2,3},{3,2},{4,5},{5,4},{6,7},{7,6},{8,9},{9,8},{10,11... | collective-permute-start | bytes 393224 | tf_op jit(solution)/shard_map/ppermute | solution.py:150
  22.3 1.3 %collective-permute-start.4 = (bf16[512,128]{1,0:T(8,128)(2,1)S(1)}, bf16[512,128]{1,0:T(8,128)(2,1)S(1)}, u32[]{:S(2)}, u32[]{:S(2)}) collective-permute-start(bf16[512,128]{1,0:T(8,128)(2,1)S(1)} %collective-permute-done.3.refs_4_), channel_id=1, source_target_pairs={{0,1},{1,0},{2,3},{3,2},{4,5},{5,4},{6,7},{7,6},{8,9},{9,8},{10,11... | collective-permute-start | bytes 393224 | tf_op jit(solution)/shard_map/ppermute | solution.py:150
  22.3 1.5 %collective-permute-start.2 = (bf16[512,128]{1,0:T(8,128)(2,1)S(1)}, bf16[512,128]{1,0:T(8,128)(2,1)S(1)}, u32[]{:S(2)}, u32[]{:S(2)}) collective-permute-start(bf16[512,128]{1,0:T(8,128)(2,1)S(1)} %collective-permute-done.1.refs_2_), channel_id=1, source_target_pairs={{0,1},{1,0},{2,3},{3,2},{4,5},{5,4},{6,7},{7,6},{8,9},{9,8},{10,11... | collective-permute-start | bytes 393224 | tf_op jit(solution)/shard_map/ppermute | solution.py:150
  23.8 1.4 %copy-start = (bf16[1,768,1024]{2,1,0:T(8,128)(2,1)S(1)}, bf16[1,768,1024]{2,1,0:T(8,128)(2,1)}, u32[]{:S(2)}) copy-start(bf16[1,768,1024]{2,1,0:T(8,128)(2,1)} %param.3) | copy-start | bytes 4718596

commit v3 on v2

v3 whole, which is shorter than its diff:
```python
import functools

import jax
import jax.numpy as jnp
from jax import lax
from jax.experimental import pallas as pl
from jax.experimental.pallas import tpu as pltpu
from jax.sharding import PartitionSpec as P

ITERS = 4
DAMPING = 0.01
WHOLE = pl.BlockSpec(memory_space=pltpu.VMEM)
ANYWHERE = pl.BlockSpec(memory_space=pl.ANY)


def dot(a, b):
    return jnp.dot(a, b, preferred_element_type=jnp.float32)


def gather_block(factor_inputs):
    pieces = jnp.transpose(factor_inputs, (1, 0, 2))
    piece = lax.all_to_all(pieces, "dp", split_axis=0, concat_axis=1, tiled=True)[0]
    return lax.all_gather(piece, "grad", axis=1, tiled=True)


def by_features(columns, tile):
    tokens, width = columns.shape
    covariance = jnp.einsum("tr,tc->rc", columns, columns, preferred_element_type=jnp.float32) * (1.0 / tokens)
    damped = covariance + DAMPING * jnp.eye(width, dtype=jnp.float32)
    scale = 1.0 / jnp.max(jnp.sum(jnp.abs(damped), axis=1))
    image = scale * damped
    result = scale * tile.astype(jnp.float32)
    for step in range(ITERS):
        low = image.astype(jnp.bfloat16)
        result = 2.0 * result - dot(result.astype(jnp.bfloat16), low)
        if step < ITERS - 1:
            image = 2.0 * image - dot(low, low)
    return result


def split_kernel(x_ref, *out_refs):
    replicas, tokens = len(out_refs), out_refs[0].shape[0]
    here = lax.axis_index("dp")
    x = x_ref[...]
    rows = lax.broadcasted_iota(jnp.int32, (tokens, tokens * replicas), 0)
    cols = lax.broadcasted_iota(jnp.int32, (tokens, tokens * replicas), 1)
    offset = cols - rows * replicas
    for far, out_ref in enumerate(out_refs):
        choice = jnp.where(offset == (here ^ far), 1.0, 0.0).astype(jnp.bfloat16)
        out_ref[...] = dot(choice, x).astype(jnp.bfloat16)


def split_blocks(factor_inputs):
    tokens, blocks, features = factor_inputs.shape
    return pl.pallas_call(
        split_kernel,
        out_shape=[jax.ShapeDtypeStruct((tokens, features), factor_inputs.dtype)] * blocks,
        in_specs=[WHOLE],
        out_specs=[WHOLE] * blocks,
        name="split_blocks",
    )(factor_inputs.reshape(tokens * blocks, features))


def column_sums(a, b):
    return jnp.sum(jnp.abs(dot(a, b)), axis=0, keepdims=True)


def absorb(fars, pieces, turned, tile, member):
    features = pieces[0].shape[1]
    pairs = [jnp.concatenate([a[...], b[...]], axis=1) for a, b in zip(pieces[::2], pieces[1::2])]
    columns = pairs[-1]
    columns_t = columns.T
    gram = dot(columns, columns_t)
    mine = jnp.concatenate([tile[:, place(member, fars[-1] + one, features)] for one in (0, 1)], axis=1)
    image = dot(mine, columns_t)
    sums = column_sums(columns_t, columns)
    before = []
    for earlier, earlier_t in zip(pairs, turned):
        sums = sums + column_sums(earlier_t[...], columns)
        before.append(column_sums(columns_t, earlier))
    return columns_t, gram, image, jnp.concatenate(before + [sums], axis=0)


def place(member, far, features):
    return pl.ds(pl.multiple_of((member ^ far) * features, features), features)


def first_kernel(fars, p0, p1, tile, turned, gram_out, image_out, sums_out):
    turned[...], gram_out[...], image_out[...], sums_out[...] = absorb(
        fars, (p0, p1), (), tile, lax.axis_index("grad")
    )


def take(fars, refs):
    count = len(fars)
    return refs[: 2 * count], refs[2 * count : 3 * count - 1], refs[3 * count - 1 :]


def next_kernel(fars, *refs):
    pieces, earlier, refs = take(fars, refs)
    tile, gram_in, image_in, sums_in, turned, gram_out, image_out, sums_out = refs
    done = len(fars) - 1
    turned[...], gram, image, sums = absorb(fars, pieces, earlier, tile, lax.axis_index("grad"))
    gram_out[...] = gram_in[...] + gram
    image_out[...] = image_in[...] + image
    sums_out[:done, :] = sums_in[...] + sums[:done]
    sums_out[done:, :] = sums[done:]


def last_kernel(fars, *refs):
    pieces, earlier, refs = take(fars, refs)
    tile, gram_in, image_in, sums_in, out_hbm, out, sems = refs
    done = len(fars) - 1
    member = lax.axis_index("grad")
    tokens, features = pieces[0].shape
    rows = tile.shape[0]
    step = rows // 3
    _, gram, image, sums = absorb(fars, pieces, earlier, tile, member)
    gram = (gram_in[...] + gram) * (1.0 / tokens)
    image = (image_in[...] + image).astype(jnp.bfloat16)
    low = gram.astype(jnp.bfloat16)
    second = dot(low, low)
    low2 = second.astype(jnp.bfloat16)
    third, fourth = dot(low2, low), dot(low2, low2)
    sums = jnp.concatenate([sums_in[...] + sums[:done], sums[done:]], axis=0)
    largest = jnp.max(jnp.max(sums, axis=0, keepdims=True), axis=1, keepdims=True)

    c = 1.0 / (largest * (1.0 / tokens) + DAMPING)
    eps = 1.0 - c * DAMPING
    eps2 = eps * eps
    eps3 = eps2 * eps
    eps4 = eps2 * eps2
    c2 = c * c
    c3 = c2 * c
    rows_id = lax.broadcasted_iota(jnp.int32, (tokens, tokens), 0)
    cols_id = lax.broadcasted_iota(jnp.int32, (tokens, tokens), 1)
    eye = (rows_id == cols_id).astype(jnp.float32)
    e1 = -c * gram
    e2 = -2.0 * eps * c * gram + c2 * second
    e3 = -3.0 * eps2 * c * gram + 3.0 * eps * c2 * second - c3 * third
    e4 = -4.0 * eps3 * c * gram + 6.0 * eps2 * c2 * second - 4.0 * eps * c3 * third + c2 * c2 * fourth
    u_m, u_n = 1.0 + eps + eps2 + eps3, e1 + e2 + e3
    w_m, w_n = 4.0 * eps3, eps2 * e1 + eps * e2 + e3
    a_m, a_n = u_m * w_m, u_m * w_n + w_m * u_n + dot(u_n.astype(jnp.bfloat16), w_n.astype(jnp.bfloat16))
    low4 = e4.astype(jnp.bfloat16)
    y_m = 1.0 + 2.0 * eps4 + 3.0 * eps4 * eps4
    y_n = (1.0 + 3.0 * eps4) * e4 + dot(low4, low4)
    q_m, q_n = a_m * y_m, a_m * y_n + y_m * a_n + dot(a_n.astype(jnp.bfloat16), y_n.astype(jnp.bfloat16))
    v = (1.0 + eps4) * (1.0 + eps4 * eps4)
    q_m = q_m + v * (1.0 + 2.0 * eps + 3.0 * eps2)
    q_n = q_n + v * ((1.0 + eps) * e1 + e2)
    q = ((q_m * eye + q_n) * (-c2 * (1.0 / tokens))).astype(jnp.bfloat16)
    p = c * (1.0 + eps) * (1.0 + eps2) * v
    stores = []
    for k, at in enumerate(range(0, rows, step)):
        some = pl.ds(at, step)
        mixed = dot(image[at : at + step, :], q).astype(jnp.bfloat16)
        for far, a, b in zip(fars, pieces[::2], pieces[1::2]):
            moved = dot(mixed, jnp.concatenate([a[...], b[...]], axis=1))
            for one in (0, 1):
                here = place(member, far + one, features)
                kept = p * tile[some, here].astype(jnp.float32)
                out[some, here] = (kept + moved[:, one * features : (one + 1) * features]).astype(jnp.bfloat16)
        store = pltpu.make_async_copy(out.at[some, :], out_hbm.at[some, :], sems.at[k])
        store.start()
        stores.append(store)
    for store in stores:
        store.wait()


def swap(value, axis, far):
    return lax.ppermute(value, axis, [(i, i ^ far) for i in range(lax.axis_size(axis))])


def by_tokens(factor_inputs, tile):
    members, replicas = lax.axis_size("grad"), lax.axis_size("dp")
    rows, width = tile.shape
    features = factor_inputs.shape[2]
    tokens = factor_inputs.shape[0] * replicas
    params = pltpu.CompilerParams(vmem_limit_bytes=24 * 2**20)

    def shape(*sizes, kind=jnp.float32):
        return jax.ShapeDtypeStruct(sizes, kind)

    parts = list(split_blocks(factor_inputs))
    arrived = [swap(parts[far], "dp", far) for far in range(replicas - 1, 0, -1)]
    own = jnp.concatenate(parts[:1] + arrived[::-1], axis=0)
    all_fars = [0] + list(range(members - 2, 0, -2))
    helds = [own] + [swap(own, "grad", far) for far in all_fars[1:]]
    pieces, turned, steps = [], [], [None]
    for count, held in enumerate(helds, 1):
        after = steps[min(count - 1, max(1, count - 2))]
        if after is None:
            near = swap(held, "grad", 1)
        else:
            near = swap(jnp.where(after[0, 0] >= 0.0, held, jnp.zeros_like(held)), "grad", 1)
        pieces += [held, near]
        fars = tuple(all_fars[:count])
        state = [
            shape(2 * features, tokens, kind=jnp.bfloat16),
            shape(tokens, tokens),
            shape(rows, tokens),
            shape(count, 2 * features),
        ]
        flops = 4 * features * tokens * (tokens + rows + 2 * features * (2 * count - 1))
        cost = pl.CostEstimate(flops=flops, bytes_accessed=0, transcendentals=0)
        if count == 1:
            one, *sums = pl.pallas_call(
                functools.partial(first_kernel, fars),
                out_shape=state,
                in_specs=[WHOLE] * 3,
                out_specs=[WHOLE] * 4,
                compiler_params=params,
                cost_estimate=cost,
                name="first_pair",
            )(*pieces, tile)
            turned.append(one)
        elif count < len(all_fars):
            one, *sums = pl.pallas_call(
                functools.partial(next_kernel, fars),
                out_shape=state,
                in_specs=[WHOLE] * (3 * count + 3),
                out_specs=[WHOLE] * 4,
                compiler_params=params,
                cost_estimate=cost,
                name="next_pair",
            )(*pieces, *turned, tile, *sums)
            turned.append(one)
        steps.append(sums[-1])
    return pl.pallas_call(
        functools.partial(last_kernel, fars),
        out_shape=shape(rows, width, kind=jnp.bfloat16),
        in_specs=[WHOLE] * (3 * count + 3),
        out_specs=ANYWHERE,
        scratch_shapes=[pltpu.VMEM((rows, width), jnp.bfloat16), pltpu.SemaphoreType.DMA((3,))],
        compiler_params=params,
        cost_estimate=pl.CostEstimate(flops=5 * 10**9, bytes_accessed=0, transcendentals=0),
        name="last_pair",
    )(*pieces, *turned, tile, *sums)


def local(factor_inputs, gradients):
    features, members = factor_inputs.shape[2], lax.axis_size("grad")
    tokens = factor_inputs.shape[0] * lax.axis_size("dp")
    tile = gradients[0]
    powers_of_two = all(size & (size - 1) == 0 for size in (members, lax.axis_size("dp")))
    if tokens < features * members and features % 128 == 0 and powers_of_two and members > 2:
        result = by_tokens(factor_inputs, tile)
    else:
        result = by_features(gather_block(factor_inputs), tile)
    return result.astype(jnp.bfloat16)[None]


def solution(mesh):
    placed = (P("dp", None, "grad"), P("dp", "grad", None))
    return jax.shard_map(
        local, mesh=mesh, in_specs=placed, out_specs=P("dp", "grad", None), check_vma=False
    )
```

time: 34.2 us -> 33.5 us (0.980)
  blocking collectives: 12.4 us -> 0 us
  starting transfers between devices: 4 us -> 9.88 us
  waiting for transfers between devices: 5.57 us -> 7.92 us
  local copies, waits for them, and re-layouts: 1.41 us -> 3.22 us
  between operations: 0.01 us -> 1.37 us
  Pallas kernels: 10.5 us -> 10.9 us
    all_to_all x1 -> x0, blocking collectives: 12.4 us -> none  [gather_pieces(): lax.all_to_all(split_blocks(factor_inputs), 'dp', split_axis=0, concat_ax...]
    ppermute x7 -> x10, starting transfers between devices: 4 us -> 9.88 us  [swap(): lax.ppermute(value, axis, [(i, i ^ far) for i in range(lax.axis_size(axis...]
    ppermute x7 -> x10, waiting for transfers between devices: 5.57 us -> 7.92 us  [swap(): lax.ppermute(value, axis, [(i, i ^ far) for i in range(lax.axis_size(axis...]
    slice x0 -> x2, local copies, waits for them, and re-layouts: none -> 1.03 us  [by_tokens(): after[0, 0] >= 0.0]
    unnamed x2 -> x5, local copies, waits for them, and re-layouts: 1.41 us -> 2.19 us
    pallas_call x2 -> x5, Pallas kernels: 10.5 us -> 10.9 us  [the longest x1 6.66 us: by_tokens(): pl.pallas_call(functools.partial(last_kernel, fars), out_shape=shape(rows...]
  transfers between devices with their start and end apart: 7 -> 10, of which waited for: 4 -> 4; matrix products, arithmetic and copies ran while one was open for 0% -> 6% of each run, Pallas kernels for 0% -> 7%
where the time goes in v3:
time: 33.5 us; the launch traced here: 33.3 us
  Pallas kernels  10.9 us (33%)
  starting transfers between devices  9.88 us (29%)
  waiting for transfers between devices  7.92 us (24%)
  local copies, waits for them, and re-layouts  3.22 us (10%)
  between operations  1.37 us (4%)
    ppermute x10, starting transfers between devices, swap(): lax.ppermute(value, axis, [(i, i ^ far) for i in range(lax.axis_size(axis...  9.88 us
    ppermute x10, waiting for transfers between devices, swap(): lax.ppermute(value, axis, [(i, i ^ far) for i in range(lax.axis_size(axis...  7.92 us
    pallas_call x1, Pallas kernels, by_tokens(): pl.pallas_call(functools.partial(last_kernel, fars), out_shape=shape(rows...  6.66 us
    unnamed x5, local copies, waits for them, and re-layouts  2.19 us
    pallas_call x1, Pallas kernels, split_blocks(): pl.pallas_call(split_kernel, out_shape=[jax.ShapeDtypeStruct((tokens, fea...  1.81 us
    pallas_call x2, Pallas kernels, by_tokens(): pl.pallas_call(functools.partial(next_kernel, fars), out_shape=state, in_...  1.74 us
    slice x2, local copies, waits for them, and re-layouts, by_tokens(): after[0, 0] >= 0.0  1.03 us
  transfers between devices with their start and end apart: 10, of which 4 were waited for; matrix products, arithmetic and copies ran while one was open for 6% of the time, Pallas kernels for 7%

profile of v3, /device:TPU:0, one launch (start us, length us, event | category | flops | bytes accessed | tf_op | source)
XLA Modules:
  0.0 33.3 jit_solution(10437549086187032550)
XLA Ops:
  0.0 1.8 %split_blocks.1 = (bf16[128,128]{1,0:T(8,128)(2,1)}, bf16[128,128]{1,0:T(8,128)(2,1)}, bf16[128,128]{1,0:T(8,128)(2,1)}, bf16[128,128]{1,0:T(8,128)(2,1)}) custom-call(bf16[512,128]{1,0:T(8,128)(2,1)} %bitcast.9), custom_call_target="tpu_custom_call" | custom-call | tf_op jit(solution)/shard_map/split_blocks/pallas_call | solution.py:55
  1.8 3.0 %collective-permute-start = (bf16[128,128]{1,0:T(8,128)(2,1)}, bf16[128,128]{1,0:T(8,128)(2,1)S(1)}, u32[]{:S(2)}, u32[]{:S(2)}) collective-permute-start(bf16[128,128]{1,0:T(8,128)(2,1)} %get-tuple-element.22), channel_id=1, source_target_pairs={{0,8},{8,0},{16,24},{24,16},{1,9},{9,1},{17,25},{25,17},{2,10},{10... | collective-permute-start | bytes 98312 | tf_op jit(solution)/shard_map/ppermute | solution.py:172
  4.8 2.6 %collective-permute-start.1 = (bf16[128,128]{1,0:T(8,128)(2,1)}, bf16[128,128]{1,0:T(8,128)(2,1)S(1)}, u32[]{:S(2)}, u32[]{:S(2)}) collective-permute-start(bf16[128,128]{1,0:T(8,128)(2,1)} %get-tuple-element.23), channel_id=1, source_target_pairs={{0,16},{8,24},{16,0},{24,8},{1,17},{9,25},{17,1},{25,9},{2,18},{10... | collective-permute-start | bytes 98312 | tf_op jit(solution)/shard_map/ppermute | solution.py:172
  7.4 0.0 collective-permute-start.2
  7.4 0.8 %constant_dynamic-update-slice_fusion.3 = bf16[512,128]{1,0:T(8,128)(2,1)S(1)} fusion(bf16[128,128]{1,0:T(8,128)(2,1)} %get-tuple-element.21), kind=kLoop, calls=%fused_computation.6 | loop fusion | bytes 65536
  8.2 0.0 collective-permute-done
  8.2 2.2 %collective-permute-done.1 = bf16[128,128]{1,0:T(8,128)(2,1)S(1)} collective-permute-done((bf16[128,128]{1,0:T(8,128)(2,1)}, bf16[128,128]{1,0:T(8,128)(2,1)S(1)}, u32[]{:S(2)}, u32[]{:S(2)}) %collective-permute-start.1) | collective-permute-done | bytes 32800 | tf_op jit(solution)/shard_map/ppermute | solution.py:172
  10.5 2.9 %collective-permute-done.2 = bf16[128,128]{1,0:T(8,128)(2,1)S(1)} collective-permute-done((bf16[128,128]{1,0:T(8,128)(2,1)}, bf16[128,128]{1,0:T(8,128)(2,1)S(1)}, u32[]{:S(2)}, u32[]{:S(2)}) %collective-permute-start.2) | collective-permute-done | bytes 32800 | tf_op jit(solution)/shard_map/ppermute | solution.py:172
  13.4 0.0 collective-permute-start.3
  13.4 2.5 %collective-permute-start.4 = (bf16[512,128]{1,0:T(8,128)(2,1)S(1)}, bf16[512,128]{1,0:T(8,128)(2,1)S(1)}, u32[]{:S(2)}, u32[]{:S(2)}) collective-permute-start(bf16[512,128]{1,0:T(8,128)(2,1)S(1)} %constant_dynamic-update-slice_fusion.p0.refs_0_), channel_id=1, source_target_pairs={{0,6},{1,7},{2,4},{3,5},{4,2},{5,3},{6,0},{7,1},{8,14},{9,15},{10,... | collective-permute-start | bytes 393224 | tf_op jit(solution)/shard_map/ppermute | solution.py:172
  15.9 0.5 %collective-permute-start.6 = (bf16[512,128]{1,0:T(8,128)(2,1)S(1)}, bf16[512,128]{1,0:T(8,128)(2,1)S(1)}, u32[]{:S(2)}, u32[]{:S(2)}) collective-permute-start(bf16[512,128]{1,0:T(8,128)(2,1)S(1)} %constant_dynamic-update-slice_fusion.p0.refs_0_), channel_id=1, source_target_pairs={{0,4},{1,5},{2,6},{3,7},{4,0},{5,1},{6,2},{7,3},{8,12},{9,13},{10,... | collective-permute-start | bytes 393224 | tf_op jit(solution)/shard_map/ppermute | solution.py:172
  16.4 0.5 %collective-permute-start.8 = (bf16[512,128]{1,0:T(8,128)(2,1)S(1)}, bf16[512,128]{1,0:T(8,128)(2,1)S(1)}, u32[]{:S(2)}, u32[]{:S(2)}) collective-permute-start(bf16[512,128]{1,0:T(8,128)(2,1)S(1)} %constant_dynamic-update-slice_fusion.p0.refs_0_), channel_id=1, source_target_pairs={{0,2},{1,3},{2,0},{3,1},{4,6},{5,7},{6,4},{7,5},{8,10},{9,11},{10,... | collective-permute-start | bytes 393224 | tf_op jit(solution)/shard_map/ppermute | solution.py:172
  16.9 0.0 collective-permute-done.3.p1.refs_1_
  16.9 0.0 copy-start
  16.9 1.4 %copy-done = bf16[1,768,1024]{2,1,0:T(8,128)(2,1)S(1)} copy-done((bf16[1,768,1024]{2,1,0:T(8,128)(2,1)S(1)}, bf16[1,768,1024]{2,1,0:T(8,128)(2,1)}, u32[]{:S(2)}) %copy-start) | copy-done | bytes 1572888
  18.3 0.6 %first_pair.1 = (bf16[256,512]{1,0:T(8,128)(2,1)S(1)}, f32[512,512]{1,0:T(8,128)S(1)}, f32[768,512]{1,0:T(8,128)S(1)}, f32[1,256]{1,0:T(1,128)S(1)}) custom-call(bf16[512,128]{1,0:T(8,128)(2,1)S(1)} %constant_dynamic-update-slice_fusion.p0.refs_0_, bf16[512,128]{1,0:T(8,128)(2,1)S(1)} %collective-permute-done.3.p1.refs_1_, bf16[768,1024]{1,0:T(8,128)(2,1)S(1)} %bitcast.5), custom_call_target="tpu_custom_call" | custom-call | flops 402653184 | tf_op jit(solution)/shard_map/first_pair/pallas_call | solution.py:208
  19.0 0.5 %slice.7 = f32[1,1]{1,0:T(1,128)} slice(f32[1,256]{1,0:T(1,128)S(1)} %get-tuple-element.25.refs_8_), slice={[0:1], [0:1]} | slice | bytes 8 | tf_op jit(solution)/shard_map/slice | solution.py:196
  20.1 0.3 collective-permute-done.4.refs_2_
  20.5 0.1 collective-permute-start.5
  20.6 2.4 %collective-permute-done.6.refs_4_ = bf16[512,128]{1,0:T(8,128)(2,1)S(1)} collective-permute-done((bf16[512,128]{1,0:T(8,128)(2,1)S(1)}, bf16[512,128]{1,0:T(8,128)(2,1)S(1)}, u32[]{:S(2)}, u32[]{:S(2)}) %collective-permute-start.6) | collective-permute-done | bytes 131104 | tf_op jit(solution)/shard_map/ppermute | solution.py:172
  23.0 0.1 collective-permute-start.7
  23.1 0.0 collective-permute-done.5.refs_3_
  23.1 0.8 %next_pair.2 = (bf16[256,512]{1,0:T(8,128)(2,1)S(1)}, f32[512,512]{1,0:T(8,128)S(1)}, f32[768,512]{1,0:T(8,128)S(1)}, f32[2,256]{1,0:T(2,128)S(1)}) custom-call(bf16[512,128]{1,0:T(8,128)(2,1)S(1)} %constant_dynamic-update-slice_fusion.p0.refs_0_, bf16[512,128]{1,0:T(8,128)(2,1)S(1)} %collective-permute-done.3.p1.refs_1_, ...), custom_call_target="tpu_custom_call" | custom-call | flops 536870912 | tf_op jit(solution)/shard_map/next_pair/pallas_call | solution.py:219
  23.9 0.5 %slice.8 = f32[1,1]{1,0:T(1,128)} slice(f32[2,256]{1,0:T(2,128)S(1)} %get-tuple-element.29.refs_11_), slice={[0:1], [0:1]} | slice | bytes 8 | tf_op jit(solution)/shard_map/slice | solution.py:196
  25.1 0.0 collective-permute-done.8.refs_6_
  25.1 0.5 %collective-permute-start.9 = (bf16[512,128]{1,0:T(8,128)(2,1)S(1)}, bf16[512,128]{1,0:T(8,128)(2,1)S(1)}, u32[]{:S(2)}, u32[]{:S(2)}) collective-permute-start(bf16[512,128]{1,0:T(8,128)(2,1)S(1)} %broadcast_select_fusion), channel_id=1, source_target_pairs={{0,1},{1,0},{2,3},{3,2},{4,5},{5,4},{6,7},{7,6},{8,9},{9,8},{10,11... | collective-permute-start | bytes 393224 | tf_op jit(solution)/shard_map/ppermute | solution.py:172
  25.6 0.0 collective-permute-done.7.refs_5_
  25.6 0.9 %next_pair.3 = (bf16[256,512]{1,0:T(8,128)(2,1)S(1)}, f32[512,512]{1,0:T(8,128)S(1)}, f32[768,512]{1,0:T(8,128)S(1)}, f32[3,256]{1,0:T(4,128)S(1)}) custom-call(bf16[512,128]{1,0:T(8,128)(2,1)S(1)} %constant_dynamic-update-slice_fusion.p0.refs_0_, bf16[512,128]{1,0:T(8,128)(2,1)S(1)} %collective-permute-done.3.p1.refs_1_, ...), custom_call_target="tpu_custom_call" | custom-call | flops 671088640 | tf_op jit(solution)/shard_map/next_pair/pallas_call | solution.py:219
  26.6 0.0 collective-permute-done.9.refs_7_
  26.6 6.7 %last_pair.1 = bf16[768,1024]{1,0:T(8,128)(2,1)} custom-call(bf16[512,128]{1,0:T(8,128)(2,1)S(1)} %constant_dynamic-update-slice_fusion.p0.refs_0_, bf16[512,128]{1,0:T(8,128)(2,1)S(1)} %collective-permute-done.3.p1.refs_1_, bf16[512,128]{1,0:T(8,128)(2,1)S(1)} %collective-permute-done.4.refs_2_, bf16[512,128]{1,0:T(8,128)(2,1)S(1)} %collective-permute-done.5.refs_3_, ...), custom_call_target="tpu_custom_call" | custom-call | flops 5000000000 | tf_op jit(solution)/shard_map/last_pair/pallas_call | solution.py:230
  (6 shorter events, 0.1 us)
Async XLA Ops:
  1.8 6.4 %collective-permute-start = (bf16[128,128]{1,0:T(8,128)(2,1)}, bf16[128,128]{1,0:T(8,128)(2,1)S(1)}, u32[]{:S(2)}, u32[]{:S(2)}) collective-permute-start(bf16[128,128]{1,0:T(8,128)(2,1)} %get-tuple-element.22), channel_id=1, source_target_pairs={{0,8},{8,0},{16,24},{24,16},{1,9},{9,1},{17,25},{25,17},{2,10},{10... | collective-permute-start | bytes 98312 | tf_op jit(solution)/shard_map/ppermute | solution.py:172
  4.8 5.6 %collective-permute-start.1 = (bf16[128,128]{1,0:T(8,128)(2,1)}, bf16[128,128]{1,0:T(8,128)(2,1)S(1)}, u32[]{:S(2)}, u32[]{:S(2)}) collective-permute-start(bf16[128,128]{1,0:T(8,128)(2,1)} %get-tuple-element.23), channel_id=1, source_target_pairs={{0,16},{8,24},{16,0},{24,8},{1,17},{9,25},{17,1},{25,9},{2,18},{10... | collective-permute-start | bytes 98312 | tf_op jit(solution)/shard_map/ppermute | solution.py:172
  7.4 5.9 %collective-permute-start.2 = (bf16[128,128]{1,0:T(8,128)(2,1)}, bf16[128,128]{1,0:T(8,128)(2,1)S(1)}, u32[]{:S(2)}, u32[]{:S(2)}) collective-permute-start(bf16[128,128]{1,0:T(8,128)(2,1)} %get-tuple-element.24), channel_id=1, source_target_pairs={{0,24},{8,16},{16,8},{24,0},{1,25},{9,17},{17,9},{25,1},{2,26},{10... | collective-permute-start | bytes 98312 | tf_op jit(solution)/shard_map/ppermute | solution.py:172
  13.4 3.6 %collective-permute-start.3 = (bf16[512,128]{1,0:T(8,128)(2,1)S(1)}, bf16[512,128]{1,0:T(8,128)(2,1)S(1)}, u32[]{:S(2)}, u32[]{:S(2)}) collective-permute-start(bf16[512,128]{1,0:T(8,128)(2,1)S(1)} %constant_dynamic-update-slice_fusion.p0.refs_0_), channel_id=1, source_target_pairs={{0,1},{1,0},{2,3},{3,2},{4,5},{5,4},{6,7},{7,6},{8,9},{9,8},{10,11... | collective-permute-start | bytes 393224 | tf_op jit(solution)/shard_map/ppermute | solution.py:172
  13.4 7.1 %collective-permute-start.4 = (bf16[512,128]{1,0:T(8,128)(2,1)S(1)}, bf16[512,128]{1,0:T(8,128)(2,1)S(1)}, u32[]{:S(2)}, u32[]{:S(2)}) collective-permute-start(bf16[512,128]{1,0:T(8,128)(2,1)S(1)} %constant_dynamic-update-slice_fusion.p0.refs_0_), channel_id=1, source_target_pairs={{0,6},{1,7},{2,4},{3,5},{4,2},{5,3},{6,0},{7,1},{8,14},{9,15},{10,... | collective-permute-start | bytes 393224 | tf_op jit(solution)/shard_map/ppermute | solution.py:172
  15.9 7.1 %collective-permute-start.6 = (bf16[512,128]{1,0:T(8,128)(2,1)S(1)}, bf16[512,128]{1,0:T(8,128)(2,1)S(1)}, u32[]{:S(2)}, u32[]{:S(2)}) collective-permute-start(bf16[512,128]{1,0:T(8,128)(2,1)S(1)} %constant_dynamic-update-slice_fusion.p0.refs_0_), channel_id=1, source_target_pairs={{0,4},{1,5},{2,6},{3,7},{4,0},{5,1},{6,2},{7,3},{8,12},{9,13},{10,... | collective-permute-start | bytes 393224 | tf_op jit(solution)/shard_map/ppermute | solution.py:172
  16.4 8.7 %collective-permute-start.8 = (bf16[512,128]{1,0:T(8,128)(2,1)S(1)}, bf16[512,128]{1,0:T(8,128)(2,1)S(1)}, u32[]{:S(2)}, u32[]{:S(2)}) collective-permute-start(bf16[512,128]{1,0:T(8,128)(2,1)S(1)} %constant_dynamic-update-slice_fusion.p0.refs_0_), channel_id=1, source_target_pairs={{0,2},{1,3},{2,0},{3,1},{4,6},{5,7},{6,4},{7,5},{8,10},{9,11},{10,... | collective-permute-start | bytes 393224 | tf_op jit(solution)/shard_map/ppermute | solution.py:172
  16.9 1.4 %copy-start = (bf16[1,768,1024]{2,1,0:T(8,128)(2,1)S(1)}, bf16[1,768,1024]{2,1,0:T(8,128)(2,1)}, u32[]{:S(2)}) copy-start(bf16[1,768,1024]{2,1,0:T(8,128)(2,1)} %param.3) | copy-start | bytes 4718596
  20.5 2.6 %collective-permute-start.5 = (bf16[512,128]{1,0:T(8,128)(2,1)S(1)}, bf16[512,128]{1,0:T(8,128)(2,1)S(1)}, u32[]{:S(2)}, u32[]{:S(2)}) collective-permute-start(bf16[512,128]{1,0:T(8,128)(2,1)S(1)} %broadcast_select_fusion.2), channel_id=1, source_target_pairs={{0,1},{1,0},{2,3},{3,2},{4,5},{5,4},{6,7},{7,6},{8,9},{9,8},{10,11... | collective-permute-start | bytes 393224 | tf_op jit(solution)/shard_map/ppermute | solution.py:172
  23.0 2.6 %collective-permute-start.7 = (bf16[512,128]{1,0:T(8,128)(2,1)S(1)}, bf16[512,128]{1,0:T(8,128)(2,1)S(1)}, u32[]{:S(2)}, u32[]{:S(2)}) collective-permute-start(bf16[512,128]{1,0:T(8,128)(2,1)S(1)} %broadcast_select_fusion.1), channel_id=1, source_target_pairs={{0,1},{1,0},{2,3},{3,2},{4,5},{5,4},{6,7},{7,6},{8,9},{9,8},{10,11... | collective-permute-start | bytes 393224 | tf_op jit(solution)/shard_map/ppermute | solution.py:172
  25.1 1.5 %collective-permute-start.9 = (bf16[512,128]{1,0:T(8,128)(2,1)S(1)}, bf16[512,128]{1,0:T(8,128)(2,1)S(1)}, u32[]{:S(2)}, u32[]{:S(2)}) collective-permute-start(bf16[512,128]{1,0:T(8,128)(2,1)S(1)} %broadcast_select_fusion), channel_id=1, source_target_pairs={{0,1},{1,0},{2,3},{3,2},{4,5},{5,4},{6,7},{7,6},{8,9},{9,8},{10,11... | collective-permute-start | bytes 393224 | tf_op jit(solution)/shard_map/ppermute | solution.py:172

commit v4 on v3

v4 whole, which is shorter than its diff:
```python
import functools

import jax
import jax.numpy as jnp
from jax import lax
from jax.experimental import pallas as pl
from jax.experimental.pallas import tpu as pltpu
from jax.sharding import PartitionSpec as P

ITERS = 4
DAMPING = 0.01
WHOLE = pl.BlockSpec(memory_space=pltpu.VMEM)
ANYWHERE = pl.BlockSpec(memory_space=pl.ANY)


def dot(a, b):
    return jnp.dot(a, b, preferred_element_type=jnp.float32)


def gather_block(factor_inputs):
    pieces = jnp.transpose(factor_inputs, (1, 0, 2))
    piece = lax.all_to_all(pieces, "dp", split_axis=0, concat_axis=1, tiled=True)[0]
    return lax.all_gather(piece, "grad", axis=1, tiled=True)


def by_features(columns, tile):
    tokens, width = columns.shape
    covariance = jnp.einsum("tr,tc->rc", columns, columns, preferred_element_type=jnp.float32) * (1.0 / tokens)
    damped = covariance + DAMPING * jnp.eye(width, dtype=jnp.float32)
    scale = 1.0 / jnp.max(jnp.sum(jnp.abs(damped), axis=1))
    image = scale * damped
    result = scale * tile.astype(jnp.float32)
    for step in range(ITERS):
        low = image.astype(jnp.bfloat16)
        result = 2.0 * result - dot(result.astype(jnp.bfloat16), low)
        if step < ITERS - 1:
            image = 2.0 * image - dot(low, low)
    return result


def split_kernel(x_ref, *out_refs):
    replicas, tokens = len(out_refs), out_refs[0].shape[0]
    here = lax.axis_index("dp")
    x = x_ref[...]
    rows = lax.broadcasted_iota(jnp.int32, (tokens, tokens * replicas), 0)
    cols = lax.broadcasted_iota(jnp.int32, (tokens, tokens * replicas), 1)
    offset = cols - rows * replicas
    for far, out_ref in enumerate(out_refs):
        choice = jnp.where(offset == lax.rem(here + far, replicas), 1.0, 0.0).astype(jnp.bfloat16)
        out_ref[...] = dot(choice, x).astype(jnp.bfloat16)


def split_blocks(factor_inputs):
    tokens, blocks, features = factor_inputs.shape
    return pl.pallas_call(
        split_kernel,
        out_shape=[jax.ShapeDtypeStruct((tokens, features), factor_inputs.dtype)] * blocks,
        in_specs=[WHOLE],
        out_specs=[WHOLE] * blocks,
        name="split_blocks",
    )(factor_inputs.reshape(tokens * blocks, features))


def place(member, far, features):
    return pl.ds(pl.multiple_of((member ^ far) * features, features), features)


def join(pieces):
    return [jnp.concatenate([a[...], b[...]], axis=1) for a, b in zip(pieces[::2], pieces[1::2])]


def column_sums(a, b):
    return jnp.sum(jnp.abs(dot(a, b)), axis=0, keepdims=True)


def absorb(fars, pairs, turned, tile, member):
    columns = pairs[-1]
    columns_t = columns.T
    features = columns.shape[1] // 2
    gram = dot(columns, columns_t)
    mine = jnp.concatenate([tile[:, place(member, fars[-1] + one, features)] for one in (0, 1)], axis=1)
    image = dot(mine, columns_t)
    sums = column_sums(columns_t, columns)
    before = []
    for earlier, earlier_t in zip(pairs, turned):
        sums = sums + column_sums(earlier_t[...], columns)
        before.append(column_sums(columns_t, earlier))
    return columns_t, gram, image, before + [sums]


def first_kernel(fars, p0, p1, tile, turned, gram_out, image_out, sums_out, zeros):
    turned[...], gram_out[...], image_out[...], sums = absorb(
        fars, join((p0, p1)), (), tile, lax.axis_index("grad")
    )
    sums_out[...] = sums[0]
    zeros[...] = jnp.zeros_like(zeros)


def take(fars, refs):
    count = 2 * len(fars)
    return refs[:count], refs[count:]


def next_kernel(fars, *refs):
    pieces, refs = take(fars, refs)
    done = len(fars) - 1
    earlier, (tile, gram_in, image_in, sums_in, turned, gram_out, image_out, sums_out, zeros) = refs[:done], refs[done:]
    turned[...], gram, image, sums = absorb(fars, join(pieces), earlier, tile, lax.axis_index("grad"))
    gram_out[...] = gram_in[...] + gram
    image_out[...] = image_in[...] + image
    for k in range(done):
        sums_out[k : k + 1, :] = sums_in[k : k + 1, :] + sums[k]
    sums_out[done:, :] = sums[done]
    zeros[...] = jnp.zeros_like(zeros)


def last_kernel(fars, *refs):
    pieces, refs = take(fars, refs)
    done = len(fars) - 2
    earlier, refs = refs[:done], refs[done:]
    tile, gram_in, image_in, sums_in, out_hbm, out, k1, k2, k3, k4, low1, low2, u, w, e4, image, mixed, sems = refs
    member = lax.axis_index("grad")
    tokens, features = pieces[0].shape
    rows = tile.shape[0]
    chunk = 16
    half = 2 * features
    halves = range(0, tokens, half)
    pairs = join(pieces)
    columns_t, gram, moved, sums = absorb(fars[:-1], pairs[:-1], earlier, tile, member)
    sums = [sums_in[k : k + 1, :] + sums[k] for k in range(done)] + [sums[done]]
    _, gram2, moved2, sums2 = absorb(fars, pairs, list(earlier) + [columns_t], tile, member)
    k1[...] = (gram_in[...] + gram + gram2) * (1.0 / tokens)
    low1[...] = k1[...].astype(jnp.bfloat16)
    image[...] = (image_in[...] + moved + moved2).astype(jnp.bfloat16)
    sums = [a + b for a, b in zip(sums, sums2)] + [sums2[-1]]
    largest = functools.reduce(jnp.maximum, sums)
    for at in halves:
        product = dot(low1[...], low1[:, at : at + half])
        k2[:, at : at + half] = product
        low2[:, at : at + half] = product.astype(jnp.bfloat16)
    for at in halves:
        k3[:, at : at + half] = dot(low2[...], low1[:, at : at + half])
        k4[:, at : at + half] = dot(low2[...], low2[:, at : at + half])

    c = 1.0 / (jnp.max(largest) * (1.0 / tokens) + DAMPING)
    eps = 1.0 - c * DAMPING
    eps2 = eps * eps
    eps3 = eps2 * eps
    eps4 = eps2 * eps2
    c2 = c * c
    c3 = c2 * c
    e1_ = (-c, 0.0, 0.0)
    e2_ = (-2.0 * eps * c, c2, 0.0)
    e3_ = (-3.0 * eps2 * c, 3.0 * eps * c2, -c3)
    e4_ = (-4.0 * eps3 * c, 6.0 * eps2 * c2, -4.0 * eps * c3, c2 * c2)
    u_m, u_ = 1.0 + eps + eps2 + eps3, [x + y + z for x, y, z in zip(e1_, e2_, e3_)]
    w_m, w_ = 4.0 * eps3, [eps2 * x + eps * y + z for x, y, z in zip(e1_, e2_, e3_)]
    a_m, a_ = u_m * w_m, [u_m * x + w_m * y for x, y in zip(w_, u_)]
    y_m, y_e = 1.0 + 2.0 * eps4 + 3.0 * eps4 * eps4, 1.0 + 3.0 * eps4
    v = (1.0 + eps4) * (1.0 + eps4 * eps4)
    q_m = a_m * y_m + v * (1.0 + 2.0 * eps + 3.0 * eps2)
    q_ = (v * (1.0 + eps) * e1_[0] + v * e2_[0], v * e2_[1])
    last = -c2 * (1.0 / tokens)
    p = c * (1.0 + eps) * (1.0 + eps2) * v

    def each_chunk(body):
        def step(i, carry):
            body(pl.ds(pl.multiple_of(i * chunk, chunk), chunk))
            return carry

        lax.fori_loop(0, tokens // chunk, step, 0, unroll=4)

    def mix(weights, some, *powers):
        return functools.reduce(jnp.add, [weight * power[some, :] for weight, power in zip(weights, powers)])

    def first(some):
        x1, x2, x3 = k1[some, :], k2[some, :], k3[some, :]
        u[some, :] = (u_[0] * x1 + u_[1] * x2 + u_[2] * x3).astype(jnp.bfloat16)
        w[some, :] = (w_[0] * x1 + w_[1] * x2 + w_[2] * x3).astype(jnp.bfloat16)
        e4[some, :] = (e4_[0] * x1 + e4_[1] * x2 + e4_[2] * x3 + e4_[3] * k4[some, :]).astype(jnp.bfloat16)

    each_chunk(first)
    for at in halves:
        k4[:, at : at + half] = dot(e4[...], e4[:, at : at + half])
    a_dot = [dot(u[...], w[:, at : at + half]) for at in halves]

    def second(some):
        y = k4[some, :] + y_e * e4[some, :].astype(jnp.float32)
        k4[some, :] = y
        low2[some, :] = y.astype(jnp.bfloat16)

    each_chunk(second)
    for at, product in zip(halves, a_dot):
        k3[:, at : at + half] = a_[2] * k3[:, at : at + half] + product

    def third(some):
        x1, x2 = k1[some, :], k2[some, :]
        a = k3[some, :] + a_[0] * x1 + a_[1] * x2
        k3[some, :] = a * y_m + a_m * k4[some, :] + q_[0] * x1 + q_[1] * x2
        low1[some, :] = a.astype(jnp.bfloat16)

    each_chunk(third)
    for at in halves:
        u[:, at : at + half] = ((k3[:, at : at + half] + dot(low1[...], low2[:, at : at + half])) * last).astype(jnp.bfloat16)
    q_m = q_m * last
    for at in halves:
        product = dot(image[...], u[:, at : at + half])
        mixed[:, at : at + half] = (product + q_m * image[:, at : at + half].astype(jnp.float32)).astype(jnp.bfloat16)
    stores = []
    for far, columns in zip(fars, pairs):
        moved = dot(mixed[...], columns)
        for one in (0, 1):
            here = place(member, far + one, features)
            kept = p * tile[:, here].astype(jnp.float32)
            out[:, here] = (kept + moved[:, one * features : (one + 1) * features]).astype(jnp.bfloat16)
            store = pltpu.make_async_copy(out.at[:, here], out_hbm.at[:, here], sems.at[len(stores)])
            store.start()
            stores.append(store)
    for store in stores:
        store.wait()


def swap(value, far):
    return lax.ppermute(value, "grad", [(i, i ^ far) for i in range(lax.axis_size("grad"))])


def by_tokens(factor_inputs, tile):
    members, replicas = lax.axis_size("grad"), lax.axis_size("dp")
    rows, width = tile.shape
    features = factor_inputs.shape[2]
    tokens = factor_inputs.shape[0] * replicas
    params = pltpu.CompilerParams(vmem_limit_bytes=24 * 2**20)

    def shape(*sizes, kind=jnp.float32):
        return jax.ShapeDtypeStruct(sizes, kind)

    def scratch(*sizes, kind=jnp.bfloat16):
        return pltpu.VMEM(sizes, kind)

    parts = list(split_blocks(factor_inputs))
    for far in range(1, replicas):
        parts[far] = lax.ppermute(parts[far], "dp", [(i, (i + far) % replicas) for i in range(replicas)])
    own = jnp.concatenate(parts, axis=0)
    all_fars = tuple(range(0, members, 2))
    helds = [own] + [swap(own, far) for far in all_fars[1:]]
    pieces, turned, sums, zeros = [], [], [], None
    for count, held in enumerate(helds, 1):
        pieces += [held, swap(held if zeros is None else held + zeros, 1)]
        if count > len(helds) - 2:
            continue
        fars = all_fars[:count]
        one, *sums, new_zeros = pl.pallas_call(
            functools.partial(first_kernel if count == 1 else next_kernel, fars),
            out_shape=[
                shape(2 * features, tokens, kind=jnp.bfloat16),
                shape(tokens, tokens),
                shape(rows, tokens),
                shape(count, 2 * features),
                shape(1, features, kind=jnp.bfloat16),
            ],
            in_specs=[WHOLE] * (3 * count + (0 if count == 1 else 3)),
            out_specs=[WHOLE] * 5,
            compiler_params=params,
            cost_estimate=pl.CostEstimate(
                flops=4 * features * tokens * (tokens + rows + 2 * features * (2 * count - 1)),
                bytes_accessed=0,
                transcendentals=0,
            ),
            name="add_pair",
        )(*pieces, *turned, tile, *sums)
        turned.append(one)
        zeros = new_zeros if zeros is None else zeros
    return pl.pallas_call(
        functools.partial(last_kernel, all_fars),
        out_shape=shape(rows, width, kind=jnp.bfloat16),
        in_specs=[WHOLE] * (len(pieces) + len(turned) + 1 + len(sums)),
        out_specs=ANYWHERE,
        scratch_shapes=[scratch(rows, width)]
        + [scratch(tokens, tokens, kind=jnp.float32)] * 4
        + [scratch(tokens, tokens)] * 5
        + [scratch(rows, tokens)] * 2
        + [pltpu.SemaphoreType.DMA((members,))],
        compiler_params=params,
        cost_estimate=pl.CostEstimate(flops=5 * 10**9, bytes_accessed=0, transcendentals=0),
        name="last_pairs",
    )(*pieces, *turned, tile, *sums)


def local(factor_inputs, gradients):
    features, members = factor_inputs.shape[2], lax.axis_size("grad")
    tokens = factor_inputs.shape[0] * lax.axis_size("dp")
    tile = gradients[0]
    powers_of_two = all(size & (size - 1) == 0 for size in (members, lax.axis_size("dp")))
    if tokens < features * members and features % 128 == 0 and powers_of_two and members > 2:
        result = by_tokens(factor_inputs, tile)
    else:
        result = by_features(gather_block(factor_inputs), tile)
    return result.astype(jnp.bfloat16)[None]


def solution(mesh):
    placed = (P("dp", None, "grad"), P("dp", "grad", None))
    return jax.shard_map(
        local, mesh=mesh, in_specs=placed, out_specs=P("dp", "grad", None), check_vma=False
    )
```

time: 33.5 us -> 32.2 us (0.961)
  between operations: 1.37 us -> 0.04 us
  starting transfers between devices: 9.88 us -> 11.2 us
  waiting for transfers between devices: 7.92 us -> 6.86 us
  local copies, waits for them, and re-layouts: 3.22 us -> 2.2 us
  Pallas kernels: 10.9 us -> 11.6 us
    ppermute x10, starting transfers between devices: 9.88 us -> 11.2 us  [the longest x3 6.96 us: by_tokens(): lax.ppermute(parts[far], 'dp', [(i, (i + far) % replicas) for i in range(...]
    ppermute x10, waiting for transfers between devices: 7.92 us -> 6.86 us  [the longest x7 4.87 us: swap(): lax.ppermute(value, 'grad', [(i, i ^ far) for i in range(lax.axis_size('g...]
    slice x2 -> x0, local copies, waits for them, and re-layouts: 1.03 us -> none  [by_tokens(): after[0, 0] >= 0.0]
    pallas_call x4 -> x3, Pallas kernels: 9.04 us -> 9.83 us  [the longest x1 7.94 us: by_tokens(): pl.pallas_call(functools.partial(last_kernel, all_fars), out_shape=shape(...]
  transfers between devices with their start and end apart: 10 -> 10, of which waited for: 4 -> 6; matrix products, arithmetic and copies ran while one was open for 6% -> 2% of each run, Pallas kernels for 7% -> 6%
where the time goes in v4:
time: 32.2 us; the launch traced here: 31.9 us
  Pallas kernels  11.6 us (36%)
  starting transfers between devices  11.2 us (35%)
  waiting for transfers between devices  6.86 us (21%)
  local copies, waits for them, and re-layouts  2.2 us (7%)
    pallas_call x1, Pallas kernels, by_tokens(): pl.pallas_call(functools.partial(last_kernel, all_fars), out_shape=shape(...  7.94 us
    ppermute x3, starting transfers between devices, by_tokens(): lax.ppermute(parts[far], 'dp', [(i, (i + far) % replicas) for i in range(...  6.96 us
    ppermute x7, waiting for transfers between devices, swap(): lax.ppermute(value, 'grad', [(i, i ^ far) for i in range(lax.axis_size('g...  4.87 us
    ppermute x7, starting transfers between devices, swap(): lax.ppermute(value, 'grad', [(i, i ^ far) for i in range(lax.axis_size('g...  4.2 us
    unnamed x5, local copies, waits for them, and re-layouts  2.19 us
    ppermute x3, waiting for transfers between devices, by_tokens(): lax.ppermute(parts[far], 'dp', [(i, (i + far) % replicas) for i in range(...  2 us
    pallas_call x2, Pallas kernels, by_tokens(): pl.pallas_call(functools.partial(first_kernel if count == 1 else next_ker...  1.89 us
    pallas_call x1, Pallas kernels, split_blocks(): pl.pallas_call(split_kernel, out_shape=[jax.ShapeDtypeStruct((tokens, fea...  1.81 us
  transfers between devices with their start and end apart: 10, of which 6 were waited for; matrix products, arithmetic and copies ran while one was open for 2% of the time, Pallas kernels for 6%

profile of v4, /device:TPU:0, one launch (start us, length us, event | category | flops | bytes accessed | tf_op | source)
XLA Modules:
  0.0 31.9 jit_solution(4642988992182204972)
XLA Ops:
  0.0 1.8 %split_blocks.1 = (bf16[128,128]{1,0:T(8,128)(2,1)}, bf16[128,128]{1,0:T(8,128)(2,1)}, bf16[128,128]{1,0:T(8,128)(2,1)}, bf16[128,128]{1,0:T(8,128)(2,1)}) custom-call(bf16[512,128]{1,0:T(8,128)(2,1)} %bitcast.8), custom_call_target="tpu_custom_call" | custom-call | tf_op jit(solution)/shard_map/split_blocks/pallas_call | solution.py:55
  1.8 3.0 %collective-permute-start = (bf16[128,128]{1,0:T(8,128)(2,1)}, bf16[128,128]{1,0:T(8,128)(2,1)S(1)}, u32[]{:S(2)}, u32[]{:S(2)}) collective-permute-start(bf16[128,128]{1,0:T(8,128)(2,1)} %get-tuple-element.19), channel_id=1, source_target_pairs={{0,8},{8,16},{16,24},{24,0},{1,9},{9,17},{17,25},{25,1},{2,10},{10... | collective-permute-start | bytes 98312 | tf_op jit(solution)/shard_map/ppermute | solution.py:242
  4.8 2.6 %collective-permute-start.1 = (bf16[128,128]{1,0:T(8,128)(2,1)}, bf16[128,128]{1,0:T(8,128)(2,1)S(1)}, u32[]{:S(2)}, u32[]{:S(2)}) collective-permute-start(bf16[128,128]{1,0:T(8,128)(2,1)} %get-tuple-element.20), channel_id=1, source_target_pairs={{0,16},{8,24},{16,0},{24,8},{1,17},{9,25},{17,1},{25,9},{2,18},{10... | collective-permute-start | bytes 98312 | tf_op jit(solution)/shard_map/ppermute | solution.py:242
  7.4 1.3 %collective-permute-start.2 = (bf16[128,128]{1,0:T(8,128)(2,1)}, bf16[128,128]{1,0:T(8,128)(2,1)S(1)}, u32[]{:S(2)}, u32[]{:S(2)}) collective-permute-start(bf16[128,128]{1,0:T(8,128)(2,1)} %get-tuple-element.21), channel_id=1, source_target_pairs={{0,24},{8,0},{16,8},{24,16},{1,25},{9,1},{17,9},{25,17},{2,26},{10... | collective-permute-start | bytes 98312 | tf_op jit(solution)/shard_map/ppermute | solution.py:242
  8.8 0.8 %constant_dynamic-update-slice_fusion.3 = bf16[512,128]{1,0:T(8,128)(2,1)S(1)} fusion(bf16[128,128]{1,0:T(8,128)(2,1)} %get-tuple-element.18), kind=kLoop, calls=%fused_computation.6 | loop fusion | bytes 65536
  9.5 0.0 collective-permute-done
  9.5 0.7 %collective-permute-done.1 = bf16[128,128]{1,0:T(8,128)(2,1)S(1)} collective-permute-done((bf16[128,128]{1,0:T(8,128)(2,1)}, bf16[128,128]{1,0:T(8,128)(2,1)S(1)}, u32[]{:S(2)}, u32[]{:S(2)}) %collective-permute-start.1) | collective-permute-done | bytes 32800 | tf_op jit(solution)/shard_map/ppermute | solution.py:242
  10.2 1.3 %collective-permute-done.2 = bf16[128,128]{1,0:T(8,128)(2,1)S(1)} collective-permute-done((bf16[128,128]{1,0:T(8,128)(2,1)}, bf16[128,128]{1,0:T(8,128)(2,1)S(1)}, u32[]{:S(2)}, u32[]{:S(2)}) %collective-permute-start.2) | collective-permute-done | bytes 32800 | tf_op jit(solution)/shard_map/ppermute | solution.py:242
  11.6 0.0 collective-permute-start.3
  11.6 2.5 %collective-permute-start.8 = (bf16[512,128]{1,0:T(8,128)(2,1)S(1)}, bf16[512,128]{1,0:T(8,128)(2,1)S(1)}, u32[]{:S(2)}, u32[]{:S(2)}) collective-permute-start(bf16[512,128]{1,0:T(8,128)(2,1)S(1)} %constant_dynamic-update-slice_fusion.p0.refs_0_), channel_id=1, source_target_pairs={{0,6},{1,7},{2,4},{3,5},{4,2},{5,3},{6,0},{7,1},{8,14},{9,15},{10,... | collective-permute-start | bytes 393224 | tf_op jit(solution)/shard_map/ppermute | solution.py:224
  14.1 0.5 %collective-permute-start.6 = (bf16[512,128]{1,0:T(8,128)(2,1)S(1)}, bf16[512,128]{1,0:T(8,128)(2,1)S(1)}, u32[]{:S(2)}, u32[]{:S(2)}) collective-permute-start(bf16[512,128]{1,0:T(8,128)(2,1)S(1)} %constant_dynamic-update-slice_fusion.p0.refs_0_), channel_id=1, source_target_pairs={{0,4},{1,5},{2,6},{3,7},{4,0},{5,1},{6,2},{7,3},{8,12},{9,13},{10,... | collective-permute-start | bytes 393224 | tf_op jit(solution)/shard_map/ppermute | solution.py:224
  14.6 0.5 %collective-permute-start.4 = (bf16[512,128]{1,0:T(8,128)(2,1)S(1)}, bf16[512,128]{1,0:T(8,128)(2,1)S(1)}, u32[]{:S(2)}, u32[]{:S(2)}) collective-permute-start(bf16[512,128]{1,0:T(8,128)(2,1)S(1)} %constant_dynamic-update-slice_fusion.p0.refs_0_), channel_id=1, source_target_pairs={{0,2},{1,3},{2,0},{3,1},{4,6},{5,7},{6,4},{7,5},{8,10},{9,11},{10,... | collective-permute-start | bytes 393224 | tf_op jit(solution)/shard_map/ppermute | solution.py:224
  15.1 0.0 collective-permute-done.3.p1.refs_1_
  15.1 0.0 copy-start
  15.1 1.4 %copy-done = bf16[1,768,1024]{2,1,0:T(8,128)(2,1)S(1)} copy-done((bf16[1,768,1024]{2,1,0:T(8,128)(2,1)S(1)}, bf16[1,768,1024]{2,1,0:T(8,128)(2,1)}, u32[]{:S(2)}) %copy-start) | copy-done | bytes 1572888
  16.5 0.6 %add_pair.2 = (bf16[256,512]{1,0:T(8,128)(2,1)S(1)}, f32[512,512]{1,0:T(8,128)S(1)}, f32[768,512]{1,0:T(8,128)S(1)}, f32[1,256]{1,0:T(1,128)S(1)}, bf16[1,128]{1,0:T(2,128)(2,1)S(1)}) custom-call(bf16[512,128]{1,0:T(8,128)(2,1)S(1)} %constant_dynamic-update-slice_fusion.p0.refs_0_, bf16[512,128]{1,0:T(8,128)(2,1)S(1)} %collective-permute-done.3.p1.refs_1_, ...), custom_call_target="tpu_custom_call" | custom-call | flops 402653184 | tf_op jit(solution)/shard_map/add_pair/pallas_call | solution.py:252
  17.2 1.5 %collective-permute-done.8.refs_6_ = bf16[512,128]{1,0:T(8,128)(2,1)S(1)} collective-permute-done((bf16[512,128]{1,0:T(8,128)(2,1)S(1)}, bf16[512,128]{1,0:T(8,128)(2,1)S(1)}, u32[]{:S(2)}, u32[]{:S(2)}) %collective-permute-start.8) | collective-permute-done | bytes 131104 | tf_op jit(solution)/shard_map/ppermute | solution.py:224
  18.7 2.5 %collective-permute-done.6.refs_4_ = bf16[512,128]{1,0:T(8,128)(2,1)S(1)} collective-permute-done((bf16[512,128]{1,0:T(8,128)(2,1)S(1)}, bf16[512,128]{1,0:T(8,128)(2,1)S(1)}, u32[]{:S(2)}, u32[]{:S(2)}) %collective-permute-start.6) | collective-permute-done | bytes 131104 | tf_op jit(solution)/shard_map/ppermute | solution.py:224
  21.2 0.1 collective-permute-done.4.refs_2_
  21.3 0.1 collective-permute-start.5
  21.4 0.5 %collective-permute-start.9 = (bf16[512,128]{1,0:T(8,128)(2,1)S(1)}, bf16[512,128]{1,0:T(8,128)(2,1)S(1)}, u32[]{:S(2)}, u32[]{:S(2)}) collective-permute-start(bf16[512,128]{1,0:T(8,128)(2,1)S(1)} %get-tuple-element.31), channel_id=1, source_target_pairs={{0,1},{1,0},{2,3},{3,2},{4,5},{5,4},{6,7},{7,6},{8,9},{9,8},{10,11... | collective-permute-start | bytes 393224 | tf_op jit(solution)/shard_map/ppermute | solution.py:224
  21.9 0.1 collective-permute-start.7
  22.0 0.8 %collective-permute-done.5.refs_3_ = bf16[512,128]{1,0:T(8,128)(2,1)S(1)} collective-permute-done((bf16[512,128]{1,0:T(8,128)(2,1)S(1)}, bf16[512,128]{1,0:T(8,128)(2,1)S(1)}, u32[]{:S(2)}, u32[]{:S(2)}) %collective-permute-start.5) | collective-permute-done | bytes 131104 | tf_op jit(solution)/shard_map/ppermute | solution.py:224
  22.7 1.3 %add_pair.3 = (bf16[256,512]{1,0:T(8,128)(2,1)S(1)}, f32[512,512]{1,0:T(8,128)S(1)}, f32[768,512]{1,0:T(8,128)S(1)}, f32[2,256]{1,0:T(2,128)S(1)}, bf16[1,128]{1,0:T(2,128)(2,1)}) custom-call(bf16[512,128]{1,0:T(8,128)(2,1)S(1)} %constant_dynamic-update-slice_fusion.p0.refs_0_, bf16[512,128]{1,0:T(8,128)(2,1)S(1)} %collective-permute-done.3.p1.refs_1_, ...), custom_call_target="tpu_custom_call" | custom-call | flops 536870912 | tf_op jit(solution)/shard_map/add_pair/pallas_call | solution.py:252
  24.0 0.0 collective-permute-done.9.refs_7_
  24.0 0.0 collective-permute-done.7.refs_5_
  24.0 7.9 %last_pairs.1 = bf16[768,1024]{1,0:T(8,128)(2,1)} custom-call(bf16[512,128]{1,0:T(8,128)(2,1)S(1)} %constant_dynamic-update-slice_fusion.p0.refs_0_, bf16[512,128]{1,0:T(8,128)(2,1)S(1)} %collective-permute-done.3.p1.refs_1_, bf16[512,128]{1,0:T(8,128)(2,1)S(1)} %collective-permute-done.4.refs_2_, bf16[512,128]{1,0:T(8,128)(2,1)S(1)} %collective-permute-done.5.refs_3_, ...), custom_call_target="tpu_custom_call" | custom-call | flops 5000000000 | tf_op jit(solution)/shard_map/last_pairs/pallas_call | solution.py:273
  (4 shorter events, 0.1 us)
Async XLA Ops:
  1.8 7.7 %collective-permute-start = (bf16[128,128]{1,0:T(8,128)(2,1)}, bf16[128,128]{1,0:T(8,128)(2,1)S(1)}, u32[]{:S(2)}, u32[]{:S(2)}) collective-permute-start(bf16[128,128]{1,0:T(8,128)(2,1)} %get-tuple-element.19), channel_id=1, source_target_pairs={{0,8},{8,16},{16,24},{24,0},{1,9},{9,17},{17,25},{25,1},{2,10},{10... | collective-permute-start | bytes 98312 | tf_op jit(solution)/shard_map/ppermute | solution.py:242
  4.8 5.4 %collective-permute-start.1 = (bf16[128,128]{1,0:T(8,128)(2,1)}, bf16[128,128]{1,0:T(8,128)(2,1)S(1)}, u32[]{:S(2)}, u32[]{:S(2)}) collective-permute-start(bf16[128,128]{1,0:T(8,128)(2,1)} %get-tuple-element.20), channel_id=1, source_target_pairs={{0,16},{8,24},{16,0},{24,8},{1,17},{9,25},{17,1},{25,9},{2,18},{10... | collective-permute-start | bytes 98312 | tf_op jit(solution)/shard_map/ppermute | solution.py:242
  7.4 4.1 %collective-permute-start.2 = (bf16[128,128]{1,0:T(8,128)(2,1)}, bf16[128,128]{1,0:T(8,128)(2,1)S(1)}, u32[]{:S(2)}, u32[]{:S(2)}) collective-permute-start(bf16[128,128]{1,0:T(8,128)(2,1)} %get-tuple-element.21), channel_id=1, source_target_pairs={{0,24},{8,0},{16,8},{24,16},{1,25},{9,1},{17,9},{25,17},{2,26},{10... | collective-permute-start | bytes 98312 | tf_op jit(solution)/shard_map/ppermute | solution.py:242
  11.6 3.6 %collective-permute-start.3 = (bf16[512,128]{1,0:T(8,128)(2,1)S(1)}, bf16[512,128]{1,0:T(8,128)(2,1)S(1)}, u32[]{:S(2)}, u32[]{:S(2)}) collective-permute-start(bf16[512,128]{1,0:T(8,128)(2,1)S(1)} %constant_dynamic-update-slice_fusion.p0.refs_0_), channel_id=1, source_target_pairs={{0,1},{1,0},{2,3},{3,2},{4,5},{5,4},{6,7},{7,6},{8,9},{9,8},{10,11... | collective-permute-start | bytes 393224 | tf_op jit(solution)/shard_map/ppermute | solution.py:224
  11.6 7.1 %collective-permute-start.8 = (bf16[512,128]{1,0:T(8,128)(2,1)S(1)}, bf16[512,128]{1,0:T(8,128)(2,1)S(1)}, u32[]{:S(2)}, u32[]{:S(2)}) collective-permute-start(bf16[512,128]{1,0:T(8,128)(2,1)S(1)} %constant_dynamic-update-slice_fusion.p0.refs_0_), channel_id=1, source_target_pairs={{0,6},{1,7},{2,4},{3,5},{4,2},{5,3},{6,0},{7,1},{8,14},{9,15},{10,... | collective-permute-start | bytes 393224 | tf_op jit(solution)/shard_map/ppermute | solution.py:224
  14.1 7.1 %collective-permute-start.6 = (bf16[512,128]{1,0:T(8,128)(2,1)S(1)}, bf16[512,128]{1,0:T(8,128)(2,1)S(1)}, u32[]{:S(2)}, u32[]{:S(2)}) collective-permute-start(bf16[512,128]{1,0:T(8,128)(2,1)S(1)} %constant_dynamic-update-slice_fusion.p0.refs_0_), channel_id=1, source_target_pairs={{0,4},{1,5},{2,6},{3,7},{4,0},{5,1},{6,2},{7,3},{8,12},{9,13},{10,... | collective-permute-start | bytes 393224 | tf_op jit(solution)/shard_map/ppermute | solution.py:224
  14.6 6.7 %collective-permute-start.4 = (bf16[512,128]{1,0:T(8,128)(2,1)S(1)}, bf16[512,128]{1,0:T(8,128)(2,1)S(1)}, u32[]{:S(2)}, u32[]{:S(2)}) collective-permute-start(bf16[512,128]{1,0:T(8,128)(2,1)S(1)} %constant_dynamic-update-slice_fusion.p0.refs_0_), channel_id=1, source_target_pairs={{0,2},{1,3},{2,0},{3,1},{4,6},{5,7},{6,4},{7,5},{8,10},{9,11},{10,... | collective-permute-start | bytes 393224 | tf_op jit(solution)/shard_map/ppermute | solution.py:224
  15.1 1.4 %copy-start = (bf16[1,768,1024]{2,1,0:T(8,128)(2,1)S(1)}, bf16[1,768,1024]{2,1,0:T(8,128)(2,1)}, u32[]{:S(2)}) copy-start(bf16[1,768,1024]{2,1,0:T(8,128)(2,1)} %param.3) | copy-start | bytes 4718596
  21.3 1.4 %collective-permute-start.5 = (bf16[512,128]{1,0:T(8,128)(2,1)S(1)}, bf16[512,128]{1,0:T(8,128)(2,1)S(1)}, u32[]{:S(2)}, u32[]{:S(2)}) collective-permute-start(bf16[512,128]{1,0:T(8,128)(2,1)S(1)} %get-tuple-element.33), channel_id=1, source_target_pairs={{0,1},{1,0},{2,3},{3,2},{4,5},{5,4},{6,7},{7,6},{8,9},{9,8},{10,11... | collective-permute-start | bytes 393224 | tf_op jit(solution)/shard_map/ppermute | solution.py:224
  21.4 2.6 %collective-permute-start.9 = (bf16[512,128]{1,0:T(8,128)(2,1)S(1)}, bf16[512,128]{1,0:T(8,128)(2,1)S(1)}, u32[]{:S(2)}, u32[]{:S(2)}) collective-permute-start(bf16[512,128]{1,0:T(8,128)(2,1)S(1)} %get-tuple-element.31), channel_id=1, source_target_pairs={{0,1},{1,0},{2,3},{3,2},{4,5},{5,4},{6,7},{7,6},{8,9},{9,8},{10,11... | collective-permute-start | bytes 393224 | tf_op jit(solution)/shard_map/ppermute | solution.py:224
  21.9 2.1 %collective-permute-start.7 = (bf16[512,128]{1,0:T(8,128)(2,1)S(1)}, bf16[512,128]{1,0:T(8,128)(2,1)S(1)}, u32[]{:S(2)}, u32[]{:S(2)}) collective-permute-start(bf16[512,128]{1,0:T(8,128)(2,1)S(1)} %get-tuple-element.32), channel_id=1, source_target_pairs={{0,1},{1,0},{2,3},{3,2},{4,5},{5,4},{6,7},{7,6},{8,9},{9,8},{10,11... | collective-permute-start | bytes 393224 | tf_op jit(solution)/shard_map/ppermute | solution.py:224

commit v5 on v0

v5 whole, which is shorter than its diff:
```python
import functools

import jax
import jax.numpy as jnp
from jax import lax
from jax.experimental import pallas as pl
from jax.experimental.pallas import tpu as pltpu
from jax.sharding import PartitionSpec as P

ITERS = 4
DAMPING = 0.01
WHOLE = pl.BlockSpec(memory_space=pltpu.VMEM)
ANYWHERE = pl.BlockSpec(memory_space=pl.ANY)


def dot(a, b):
    return jnp.dot(a, b, preferred_element_type=jnp.float32)


def gather_block(factor_inputs):
    pieces = jnp.transpose(factor_inputs, (1, 0, 2))
    piece = lax.all_to_all(pieces, "dp", split_axis=0, concat_axis=1, tiled=True)[0]
    return lax.all_gather(piece, "grad", axis=1, tiled=True)


def by_features(columns, tile):
    tokens, width = columns.shape
    covariance = jnp.einsum("tr,tc->rc", columns, columns, preferred_element_type=jnp.float32) * (1.0 / tokens)
    damped = covariance + DAMPING * jnp.eye(width, dtype=jnp.float32)
    scale = 1.0 / jnp.max(jnp.sum(jnp.abs(damped), axis=1))
    image = scale * damped
    result = scale * tile.astype(jnp.float32)
    for step in range(ITERS):
        low = image.astype(jnp.bfloat16)
        result = 2.0 * result - dot(result.astype(jnp.bfloat16), low)
        if step < ITERS - 1:
            image = 2.0 * image - dot(low, low)
    return result


def split_kernel(x_ref, tile_hbm, *refs):
    *out_refs, tile, sem = refs
    load = pltpu.make_async_copy(tile_hbm, tile, sem)
    load.start()
    replicas, tokens = len(out_refs), out_refs[0].shape[0]
    here = lax.axis_index("dp")
    x = x_ref[...]
    rows = lax.broadcasted_iota(jnp.int32, (tokens, tokens * replicas), 0)
    cols = lax.broadcasted_iota(jnp.int32, (tokens, tokens * replicas), 1)
    offset = cols - rows * replicas
    for far, out_ref in enumerate(out_refs):
        choice = jnp.where(offset == lax.rem(here + far, replicas), 1.0, 0.0).astype(jnp.bfloat16)
        out_ref[...] = dot(choice, x).astype(jnp.bfloat16)
    load.wait()


def split_blocks(factor_inputs, tile):
    tokens, blocks, features = factor_inputs.shape
    return pl.pallas_call(
        split_kernel,
        out_shape=[jax.ShapeDtypeStruct((tokens, features), factor_inputs.dtype)] * blocks
        + [jax.ShapeDtypeStruct(tile.shape, tile.dtype)],
        in_specs=[WHOLE, ANYWHERE],
        out_specs=[WHOLE] * (blocks + 1),
        scratch_shapes=[pltpu.SemaphoreType.DMA],
        compiler_params=pltpu.CompilerParams(vmem_limit_bytes=52 * 2**20),
        name="split_blocks",
    )(factor_inputs.reshape(tokens * blocks, features), tile)


def place(member, far, features):
    return pl.ds(pl.multiple_of((member ^ far) * features, features), features)


def chosen(tile, member, fars, features):
    return jnp.concatenate([tile[:, place(member, far, features)] for far in fars], axis=1)


def magnitudes(a, b):
    return jnp.abs(dot(a, b))


def first_kernel(own, near, tile, turned, gram, image, sums, zeros):
    member = lax.axis_index("grad")
    features = own.shape[1]
    columns = jnp.concatenate([own[...], near[...]], axis=1)
    turned[...] = columns.T
    gram[...] = dot(columns, turned[...])
    image[...] = dot(chosen(tile, member, (0, 1), features), turned[...])
    sums[...] = jnp.sum(magnitudes(turned[...], columns), axis=0, keepdims=True)
    zeros[...] = jnp.zeros_like(zeros)


def last_kernel(fars, *refs):
    count = len(fars)
    pieces, refs = refs[: 2 * count + 2], refs[2 * count + 2 :]
    turned, tile, gram_in, image_in, sums_in, out_hbm, *refs = refs
    out, x, xt, k1, k2, k3, k4, low1, low2, g, h, z, image, mixed, sems = refs
    member = lax.axis_index("grad")
    tokens, features = pieces[0].shape
    half = 2 * features
    halves = [slice(at, at + half) for at in range(0, tokens, half)]
    blocks = [slice(at, at + half) for at in range(0, x.shape[1], half)]
    chunks = [slice(at, at + 32) for at in range(0, tokens, 32)]
    all_fars = [far + one for far in (0,) + fars for one in (0, 1)]

    xt[:half, :] = turned[...]
    for k, piece in enumerate(pieces):
        some = slice(k * features, (k + 1) * features)
        x[:, some] = piece[...]
        if k > 1:
            xt[some, :] = piece[...].T
    for some in halves:
        gram = (gram_in[:, some] + dot(x[:, half:], xt[half:, some])) * (1.0 / tokens)
        k1[:, some] = gram
        low1[:, some] = gram.astype(jnp.bfloat16)

    column_sums = [sums_in[...]] + [0.0] * count
    row_sums = [0.0] * (count + 1)
    for j in range(1, count + 1):
        for i in range(j + 1):
            block = magnitudes(xt[blocks[i], :], x[:, blocks[j]])
            column_sums[j] = column_sums[j] + jnp.sum(block, axis=0, keepdims=True)
            if i < j:
                row_sums[i] = row_sums[i] + block[:, :features] + block[:, features:]
    largest = column_sums[count]
    for i in range(count):
        largest = jnp.maximum(largest, column_sums[i] + jnp.sum(row_sums[i].T, axis=0, keepdims=True))
    c = 1.0 / (jnp.max(largest) * (1.0 / tokens) + DAMPING)

    eps = 1.0 - c * DAMPING
    eps2 = eps * eps
    zeta = eps2 * eps2
    eps8 = zeta * zeta
    e2_1, e2_2 = -2.0 * eps * c, c * c
    g_1 = -(1.0 + eps) * c
    g_m = eps2 + (1.0 + eps) * eps + eps
    h_m = zeta + (1.0 + eps2) * eps2 + eps2
    k_m = eps8 + (1.0 + zeta) * zeta + zeta + 1.0 + eps8
    k_z = 1.0 + 3.0 * zeta
    a_m = g_m * h_m
    a_e2 = g_m * (1.0 + eps2) + h_m
    a_1 = h_m * g_1
    beta = (1.0 + zeta) * (1.0 + eps8)
    q_m = a_m * k_m + beta * g_m + (1.0 + eps2) * beta
    last = -c * c * (1.0 / tokens)
    p = c * (1.0 + eps) * (1.0 + eps2) * beta

    def move(some):
        product = dot(chosen(tile, member, all_fars[2:], features), xt[half:, some])
        image[:, some] = (image_in[:, some] + product).astype(jnp.bfloat16)

    for some in halves:
        product = dot(low1[...], low1[:, some])
        for r in chunks:
            x1 = k1[r, some]
            e2 = e2_1 * x1 + e2_2 * product[r]
            k2[r, some] = e2
            low2[r, some] = e2.astype(jnp.bfloat16)
            g[r, some] = (e2 + g_1 * x1).astype(jnp.bfloat16)
    move(halves[0])
    for some in halves:
        product = dot(low2[...], low2[:, some])
        for r in chunks:
            e2 = k2[r, some]
            fourth = 2.0 * eps2 * e2 + product[r]
            k3[r, some] = fourth
            z[r, some] = fourth.astype(jnp.bfloat16)
            h[r, some] = (fourth + (1.0 + eps2) * e2).astype(jnp.bfloat16)
    for some in halves[1:]:
        move(some)
    for some in halves:
        product = dot(z[...], z[:, some])
        for r in chunks:
            k = product[r] + k_z * k3[r, some]
            k4[r, some] = k
            low2[r, some] = k.astype(jnp.bfloat16)
    for some in halves:
        product = dot(g[...], h[:, some])
        for r in chunks:
            x1, e2 = k1[r, some], k2[r, some]
            a = product[r] + g_m * k3[r, some] + a_e2 * e2 + a_1 * x1
            low1[r, some] = a.astype(jnp.bfloat16)
            k4[r, some] = last * (a_m * k4[r, some] + k_m * a + beta * (e2 + g_1 * x1))
    for some in halves:
        product = dot(low1[...], low2[:, some])
        for r in chunks:
            g[r, some] = (k4[r, some] + last * product[r]).astype(jnp.bfloat16)
    q_m = q_m * last
    for some in halves:
        product = dot(image[...], g[:, some])
        mixed[:, some] = (product + q_m * image[:, some].astype(jnp.float32)).astype(jnp.bfloat16)
    stores = []
    for k, some in enumerate(blocks):
        moved = dot(mixed[...], x[:, some])
        for one in (0, 1):
            here = place(member, all_fars[2 * k + one], features)
            kept = p * tile[:, here].astype(jnp.float32)
            out[:, here] = (kept + moved[:, one * features : (one + 1) * features]).astype(jnp.bfloat16)
            store = pltpu.make_async_copy(out.at[:, here], out_hbm.at[:, here], sems.at[len(stores)])
            store.start()
            stores.append(store)
    for store in stores:
        store.wait()


def swap(value, far):
    return lax.ppermute(value, "grad", [(i, i ^ far) for i in range(lax.axis_size("grad"))])


def by_tokens(factor_inputs, tile):
    members, replicas = lax.axis_size("grad"), lax.axis_size("dp")
    rows, width = tile.shape
    features = factor_inputs.shape[2]
    tokens = factor_inputs.shape[0] * replicas
    params = pltpu.CompilerParams(vmem_limit_bytes=24 * 2**20)

    def shape(*sizes, kind=jnp.float32):
        return jax.ShapeDtypeStruct(sizes, kind)

    def scratch(*sizes, kind=jnp.bfloat16):
        return pltpu.VMEM(sizes, kind)

    *parts, tile = split_blocks(factor_inputs, tile)
    arrived = [
        lax.ppermute(parts[far], "dp", [(i, (i + far) % replicas) for i in range(replicas)])
        for far in range(1, replicas)
    ]
    fars = tuple(range(2, members, 2))
    own = jnp.concatenate([parts[0]] + arrived, axis=0)
    near = swap(own, 1)
    held = [swap(own, far) for far in fars]
    *state, zeros = pl.pallas_call(
        first_kernel,
        out_shape=[
            shape(2 * features, tokens, kind=jnp.bfloat16),
            shape(tokens, tokens),
            shape(rows, tokens),
            shape(1, 2 * features),
            shape(1, features, kind=jnp.bfloat16),
        ],
        in_specs=[WHOLE] * 3,
        out_specs=[WHOLE] * 5,
        compiler_params=params,
        cost_estimate=pl.CostEstimate(flops=4 * 10**8, bytes_accessed=0, transcendentals=0),
        name="first_pair",
    )(own, near, tile)
    pieces = [own, near]
    for k, piece in enumerate(held):
        pieces += [piece, swap(piece if k else piece + zeros, 1)]
    inputs = [*pieces, state[0], tile, *state[1:]]
    return pl.pallas_call(
        functools.partial(last_kernel, fars),
        out_shape=shape(rows, width, kind=jnp.bfloat16),
        in_specs=[WHOLE] * len(inputs),
        out_specs=ANYWHERE,
        scratch_shapes=[scratch(rows, width), scratch(tokens, width), scratch(width, tokens)]
        + [scratch(tokens, tokens, kind=jnp.float32)] * 4
        + [scratch(tokens, tokens)] * 5
        + [scratch(rows, tokens)] * 2
        + [pltpu.SemaphoreType.DMA((members,))],
        compiler_params=params,
        cost_estimate=pl.CostEstimate(flops=5 * 10**9, bytes_accessed=0, transcendentals=0),
        name="last_pairs",
    )(*inputs)


def local(factor_inputs, gradients):
    features, members = factor_inputs.shape[2], lax.axis_size("grad")
    tokens = factor_inputs.shape[0] * lax.axis_size("dp")
    tile = gradients[0]
    powers_of_two = all(size & (size - 1) == 0 for size in (members, lax.axis_size("dp")))
    if tokens < features * members and features % 128 == 0 and powers_of_two and members > 2:
        result = by_tokens(factor_inputs, tile)
    else:
        result = by_features(gather_block(factor_inputs), tile)
    return result.astype(jnp.bfloat16)[None]


def solution(mesh):
    placed = (P("dp", None, "grad"), P("dp", "grad", None))
    return jax.shard_map(
        local, mesh=mesh, in_specs=placed, out_specs=P("dp", "grad", None), check_vma=False
    )
```

time: 265 us -> 29.2 us (0.11)
  waiting for transfers between devices: 209 us -> 8.46 us
  matrix products: 21.3 us -> 0 us
  between operations: 14.2 us -> 0.03 us
  blocking collectives: 14.1 us -> 0 us
  starting transfers between devices: 0.25 us -> 10.7 us
  Pallas kernels: 0 us -> 8.87 us
  other arithmetic: 2.73 us -> 0.01 us
    all_gather x6 -> x0, waiting for transfers between devices: 165 us -> none  [the longest x4 110 us: local(): whole = lax.all_gather(iterate, 'grad', axis=0, tiled=True)]
    reduce_scatter x1 -> x0, waiting for transfers between devices: 43.9 us -> none  [local(): lax.psum_scatter(partial_value, 'dp', scatter_dimension=0, tiled=True)]
    dot_general x6 -> x0, matrix products: 21.3 us -> none  [the longest x4 14.8 us: local(): product = jnp.dot(image, whole, preferred_element_type=jnp.float32)]
    pmax x1 -> x0, blocking collectives: 14.1 us -> none  [local(): bound = lax.pmax(jnp.max(jnp.sum(jnp.abs(damped), axis=1)), 'grad')]
    ppermute x0 -> x10, starting transfers between devices: none -> 10.7 us  [the longest x3 7.01 us: by_tokens(): lax.ppermute(parts[far], 'dp', [(i, (i + far) % replicas) for i in range(...]
    pallas_call x0 -> x3, Pallas kernels: none -> 8.87 us  [the longest x1 6.73 us: by_tokens(): pl.pallas_call(functools.partial(last_kernel, fars), out_shape=shape(rows...]
    ppermute x0 -> x10, waiting for transfers between devices: none -> 8.46 us  [the longest x7 5.92 us: swap(): lax.ppermute(value, 'grad', [(i, i ^ far) for i in range(lax.axis_size('g...]
  transfers between devices with their start and end apart: 7 -> 10, of which waited for: 7 -> 7; matrix products, arithmetic and copies ran while one was open for 0% -> 0% of each run, Pallas kernels for 0% -> 2%
where the time goes in v5:
time: 29.2 us; the launch traced here: 29 us
  starting transfers between devices  10.7 us (37%)
  Pallas kernels  8.87 us (30%)
  waiting for transfers between devices  8.46 us (29%)
  local copies, waits for them, and re-layouts  0.93 us (3%)
    ppermute x3, starting transfers between devices, by_tokens(): lax.ppermute(parts[far], 'dp', [(i, (i + far) % replicas) for i in range(...  7.01 us
    pallas_call x1, Pallas kernels, by_tokens(): pl.pallas_call(functools.partial(last_kernel, fars), out_shape=shape(rows...  6.73 us
    ppermute x7, waiting for transfers between devices, swap(): lax.ppermute(value, 'grad', [(i, i ^ far) for i in range(lax.axis_size('g...  5.92 us
    ppermute x7, starting transfers between devices, swap(): lax.ppermute(value, 'grad', [(i, i ^ far) for i in range(lax.axis_size('g...  3.71 us
    ppermute x3, waiting for transfers between devices, by_tokens(): lax.ppermute(parts[far], 'dp', [(i, (i + far) % replicas) for i in range(...  2.54 us
    pallas_call x1, Pallas kernels, split_blocks(): pl.pallas_call(split_kernel, out_shape=[jax.ShapeDtypeStruct((tokens, fea...  1.5 us
    unnamed x5, local copies, waits for them, and re-layouts  0.92 us
    pallas_call x1, Pallas kernels, by_tokens(): pl.pallas_call(first_kernel, out_shape=[shape(2 * features, tokens, kind=...  0.64 us
  transfers between devices with their start and end apart: 10, of which 7 were waited for; matrix products, arithmetic and copies ran while one was open for 0% of the time, Pallas kernels for 2%

profile of v5, /device:TPU:0, one launch (start us, length us, event | category | flops | bytes accessed | tf_op | source)
XLA Modules:
  0.0 29.0 jit_solution(16357749114272256975)
XLA Ops:
  0.0 0.0 copy-start
  0.0 0.9 %copy-done = bf16[128,4,128]{2,1,0:T(4,128)(2,1)S(1)} copy-done((bf16[128,4,128]{2,1,0:T(4,128)(2,1)S(1)}, bf16[128,4,128]{2,1,0:T(4,128)(2,1)}, u32[]{:S(2)}) %copy-start) | copy-done | bytes 131096
  0.9 1.5 %split_blocks.1 = (bf16[128,128]{1,0:T(8,128)(2,1)S(1)}, bf16[128,128]{1,0:T(8,128)(2,1)S(1)}, bf16[128,128]{1,0:T(8,128)(2,1)S(1)}, bf16[128,128]{1,0:T(8,128)(2,1)S(1)}, bf16[768,1024]{1,0:T(8,128)(2,1)S(1)}) custom-call(bf16[512,128]{1,0:T(8,128)(2,1)S(1)} %bitcast.4, bf16[768,1024]{1,0:T(8,128)(2,1)} %bitcast.6), custom_call_target="tpu_custom_call" | custom-call | tf_op jit(solution)/shard_map/split_blocks/pallas_call | solution.py:59
  2.4 3.1 %collective-permute-start = (bf16[128,128]{1,0:T(8,128)(2,1)S(1)}, bf16[128,128]{1,0:T(8,128)(2,1)S(1)}, u32[]{:S(2)}, u32[]{:S(2)}) collective-permute-start(bf16[128,128]{1,0:T(8,128)(2,1)S(1)} %get-tuple-element.16), channel_id=1, source_target_pairs={{0,8},{8,16},{16,24},{24,0},{1,9},{9,17},{17,25},{25,1},{2,10},{10... | collective-permute-start | bytes 98312 | tf_op jit(solution)/shard_map/ppermute | solution.py:226
  5.5 2.6 %collective-permute-start.1 = (bf16[128,128]{1,0:T(8,128)(2,1)S(1)}, bf16[128,128]{1,0:T(8,128)(2,1)S(1)}, u32[]{:S(2)}, u32[]{:S(2)}) collective-permute-start(bf16[128,128]{1,0:T(8,128)(2,1)S(1)} %get-tuple-element.17), channel_id=1, source_target_pairs={{0,16},{8,24},{16,0},{24,8},{1,17},{9,25},{17,1},{25,9},{2,18},{10... | collective-permute-start | bytes 98312 | tf_op jit(solution)/shard_map/ppermute | solution.py:226
  8.1 1.3 %collective-permute-start.2 = (bf16[128,128]{1,0:T(8,128)(2,1)S(1)}, bf16[128,128]{1,0:T(8,128)(2,1)S(1)}, u32[]{:S(2)}, u32[]{:S(2)}) collective-permute-start(bf16[128,128]{1,0:T(8,128)(2,1)S(1)} %get-tuple-element.18), channel_id=1, source_target_pairs={{0,24},{8,0},{16,8},{24,16},{1,25},{9,1},{17,9},{25,17},{2,26},{10... | collective-permute-start | bytes 98312 | tf_op jit(solution)/shard_map/ppermute | solution.py:226
  9.4 0.0 collective-permute-done
  9.4 1.2 %collective-permute-done.1 = bf16[128,128]{1,0:T(8,128)(2,1)S(1)} collective-permute-done((bf16[128,128]{1,0:T(8,128)(2,1)S(1)}, bf16[128,128]{1,0:T(8,128)(2,1)S(1)}, u32[]{:S(2)}, u32[]{:S(2)}) %collective-permute-start.1) | collective-permute-done | bytes 32800 | tf_op jit(solution)/shard_map/ppermute | solution.py:226
  10.7 1.3 %collective-permute-done.2 = bf16[128,128]{1,0:T(8,128)(2,1)S(1)} collective-permute-done((bf16[128,128]{1,0:T(8,128)(2,1)S(1)}, bf16[128,128]{1,0:T(8,128)(2,1)S(1)}, u32[]{:S(2)}, u32[]{:S(2)}) %collective-permute-start.2) | collective-permute-done | bytes 32800 | tf_op jit(solution)/shard_map/ppermute | solution.py:226
  12.0 2.4 %collective-permute-start.8 = (bf16[512,128]{1,0:T(8,128)(2,1)S(1)}, bf16[512,128]{1,0:T(8,128)(2,1)S(1)}, u32[]{:S(2)}, u32[]{:S(2)}) collective-permute-start(bf16[512,128]{1,0:T(8,128)(2,1)S(1)} %constant_dynamic-update-slice_fusion.own.refs_0_), channel_id=1, source_target_pairs={{0,6},{1,7},{2,4},{3,5},{4,2},{5,3},{6,0},{7,1},{8,14},{9,15},{10,... | collective-permute-start | bytes 393224 | tf_op jit(solution)/shard_map/ppermute | solution.py:208
  14.5 0.5 %collective-permute-start.6 = (bf16[512,128]{1,0:T(8,128)(2,1)S(1)}, bf16[512,128]{1,0:T(8,128)(2,1)S(1)}, u32[]{:S(2)}, u32[]{:S(2)}) collective-permute-start(bf16[512,128]{1,0:T(8,128)(2,1)S(1)} %constant_dynamic-update-slice_fusion.own.refs_0_), channel_id=1, source_target_pairs={{0,4},{1,5},{2,6},{3,7},{4,0},{5,1},{6,2},{7,3},{8,12},{9,13},{10,... | collective-permute-start | bytes 393224 | tf_op jit(solution)/shard_map/ppermute | solution.py:208
  15.0 0.0 collective-permute-start.3
  15.0 0.5 %collective-permute-start.4 = (bf16[512,128]{1,0:T(8,128)(2,1)S(1)}, bf16[512,128]{1,0:T(8,128)(2,1)S(1)}, u32[]{:S(2)}, u32[]{:S(2)}) collective-permute-start(bf16[512,128]{1,0:T(8,128)(2,1)S(1)} %constant_dynamic-update-slice_fusion.own.refs_0_), channel_id=1, source_target_pairs={{0,2},{1,3},{2,0},{3,1},{4,6},{5,7},{6,4},{7,5},{8,10},{9,11},{10,... | collective-permute-start | bytes 393224 | tf_op jit(solution)/shard_map/ppermute | solution.py:208
  15.5 2.5 %collective-permute-done.8.refs_6_ = bf16[512,128]{1,0:T(8,128)(2,1)S(1)} collective-permute-done((bf16[512,128]{1,0:T(8,128)(2,1)S(1)}, bf16[512,128]{1,0:T(8,128)(2,1)S(1)}, u32[]{:S(2)}, u32[]{:S(2)}) %collective-permute-start.8) | collective-permute-done | bytes 131104 | tf_op jit(solution)/shard_map/ppermute | solution.py:208
  18.0 0.0 collective-permute-start.9
  18.0 1.9 %collective-permute-done.6.refs_4_ = bf16[512,128]{1,0:T(8,128)(2,1)S(1)} collective-permute-done((bf16[512,128]{1,0:T(8,128)(2,1)S(1)}, bf16[512,128]{1,0:T(8,128)(2,1)S(1)}, u32[]{:S(2)}, u32[]{:S(2)}) %collective-permute-start.6) | collective-permute-done | bytes 131104 | tf_op jit(solution)/shard_map/ppermute | solution.py:208
  19.8 0.0 collective-permute-start.7
  19.8 0.0 collective-permute-done.3.near.refs_1_
  19.8 0.6 %first_pair.1 = (bf16[256,512]{1,0:T(8,128)(2,1)S(1)}, f32[512,512]{1,0:T(8,128)S(1)}, f32[768,512]{1,0:T(8,128)S(1)}, f32[1,256]{1,0:T(1,128)S(1)}, bf16[1,128]{1,0:T(2,128)(2,1)S(1)}) custom-call(bf16[512,128]{1,0:T(8,128)(2,1)S(1)} %constant_dynamic-update-slice_fusion.own.refs_0_, bf16[512,128]{1,0:T(8,128)(2,1)S(1)} %collective-permute-done.3.near.refs_1_, ...), custom_call_target="tpu_custom_call" | custom-call | flops 400000000 | tf_op jit(solution)/shard_map/first_pair/pallas_call | solution.py:233
  20.5 0.4 %collective-permute-done.4.refs_2_ = bf16[512,128]{1,0:T(8,128)(2,1)S(1)} collective-permute-done((bf16[512,128]{1,0:T(8,128)(2,1)S(1)}, bf16[512,128]{1,0:T(8,128)(2,1)S(1)}, u32[]{:S(2)}, u32[]{:S(2)}) %collective-permute-start.4) | collective-permute-done | bytes 131104 | tf_op jit(solution)/shard_map/ppermute | solution.py:208
  20.9 0.2 collective-permute-start.5
  21.1 0.0 collective-permute-done.9.refs_7_
  21.1 0.1 collective-permute-done.7.refs_5_
  21.2 1.1 %collective-permute-done.5.refs_3_ = bf16[512,128]{1,0:T(8,128)(2,1)S(1)} collective-permute-done((bf16[512,128]{1,0:T(8,128)(2,1)S(1)}, bf16[512,128]{1,0:T(8,128)(2,1)S(1)}, u32[]{:S(2)}, u32[]{:S(2)}) %collective-permute-start.5) | collective-permute-done | bytes 131104 | tf_op jit(solution)/shard_map/ppermute | solution.py:208
  22.3 6.7 %last_pairs.1 = bf16[768,1024]{1,0:T(8,128)(2,1)} custom-call(bf16[512,128]{1,0:T(8,128)(2,1)S(1)} %constant_dynamic-update-slice_fusion.own.refs_0_, bf16[512,128]{1,0:T(8,128)(2,1)S(1)} %collective-permute-done.3.near.refs_1_, bf16[512,128]{1,0:T(8,128)(2,1)S(1)} %collective-permute-done.4.refs_2_, bf16[512,128]{1,0:T(8,128)(2,1)S(1)} %collective-permute-done.5.refs_3_, ...), custom_call_target="tpu_custom_call" | custom-call | flops 5000000000 | tf_op jit(solution)/shard_map/last_pairs/pallas_call | solution.py:252
  (5 shorter events, 0.0 us)
Async XLA Ops:
  0.0 0.9 %copy-start = (bf16[128,4,128]{2,1,0:T(4,128)(2,1)S(1)}, bf16[128,4,128]{2,1,0:T(4,128)(2,1)}, u32[]{:S(2)}) copy-start(bf16[128,4,128]{2,1,0:T(4,128)(2,1)} %param.2) | copy-start | bytes 393220
  2.4 7.0 %collective-permute-start = (bf16[128,128]{1,0:T(8,128)(2,1)S(1)}, bf16[128,128]{1,0:T(8,128)(2,1)S(1)}, u32[]{:S(2)}, u32[]{:S(2)}) collective-permute-start(bf16[128,128]{1,0:T(8,128)(2,1)S(1)} %get-tuple-element.16), channel_id=1, source_target_pairs={{0,8},{8,16},{16,24},{24,0},{1,9},{9,17},{17,25},{25,1},{2,10},{10... | collective-permute-start | bytes 98312 | tf_op jit(solution)/shard_map/ppermute | solution.py:226
  5.5 5.2 %collective-permute-start.1 = (bf16[128,128]{1,0:T(8,128)(2,1)S(1)}, bf16[128,128]{1,0:T(8,128)(2,1)S(1)}, u32[]{:S(2)}, u32[]{:S(2)}) collective-permute-start(bf16[128,128]{1,0:T(8,128)(2,1)S(1)} %get-tuple-element.17), channel_id=1, source_target_pairs={{0,16},{8,24},{16,0},{24,8},{1,17},{9,25},{17,1},{25,9},{2,18},{10... | collective-permute-start | bytes 98312 | tf_op jit(solution)/shard_map/ppermute | solution.py:226
  8.1 3.9 %collective-permute-start.2 = (bf16[128,128]{1,0:T(8,128)(2,1)S(1)}, bf16[128,128]{1,0:T(8,128)(2,1)S(1)}, u32[]{:S(2)}, u32[]{:S(2)}) collective-permute-start(bf16[128,128]{1,0:T(8,128)(2,1)S(1)} %get-tuple-element.18), channel_id=1, source_target_pairs={{0,24},{8,0},{16,8},{24,16},{1,25},{9,1},{17,9},{25,17},{2,26},{10... | collective-permute-start | bytes 98312 | tf_op jit(solution)/shard_map/ppermute | solution.py:226
  12.0 6.0 %collective-permute-start.8 = (bf16[512,128]{1,0:T(8,128)(2,1)S(1)}, bf16[512,128]{1,0:T(8,128)(2,1)S(1)}, u32[]{:S(2)}, u32[]{:S(2)}) collective-permute-start(bf16[512,128]{1,0:T(8,128)(2,1)S(1)} %constant_dynamic-update-slice_fusion.own.refs_0_), channel_id=1, source_target_pairs={{0,6},{1,7},{2,4},{3,5},{4,2},{5,3},{6,0},{7,1},{8,14},{9,15},{10,... | collective-permute-start | bytes 393224 | tf_op jit(solution)/shard_map/ppermute | solution.py:208
  14.5 5.4 %collective-permute-start.6 = (bf16[512,128]{1,0:T(8,128)(2,1)S(1)}, bf16[512,128]{1,0:T(8,128)(2,1)S(1)}, u32[]{:S(2)}, u32[]{:S(2)}) collective-permute-start(bf16[512,128]{1,0:T(8,128)(2,1)S(1)} %constant_dynamic-update-slice_fusion.own.refs_0_), channel_id=1, source_target_pairs={{0,4},{1,5},{2,6},{3,7},{4,0},{5,1},{6,2},{7,3},{8,12},{9,13},{10,... | collective-permute-start | bytes 393224 | tf_op jit(solution)/shard_map/ppermute | solution.py:208
  15.0 4.9 %collective-permute-start.3 = (bf16[512,128]{1,0:T(8,128)(2,1)S(1)}, bf16[512,128]{1,0:T(8,128)(2,1)S(1)}, u32[]{:S(2)}, u32[]{:S(2)}) collective-permute-start(bf16[512,128]{1,0:T(8,128)(2,1)S(1)} %constant_dynamic-update-slice_fusion.own.refs_0_), channel_id=1, source_target_pairs={{0,1},{1,0},{2,3},{3,2},{4,5},{5,4},{6,7},{7,6},{8,9},{9,8},{10,11... | collective-permute-start | bytes 393224 | tf_op jit(solution)/shard_map/ppermute | solution.py:208
  15.0 5.9 %collective-permute-start.4 = (bf16[512,128]{1,0:T(8,128)(2,1)S(1)}, bf16[512,128]{1,0:T(8,128)(2,1)S(1)}, u32[]{:S(2)}, u32[]{:S(2)}) collective-permute-start(bf16[512,128]{1,0:T(8,128)(2,1)S(1)} %constant_dynamic-update-slice_fusion.own.refs_0_), channel_id=1, source_target_pairs={{0,2},{1,3},{2,0},{3,1},{4,6},{5,7},{6,4},{7,5},{8,10},{9,11},{10,... | collective-permute-start | bytes 393224 | tf_op jit(solution)/shard_map/ppermute | solution.py:208
  18.0 3.1 %collective-permute-start.9 = (bf16[512,128]{1,0:T(8,128)(2,1)S(1)}, bf16[512,128]{1,0:T(8,128)(2,1)S(1)}, u32[]{:S(2)}, u32[]{:S(2)}) collective-permute-start(bf16[512,128]{1,0:T(8,128)(2,1)S(1)} %collective-permute-done.8.refs_6_), channel_id=1, source_target_pairs={{0,1},{1,0},{2,3},{3,2},{4,5},{5,4},{6,7},{7,6},{8,9},{9,8},{10,11... | collective-permute-start | bytes 393224 | tf_op jit(solution)/shard_map/ppermute | solution.py:208
  19.8 1.3 %collective-permute-start.7 = (bf16[512,128]{1,0:T(8,128)(2,1)S(1)}, bf16[512,128]{1,0:T(8,128)(2,1)S(1)}, u32[]{:S(2)}, u32[]{:S(2)}) collective-permute-start(bf16[512,128]{1,0:T(8,128)(2,1)S(1)} %collective-permute-done.6.refs_4_), channel_id=1, source_target_pairs={{0,1},{1,0},{2,3},{3,2},{4,5},{5,4},{6,7},{7,6},{8,9},{9,8},{10,11... | collective-permute-start | bytes 393224 | tf_op jit(solution)/shard_map/ppermute | solution.py:208
  20.9 1.4 %collective-permute-start.5 = (bf16[512,128]{1,0:T(8,128)(2,1)S(1)}, bf16[512,128]{1,0:T(8,128)(2,1)S(1)}, u32[]{:S(2)}, u32[]{:S(2)}) collective-permute-start(bf16[512,128]{1,0:T(8,128)(2,1)S(1)} %broadcast_add_fusion), channel_id=1, source_target_pairs={{0,1},{1,0},{2,3},{3,2},{4,5},{5,4},{6,7},{7,6},{8,9},{9,8},{10,11... | collective-permute-start | bytes 393224 | tf_op jit(solution)/shard_map/ppermute | solution.py:208

commit v6 on v5

v6 whole, which is shorter than its diff:
```python
import functools

import jax
import jax.numpy as jnp
from jax import lax
from jax.experimental import pallas as pl
from jax.experimental.pallas import tpu as pltpu
from jax.sharding import PartitionSpec as P

ITERS = 4
DAMPING = 0.01
WHOLE = pl.BlockSpec(memory_space=pltpu.VMEM)
ANYWHERE = pl.BlockSpec(memory_space=pl.ANY)


def dot(a, b):
    return jnp.dot(a, b, preferred_element_type=jnp.float32)


def gather_block(factor_inputs):
    pieces = jnp.transpose(factor_inputs, (1, 0, 2))
    piece = lax.all_to_all(pieces, "dp", split_axis=0, concat_axis=1, tiled=True)[0]
    return lax.all_gather(piece, "grad", axis=1, tiled=True)


def by_features(columns, tile):
    tokens, width = columns.shape
    covariance = jnp.einsum("tr,tc->rc", columns, columns, preferred_element_type=jnp.float32) * (1.0 / tokens)
    damped = covariance + DAMPING * jnp.eye(width, dtype=jnp.float32)
    scale = 1.0 / jnp.max(jnp.sum(jnp.abs(damped), axis=1))
    image = scale * damped
    result = scale * tile.astype(jnp.float32)
    for step in range(ITERS):
        low = image.astype(jnp.bfloat16)
        result = 2.0 * result - dot(result.astype(jnp.bfloat16), low)
        if step < ITERS - 1:
            image = 2.0 * image - dot(low, low)
    return result


def split_kernel(x_ref, *out_refs):
    replicas, tokens = len(out_refs), out_refs[0].shape[0]
    here = lax.axis_index("dp")
    x = x_ref[...]
    rows = lax.broadcasted_iota(jnp.int32, (tokens, tokens * replicas), 0)
    cols = lax.broadcasted_iota(jnp.int32, (tokens, tokens * replicas), 1)
    offset = cols - rows * replicas
    for far, out_ref in enumerate(out_refs):
        choice = jnp.where(offset == lax.rem(here + far, replicas), 1.0, 0.0).astype(jnp.bfloat16)
        out_ref[...] = dot(choice, x).astype(jnp.bfloat16)


def split_blocks(factor_inputs):
    tokens, blocks, features = factor_inputs.shape
    return pl.pallas_call(
        split_kernel,
        out_shape=[jax.ShapeDtypeStruct((tokens, features), factor_inputs.dtype)] * blocks,
        in_specs=[WHOLE],
        out_specs=[WHOLE] * blocks,
        compiler_params=pltpu.CompilerParams(vmem_limit_bytes=16 * 2**20),
        name="split_blocks",
    )(factor_inputs.reshape(tokens * blocks, features))


def first_kernel(*refs):
    *pieces, turned, gram = refs
    features = pieces[0].shape[1]
    for k, piece in enumerate(pieces):
        turned[k * features : (k + 1) * features, :] = piece[...].T
    gram[...] = dot(jnp.concatenate([piece[...] for piece in pieces], axis=1), turned[...])


def last_kernel(fars, count, *refs):
    pieces, refs = refs[: len(fars)], refs[len(fars) :]
    turned, gram_in, tile_hbm, out_hbm, *refs = refs
    tile, out, x, xt, k1, k2, k3, k4, low1, low2, g, h, z, image, mixed, sems = refs
    load = pltpu.make_async_copy(tile_hbm, tile, sems.at[0])
    load.start()
    member = lax.axis_index("grad")
    tokens, features = pieces[0].shape
    half = 2 * features
    halves = [slice(at, at + half) for at in range(0, tokens, half)]
    blocks = [slice(at, at + half) for at in range(0, x.shape[1], half)]
    chunks = [slice(at, at + 32) for at in range(0, tokens, 32)]

    rest = []
    for k, (far, piece) in enumerate(zip(fars, pieces)):
        here = pl.ds(pl.multiple_of((member ^ far) * features, features), features)
        x[:, here] = piece[...]
        if k < count:
            xt[here, :] = turned[k * features : (k + 1) * features, :]
        else:
            rest.append(piece[...].T)
            xt[here, :] = rest[-1]
    late = jnp.concatenate([piece[...] for piece in pieces[count:]], axis=1)
    late_t = jnp.concatenate(rest, axis=0)
    for some in halves:
        gram = (gram_in[:, some] + dot(late, late_t[:, some])) * (1.0 / tokens)
        k1[:, some] = gram
        low1[:, some] = gram.astype(jnp.bfloat16)

    column_sums, row_sums = [0.0] * len(blocks), [0.0] * len(blocks)

    def add_sums(j):
        for i in range(j + 1):
            block = jnp.abs(dot(xt[blocks[i], :], x[:, blocks[j]]))
            column_sums[j] = column_sums[j] + jnp.sum(block, axis=0, keepdims=True)
            if i < j:
                row_sums[i] = row_sums[i] + block[:, :features] + block[:, features:]

    def move(some):
        image[:, some] = dot(tile[...], xt[:, some]).astype(jnp.bfloat16)

    for j in range(len(blocks) - 1):
        add_sums(j)
    for some in halves:
        k2[:, some] = dot(low1[...], low1[:, some])
    add_sums(len(blocks) - 1)
    load.wait()
    move(halves[0])

    largest = column_sums[-1]
    for column, row in zip(column_sums[:-1], row_sums):
        largest = jnp.maximum(largest, column + jnp.sum(row.T, axis=0, keepdims=True))
    c = 1.0 / (jnp.max(largest) * (1.0 / tokens) + DAMPING)
    eps = 1.0 - c * DAMPING
    eps2 = eps * eps
    zeta = eps2 * eps2
    eps8 = zeta * zeta
    e2_1, e2_2 = -2.0 * eps * c, c * c
    g_1 = -(1.0 + eps) * c
    g_m = eps2 + (1.0 + eps) * eps + eps
    h_m = zeta + (1.0 + eps2) * eps2 + eps2
    k_m = eps8 + (1.0 + zeta) * zeta + zeta + 1.0 + eps8
    k_z = 1.0 + 3.0 * zeta
    a_m = g_m * h_m
    a_e2 = g_m * (1.0 + eps2) + h_m
    a_1 = h_m * g_1
    beta = (1.0 + zeta) * (1.0 + eps8)
    q_m = a_m * k_m + beta * g_m + (1.0 + eps2) * beta
    last = -c * c * (1.0 / tokens)
    q_m = q_m * last
    p = c * (1.0 + eps) * (1.0 + eps2) * beta

    for some in halves:
        for r in chunks:
            x1 = k1[r, some]
            e2 = e2_1 * x1 + e2_2 * k2[r, some]
            k2[r, some] = e2
            low2[r, some] = e2.astype(jnp.bfloat16)
            g[r, some] = (e2 + g_1 * x1).astype(jnp.bfloat16)
    for some in halves:
        product = dot(low2[...], low2[:, some])
        for r in chunks:
            e2 = k2[r, some]
            fourth = 2.0 * eps2 * e2 + product[r]
            k3[r, some] = fourth
            z[r, some] = fourth.astype(jnp.bfloat16)
            h[r, some] = (fourth + (1.0 + eps2) * e2).astype(jnp.bfloat16)
    for some in halves[1:]:
        move(some)

    def add_a(some):
        product = dot(g[...], h[:, some])
        for r in chunks:
            x1, e2 = k1[r, some], k2[r, some]
            a = product[r] + g_m * k3[r, some] + a_e2 * e2 + a_1 * x1
            low1[r, some] = a.astype(jnp.bfloat16)
            k1[r, some] = last * (k_m * a + beta * (e2 + g_1 * x1))

    add_a(halves[0])
    for some in halves:
        product = dot(z[...], z[:, some])
        for r in chunks:
            k = product[r] + k_z * k3[r, some]
            k4[r, some] = k
            low2[r, some] = k.astype(jnp.bfloat16)
    for some in halves[1:]:
        add_a(some)
    for some in halves:
        product = dot(low2[...], low1[:, some])
        for r in chunks:
            g[r, some] = (k1[r, some] + last * (product[r] + a_m * k4[r, some])).astype(jnp.bfloat16)
    for some in halves:
        product = dot(image[...], g[:, some])
        mixed[:, some] = (product + q_m * image[:, some].astype(jnp.float32)).astype(jnp.bfloat16)
    stores = []
    for k, some in enumerate(blocks):
        moved = dot(mixed[...], x[:, some])
        out[:, some] = (p * tile[:, some].astype(jnp.float32) + moved).astype(jnp.bfloat16)
        store = pltpu.make_async_copy(out.at[:, some], out_hbm.at[:, some], sems.at[1 + k])
        store.start()
        stores.append(store)
    for store in stores:
        store.wait()


def swap(value, far):
    return lax.ppermute(value, "grad", [(i, i ^ far) for i in range(lax.axis_size("grad"))])


def by_tokens(factor_inputs, tile):
    members, replicas = lax.axis_size("grad"), lax.axis_size("dp")
    rows, width = tile.shape
    features = factor_inputs.shape[2]
    tokens = factor_inputs.shape[0] * replicas

    def shape(*sizes, kind=jnp.float32):
        return jax.ShapeDtypeStruct(sizes, kind)

    def scratch(*sizes, kind=jnp.bfloat16):
        return pltpu.VMEM(sizes, kind)

    parts = split_blocks(factor_inputs)
    arrived = [
        lax.ppermute(parts[far], "dp", [(i, (i + far) % replicas) for i in range(replicas)])
        for far in range(1, replicas)
    ]
    fars = tuple(range(2, members, 2))
    own = jnp.concatenate([parts[0]] + arrived, axis=0)
    near = swap(own, 1)
    held = [swap(own, far) for far in fars]
    far_near = [swap(piece, 1) for piece in held]
    here, there = [own, near, *held], far_near
    turned, gram = pl.pallas_call(
        first_kernel,
        out_shape=[shape(len(here) * features, tokens, kind=jnp.bfloat16), shape(tokens, tokens)],
        in_specs=[WHOLE] * len(here),
        out_specs=[WHOLE] * 2,
        compiler_params=pltpu.CompilerParams(vmem_limit_bytes=16 * 2**20),
        cost_estimate=pl.CostEstimate(flops=4 * 10**8, bytes_accessed=0, transcendentals=0),
        name="first_pieces",
    )(*here)
    return pl.pallas_call(
        functools.partial(last_kernel, (0, 1, *fars, *[far + 1 for far in fars]), len(here)),
        out_shape=shape(rows, width, kind=jnp.bfloat16),
        in_specs=[WHOLE] * (members + 2) + [ANYWHERE],
        out_specs=ANYWHERE,
        scratch_shapes=[scratch(rows, width)] * 2
        + [scratch(tokens, width), scratch(width, tokens)]
        + [scratch(tokens, tokens, kind=jnp.float32)] * 4
        + [scratch(tokens, tokens)] * 5
        + [scratch(rows, tokens)] * 2
        + [pltpu.SemaphoreType.DMA((1 + members // 2,))],
        compiler_params=pltpu.CompilerParams(vmem_limit_bytes=51 * 2**20),
        cost_estimate=pl.CostEstimate(flops=5 * 10**9, bytes_accessed=0, transcendentals=0),
        name="whole_block",
    )(*here, *there, turned, gram, tile)


def local(factor_inputs, gradients):
    features, members = factor_inputs.shape[2], lax.axis_size("grad")
    tokens = factor_inputs.shape[0] * lax.axis_size("dp")
    tile = gradients[0]
    powers_of_two = all(size & (size - 1) == 0 for size in (members, lax.axis_size("dp")))
    if tokens < features * members and features % 128 == 0 and powers_of_two and members > 2:
        result = by_tokens(factor_inputs, tile)
    else:
        result = by_features(gather_block(factor_inputs), tile)
    return result.astype(jnp.bfloat16)[None]


def solution(mesh):
    placed = (P("dp", None, "grad"), P("dp", "grad", None))
    return jax.shard_map(
        local, mesh=mesh, in_specs=placed, out_specs=P("dp", "grad", None), check_vma=False
    )
```

time: 29.2 us -> 27.5 us (0.942)
  waiting for transfers between devices: 8.46 us -> 7.35 us
  Pallas kernels: 8.87 us -> 8.06 us
  starting transfers between devices: 10.7 us -> 11 us
    pallas_call x1, Pallas kernels: 1.5 us -> 0.28 us  [split_blocks(): pl.pallas_call(split_kernel, out_shape=[jax.ShapeDtypeStruct((tokens, fea...]
    ppermute x7, waiting for transfers between devices: 5.92 us -> 4.8 us  [swap(): lax.ppermute(value, 'grad', [(i, i ^ far) for i in range(lax.axis_size('g...]
    pallas_call x2, Pallas kernels: 7.37 us -> 7.78 us  [the longest x1 7.12 us: by_tokens(): pl.pallas_call(functools.partial(last_kernel, (0, 1, *fars, *[far + 1 for...]
    ppermute x7, starting transfers between devices: 3.71 us -> 4 us  [swap(): lax.ppermute(value, 'grad', [(i, i ^ far) for i in range(lax.axis_size('g...]
  transfers between devices with their start and end apart: 10 -> 10, of which waited for: 7 -> 6; matrix products, arithmetic and copies ran while one was open for 0% -> 0% of each run, Pallas kernels for 2% -> 2%
where the time goes in v6:
time: 27.5 us; the launch traced here: 27.4 us
  starting transfers between devices  11 us (40%)
  Pallas kernels  8.06 us (29%)
  waiting for transfers between devices  7.35 us (27%)
  local copies, waits for them, and re-layouts  0.93 us (3%)
    pallas_call x1, Pallas kernels, by_tokens(): pl.pallas_call(functools.partial(last_kernel, (0, 1, *fars, *[far + 1 for...  7.12 us
    ppermute x3, starting transfers between devices, by_tokens(): lax.ppermute(parts[far], 'dp', [(i, (i + far) % replicas) for i in range(...  7.01 us
    ppermute x7, waiting for transfers between devices, swap(): lax.ppermute(value, 'grad', [(i, i ^ far) for i in range(lax.axis_size('g...  4.8 us
    ppermute x7, starting transfers between devices, swap(): lax.ppermute(value, 'grad', [(i, i ^ far) for i in range(lax.axis_size('g...  4 us
    ppermute x3, waiting for transfers between devices, by_tokens(): lax.ppermute(parts[far], 'dp', [(i, (i + far) % replicas) for i in range(...  2.54 us
    unnamed x5, local copies, waits for them, and re-layouts  0.92 us
    pallas_call x1, Pallas kernels, by_tokens(): pl.pallas_call(first_kernel, out_shape=[shape(len(here) * features, token...  0.66 us
  transfers between devices with their start and end apart: 10, of which 6 were waited for; matrix products, arithmetic and copies ran while one was open for 0% of the time, Pallas kernels for 2%

profile of v6, /device:TPU:0, one launch (start us, length us, event | category | flops | bytes accessed | tf_op | source)
XLA Modules:
  0.0 27.4 jit_solution(12352506420097466426)
XLA Ops:
  0.0 0.0 copy-start
  0.0 0.9 %copy-done = bf16[128,4,128]{2,1,0:T(4,128)(2,1)S(1)} copy-done((bf16[128,4,128]{2,1,0:T(4,128)(2,1)S(1)}, bf16[128,4,128]{2,1,0:T(4,128)(2,1)}, u32[]{:S(2)}) %copy-start) | copy-done | bytes 131096
  0.9 0.3 %split_blocks.1 = (bf16[128,128]{1,0:T(8,128)(2,1)S(1)}, bf16[128,128]{1,0:T(8,128)(2,1)S(1)}, bf16[128,128]{1,0:T(8,128)(2,1)S(1)}, bf16[128,128]{1,0:T(8,128)(2,1)S(1)}) custom-call(bf16[512,128]{1,0:T(8,128)(2,1)S(1)} %bitcast.3), custom_call_target="tpu_custom_call" | custom-call | tf_op jit(solution)/shard_map/split_blocks/pallas_call | solution.py:55
  1.2 3.1 %collective-permute-start = (bf16[128,128]{1,0:T(8,128)(2,1)S(1)}, bf16[128,128]{1,0:T(8,128)(2,1)S(1)}, u32[]{:S(2)}, u32[]{:S(2)}) collective-permute-start(bf16[128,128]{1,0:T(8,128)(2,1)S(1)} %get-tuple-element.12), channel_id=1, source_target_pairs={{0,8},{8,16},{16,24},{24,0},{1,9},{9,17},{17,25},{25,1},{2,10},{10... | collective-permute-start | bytes 98312 | tf_op jit(solution)/shard_map/ppermute | solution.py:216
  4.3 2.6 %collective-permute-start.1 = (bf16[128,128]{1,0:T(8,128)(2,1)S(1)}, bf16[128,128]{1,0:T(8,128)(2,1)S(1)}, u32[]{:S(2)}, u32[]{:S(2)}) collective-permute-start(bf16[128,128]{1,0:T(8,128)(2,1)S(1)} %get-tuple-element.13), channel_id=1, source_target_pairs={{0,16},{8,24},{16,0},{24,8},{1,17},{9,25},{17,1},{25,9},{2,18},{10... | collective-permute-start | bytes 98312 | tf_op jit(solution)/shard_map/ppermute | solution.py:216
  6.9 1.3 %collective-permute-start.2 = (bf16[128,128]{1,0:T(8,128)(2,1)S(1)}, bf16[128,128]{1,0:T(8,128)(2,1)S(1)}, u32[]{:S(2)}, u32[]{:S(2)}) collective-permute-start(bf16[128,128]{1,0:T(8,128)(2,1)S(1)} %get-tuple-element.14), channel_id=1, source_target_pairs={{0,24},{8,0},{16,8},{24,16},{1,25},{9,1},{17,9},{25,17},{2,26},{10... | collective-permute-start | bytes 98312 | tf_op jit(solution)/shard_map/ppermute | solution.py:216
  8.2 0.0 collective-permute-done
  8.2 1.2 %collective-permute-done.1 = bf16[128,128]{1,0:T(8,128)(2,1)S(1)} collective-permute-done((bf16[128,128]{1,0:T(8,128)(2,1)S(1)}, bf16[128,128]{1,0:T(8,128)(2,1)S(1)}, u32[]{:S(2)}, u32[]{:S(2)}) %collective-permute-start.1) | collective-permute-done | bytes 32800 | tf_op jit(solution)/shard_map/ppermute | solution.py:216
  9.4 1.3 %collective-permute-done.2 = bf16[128,128]{1,0:T(8,128)(2,1)S(1)} collective-permute-done((bf16[128,128]{1,0:T(8,128)(2,1)S(1)}, bf16[128,128]{1,0:T(8,128)(2,1)S(1)}, u32[]{:S(2)}, u32[]{:S(2)}) %collective-permute-start.2) | collective-permute-done | bytes 32800 | tf_op jit(solution)/shard_map/ppermute | solution.py:216
  10.8 2.4 %collective-permute-start.6 = (bf16[512,128]{1,0:T(8,128)(2,1)S(1)}, bf16[512,128]{1,0:T(8,128)(2,1)S(1)}, u32[]{:S(2)}, u32[]{:S(2)}) collective-permute-start(bf16[512,128]{1,0:T(8,128)(2,1)S(1)} %constant_dynamic-update-slice_fusion.refs_0_), channel_id=1, source_target_pairs={{0,6},{1,7},{2,4},{3,5},{4,2},{5,3},{6,0},{7,1},{8,14},{9,15},{10,... | collective-permute-start | bytes 393224 | tf_op jit(solution)/shard_map/ppermute | solution.py:199
  13.2 0.5 %collective-permute-start.5 = (bf16[512,128]{1,0:T(8,128)(2,1)S(1)}, bf16[512,128]{1,0:T(8,128)(2,1)S(1)}, u32[]{:S(2)}, u32[]{:S(2)}) collective-permute-start(bf16[512,128]{1,0:T(8,128)(2,1)S(1)} %constant_dynamic-update-slice_fusion.refs_0_), channel_id=1, source_target_pairs={{0,4},{1,5},{2,6},{3,7},{4,0},{5,1},{6,2},{7,3},{8,12},{9,13},{10,... | collective-permute-start | bytes 393224 | tf_op jit(solution)/shard_map/ppermute | solution.py:199
  13.7 0.5 %collective-permute-start.4 = (bf16[512,128]{1,0:T(8,128)(2,1)S(1)}, bf16[512,128]{1,0:T(8,128)(2,1)S(1)}, u32[]{:S(2)}, u32[]{:S(2)}) collective-permute-start(bf16[512,128]{1,0:T(8,128)(2,1)S(1)} %constant_dynamic-update-slice_fusion.refs_0_), channel_id=1, source_target_pairs={{0,2},{1,3},{2,0},{3,1},{4,6},{5,7},{6,4},{7,5},{8,10},{9,11},{10,... | collective-permute-start | bytes 393224 | tf_op jit(solution)/shard_map/ppermute | solution.py:199
  14.3 0.0 collective-permute-start.3
  14.3 3.6 %collective-permute-done.6.refs_4_ = bf16[512,128]{1,0:T(8,128)(2,1)S(1)} collective-permute-done((bf16[512,128]{1,0:T(8,128)(2,1)S(1)}, bf16[512,128]{1,0:T(8,128)(2,1)S(1)}, u32[]{:S(2)}, u32[]{:S(2)}) %collective-permute-start.6) | collective-permute-done | bytes 131104 | tf_op jit(solution)/shard_map/ppermute | solution.py:199
  17.9 0.0 collective-permute-start.9
  17.9 0.9 %collective-permute-done.5.refs_3_ = bf16[512,128]{1,0:T(8,128)(2,1)S(1)} collective-permute-done((bf16[512,128]{1,0:T(8,128)(2,1)S(1)}, bf16[512,128]{1,0:T(8,128)(2,1)S(1)}, u32[]{:S(2)}, u32[]{:S(2)}) %collective-permute-start.5) | collective-permute-done | bytes 131104 | tf_op jit(solution)/shard_map/ppermute | solution.py:199
  18.7 0.0 collective-permute-start.8
  18.7 0.0 collective-permute-done.4.refs_2_
  18.7 0.5 %collective-permute-start.7 = (bf16[512,128]{1,0:T(8,128)(2,1)S(1)}, bf16[512,128]{1,0:T(8,128)(2,1)S(1)}, u32[]{:S(2)}, u32[]{:S(2)}) collective-permute-start(bf16[512,128]{1,0:T(8,128)(2,1)S(1)} %collective-permute-done.4.refs_2_), channel_id=1, source_target_pairs={{0,1},{1,0},{2,3},{3,2},{4,5},{5,4},{6,7},{7,6},{8,9},{9,8},{10,11... | collective-permute-start | bytes 393224 | tf_op jit(solution)/shard_map/ppermute | solution.py:199
  19.2 0.0 collective-permute-done.3.refs_1_
  19.3 0.7 %first_pieces.1 = (bf16[640,512]{1,0:T(8,128)(2,1)S(1)}, f32[512,512]{1,0:T(8,128)S(1)}) custom-call(bf16[512,128]{1,0:T(8,128)(2,1)S(1)} %constant_dynamic-update-slice_fusion.refs_0_, bf16[512,128]{1,0:T(8,128)(2,1)S(1)} %collective-permute-done.3.refs_1_, bf16[512,128]{1,0:T(8,128)(2,1)S(1)} %collective-permute-done.4.refs_2_, ...), custom_call_target="tpu_custom_call" | custom-call | flops 400000000 | tf_op jit(solution)/shard_map/first_pieces/pallas_call | solution.py:225
  19.9 0.0 collective-permute-done.9.refs_7_
  19.9 0.2 collective-permute-done.8.refs_6_
  20.1 0.2 collective-permute-done.7.refs_5_
  20.3 7.1 %whole_block.1 = bf16[768,1024]{1,0:T(8,128)(2,1)} custom-call(bf16[512,128]{1,0:T(8,128)(2,1)S(1)} %constant_dynamic-update-slice_fusion.refs_0_, bf16[512,128]{1,0:T(8,128)(2,1)S(1)} %collective-permute-done.3.refs_1_, bf16[512,128]{1,0:T(8,128)(2,1)S(1)} %collective-permute-done.4.refs_2_, bf16[512,128]{1,0:T(8,128)(2,1)S(1)} %collective-permute-done.5.refs_3_, ...), custom_call_target="tpu_custom_call" | custom-call | flops 5000000000 | tf_op jit(solution)/shard_map/whole_block/pallas_call | solution.py:234
  (4 shorter events, 0.0 us)
Async XLA Ops:
  0.0 0.9 %copy-start = (bf16[128,4,128]{2,1,0:T(4,128)(2,1)S(1)}, bf16[128,4,128]{2,1,0:T(4,128)(2,1)}, u32[]{:S(2)}) copy-start(bf16[128,4,128]{2,1,0:T(4,128)(2,1)} %param.2) | copy-start | bytes 393220
  1.2 7.0 %collective-permute-start = (bf16[128,128]{1,0:T(8,128)(2,1)S(1)}, bf16[128,128]{1,0:T(8,128)(2,1)S(1)}, u32[]{:S(2)}, u32[]{:S(2)}) collective-permute-start(bf16[128,128]{1,0:T(8,128)(2,1)S(1)} %get-tuple-element.12), channel_id=1, source_target_pairs={{0,8},{8,16},{16,24},{24,0},{1,9},{9,17},{17,25},{25,1},{2,10},{10... | collective-permute-start | bytes 98312 | tf_op jit(solution)/shard_map/ppermute | solution.py:216
  4.3 5.2 %collective-permute-start.1 = (bf16[128,128]{1,0:T(8,128)(2,1)S(1)}, bf16[128,128]{1,0:T(8,128)(2,1)S(1)}, u32[]{:S(2)}, u32[]{:S(2)}) collective-permute-start(bf16[128,128]{1,0:T(8,128)(2,1)S(1)} %get-tuple-element.13), channel_id=1, source_target_pairs={{0,16},{8,24},{16,0},{24,8},{1,17},{9,25},{17,1},{25,9},{2,18},{10... | collective-permute-start | bytes 98312 | tf_op jit(solution)/shard_map/ppermute | solution.py:216
  6.9 3.9 %collective-permute-start.2 = (bf16[128,128]{1,0:T(8,128)(2,1)S(1)}, bf16[128,128]{1,0:T(8,128)(2,1)S(1)}, u32[]{:S(2)}, u32[]{:S(2)}) collective-permute-start(bf16[128,128]{1,0:T(8,128)(2,1)S(1)} %get-tuple-element.14), channel_id=1, source_target_pairs={{0,24},{8,0},{16,8},{24,16},{1,25},{9,1},{17,9},{25,17},{2,26},{10... | collective-permute-start | bytes 98312 | tf_op jit(solution)/shard_map/ppermute | solution.py:216
  10.8 7.1 %collective-permute-start.6 = (bf16[512,128]{1,0:T(8,128)(2,1)S(1)}, bf16[512,128]{1,0:T(8,128)(2,1)S(1)}, u32[]{:S(2)}, u32[]{:S(2)}) collective-permute-start(bf16[512,128]{1,0:T(8,128)(2,1)S(1)} %constant_dynamic-update-slice_fusion.refs_0_), channel_id=1, source_target_pairs={{0,6},{1,7},{2,4},{3,5},{4,2},{5,3},{6,0},{7,1},{8,14},{9,15},{10,... | collective-permute-start | bytes 393224 | tf_op jit(solution)/shard_map/ppermute | solution.py:199
  13.2 5.5 %collective-permute-start.5 = (bf16[512,128]{1,0:T(8,128)(2,1)S(1)}, bf16[512,128]{1,0:T(8,128)(2,1)S(1)}, u32[]{:S(2)}, u32[]{:S(2)}) collective-permute-start(bf16[512,128]{1,0:T(8,128)(2,1)S(1)} %constant_dynamic-update-slice_fusion.refs_0_), channel_id=1, source_target_pairs={{0,4},{1,5},{2,6},{3,7},{4,0},{5,1},{6,2},{7,3},{8,12},{9,13},{10,... | collective-permute-start | bytes 393224 | tf_op jit(solution)/shard_map/ppermute | solution.py:199
  13.7 5.0 %collective-permute-start.4 = (bf16[512,128]{1,0:T(8,128)(2,1)S(1)}, bf16[512,128]{1,0:T(8,128)(2,1)S(1)}, u32[]{:S(2)}, u32[]{:S(2)}) collective-permute-start(bf16[512,128]{1,0:T(8,128)(2,1)S(1)} %constant_dynamic-update-slice_fusion.refs_0_), channel_id=1, source_target_pairs={{0,2},{1,3},{2,0},{3,1},{4,6},{5,7},{6,4},{7,5},{8,10},{9,11},{10,... | collective-permute-start | bytes 393224 | tf_op jit(solution)/shard_map/ppermute | solution.py:199
  14.3 5.0 %collective-permute-start.3 = (bf16[512,128]{1,0:T(8,128)(2,1)S(1)}, bf16[512,128]{1,0:T(8,128)(2,1)S(1)}, u32[]{:S(2)}, u32[]{:S(2)}) collective-permute-start(bf16[512,128]{1,0:T(8,128)(2,1)S(1)} %constant_dynamic-update-slice_fusion.refs_0_), channel_id=1, source_target_pairs={{0,1},{1,0},{2,3},{3,2},{4,5},{5,4},{6,7},{7,6},{8,9},{9,8},{10,11... | collective-permute-start | bytes 393224 | tf_op jit(solution)/shard_map/ppermute | solution.py:199
  17.9 2.1 %collective-permute-start.9 = (bf16[512,128]{1,0:T(8,128)(2,1)S(1)}, bf16[512,128]{1,0:T(8,128)(2,1)S(1)}, u32[]{:S(2)}, u32[]{:S(2)}) collective-permute-start(bf16[512,128]{1,0:T(8,128)(2,1)S(1)} %collective-permute-done.6.refs_4_), channel_id=1, source_target_pairs={{0,1},{1,0},{2,3},{3,2},{4,5},{5,4},{6,7},{7,6},{8,9},{9,8},{10,11... | collective-permute-start | bytes 393224 | tf_op jit(solution)/shard_map/ppermute | solution.py:199
  18.7 1.3 %collective-permute-start.8 = (bf16[512,128]{1,0:T(8,128)(2,1)S(1)}, bf16[512,128]{1,0:T(8,128)(2,1)S(1)}, u32[]{:S(2)}, u32[]{:S(2)}) collective-permute-start(bf16[512,128]{1,0:T(8,128)(2,1)S(1)} %collective-permute-done.5.refs_3_), channel_id=1, source_target_pairs={{0,1},{1,0},{2,3},{3,2},{4,5},{5,4},{6,7},{7,6},{8,9},{9,8},{10,11... | collective-permute-start | bytes 393224 | tf_op jit(solution)/shard_map/ppermute | solution.py:199
  18.7 1.5 %collective-permute-start.7 = (bf16[512,128]{1,0:T(8,128)(2,1)S(1)}, bf16[512,128]{1,0:T(8,128)(2,1)S(1)}, u32[]{:S(2)}, u32[]{:S(2)}) collective-permute-start(bf16[512,128]{1,0:T(8,128)(2,1)S(1)} %collective-permute-done.4.refs_2_), channel_id=1, source_target_pairs={{0,1},{1,0},{2,3},{3,2},{4,5},{5,4},{6,7},{7,6},{8,9},{9,8},{10,11... | collective-permute-start | bytes 393224 | tf_op jit(solution)/shard_map/ppermute | solution.py:199

commit v7 on v6

--- a/solution.py
+++ b/solution.py
@@ -83,30 +83,25 @@
     blocks = [slice(at, at + half) for at in range(0, x.shape[1], half)]
     chunks = [slice(at, at + 32) for at in range(0, tokens, 32)]
 
-    rest = []
     for k, (far, piece) in enumerate(zip(fars, pieces)):
         here = pl.ds(pl.multiple_of((member ^ far) * features, features), features)
         x[:, here] = piece[...]
-        if k < count:
-            xt[here, :] = turned[k * features : (k + 1) * features, :]
-        else:
-            rest.append(piece[...].T)
-            xt[here, :] = rest[-1]
+        xt[here, :] = turned[k * features : (k + 1) * features, :] if k < count else piece[...].T
     late = jnp.concatenate([piece[...] for piece in pieces[count:]], axis=1)
-    late_t = jnp.concatenate(rest, axis=0)
-    for some in halves:
-        gram = (gram_in[:, some] + dot(late, late_t[:, some])) * (1.0 / tokens)
+    for some in halves:
+        product = lax.dot_general(late, late[some], (((1,), (1,)), ((), ())), preferred_element_type=jnp.float32)
+        gram = (gram_in[:, some] + product) * (1.0 / tokens)
         k1[:, some] = gram
         low1[:, some] = gram.astype(jnp.bfloat16)
 
     column_sums, row_sums = [0.0] * len(blocks), [0.0] * len(blocks)
 
     def add_sums(j):
-        for i in range(j + 1):
-            block = jnp.abs(dot(xt[blocks[i], :], x[:, blocks[j]]))
-            column_sums[j] = column_sums[j] + jnp.sum(block, axis=0, keepdims=True)
-            if i < j:
-                row_sums[i] = row_sums[i] + block[:, :features] + block[:, features:]
+        column = jnp.abs(dot(xt[: half * (j + 1), :], x[:, blocks[j]]))
+        column_sums[j] = column_sums[j] + jnp.sum(column, axis=0, keepdims=True)
+        for i in range(j):
+            block = column[blocks[i]]
+            row_sums[i] = row_sums[i] + block[:, :features] + block[:, features:]
 
     def move(some):
         image[:, some] = dot(tile[...], xt[:, some]).astype(jnp.bfloat16)
@@ -185,12 +180,16 @@
         product = dot(image[...], g[:, some])
         mixed[:, some] = (product + q_m * image[:, some].astype(jnp.float32)).astype(jnp.bfloat16)
     stores = []
-    for k, some in enumerate(blocks):
+    for some in blocks:
         moved = dot(mixed[...], x[:, some])
-        out[:, some] = (p * tile[:, some].astype(jnp.float32) + moved).astype(jnp.bfloat16)
-        store = pltpu.make_async_copy(out.at[:, some], out_hbm.at[:, some], sems.at[1 + k])
-        store.start()
-        stores.append(store)
+        parts = 1 if some is not blocks[-1] else 3
+        step = moved.shape[0] // parts
+        for at in range(0, parts * step, step):
+            r = slice(at, at + step)
+            out[r, some] = (p * tile[r, some].astype(jnp.float32) + moved[r]).astype(jnp.bfloat16)
+            store = pltpu.make_async_copy(out.at[r, some], out_hbm.at[r, some], sems.at[1 + len(stores)])
+            store.start()
+            stores.append(store)
     for store in stores:
         store.wait()
 
@@ -212,12 +211,12 @@
         return pltpu.VMEM(sizes, kind)
 
     parts = split_blocks(factor_inputs)
-    arrived = [
-        lax.ppermute(parts[far], "dp", [(i, (i + far) % replicas) for i in range(replicas)])
-        for far in range(1, replicas)
-    ]
+    arrived = {
+        far: lax.ppermute(parts[far], "dp", [(i, (i + far) % replicas) for i in range(replicas)])
+        for far in sorted(range(1, replicas), key=lambda far: abs(far - replicas // 2))
+    }
     fars = tuple(range(2, members, 2))
-    own = jnp.concatenate([parts[0]] + arrived, axis=0)
+    own = jnp.concatenate([parts[0]] + [arrived[far] for far in range(1, replicas)], axis=0)
     near = swap(own, 1)
     held = [swap(own, far) for far in fars]
     far_near = [swap(piece, 1) for piece in held]
@@ -241,7 +240,7 @@
         + [scratch(tokens, tokens, kind=jnp.float32)] * 4
         + [scratch(tokens, tokens)] * 5
         + [scratch(rows, tokens)] * 2
-        + [pltpu.SemaphoreType.DMA((1 + members // 2,))],
+        + [pltpu.SemaphoreType.DMA((3 + members // 2,))],
         compiler_params=pltpu.CompilerParams(vmem_limit_bytes=51 * 2**20),
         cost_estimate=pl.CostEstimate(flops=5 * 10**9, bytes_accessed=0, transcendentals=0),
         name="whole_block",

time: 27.5 us -> 27.5 us (level)
  no operation moved by 1% of the time
where the time goes in v7:
time: 27.5 us; the launch traced here: 27.3 us
  starting transfers between devices  11 us (40%)
  Pallas kernels  7.97 us (29%)
  waiting for transfers between devices  7.35 us (27%)
  local copies, waits for them, and re-layouts  0.93 us (3%)
    pallas_call x1, Pallas kernels, by_tokens(): pl.pallas_call(functools.partial(last_kernel, (0, 1, *fars, *[far + 1 for...  7.03 us
    ppermute x3, starting transfers between devices, by_tokens(): lax.ppermute(parts[far], 'dp', [(i, (i + far) % replicas) for i in range(...  7.01 us
    ppermute x7, waiting for transfers between devices, swap(): lax.ppermute(value, 'grad', [(i, i ^ far) for i in range(lax.axis_size('g...  4.8 us
    ppermute x7, starting transfers between devices, swap(): lax.ppermute(value, 'grad', [(i, i ^ far) for i in range(lax.axis_size('g...  4 us
    ppermute x3, waiting for transfers between devices, by_tokens(): lax.ppermute(parts[far], 'dp', [(i, (i + far) % replicas) for i in range(...  2.54 us
    unnamed x5, local copies, waits for them, and re-layouts  0.92 us
    pallas_call x1, Pallas kernels, by_tokens(): pl.pallas_call(first_kernel, out_shape=[shape(len(here) * features, token...  0.66 us
  transfers between devices with their start and end apart: 10, of which 6 were waited for; matrix products, arithmetic and copies ran while one was open for 0% of the time, Pallas kernels for 2%

profile of v7, /device:TPU:0, one launch (start us, length us, event | category | flops | bytes accessed | tf_op | source)
XLA Modules:
  0.0 27.3 jit_solution(13228541193650848469)
XLA Ops:
  0.0 0.0 copy-start
  0.0 0.9 %copy-done = bf16[128,4,128]{2,1,0:T(4,128)(2,1)S(1)} copy-done((bf16[128,4,128]{2,1,0:T(4,128)(2,1)S(1)}, bf16[128,4,128]{2,1,0:T(4,128)(2,1)}, u32[]{:S(2)}) %copy-start) | copy-done | bytes 131096
  0.9 0.3 %split_blocks.1 = (bf16[128,128]{1,0:T(8,128)(2,1)S(1)}, bf16[128,128]{1,0:T(8,128)(2,1)S(1)}, bf16[128,128]{1,0:T(8,128)(2,1)S(1)}, bf16[128,128]{1,0:T(8,128)(2,1)S(1)}) custom-call(bf16[512,128]{1,0:T(8,128)(2,1)S(1)} %bitcast.3), custom_call_target="tpu_custom_call" | custom-call | tf_op jit(solution)/shard_map/split_blocks/pallas_call | solution.py:55
  1.2 3.1 %collective-permute-start = (bf16[128,128]{1,0:T(8,128)(2,1)S(1)}, bf16[128,128]{1,0:T(8,128)(2,1)S(1)}, u32[]{:S(2)}, u32[]{:S(2)}) collective-permute-start(bf16[128,128]{1,0:T(8,128)(2,1)S(1)} %get-tuple-element.12), channel_id=1, source_target_pairs={{0,8},{8,16},{16,24},{24,0},{1,9},{9,17},{17,25},{25,1},{2,10},{10... | collective-permute-start | bytes 98312 | tf_op jit(solution)/shard_map/ppermute | solution.py:215
  4.3 2.6 %collective-permute-start.1 = (bf16[128,128]{1,0:T(8,128)(2,1)S(1)}, bf16[128,128]{1,0:T(8,128)(2,1)S(1)}, u32[]{:S(2)}, u32[]{:S(2)}) collective-permute-start(bf16[128,128]{1,0:T(8,128)(2,1)S(1)} %get-tuple-element.13), channel_id=1, source_target_pairs={{0,16},{8,24},{16,0},{24,8},{1,17},{9,25},{17,1},{25,9},{2,18},{10... | collective-permute-start | bytes 98312 | tf_op jit(solution)/shard_map/ppermute | solution.py:215
  6.9 1.3 %collective-permute-start.2 = (bf16[128,128]{1,0:T(8,128)(2,1)S(1)}, bf16[128,128]{1,0:T(8,128)(2,1)S(1)}, u32[]{:S(2)}, u32[]{:S(2)}) collective-permute-start(bf16[128,128]{1,0:T(8,128)(2,1)S(1)} %get-tuple-element.14), channel_id=1, source_target_pairs={{0,24},{8,0},{16,8},{24,16},{1,25},{9,1},{17,9},{25,17},{2,26},{10... | collective-permute-start | bytes 98312 | tf_op jit(solution)/shard_map/ppermute | solution.py:215
  8.2 0.0 collective-permute-done
  8.2 1.2 %collective-permute-done.1 = bf16[128,128]{1,0:T(8,128)(2,1)S(1)} collective-permute-done((bf16[128,128]{1,0:T(8,128)(2,1)S(1)}, bf16[128,128]{1,0:T(8,128)(2,1)S(1)}, u32[]{:S(2)}, u32[]{:S(2)}) %collective-permute-start.1) | collective-permute-done | bytes 32800 | tf_op jit(solution)/shard_map/ppermute | solution.py:215
  9.4 1.3 %collective-permute-done.2 = bf16[128,128]{1,0:T(8,128)(2,1)S(1)} collective-permute-done((bf16[128,128]{1,0:T(8,128)(2,1)S(1)}, bf16[128,128]{1,0:T(8,128)(2,1)S(1)}, u32[]{:S(2)}, u32[]{:S(2)}) %collective-permute-start.2) | collective-permute-done | bytes 32800 | tf_op jit(solution)/shard_map/ppermute | solution.py:215
  10.8 2.4 %collective-permute-start.6 = (bf16[512,128]{1,0:T(8,128)(2,1)S(1)}, bf16[512,128]{1,0:T(8,128)(2,1)S(1)}, u32[]{:S(2)}, u32[]{:S(2)}) collective-permute-start(bf16[512,128]{1,0:T(8,128)(2,1)S(1)} %constant_dynamic-update-slice_fusion.refs_0_), channel_id=1, source_target_pairs={{0,6},{1,7},{2,4},{3,5},{4,2},{5,3},{6,0},{7,1},{8,14},{9,15},{10,... | collective-permute-start | bytes 393224 | tf_op jit(solution)/shard_map/ppermute | solution.py:198
  13.2 0.5 %collective-permute-start.5 = (bf16[512,128]{1,0:T(8,128)(2,1)S(1)}, bf16[512,128]{1,0:T(8,128)(2,1)S(1)}, u32[]{:S(2)}, u32[]{:S(2)}) collective-permute-start(bf16[512,128]{1,0:T(8,128)(2,1)S(1)} %constant_dynamic-update-slice_fusion.refs_0_), channel_id=1, source_target_pairs={{0,4},{1,5},{2,6},{3,7},{4,0},{5,1},{6,2},{7,3},{8,12},{9,13},{10,... | collective-permute-start | bytes 393224 | tf_op jit(solution)/shard_map/ppermute | solution.py:198
  13.7 0.5 %collective-permute-start.4 = (bf16[512,128]{1,0:T(8,128)(2,1)S(1)}, bf16[512,128]{1,0:T(8,128)(2,1)S(1)}, u32[]{:S(2)}, u32[]{:S(2)}) collective-permute-start(bf16[512,128]{1,0:T(8,128)(2,1)S(1)} %constant_dynamic-update-slice_fusion.refs_0_), channel_id=1, source_target_pairs={{0,2},{1,3},{2,0},{3,1},{4,6},{5,7},{6,4},{7,5},{8,10},{9,11},{10,... | collective-permute-start | bytes 393224 | tf_op jit(solution)/shard_map/ppermute | solution.py:198
  14.3 0.0 collective-permute-start.3
  14.3 3.6 %collective-permute-done.6.refs_4_ = bf16[512,128]{1,0:T(8,128)(2,1)S(1)} collective-permute-done((bf16[512,128]{1,0:T(8,128)(2,1)S(1)}, bf16[512,128]{1,0:T(8,128)(2,1)S(1)}, u32[]{:S(2)}, u32[]{:S(2)}) %collective-permute-start.6) | collective-permute-done | bytes 131104 | tf_op jit(solution)/shard_map/ppermute | solution.py:198
  17.9 0.0 collective-permute-start.9
  17.9 0.9 %collective-permute-done.5.refs_3_ = bf16[512,128]{1,0:T(8,128)(2,1)S(1)} collective-permute-done((bf16[512,128]{1,0:T(8,128)(2,1)S(1)}, bf16[512,128]{1,0:T(8,128)(2,1)S(1)}, u32[]{:S(2)}, u32[]{:S(2)}) %collective-permute-start.5) | collective-permute-done | bytes 131104 | tf_op jit(solution)/shard_map/ppermute | solution.py:198
  18.7 0.0 collective-permute-start.8
  18.7 0.0 collective-permute-done.4.refs_2_
  18.7 0.5 %collective-permute-start.7 = (bf16[512,128]{1,0:T(8,128)(2,1)S(1)}, bf16[512,128]{1,0:T(8,128)(2,1)S(1)}, u32[]{:S(2)}, u32[]{:S(2)}) collective-permute-start(bf16[512,128]{1,0:T(8,128)(2,1)S(1)} %collective-permute-done.4.refs_2_), channel_id=1, source_target_pairs={{0,1},{1,0},{2,3},{3,2},{4,5},{5,4},{6,7},{7,6},{8,9},{9,8},{10,11... | collective-permute-start | bytes 393224 | tf_op jit(solution)/shard_map/ppermute | solution.py:198
  19.2 0.0 collective-permute-done.3.refs_1_
  19.3 0.7 %first_pieces.1 = (bf16[640,512]{1,0:T(8,128)(2,1)S(1)}, f32[512,512]{1,0:T(8,128)S(1)}) custom-call(bf16[512,128]{1,0:T(8,128)(2,1)S(1)} %constant_dynamic-update-slice_fusion.refs_0_, bf16[512,128]{1,0:T(8,128)(2,1)S(1)} %collective-permute-done.3.refs_1_, bf16[512,128]{1,0:T(8,128)(2,1)S(1)} %collective-permute-done.4.refs_2_, ...), custom_call_target="tpu_custom_call" | custom-call | flops 400000000 | tf_op jit(solution)/shard_map/first_pieces/pallas_call | solution.py:224
  19.9 0.0 collective-permute-done.9.refs_7_
  19.9 0.2 collective-permute-done.8.refs_6_
  20.1 0.2 collective-permute-done.7.refs_5_
  20.3 7.0 %whole_block.1 = bf16[768,1024]{1,0:T(8,128)(2,1)} custom-call(bf16[512,128]{1,0:T(8,128)(2,1)S(1)} %constant_dynamic-update-slice_fusion.refs_0_, bf16[512,128]{1,0:T(8,128)(2,1)S(1)} %collective-permute-done.3.refs_1_, bf16[512,128]{1,0:T(8,128)(2,1)S(1)} %collective-permute-done.4.refs_2_, bf16[512,128]{1,0:T(8,128)(2,1)S(1)} %collective-permute-done.5.refs_3_, ...), custom_call_target="tpu_custom_call" | custom-call | flops 5000000000 | tf_op jit(solution)/shard_map/whole_block/pallas_call | solution.py:233
  (4 shorter events, 0.0 us)
Async XLA Ops:
  0.0 0.9 %copy-start = (bf16[128,4,128]{2,1,0:T(4,128)(2,1)S(1)}, bf16[128,4,128]{2,1,0:T(4,128)(2,1)}, u32[]{:S(2)}) copy-start(bf16[128,4,128]{2,1,0:T(4,128)(2,1)} %param.2) | copy-start | bytes 393220
  1.2 7.0 %collective-permute-start = (bf16[128,128]{1,0:T(8,128)(2,1)S(1)}, bf16[128,128]{1,0:T(8,128)(2,1)S(1)}, u32[]{:S(2)}, u32[]{:S(2)}) collective-permute-start(bf16[128,128]{1,0:T(8,128)(2,1)S(1)} %get-tuple-element.12), channel_id=1, source_target_pairs={{0,8},{8,16},{16,24},{24,0},{1,9},{9,17},{17,25},{25,1},{2,10},{10... | collective-permute-start | bytes 98312 | tf_op jit(solution)/shard_map/ppermute | solution.py:215
  4.3 5.2 %collective-permute-start.1 = (bf16[128,128]{1,0:T(8,128)(2,1)S(1)}, bf16[128,128]{1,0:T(8,128)(2,1)S(1)}, u32[]{:S(2)}, u32[]{:S(2)}) collective-permute-start(bf16[128,128]{1,0:T(8,128)(2,1)S(1)} %get-tuple-element.13), channel_id=1, source_target_pairs={{0,16},{8,24},{16,0},{24,8},{1,17},{9,25},{17,1},{25,9},{2,18},{10... | collective-permute-start | bytes 98312 | tf_op jit(solution)/shard_map/ppermute | solution.py:215
  6.9 3.9 %collective-permute-start.2 = (bf16[128,128]{1,0:T(8,128)(2,1)S(1)}, bf16[128,128]{1,0:T(8,128)(2,1)S(1)}, u32[]{:S(2)}, u32[]{:S(2)}) collective-permute-start(bf16[128,128]{1,0:T(8,128)(2,1)S(1)} %get-tuple-element.14), channel_id=1, source_target_pairs={{0,24},{8,0},{16,8},{24,16},{1,25},{9,1},{17,9},{25,17},{2,26},{10... | collective-permute-start | bytes 98312 | tf_op jit(solution)/shard_map/ppermute | solution.py:215
  10.8 7.1 %collective-permute-start.6 = (bf16[512,128]{1,0:T(8,128)(2,1)S(1)}, bf16[512,128]{1,0:T(8,128)(2,1)S(1)}, u32[]{:S(2)}, u32[]{:S(2)}) collective-permute-start(bf16[512,128]{1,0:T(8,128)(2,1)S(1)} %constant_dynamic-update-slice_fusion.refs_0_), channel_id=1, source_target_pairs={{0,6},{1,7},{2,4},{3,5},{4,2},{5,3},{6,0},{7,1},{8,14},{9,15},{10,... | collective-permute-start | bytes 393224 | tf_op jit(solution)/shard_map/ppermute | solution.py:198
  13.2 5.5 %collective-permute-start.5 = (bf16[512,128]{1,0:T(8,128)(2,1)S(1)}, bf16[512,128]{1,0:T(8,128)(2,1)S(1)}, u32[]{:S(2)}, u32[]{:S(2)}) collective-permute-start(bf16[512,128]{1,0:T(8,128)(2,1)S(1)} %constant_dynamic-update-slice_fusion.refs_0_), channel_id=1, source_target_pairs={{0,4},{1,5},{2,6},{3,7},{4,0},{5,1},{6,2},{7,3},{8,12},{9,13},{10,... | collective-permute-start | bytes 393224 | tf_op jit(solution)/shard_map/ppermute | solution.py:198
  13.7 5.0 %collective-permute-start.4 = (bf16[512,128]{1,0:T(8,128)(2,1)S(1)}, bf16[512,128]{1,0:T(8,128)(2,1)S(1)}, u32[]{:S(2)}, u32[]{:S(2)}) collective-permute-start(bf16[512,128]{1,0:T(8,128)(2,1)S(1)} %constant_dynamic-update-slice_fusion.refs_0_), channel_id=1, source_target_pairs={{0,2},{1,3},{2,0},{3,1},{4,6},{5,7},{6,4},{7,5},{8,10},{9,11},{10,... | collective-permute-start | bytes 393224 | tf_op jit(solution)/shard_map/ppermute | solution.py:198
  14.3 5.0 %collective-permute-start.3 = (bf16[512,128]{1,0:T(8,128)(2,1)S(1)}, bf16[512,128]{1,0:T(8,128)(2,1)S(1)}, u32[]{:S(2)}, u32[]{:S(2)}) collective-permute-start(bf16[512,128]{1,0:T(8,128)(2,1)S(1)} %constant_dynamic-update-slice_fusion.refs_0_), channel_id=1, source_target_pairs={{0,1},{1,0},{2,3},{3,2},{4,5},{5,4},{6,7},{7,6},{8,9},{9,8},{10,11... | collective-permute-start | bytes 393224 | tf_op jit(solution)/shard_map/ppermute | solution.py:198
  17.9 2.1 %collective-permute-start.9 = (bf16[512,128]{1,0:T(8,128)(2,1)S(1)}, bf16[512,128]{1,0:T(8,128)(2,1)S(1)}, u32[]{:S(2)}, u32[]{:S(2)}) collective-permute-start(bf16[512,128]{1,0:T(8,128)(2,1)S(1)} %collective-permute-done.6.refs_4_), channel_id=1, source_target_pairs={{0,1},{1,0},{2,3},{3,2},{4,5},{5,4},{6,7},{7,6},{8,9},{9,8},{10,11... | collective-permute-start | bytes 393224 | tf_op jit(solution)/shard_map/ppermute | solution.py:198
  18.7 1.3 %collective-permute-start.8 = (bf16[512,128]{1,0:T(8,128)(2,1)S(1)}, bf16[512,128]{1,0:T(8,128)(2,1)S(1)}, u32[]{:S(2)}, u32[]{:S(2)}) collective-permute-start(bf16[512,128]{1,0:T(8,128)(2,1)S(1)} %collective-permute-done.5.refs_3_), channel_id=1, source_target_pairs={{0,1},{1,0},{2,3},{3,2},{4,5},{5,4},{6,7},{7,6},{8,9},{9,8},{10,11... | collective-permute-start | bytes 393224 | tf_op jit(solution)/shard_map/ppermute | solution.py:198
  18.7 1.5 %collective-permute-start.7 = (bf16[512,128]{1,0:T(8,128)(2,1)S(1)}, bf16[512,128]{1,0:T(8,128)(2,1)S(1)}, u32[]{:S(2)}, u32[]{:S(2)}) collective-permute-start(bf16[512,128]{1,0:T(8,128)(2,1)S(1)} %collective-permute-done.4.refs_2_), channel_id=1, source_target_pairs={{0,1},{1,0},{2,3},{3,2},{4,5},{5,4},{6,7},{7,6},{8,9},{9,8},{10,11... | collective-permute-start | bytes 393224 | tf_op jit(solution)/shard_map/ppermute | solution.py:198

commit v8 on v7

--- a/solution.py
+++ b/solution.py
@@ -70,6 +70,15 @@
     gram[...] = dot(jnp.concatenate([piece[...] for piece in pieces], axis=1), turned[...])
 
 
+def each(size, step, body, index=False, unroll=1):
+    def run(i, carry):
+        some = pl.ds(pl.multiple_of(i * step, step), step)
+        body(some, i) if index else body(some)
+        return carry
+
+    lax.fori_loop(0, size // step, run, 0, unroll=unroll)
+
+
 def last_kernel(fars, count, *refs):
     pieces, refs = refs[: len(fars)], refs[len(fars) :]
     turned, gram_in, tile_hbm, out_hbm, *refs = refs
@@ -79,7 +88,6 @@
     member = lax.axis_index("grad")
     tokens, features = pieces[0].shape
     half = 2 * features
-    halves = [slice(at, at + half) for at in range(0, tokens, half)]
     blocks = [slice(at, at + half) for at in range(0, x.shape[1], half)]
     chunks = [slice(at, at + 32) for at in range(0, tokens, 32)]
 
@@ -88,11 +96,14 @@
         x[:, here] = piece[...]
         xt[here, :] = turned[k * features : (k + 1) * features, :] if k < count else piece[...].T
     late = jnp.concatenate([piece[...] for piece in pieces[count:]], axis=1)
-    for some in halves:
-        product = lax.dot_general(late, late[some], (((1,), (1,)), ((), ())), preferred_element_type=jnp.float32)
+    def gram_half(some):
+        other = jnp.concatenate([piece[some, :] for piece in pieces[count:]], axis=1)
+        product = lax.dot_general(late, other, (((1,), (1,)), ((), ())), preferred_element_type=jnp.float32)
         gram = (gram_in[:, some] + product) * (1.0 / tokens)
         k1[:, some] = gram
         low1[:, some] = gram.astype(jnp.bfloat16)
+
+    each(tokens, half, gram_half)
 
     column_sums, row_sums = [0.0] * len(blocks), [0.0] * len(blocks)
 
@@ -108,11 +119,13 @@
 
     for j in range(len(blocks) - 1):
         add_sums(j)
-    for some in halves:
+    def second(some):
         k2[:, some] = dot(low1[...], low1[:, some])
+
+    each(tokens, half, second)
     add_sums(len(blocks) - 1)
     load.wait()
-    move(halves[0])
+    each(tokens, half, move)
 
     largest = column_sums[-1]
     for column, row in zip(column_sums[:-1], row_sums):
@@ -137,14 +150,16 @@
     q_m = q_m * last
     p = c * (1.0 + eps) * (1.0 + eps2) * beta
 
-    for some in halves:
-        for r in chunks:
-            x1 = k1[r, some]
-            e2 = e2_1 * x1 + e2_2 * k2[r, some]
-            k2[r, some] = e2
-            low2[r, some] = e2.astype(jnp.bfloat16)
-            g[r, some] = (e2 + g_1 * x1).astype(jnp.bfloat16)
-    for some in halves:
+    def squares(r):
+        x1 = k1[r, :]
+        e2 = e2_1 * x1 + e2_2 * k2[r, :]
+        k2[r, :] = e2
+        low2[r, :] = e2.astype(jnp.bfloat16)
+        g[r, :] = (e2 + g_1 * x1).astype(jnp.bfloat16)
+
+    each(tokens, 32, squares, unroll=2)
+
+    def fourths(some):
         product = dot(low2[...], low2[:, some])
         for r in chunks:
             e2 = k2[r, some]
@@ -152,8 +167,8 @@
             k3[r, some] = fourth
             z[r, some] = fourth.astype(jnp.bfloat16)
             h[r, some] = (fourth + (1.0 + eps2) * e2).astype(jnp.bfloat16)
-    for some in halves[1:]:
-        move(some)
+
+    each(tokens, half, fourths)
 
     def add_a(some):
         product = dot(g[...], h[:, some])
@@ -163,35 +178,40 @@
             low1[r, some] = a.astype(jnp.bfloat16)
             k1[r, some] = last * (k_m * a + beta * (e2 + g_1 * x1))
 
-    add_a(halves[0])
-    for some in halves:
+    each(tokens, half, add_a)
+
+    def add_k(some):
         product = dot(z[...], z[:, some])
         for r in chunks:
             k = product[r] + k_z * k3[r, some]
             k4[r, some] = k
             low2[r, some] = k.astype(jnp.bfloat16)
-    for some in halves[1:]:
-        add_a(some)
-    for some in halves:
+
+    each(tokens, half, add_k)
+
+    def add_q(some):
         product = dot(low2[...], low1[:, some])
         for r in chunks:
             g[r, some] = (k1[r, some] + last * (product[r] + a_m * k4[r, some])).astype(jnp.bfloat16)
-    for some in halves:
+
+    each(tokens, half, add_q)
+
+    def mix(some):
         product = dot(image[...], g[:, some])
         mixed[:, some] = (product + q_m * image[:, some].astype(jnp.float32)).astype(jnp.bfloat16)
-    stores = []
-    for some in blocks:
+
+    each(tokens, half, mix)
+
+    def store(some, i):
+        return pltpu.make_async_copy(out.at[:, some], out_hbm.at[:, some], sems.at[1 + i])
+
+    def result(some, i):
         moved = dot(mixed[...], x[:, some])
-        parts = 1 if some is not blocks[-1] else 3
-        step = moved.shape[0] // parts
-        for at in range(0, parts * step, step):
-            r = slice(at, at + step)
-            out[r, some] = (p * tile[r, some].astype(jnp.float32) + moved[r]).astype(jnp.bfloat16)
-            store = pltpu.make_async_copy(out.at[r, some], out_hbm.at[r, some], sems.at[1 + len(stores)])
-            store.start()
-            stores.append(store)
-    for store in stores:
-        store.wait()
+        out[:, some] = (p * tile[:, some].astype(jnp.float32) + moved).astype(jnp.bfloat16)
+        store(some, i).start()
+
+    each(x.shape[1], half, result, index=True)
+    each(x.shape[1], half, lambda some, i: store(some, i).wait(), index=True)
 
 
 def swap(value, far):
@@ -240,7 +260,7 @@
         + [scratch(tokens, tokens, kind=jnp.float32)] * 4
         + [scratch(tokens, tokens)] * 5
         + [scratch(rows, tokens)] * 2
-        + [pltpu.SemaphoreType.DMA((3 + members // 2,))],
+        + [pltpu.SemaphoreType.DMA((1 + members // 2,))],
         compiler_params=pltpu.CompilerParams(vmem_limit_bytes=51 * 2**20),
         cost_estimate=pl.CostEstimate(flops=5 * 10**9, bytes_accessed=0, transcendentals=0),
         name="whole_block",

time: 27.5 us -> 30.5 us (1.11)
  Pallas kernels: 7.97 us -> 11 us
    pallas_call x1, Pallas kernels: 7.03 us -> 10 us  [by_tokens(): pl.pallas_call(functools.partial(last_kernel, (0, 1, *fars, *[far + 1 for...]
where the time goes in v8:
time: 30.5 us; the launch traced here: 30.3 us
  Pallas kernels  11 us (36%)
  starting transfers between devices  11 us (36%)
  waiting for transfers between devices  7.35 us (24%)
  local copies, waits for them, and re-layouts  0.93 us (3%)
    pallas_call x1, Pallas kernels, by_tokens(): pl.pallas_call(functools.partial(last_kernel, (0, 1, *fars, *[far + 1 for...  10 us
    ppermute x3, starting transfers between devices, by_tokens(): lax.ppermute(parts[far], 'dp', [(i, (i + far) % replicas) for i in range(...  7.01 us
    ppermute x7, waiting for transfers between devices, swap(): lax.ppermute(value, 'grad', [(i, i ^ far) for i in range(lax.axis_size('g...  4.8 us
    ppermute x7, starting transfers between devices, swap(): lax.ppermute(value, 'grad', [(i, i ^ far) for i in range(lax.axis_size('g...  4 us
    ppermute x3, waiting for transfers between devices, by_tokens(): lax.ppermute(parts[far], 'dp', [(i, (i + far) % replicas) for i in range(...  2.54 us
    unnamed x5, local copies, waits for them, and re-layouts  0.92 us
    pallas_call x1, Pallas kernels, by_tokens(): pl.pallas_call(first_kernel, out_shape=[shape(len(here) * features, token...  0.66 us
  transfers between devices with their start and end apart: 10, of which 6 were waited for; matrix products, arithmetic and copies ran while one was open for 0% of the time, Pallas kernels for 2%

profile of v8, /device:TPU:0, one launch (start us, length us, event | category | flops | bytes accessed | tf_op | source)
XLA Modules:
  0.0 30.3 jit_solution(12187525028204516414)
XLA Ops:
  0.0 0.0 copy-start
  0.0 0.9 %copy-done = bf16[128,4,128]{2,1,0:T(4,128)(2,1)S(1)} copy-done((bf16[128,4,128]{2,1,0:T(4,128)(2,1)S(1)}, bf16[128,4,128]{2,1,0:T(4,128)(2,1)}, u32[]{:S(2)}) %copy-start) | copy-done | bytes 131096
  0.9 0.3 split_blocks.1
  1.2 3.1 %collective-permute-start = (bf16[128,128]{1,0:T(8,128)(2,1)S(1)}, bf16[128,128]{1,0:T(8,128)(2,1)S(1)}, u32[]{:S(2)}, u32[]{:S(2)}) collective-permute-start(bf16[128,128]{1,0:T(8,128)(2,1)S(1)} %get-tuple-element.12), channel_id=1, source_target_pairs={{0,8},{8,16},{16,24},{24,0},{1,9},{9,17},{17,25},{25,1},{2,10},{10... | collective-permute-start | bytes 98312 | tf_op jit(solution)/shard_map/ppermute | solution.py:235
  4.3 2.6 %collective-permute-start.1 = (bf16[128,128]{1,0:T(8,128)(2,1)S(1)}, bf16[128,128]{1,0:T(8,128)(2,1)S(1)}, u32[]{:S(2)}, u32[]{:S(2)}) collective-permute-start(bf16[128,128]{1,0:T(8,128)(2,1)S(1)} %get-tuple-element.13), channel_id=1, source_target_pairs={{0,16},{8,24},{16,0},{24,8},{1,17},{9,25},{17,1},{25,9},{2,18},{10... | collective-permute-start | bytes 98312 | tf_op jit(solution)/shard_map/ppermute | solution.py:235
  6.9 1.3 %collective-permute-start.2 = (bf16[128,128]{1,0:T(8,128)(2,1)S(1)}, bf16[128,128]{1,0:T(8,128)(2,1)S(1)}, u32[]{:S(2)}, u32[]{:S(2)}) collective-permute-start(bf16[128,128]{1,0:T(8,128)(2,1)S(1)} %get-tuple-element.14), channel_id=1, source_target_pairs={{0,24},{8,0},{16,8},{24,16},{1,25},{9,1},{17,9},{25,17},{2,26},{10... | collective-permute-start | bytes 98312 | tf_op jit(solution)/shard_map/ppermute | solution.py:235
  8.2 0.0 collective-permute-done
  8.2 1.2 %collective-permute-done.1 = bf16[128,128]{1,0:T(8,128)(2,1)S(1)} collective-permute-done((bf16[128,128]{1,0:T(8,128)(2,1)S(1)}, bf16[128,128]{1,0:T(8,128)(2,1)S(1)}, u32[]{:S(2)}, u32[]{:S(2)}) %collective-permute-start.1) | collective-permute-done | bytes 32800 | tf_op jit(solution)/shard_map/ppermute | solution.py:235
  9.4 1.3 %collective-permute-done.2 = bf16[128,128]{1,0:T(8,128)(2,1)S(1)} collective-permute-done((bf16[128,128]{1,0:T(8,128)(2,1)S(1)}, bf16[128,128]{1,0:T(8,128)(2,1)S(1)}, u32[]{:S(2)}, u32[]{:S(2)}) %collective-permute-start.2) | collective-permute-done | bytes 32800 | tf_op jit(solution)/shard_map/ppermute | solution.py:235
  10.8 2.4 %collective-permute-start.6 = (bf16[512,128]{1,0:T(8,128)(2,1)S(1)}, bf16[512,128]{1,0:T(8,128)(2,1)S(1)}, u32[]{:S(2)}, u32[]{:S(2)}) collective-permute-start(bf16[512,128]{1,0:T(8,128)(2,1)S(1)} %constant_dynamic-update-slice_fusion.refs_0_), channel_id=1, source_target_pairs={{0,6},{1,7},{2,4},{3,5},{4,2},{5,3},{6,0},{7,1},{8,14},{9,15},{10,... | collective-permute-start | bytes 393224 | tf_op jit(solution)/shard_map/ppermute | solution.py:218
  13.2 0.5 %collective-permute-start.5 = (bf16[512,128]{1,0:T(8,128)(2,1)S(1)}, bf16[512,128]{1,0:T(8,128)(2,1)S(1)}, u32[]{:S(2)}, u32[]{:S(2)}) collective-permute-start(bf16[512,128]{1,0:T(8,128)(2,1)S(1)} %constant_dynamic-update-slice_fusion.refs_0_), channel_id=1, source_target_pairs={{0,4},{1,5},{2,6},{3,7},{4,0},{5,1},{6,2},{7,3},{8,12},{9,13},{10,... | collective-permute-start | bytes 393224 | tf_op jit(solution)/shard_map/ppermute | solution.py:218
  13.7 0.5 %collective-permute-start.4 = (bf16[512,128]{1,0:T(8,128)(2,1)S(1)}, bf16[512,128]{1,0:T(8,128)(2,1)S(1)}, u32[]{:S(2)}, u32[]{:S(2)}) collective-permute-start(bf16[512,128]{1,0:T(8,128)(2,1)S(1)} %constant_dynamic-update-slice_fusion.refs_0_), channel_id=1, source_target_pairs={{0,2},{1,3},{2,0},{3,1},{4,6},{5,7},{6,4},{7,5},{8,10},{9,11},{10,... | collective-permute-start | bytes 393224 | tf_op jit(solution)/shard_map/ppermute | solution.py:218
  14.3 0.0 collective-permute-start.3
  14.3 3.6 %collective-permute-done.6.refs_4_ = bf16[512,128]{1,0:T(8,128)(2,1)S(1)} collective-permute-done((bf16[512,128]{1,0:T(8,128)(2,1)S(1)}, bf16[512,128]{1,0:T(8,128)(2,1)S(1)}, u32[]{:S(2)}, u32[]{:S(2)}) %collective-permute-start.6) | collective-permute-done | bytes 131104 | tf_op jit(solution)/shard_map/ppermute | solution.py:218
  17.9 0.0 collective-permute-start.9
  17.9 0.9 %collective-permute-done.5.refs_3_ = bf16[512,128]{1,0:T(8,128)(2,1)S(1)} collective-permute-done((bf16[512,128]{1,0:T(8,128)(2,1)S(1)}, bf16[512,128]{1,0:T(8,128)(2,1)S(1)}, u32[]{:S(2)}, u32[]{:S(2)}) %collective-permute-start.5) | collective-permute-done | bytes 131104 | tf_op jit(solution)/shard_map/ppermute | solution.py:218
  18.7 0.0 collective-permute-start.8
  18.7 0.0 collective-permute-done.4.refs_2_
  18.7 0.5 %collective-permute-start.7 = (bf16[512,128]{1,0:T(8,128)(2,1)S(1)}, bf16[512,128]{1,0:T(8,128)(2,1)S(1)}, u32[]{:S(2)}, u32[]{:S(2)}) collective-permute-start(bf16[512,128]{1,0:T(8,128)(2,1)S(1)} %collective-permute-done.4.refs_2_), channel_id=1, source_target_pairs={{0,1},{1,0},{2,3},{3,2},{4,5},{5,4},{6,7},{7,6},{8,9},{9,8},{10,11... | collective-permute-start | bytes 393224 | tf_op jit(solution)/shard_map/ppermute | solution.py:218
  19.2 0.0 collective-permute-done.3.refs_1_
  19.3 0.7 %first_pieces.1 = (bf16[640,512]{1,0:T(8,128)(2,1)S(1)}, f32[512,512]{1,0:T(8,128)S(1)}) custom-call(bf16[512,128]{1,0:T(8,128)(2,1)S(1)} %constant_dynamic-update-slice_fusion.refs_0_, bf16[512,128]{1,0:T(8,128)(2,1)S(1)} %collective-permute-done.3.refs_1_, bf16[512,128]{1,0:T(8,128)(2,1)S(1)} %collective-permute-done.4.refs_2_, ...), custom_call_target="tpu_custom_call" | custom-call | flops 400000000 | tf_op jit(solution)/shard_map/first_pieces/pallas_call | solution.py:244
  19.9 0.0 collective-permute-done.9.refs_7_
  19.9 0.2 collective-permute-done.8.refs_6_
  20.1 0.2 collective-permute-done.7.refs_5_
  20.3 10.0 %whole_block.1 = bf16[768,1024]{1,0:T(8,128)(2,1)} custom-call(bf16[512,128]{1,0:T(8,128)(2,1)S(1)} %constant_dynamic-update-slice_fusion.refs_0_, bf16[512,128]{1,0:T(8,128)(2,1)S(1)} %collective-permute-done.3.refs_1_, bf16[512,128]{1,0:T(8,128)(2,1)S(1)} %collective-permute-done.4.refs_2_, bf16[512,128]{1,0:T(8,128)(2,1)S(1)} %collective-permute-done.5.refs_3_, ...), custom_call_target="tpu_custom_call" | custom-call | flops 5000000000 | tf_op jit(solution)/shard_map/whole_block/pallas_call | solution.py:253
  (4 shorter events, 0.0 us)
Async XLA Ops:
  0.0 0.9 %copy-start = (bf16[128,4,128]{2,1,0:T(4,128)(2,1)S(1)}, bf16[128,4,128]{2,1,0:T(4,128)(2,1)}, u32[]{:S(2)}) copy-start(bf16[128,4,128]{2,1,0:T(4,128)(2,1)} %param.2) | copy-start | bytes 393220
  1.2 7.0 %collective-permute-start = (bf16[128,128]{1,0:T(8,128)(2,1)S(1)}, bf16[128,128]{1,0:T(8,128)(2,1)S(1)}, u32[]{:S(2)}, u32[]{:S(2)}) collective-permute-start(bf16[128,128]{1,0:T(8,128)(2,1)S(1)} %get-tuple-element.12), channel_id=1, source_target_pairs={{0,8},{8,16},{16,24},{24,0},{1,9},{9,17},{17,25},{25,1},{2,10},{10... | collective-permute-start | bytes 98312 | tf_op jit(solution)/shard_map/ppermute | solution.py:235
  4.3 5.2 %collective-permute-start.1 = (bf16[128,128]{1,0:T(8,128)(2,1)S(1)}, bf16[128,128]{1,0:T(8,128)(2,1)S(1)}, u32[]{:S(2)}, u32[]{:S(2)}) collective-permute-start(bf16[128,128]{1,0:T(8,128)(2,1)S(1)} %get-tuple-element.13), channel_id=1, source_target_pairs={{0,16},{8,24},{16,0},{24,8},{1,17},{9,25},{17,1},{25,9},{2,18},{10... | collective-permute-start | bytes 98312 | tf_op jit(solution)/shard_map/ppermute | solution.py:235
  6.9 3.9 %collective-permute-start.2 = (bf16[128,128]{1,0:T(8,128)(2,1)S(1)}, bf16[128,128]{1,0:T(8,128)(2,1)S(1)}, u32[]{:S(2)}, u32[]{:S(2)}) collective-permute-start(bf16[128,128]{1,0:T(8,128)(2,1)S(1)} %get-tuple-element.14), channel_id=1, source_target_pairs={{0,24},{8,0},{16,8},{24,16},{1,25},{9,1},{17,9},{25,17},{2,26},{10... | collective-permute-start | bytes 98312 | tf_op jit(solution)/shard_map/ppermute | solution.py:235
  10.8 7.1 %collective-permute-start.6 = (bf16[512,128]{1,0:T(8,128)(2,1)S(1)}, bf16[512,128]{1,0:T(8,128)(2,1)S(1)}, u32[]{:S(2)}, u32[]{:S(2)}) collective-permute-start(bf16[512,128]{1,0:T(8,128)(2,1)S(1)} %constant_dynamic-update-slice_fusion.refs_0_), channel_id=1, source_target_pairs={{0,6},{1,7},{2,4},{3,5},{4,2},{5,3},{6,0},{7,1},{8,14},{9,15},{10,... | collective-permute-start | bytes 393224 | tf_op jit(solution)/shard_map/ppermute | solution.py:218
  13.2 5.5 %collective-permute-start.5 = (bf16[512,128]{1,0:T(8,128)(2,1)S(1)}, bf16[512,128]{1,0:T(8,128)(2,1)S(1)}, u32[]{:S(2)}, u32[]{:S(2)}) collective-permute-start(bf16[512,128]{1,0:T(8,128)(2,1)S(1)} %constant_dynamic-update-slice_fusion.refs_0_), channel_id=1, source_target_pairs={{0,4},{1,5},{2,6},{3,7},{4,0},{5,1},{6,2},{7,3},{8,12},{9,13},{10,... | collective-permute-start | bytes 393224 | tf_op jit(solution)/shard_map/ppermute | solution.py:218
  13.7 5.0 %collective-permute-start.4 = (bf16[512,128]{1,0:T(8,128)(2,1)S(1)}, bf16[512,128]{1,0:T(8,128)(2,1)S(1)}, u32[]{:S(2)}, u32[]{:S(2)}) collective-permute-start(bf16[512,128]{1,0:T(8,128)(2,1)S(1)} %constant_dynamic-update-slice_fusion.refs_0_), channel_id=1, source_target_pairs={{0,2},{1,3},{2,0},{3,1},{4,6},{5,7},{6,4},{7,5},{8,10},{9,11},{10,... | collective-permute-start | bytes 393224 | tf_op jit(solution)/shard_map/ppermute | solution.py:218
  14.3 5.0 %collective-permute-start.3 = (bf16[512,128]{1,0:T(8,128)(2,1)S(1)}, bf16[512,128]{1,0:T(8,128)(2,1)S(1)}, u32[]{:S(2)}, u32[]{:S(2)}) collective-permute-start(bf16[512,128]{1,0:T(8,128)(2,1)S(1)} %constant_dynamic-update-slice_fusion.refs_0_), channel_id=1, source_target_pairs={{0,1},{1,0},{2,3},{3,2},{4,5},{5,4},{6,7},{7,6},{8,9},{9,8},{10,11... | collective-permute-start | bytes 393224 | tf_op jit(solution)/shard_map/ppermute | solution.py:218
  17.9 2.1 %collective-permute-start.9 = (bf16[512,128]{1,0:T(8,128)(2,1)S(1)}, bf16[512,128]{1,0:T(8,128)(2,1)S(1)}, u32[]{:S(2)}, u32[]{:S(2)}) collective-permute-start(bf16[512,128]{1,0:T(8,128)(2,1)S(1)} %collective-permute-done.6.refs_4_), channel_id=1, source_target_pairs={{0,1},{1,0},{2,3},{3,2},{4,5},{5,4},{6,7},{7,6},{8,9},{9,8},{10,11... | collective-permute-start | bytes 393224 | tf_op jit(solution)/shard_map/ppermute | solution.py:218
  18.7 1.3 %collective-permute-start.8 = (bf16[512,128]{1,0:T(8,128)(2,1)S(1)}, bf16[512,128]{1,0:T(8,128)(2,1)S(1)}, u32[]{:S(2)}, u32[]{:S(2)}) collective-permute-start(bf16[512,128]{1,0:T(8,128)(2,1)S(1)} %collective-permute-done.5.refs_3_), channel_id=1, source_target_pairs={{0,1},{1,0},{2,3},{3,2},{4,5},{5,4},{6,7},{7,6},{8,9},{9,8},{10,11... | collective-permute-start | bytes 393224 | tf_op jit(solution)/shard_map/ppermute | solution.py:218
  18.7 1.5 %collective-permute-start.7 = (bf16[512,128]{1,0:T(8,128)(2,1)S(1)}, bf16[512,128]{1,0:T(8,128)(2,1)S(1)}, u32[]{:S(2)}, u32[]{:S(2)}) collective-permute-start(bf16[512,128]{1,0:T(8,128)(2,1)S(1)} %collective-permute-done.4.refs_2_), channel_id=1, source_target_pairs={{0,1},{1,0},{2,3},{3,2},{4,5},{5,4},{6,7},{7,6},{8,9},{9,8},{10,11... | collective-permute-start | bytes 393224 | tf_op jit(solution)/shard_map/ppermute | solution.py:218

commit v9 on v7

--- a/solution.py
+++ b/solution.py
@@ -73,7 +73,7 @@
 def last_kernel(fars, count, *refs):
     pieces, refs = refs[: len(fars)], refs[len(fars) :]
     turned, gram_in, tile_hbm, out_hbm, *refs = refs
-    tile, out, x, xt, k1, k2, k3, k4, low1, low2, g, h, z, image, mixed, sems = refs
+    tile, out, x, xt, k1, k2, e2, g, z, h, a, k, q, image, mixed, sems = refs
     load = pltpu.make_async_copy(tile_hbm, tile, sems.at[0])
     load.start()
     member = lax.axis_index("grad")
@@ -83,16 +83,14 @@
     blocks = [slice(at, at + half) for at in range(0, x.shape[1], half)]
     chunks = [slice(at, at + 32) for at in range(0, tokens, 32)]
 
-    for k, (far, piece) in enumerate(zip(fars, pieces)):
+    for n, (far, piece) in enumerate(zip(fars, pieces)):
         here = pl.ds(pl.multiple_of((member ^ far) * features, features), features)
         x[:, here] = piece[...]
-        xt[here, :] = turned[k * features : (k + 1) * features, :] if k < count else piece[...].T
+        xt[here, :] = turned[n * features : (n + 1) * features, :] if n < count else piece[...].T
     late = jnp.concatenate([piece[...] for piece in pieces[count:]], axis=1)
     for some in halves:
         product = lax.dot_general(late, late[some], (((1,), (1,)), ((), ())), preferred_element_type=jnp.float32)
-        gram = (gram_in[:, some] + product) * (1.0 / tokens)
-        k1[:, some] = gram
-        low1[:, some] = gram.astype(jnp.bfloat16)
+        k1[:, some] = ((gram_in[:, some] + product) * (1.0 / tokens)).astype(jnp.bfloat16)
 
     column_sums, row_sums = [0.0] * len(blocks), [0.0] * len(blocks)
 
@@ -109,7 +107,7 @@
     for j in range(len(blocks) - 1):
         add_sums(j)
     for some in halves:
-        k2[:, some] = dot(low1[...], low1[:, some])
+        k2[:, some] = dot(k1[...], k1[:, some]).astype(jnp.bfloat16)
     add_sums(len(blocks) - 1)
     load.wait()
     move(halves[0])
@@ -129,55 +127,51 @@
     k_m = eps8 + (1.0 + zeta) * zeta + zeta + 1.0 + eps8
     k_z = 1.0 + 3.0 * zeta
     a_m = g_m * h_m
-    a_e2 = g_m * (1.0 + eps2) + h_m
-    a_1 = h_m * g_1
     beta = (1.0 + zeta) * (1.0 + eps8)
     q_m = a_m * k_m + beta * g_m + (1.0 + eps2) * beta
     last = -c * c * (1.0 / tokens)
     q_m = q_m * last
     p = c * (1.0 + eps) * (1.0 + eps2) * beta
 
-    for some in halves:
-        for r in chunks:
-            x1 = k1[r, some]
-            e2 = e2_1 * x1 + e2_2 * k2[r, some]
-            k2[r, some] = e2
-            low2[r, some] = e2.astype(jnp.bfloat16)
-            g[r, some] = (e2 + g_1 * x1).astype(jnp.bfloat16)
-    for some in halves:
-        product = dot(low2[...], low2[:, some])
-        for r in chunks:
-            e2 = k2[r, some]
-            fourth = 2.0 * eps2 * e2 + product[r]
-            k3[r, some] = fourth
+    def wide(ref, r, some):
+        return ref[r, some].astype(jnp.float32)
+
+    for some in halves:
+        for r in chunks:
+            first = wide(k1, r, some)
+            square = e2_1 * first + e2_2 * wide(k2, r, some)
+            e2[r, some] = square.astype(jnp.bfloat16)
+            g[r, some] = (square + g_1 * first).astype(jnp.bfloat16)
+    for some in halves:
+        product = dot(e2[...], e2[:, some])
+        for r in chunks:
+            square = wide(e2, r, some)
+            fourth = 2.0 * eps2 * square + product[r]
             z[r, some] = fourth.astype(jnp.bfloat16)
-            h[r, some] = (fourth + (1.0 + eps2) * e2).astype(jnp.bfloat16)
+            h[r, some] = (fourth + (1.0 + eps2) * square).astype(jnp.bfloat16)
     for some in halves[1:]:
         move(some)
 
     def add_a(some):
         product = dot(g[...], h[:, some])
         for r in chunks:
-            x1, e2 = k1[r, some], k2[r, some]
-            a = product[r] + g_m * k3[r, some] + a_e2 * e2 + a_1 * x1
-            low1[r, some] = a.astype(jnp.bfloat16)
-            k1[r, some] = last * (k_m * a + beta * (e2 + g_1 * x1))
+            a[r, some] = (product[r] + g_m * wide(h, r, some) + h_m * wide(g, r, some)).astype(jnp.bfloat16)
 
     add_a(halves[0])
     for some in halves:
         product = dot(z[...], z[:, some])
         for r in chunks:
-            k = product[r] + k_z * k3[r, some]
-            k4[r, some] = k
-            low2[r, some] = k.astype(jnp.bfloat16)
+            k[r, some] = (product[r] + k_z * wide(z, r, some)).astype(jnp.bfloat16)
     for some in halves[1:]:
         add_a(some)
-    for some in halves:
-        product = dot(low2[...], low1[:, some])
-        for r in chunks:
-            g[r, some] = (k1[r, some] + last * (product[r] + a_m * k4[r, some])).astype(jnp.bfloat16)
-    for some in halves:
-        product = dot(image[...], g[:, some])
+    q_k, q_a, q_g = last * a_m, last * k_m, last * beta
+    for some in halves:
+        product = dot(k[...], a[:, some])
+        for r in chunks:
+            rest = q_k * wide(k, r, some) + q_a * wide(a, r, some) + q_g * wide(g, r, some)
+            q[r, some] = (last * product[r] + rest).astype(jnp.bfloat16)
+    for some in halves:
+        product = dot(image[...], q[:, some])
         mixed[:, some] = (product + q_m * image[:, some].astype(jnp.float32)).astype(jnp.bfloat16)
     stores = []
     for some in blocks:
@@ -237,8 +231,7 @@
         out_specs=ANYWHERE,
         scratch_shapes=[scratch(rows, width)] * 2
         + [scratch(tokens, width), scratch(width, tokens)]
-        + [scratch(tokens, tokens, kind=jnp.float32)] * 4
-        + [scratch(tokens, tokens)] * 5
+        + [scratch(tokens, tokens)] * 9
         + [scratch(rows, tokens)] * 2
         + [pltpu.SemaphoreType.DMA((3 + members // 2,))],
         compiler_params=pltpu.CompilerParams(vmem_limit_bytes=51 * 2**20),

time: 27.5 us -> 27.4 us (level)
  no operation moved by 1% of the time
where the time goes in v9:
time: 27.4 us; the launch traced here: 27.2 us
  starting transfers between devices  11 us (40%)
  Pallas kernels  7.91 us (29%)
  waiting for transfers between devices  7.35 us (27%)
  local copies, waits for them, and re-layouts  0.93 us (3%)
    ppermute x3, starting transfers between devices, by_tokens(): lax.ppermute(parts[far], 'dp', [(i, (i + far) % replicas) for i in range(...  7.01 us
    pallas_call x1, Pallas kernels, by_tokens(): pl.pallas_call(functools.partial(last_kernel, (0, 1, *fars, *[far + 1 for...  6.97 us
    ppermute x7, waiting for transfers between devices, swap(): lax.ppermute(value, 'grad', [(i, i ^ far) for i in range(lax.axis_size('g...  4.8 us
    ppermute x7, starting transfers between devices, swap(): lax.ppermute(value, 'grad', [(i, i ^ far) for i in range(lax.axis_size('g...  4 us
    ppermute x3, waiting for transfers between devices, by_tokens(): lax.ppermute(parts[far], 'dp', [(i, (i + far) % replicas) for i in range(...  2.54 us
    unnamed x5, local copies, waits for them, and re-layouts  0.92 us
    pallas_call x1, Pallas kernels, by_tokens(): pl.pallas_call(first_kernel, out_shape=[shape(len(here) * features, token...  0.66 us
  transfers between devices with their start and end apart: 10, of which 6 were waited for; matrix products, arithmetic and copies ran while one was open for 0% of the time, Pallas kernels for 2%

profile of v9, /device:TPU:0, one launch (start us, length us, event | category | flops | bytes accessed | tf_op | source)
XLA Modules:
  0.0 27.2 jit_solution(595404828565668017)
XLA Ops:
  0.0 0.0 copy-start
  0.0 0.9 %copy-done = bf16[128,4,128]{2,1,0:T(4,128)(2,1)S(1)} copy-done((bf16[128,4,128]{2,1,0:T(4,128)(2,1)S(1)}, bf16[128,4,128]{2,1,0:T(4,128)(2,1)}, u32[]{:S(2)}) %copy-start) | copy-done | bytes 131096
  0.9 0.3 %split_blocks.1 = (bf16[128,128]{1,0:T(8,128)(2,1)S(1)}, bf16[128,128]{1,0:T(8,128)(2,1)S(1)}, bf16[128,128]{1,0:T(8,128)(2,1)S(1)}, bf16[128,128]{1,0:T(8,128)(2,1)S(1)}) custom-call(bf16[512,128]{1,0:T(8,128)(2,1)S(1)} %bitcast.3), custom_call_target="tpu_custom_call" | custom-call | tf_op jit(solution)/shard_map/split_blocks/pallas_call | solution.py:55
  1.2 3.1 %collective-permute-start = (bf16[128,128]{1,0:T(8,128)(2,1)S(1)}, bf16[128,128]{1,0:T(8,128)(2,1)S(1)}, u32[]{:S(2)}, u32[]{:S(2)}) collective-permute-start(bf16[128,128]{1,0:T(8,128)(2,1)S(1)} %get-tuple-element.12), channel_id=1, source_target_pairs={{0,8},{8,16},{16,24},{24,0},{1,9},{9,17},{17,25},{25,1},{2,10},{10... | collective-permute-start | bytes 98312 | tf_op jit(solution)/shard_map/ppermute | solution.py:209
  4.3 2.6 %collective-permute-start.1 = (bf16[128,128]{1,0:T(8,128)(2,1)S(1)}, bf16[128,128]{1,0:T(8,128)(2,1)S(1)}, u32[]{:S(2)}, u32[]{:S(2)}) collective-permute-start(bf16[128,128]{1,0:T(8,128)(2,1)S(1)} %get-tuple-element.13), channel_id=1, source_target_pairs={{0,16},{8,24},{16,0},{24,8},{1,17},{9,25},{17,1},{25,9},{2,18},{10... | collective-permute-start | bytes 98312 | tf_op jit(solution)/shard_map/ppermute | solution.py:209
  6.9 1.3 %collective-permute-start.2 = (bf16[128,128]{1,0:T(8,128)(2,1)S(1)}, bf16[128,128]{1,0:T(8,128)(2,1)S(1)}, u32[]{:S(2)}, u32[]{:S(2)}) collective-permute-start(bf16[128,128]{1,0:T(8,128)(2,1)S(1)} %get-tuple-element.14), channel_id=1, source_target_pairs={{0,24},{8,0},{16,8},{24,16},{1,25},{9,1},{17,9},{25,17},{2,26},{10... | collective-permute-start | bytes 98312 | tf_op jit(solution)/shard_map/ppermute | solution.py:209
  8.2 0.0 collective-permute-done
  8.2 1.2 %collective-permute-done.1 = bf16[128,128]{1,0:T(8,128)(2,1)S(1)} collective-permute-done((bf16[128,128]{1,0:T(8,128)(2,1)S(1)}, bf16[128,128]{1,0:T(8,128)(2,1)S(1)}, u32[]{:S(2)}, u32[]{:S(2)}) %collective-permute-start.1) | collective-permute-done | bytes 32800 | tf_op jit(solution)/shard_map/ppermute | solution.py:209
  9.4 1.3 %collective-permute-done.2 = bf16[128,128]{1,0:T(8,128)(2,1)S(1)} collective-permute-done((bf16[128,128]{1,0:T(8,128)(2,1)S(1)}, bf16[128,128]{1,0:T(8,128)(2,1)S(1)}, u32[]{:S(2)}, u32[]{:S(2)}) %collective-permute-start.2) | collective-permute-done | bytes 32800 | tf_op jit(solution)/shard_map/ppermute | solution.py:209
  10.8 2.4 %collective-permute-start.6 = (bf16[512,128]{1,0:T(8,128)(2,1)S(1)}, bf16[512,128]{1,0:T(8,128)(2,1)S(1)}, u32[]{:S(2)}, u32[]{:S(2)}) collective-permute-start(bf16[512,128]{1,0:T(8,128)(2,1)S(1)} %constant_dynamic-update-slice_fusion.refs_0_), channel_id=1, source_target_pairs={{0,6},{1,7},{2,4},{3,5},{4,2},{5,3},{6,0},{7,1},{8,14},{9,15},{10,... | collective-permute-start | bytes 393224 | tf_op jit(solution)/shard_map/ppermute | solution.py:192
  13.2 0.5 %collective-permute-start.5 = (bf16[512,128]{1,0:T(8,128)(2,1)S(1)}, bf16[512,128]{1,0:T(8,128)(2,1)S(1)}, u32[]{:S(2)}, u32[]{:S(2)}) collective-permute-start(bf16[512,128]{1,0:T(8,128)(2,1)S(1)} %constant_dynamic-update-slice_fusion.refs_0_), channel_id=1, source_target_pairs={{0,4},{1,5},{2,6},{3,7},{4,0},{5,1},{6,2},{7,3},{8,12},{9,13},{10,... | collective-permute-start | bytes 393224 | tf_op jit(solution)/shard_map/ppermute | solution.py:192
  13.7 0.5 %collective-permute-start.4 = (bf16[512,128]{1,0:T(8,128)(2,1)S(1)}, bf16[512,128]{1,0:T(8,128)(2,1)S(1)}, u32[]{:S(2)}, u32[]{:S(2)}) collective-permute-start(bf16[512,128]{1,0:T(8,128)(2,1)S(1)} %constant_dynamic-update-slice_fusion.refs_0_), channel_id=1, source_target_pairs={{0,2},{1,3},{2,0},{3,1},{4,6},{5,7},{6,4},{7,5},{8,10},{9,11},{10,... | collective-permute-start | bytes 393224 | tf_op jit(solution)/shard_map/ppermute | solution.py:192
  14.3 0.0 collective-permute-start.3
  14.3 3.6 %collective-permute-done.6.refs_4_ = bf16[512,128]{1,0:T(8,128)(2,1)S(1)} collective-permute-done((bf16[512,128]{1,0:T(8,128)(2,1)S(1)}, bf16[512,128]{1,0:T(8,128)(2,1)S(1)}, u32[]{:S(2)}, u32[]{:S(2)}) %collective-permute-start.6) | collective-permute-done | bytes 131104 | tf_op jit(solution)/shard_map/ppermute | solution.py:192
  17.9 0.0 collective-permute-start.9
  17.9 0.9 %collective-permute-done.5.refs_3_ = bf16[512,128]{1,0:T(8,128)(2,1)S(1)} collective-permute-done((bf16[512,128]{1,0:T(8,128)(2,1)S(1)}, bf16[512,128]{1,0:T(8,128)(2,1)S(1)}, u32[]{:S(2)}, u32[]{:S(2)}) %collective-permute-start.5) | collective-permute-done | bytes 131104 | tf_op jit(solution)/shard_map/ppermute | solution.py:192
  18.7 0.0 collective-permute-start.8
  18.7 0.0 collective-permute-done.4.refs_2_
  18.7 0.5 %collective-permute-start.7 = (bf16[512,128]{1,0:T(8,128)(2,1)S(1)}, bf16[512,128]{1,0:T(8,128)(2,1)S(1)}, u32[]{:S(2)}, u32[]{:S(2)}) collective-permute-start(bf16[512,128]{1,0:T(8,128)(2,1)S(1)} %collective-permute-done.4.refs_2_), channel_id=1, source_target_pairs={{0,1},{1,0},{2,3},{3,2},{4,5},{5,4},{6,7},{7,6},{8,9},{9,8},{10,11... | collective-permute-start | bytes 393224 | tf_op jit(solution)/shard_map/ppermute | solution.py:192
  19.2 0.0 collective-permute-done.3.refs_1_
  19.3 0.7 %first_pieces.1 = (bf16[640,512]{1,0:T(8,128)(2,1)S(1)}, f32[512,512]{1,0:T(8,128)S(1)}) custom-call(bf16[512,128]{1,0:T(8,128)(2,1)S(1)} %constant_dynamic-update-slice_fusion.refs_0_, bf16[512,128]{1,0:T(8,128)(2,1)S(1)} %collective-permute-done.3.refs_1_, bf16[512,128]{1,0:T(8,128)(2,1)S(1)} %collective-permute-done.4.refs_2_, ...), custom_call_target="tpu_custom_call" | custom-call | flops 400000000 | tf_op jit(solution)/shard_map/first_pieces/pallas_call | solution.py:218
  19.9 0.0 collective-permute-done.9.refs_7_
  19.9 0.2 collective-permute-done.8.refs_6_
  20.1 0.2 collective-permute-done.7.refs_5_
  20.3 7.0 %whole_block.1 = bf16[768,1024]{1,0:T(8,128)(2,1)} custom-call(bf16[512,128]{1,0:T(8,128)(2,1)S(1)} %constant_dynamic-update-slice_fusion.refs_0_, bf16[512,128]{1,0:T(8,128)(2,1)S(1)} %collective-permute-done.3.refs_1_, bf16[512,128]{1,0:T(8,128)(2,1)S(1)} %collective-permute-done.4.refs_2_, bf16[512,128]{1,0:T(8,128)(2,1)S(1)} %collective-permute-done.5.refs_3_, ...), custom_call_target="tpu_custom_call" | custom-call | flops 5000000000 | tf_op jit(solution)/shard_map/whole_block/pallas_call | solution.py:227
  (4 shorter events, 0.0 us)
Async XLA Ops:
  0.0 0.9 %copy-start = (bf16[128,4,128]{2,1,0:T(4,128)(2,1)S(1)}, bf16[128,4,128]{2,1,0:T(4,128)(2,1)}, u32[]{:S(2)}) copy-start(bf16[128,4,128]{2,1,0:T(4,128)(2,1)} %param.2) | copy-start | bytes 393220
  1.2 7.0 %collective-permute-start = (bf16[128,128]{1,0:T(8,128)(2,1)S(1)}, bf16[128,128]{1,0:T(8,128)(2,1)S(1)}, u32[]{:S(2)}, u32[]{:S(2)}) collective-permute-start(bf16[128,128]{1,0:T(8,128)(2,1)S(1)} %get-tuple-element.12), channel_id=1, source_target_pairs={{0,8},{8,16},{16,24},{24,0},{1,9},{9,17},{17,25},{25,1},{2,10},{10... | collective-permute-start | bytes 98312 | tf_op jit(solution)/shard_map/ppermute | solution.py:209
  4.3 5.2 %collective-permute-start.1 = (bf16[128,128]{1,0:T(8,128)(2,1)S(1)}, bf16[128,128]{1,0:T(8,128)(2,1)S(1)}, u32[]{:S(2)}, u32[]{:S(2)}) collective-permute-start(bf16[128,128]{1,0:T(8,128)(2,1)S(1)} %get-tuple-element.13), channel_id=1, source_target_pairs={{0,16},{8,24},{16,0},{24,8},{1,17},{9,25},{17,1},{25,9},{2,18},{10... | collective-permute-start | bytes 98312 | tf_op jit(solution)/shard_map/ppermute | solution.py:209
  6.9 3.9 %collective-permute-start.2 = (bf16[128,128]{1,0:T(8,128)(2,1)S(1)}, bf16[128,128]{1,0:T(8,128)(2,1)S(1)}, u32[]{:S(2)}, u32[]{:S(2)}) collective-permute-start(bf16[128,128]{1,0:T(8,128)(2,1)S(1)} %get-tuple-element.14), channel_id=1, source_target_pairs={{0,24},{8,0},{16,8},{24,16},{1,25},{9,1},{17,9},{25,17},{2,26},{10... | collective-permute-start | bytes 98312 | tf_op jit(solution)/shard_map/ppermute | solution.py:209
  10.8 7.1 %collective-permute-start.6 = (bf16[512,128]{1,0:T(8,128)(2,1)S(1)}, bf16[512,128]{1,0:T(8,128)(2,1)S(1)}, u32[]{:S(2)}, u32[]{:S(2)}) collective-permute-start(bf16[512,128]{1,0:T(8,128)(2,1)S(1)} %constant_dynamic-update-slice_fusion.refs_0_), channel_id=1, source_target_pairs={{0,6},{1,7},{2,4},{3,5},{4,2},{5,3},{6,0},{7,1},{8,14},{9,15},{10,... | collective-permute-start | bytes 393224 | tf_op jit(solution)/shard_map/ppermute | solution.py:192
  13.2 5.5 %collective-permute-start.5 = (bf16[512,128]{1,0:T(8,128)(2,1)S(1)}, bf16[512,128]{1,0:T(8,128)(2,1)S(1)}, u32[]{:S(2)}, u32[]{:S(2)}) collective-permute-start(bf16[512,128]{1,0:T(8,128)(2,1)S(1)} %constant_dynamic-update-slice_fusion.refs_0_), channel_id=1, source_target_pairs={{0,4},{1,5},{2,6},{3,7},{4,0},{5,1},{6,2},{7,3},{8,12},{9,13},{10,... | collective-permute-start | bytes 393224 | tf_op jit(solution)/shard_map/ppermute | solution.py:192
  13.7 5.0 %collective-permute-start.4 = (bf16[512,128]{1,0:T(8,128)(2,1)S(1)}, bf16[512,128]{1,0:T(8,128)(2,1)S(1)}, u32[]{:S(2)}, u32[]{:S(2)}) collective-permute-start(bf16[512,128]{1,0:T(8,128)(2,1)S(1)} %constant_dynamic-update-slice_fusion.refs_0_), channel_id=1, source_target_pairs={{0,2},{1,3},{2,0},{3,1},{4,6},{5,7},{6,4},{7,5},{8,10},{9,11},{10,... | collective-permute-start | bytes 393224 | tf_op jit(solution)/shard_map/ppermute | solution.py:192
  14.3 5.0 %collective-permute-start.3 = (bf16[512,128]{1,0:T(8,128)(2,1)S(1)}, bf16[512,128]{1,0:T(8,128)(2,1)S(1)}, u32[]{:S(2)}, u32[]{:S(2)}) collective-permute-start(bf16[512,128]{1,0:T(8,128)(2,1)S(1)} %constant_dynamic-update-slice_fusion.refs_0_), channel_id=1, source_target_pairs={{0,1},{1,0},{2,3},{3,2},{4,5},{5,4},{6,7},{7,6},{8,9},{9,8},{10,11... | collective-permute-start | bytes 393224 | tf_op jit(solution)/shard_map/ppermute | solution.py:192
  17.9 2.1 %collective-permute-start.9 = (bf16[512,128]{1,0:T(8,128)(2,1)S(1)}, bf16[512,128]{1,0:T(8,128)(2,1)S(1)}, u32[]{:S(2)}, u32[]{:S(2)}) collective-permute-start(bf16[512,128]{1,0:T(8,128)(2,1)S(1)} %collective-permute-done.6.refs_4_), channel_id=1, source_target_pairs={{0,1},{1,0},{2,3},{3,2},{4,5},{5,4},{6,7},{7,6},{8,9},{9,8},{10,11... | collective-permute-start | bytes 393224 | tf_op jit(solution)/shard_map/ppermute | solution.py:192
  18.7 1.3 %collective-permute-start.8 = (bf16[512,128]{1,0:T(8,128)(2,1)S(1)}, bf16[512,128]{1,0:T(8,128)(2,1)S(1)}, u32[]{:S(2)}, u32[]{:S(2)}) collective-permute-start(bf16[512,128]{1,0:T(8,128)(2,1)S(1)} %collective-permute-done.5.refs_3_), channel_id=1, source_target_pairs={{0,1},{1,0},{2,3},{3,2},{4,5},{5,4},{6,7},{7,6},{8,9},{9,8},{10,11... | collective-permute-start | bytes 393224 | tf_op jit(solution)/shard_map/ppermute | solution.py:192
  18.7 1.5 %collective-permute-start.7 = (bf16[512,128]{1,0:T(8,128)(2,1)S(1)}, bf16[512,128]{1,0:T(8,128)(2,1)S(1)}, u32[]{:S(2)}, u32[]{:S(2)}) collective-permute-start(bf16[512,128]{1,0:T(8,128)(2,1)S(1)} %collective-permute-done.4.refs_2_), channel_id=1, source_target_pairs={{0,1},{1,0},{2,3},{3,2},{4,5},{5,4},{6,7},{7,6},{8,9},{9,8},{10,11... | collective-permute-start | bytes 393224 | tf_op jit(solution)/shard_map/ppermute | solution.py:192

commit v10 on v9

--- a/solution.py
+++ b/solution.py
@@ -88,9 +88,23 @@
         x[:, here] = piece[...]
         xt[here, :] = turned[n * features : (n + 1) * features, :] if n < count else piece[...].T
     late = jnp.concatenate([piece[...] for piece in pieces[count:]], axis=1)
-    for some in halves:
-        product = lax.dot_general(late, late[some], (((1,), (1,)), ((), ())), preferred_element_type=jnp.float32)
-        k1[:, some] = ((gram_in[:, some] + product) * (1.0 / tokens)).astype(jnp.bfloat16)
+
+    def symmetric(left, right, finish, *refs):
+        for n, some in enumerate(halves):
+            rows = slice(some.start, tokens)
+            product = left(rows, some) if right is None else dot(left[rows, :], right[:, some])
+            for r in chunks[some.start // 32 :]:
+                values = finish(product[r.start - some.start : r.stop - some.start], r, some)
+                for ref, value in zip(refs, values):
+                    ref[r, some] = value.astype(jnp.bfloat16)
+            for other in halves[n + 1 :]:
+                for ref in refs:
+                    ref[some, other] = ref[other, some].T
+
+    def gram(rows, some):
+        return lax.dot_general(late[rows], late[some], (((1,), (1,)), ((), ())), preferred_element_type=jnp.float32)
+
+    symmetric(gram, None, lambda product, r, some: [(gram_in[r, some] + product) * (1.0 / tokens)], k1)
 
     column_sums, row_sums = [0.0] * len(blocks), [0.0] * len(blocks)
 
@@ -106,8 +120,7 @@
 
     for j in range(len(blocks) - 1):
         add_sums(j)
-    for some in halves:
-        k2[:, some] = dot(k1[...], k1[:, some]).astype(jnp.bfloat16)
+    symmetric(k1, k1, lambda product, r, some: [product], k2)
     add_sums(len(blocks) - 1)
     load.wait()
     move(halves[0])
@@ -142,34 +155,23 @@
             square = e2_1 * first + e2_2 * wide(k2, r, some)
             e2[r, some] = square.astype(jnp.bfloat16)
             g[r, some] = (square + g_1 * first).astype(jnp.bfloat16)
-    for some in halves:
-        product = dot(e2[...], e2[:, some])
-        for r in chunks:
-            square = wide(e2, r, some)
-            fourth = 2.0 * eps2 * square + product[r]
-            z[r, some] = fourth.astype(jnp.bfloat16)
-            h[r, some] = (fourth + (1.0 + eps2) * square).astype(jnp.bfloat16)
+
+    def fourth(product, r, some):
+        square = wide(e2, r, some)
+        value = 2.0 * eps2 * square + product
+        return value, value + (1.0 + eps2) * square
+
+    symmetric(e2, e2, fourth, z, h)
     for some in halves[1:]:
         move(some)
-
-    def add_a(some):
-        product = dot(g[...], h[:, some])
-        for r in chunks:
-            a[r, some] = (product[r] + g_m * wide(h, r, some) + h_m * wide(g, r, some)).astype(jnp.bfloat16)
-
-    add_a(halves[0])
-    for some in halves:
-        product = dot(z[...], z[:, some])
-        for r in chunks:
-            k[r, some] = (product[r] + k_z * wide(z, r, some)).astype(jnp.bfloat16)
-    for some in halves[1:]:
-        add_a(some)
+    symmetric(z, z, lambda product, r, some: [product + k_z * wide(z, r, some)], k)
+    symmetric(g, h, lambda product, r, some: [product + g_m * wide(h, r, some) + h_m * wide(g, r, some)], a)
     q_k, q_a, q_g = last * a_m, last * k_m, last * beta
-    for some in halves:
-        product = dot(k[...], a[:, some])
-        for r in chunks:
-            rest = q_k * wide(k, r, some) + q_a * wide(a, r, some) + q_g * wide(g, r, some)
-            q[r, some] = (last * product[r] + rest).astype(jnp.bfloat16)
+
+    def whole(product, r, some):
+        return [last * product + q_k * wide(k, r, some) + q_a * wide(a, r, some) + q_g * wide(g, r, some)]
+
+    symmetric(k, a, whole, q)
     for some in halves:
         product = dot(image[...], q[:, some])
         mixed[:, some] = (product + q_m * image[:, some].astype(jnp.float32)).astype(jnp.bfloat16)
@@ -210,11 +212,14 @@
         for far in sorted(range(1, replicas), key=lambda far: abs(far - replicas // 2))
     }
     fars = tuple(range(2, members, 2))
-    own = jnp.concatenate([parts[0]] + [arrived[far] for far in range(1, replicas)], axis=0)
+    rest = jnp.concatenate([arrived[far] for far in range(1, replicas)], axis=0)
+    early = swap(parts[0], fars[-1])
+    own = jnp.concatenate([parts[0] + 0.0 * early, rest], axis=0)
     near = swap(own, 1)
-    held = [swap(own, far) for far in fars]
-    far_near = [swap(piece, 1) for piece in held]
-    here, there = [own, near, *held], far_near
+    held = [swap(own, far) for far in fars[:-1]]
+    held.append(jnp.concatenate([early, swap(own[parts[0].shape[0] :], fars[-1])], axis=0))
+    held_near = [swap(piece, 1) for piece in held]
+    here, there = [own, near, *held, held_near[-1]], held_near[:-1]
     turned, gram = pl.pallas_call(
         first_kernel,
         out_shape=[shape(len(here) * features, tokens, kind=jnp.bfloat16), shape(tokens, tokens)],
@@ -225,7 +230,7 @@
         name="first_pieces",
     )(*here)
     return pl.pallas_call(
-        functools.partial(last_kernel, (0, 1, *fars, *[far + 1 for far in fars]), len(here)),
+        functools.partial(last_kernel, (0, 1, *fars, fars[-1] + 1, *[far + 1 for far in fars[:-1]]), len(here)),
         out_shape=shape(rows, width, kind=jnp.bfloat16),
         in_specs=[WHOLE] * (members + 2) + [ANYWHERE],
         out_specs=ANYWHERE,

time: 27.4 us -> 28 us (1.022)
  starting transfers between devices: 11 us -> 14.8 us
  waiting for transfers between devices: 7.35 us -> 4.17 us
    ppermute x7 -> x8, starting transfers between devices: 4 us -> 7.83 us  [swap(): lax.ppermute(value, 'grad', [(i, i ^ far) for i in range(lax.axis_size('g...]
    ppermute x3, waiting for transfers between devices: 2.54 us -> 0.12 us  [by_tokens(): lax.ppermute(parts[far], 'dp', [(i, (i + far) % replicas) for i in range(...]
    ppermute x7 -> x8, waiting for transfers between devices: 4.8 us -> 4.05 us  [swap(): lax.ppermute(value, 'grad', [(i, i ^ far) for i in range(lax.axis_size('g...]
    unnamed x5 -> x2, local copies, waits for them, and re-layouts: 0.92 us -> 0.9 us
  transfers between devices with their start and end apart: 10 -> 11, of which waited for: 6 -> 5; matrix products, arithmetic and copies ran while one was open for 0% -> 0% of each run, Pallas kernels for 2% -> 2%
where the time goes in v10:
time: 28 us; the launch traced here: 27.8 us
  starting transfers between devices  14.8 us (53%)
  Pallas kernels  7.82 us (28%)
  waiting for transfers between devices  4.17 us (15%)
  local copies, waits for them, and re-layouts  0.92 us (3%)
    ppermute x8, starting transfers between devices, swap(): lax.ppermute(value, 'grad', [(i, i ^ far) for i in range(lax.axis_size('g...  7.83 us
    ppermute x3, starting transfers between devices, by_tokens(): lax.ppermute(parts[far], 'dp', [(i, (i + far) % replicas) for i in range(...  7.01 us
    pallas_call x1, Pallas kernels, by_tokens(): pl.pallas_call(functools.partial(last_kernel, (0, 1, *fars, fars[-1] + 1,...  6.88 us
    ppermute x8, waiting for transfers between devices, swap(): lax.ppermute(value, 'grad', [(i, i ^ far) for i in range(lax.axis_size('g...  4.05 us
    unnamed x2, local copies, waits for them, and re-layouts  0.9 us
    pallas_call x1, Pallas kernels, by_tokens(): pl.pallas_call(first_kernel, out_shape=[shape(len(here) * features, token...  0.66 us
  transfers between devices with their start and end apart: 11, of which 5 were waited for; matrix products, arithmetic and copies ran while one was open for 0% of the time, Pallas kernels for 2%

profile of v10, /device:TPU:0, one launch (start us, length us, event | category | flops | bytes accessed | tf_op | source)
XLA Modules:
  0.0 27.8 jit_solution(7709471331456794066)
XLA Ops:
  0.0 0.0 copy-start
  0.0 0.9 %copy-done = bf16[128,4,128]{2,1,0:T(4,128)(2,1)S(1)} copy-done((bf16[128,4,128]{2,1,0:T(4,128)(2,1)S(1)}, bf16[128,4,128]{2,1,0:T(4,128)(2,1)}, u32[]{:S(2)}) %copy-start) | copy-done | bytes 131096
  0.9 0.3 %split_blocks.1 = (bf16[128,128]{1,0:T(8,128)(2,1)S(1)}, bf16[128,128]{1,0:T(8,128)(2,1)S(1)}, bf16[128,128]{1,0:T(8,128)(2,1)S(1)}, bf16[128,128]{1,0:T(8,128)(2,1)S(1)}) custom-call(bf16[512,128]{1,0:T(8,128)(2,1)S(1)} %bitcast.3), custom_call_target="tpu_custom_call" | custom-call | tf_op jit(solution)/shard_map/split_blocks/pallas_call | solution.py:55
  1.2 3.1 %collective-permute-start.1 = (bf16[128,128]{1,0:T(8,128)(2,1)S(1)}, bf16[128,128]{1,0:T(8,128)(2,1)S(1)}, u32[]{:S(2)}, u32[]{:S(2)}) collective-permute-start(bf16[128,128]{1,0:T(8,128)(2,1)S(1)} %get-tuple-element.12), channel_id=1, source_target_pairs={{0,8},{8,16},{16,24},{24,0},{1,9},{9,17},{17,25},{25,1},{2,10},{10... | collective-permute-start | bytes 98312 | tf_op jit(solution)/shard_map/ppermute | solution.py:211
  4.3 2.6 %collective-permute-start.2 = (bf16[128,128]{1,0:T(8,128)(2,1)S(1)}, bf16[128,128]{1,0:T(8,128)(2,1)S(1)}, u32[]{:S(2)}, u32[]{:S(2)}) collective-permute-start(bf16[128,128]{1,0:T(8,128)(2,1)S(1)} %get-tuple-element.13), channel_id=1, source_target_pairs={{0,16},{8,24},{16,0},{24,8},{1,17},{9,25},{17,1},{25,9},{2,18},{10... | collective-permute-start | bytes 98312 | tf_op jit(solution)/shard_map/ppermute | solution.py:211
  6.9 1.3 %collective-permute-start.3 = (bf16[128,128]{1,0:T(8,128)(2,1)S(1)}, bf16[128,128]{1,0:T(8,128)(2,1)S(1)}, u32[]{:S(2)}, u32[]{:S(2)}) collective-permute-start(bf16[128,128]{1,0:T(8,128)(2,1)S(1)} %get-tuple-element.14), channel_id=1, source_target_pairs={{0,24},{8,0},{16,8},{24,16},{1,25},{9,1},{17,9},{25,17},{2,26},{10... | collective-permute-start | bytes 98312 | tf_op jit(solution)/shard_map/ppermute | solution.py:211
  8.2 2.4 %collective-permute-start = (bf16[128,128]{1,0:T(8,128)(2,1)S(1)}, bf16[128,128]{1,0:T(8,128)(2,1)S(1)}, u32[]{:S(2)}, u32[]{:S(2)}) collective-permute-start(bf16[128,128]{1,0:T(8,128)(2,1)S(1)} %get-tuple-element.11), channel_id=1, source_target_pairs={{0,6},{1,7},{2,4},{3,5},{4,2},{5,3},{6,0},{7,1},{8,14},{9,15},{10,... | collective-permute-start | bytes 98312 | tf_op jit(solution)/shard_map/ppermute | solution.py:194
  10.7 0.0 collective-permute-done.1
  10.7 0.0 collective-permute-done.2
  10.7 0.1 collective-permute-done.3
  10.8 2.5 %collective-permute-start.7 = (bf16[384,128]{1,0:T(8,128)(2,1)S(1)}, bf16[384,128]{1,0:T(8,128)(2,1)S(1)}, u32[]{:S(2)}, u32[]{:S(2)}) collective-permute-start(bf16[384,128]{1,0:T(8,128)(2,1)S(1)} %pad_maximum_fusion.1), channel_id=1, source_target_pairs={{0,6},{1,7},{2,4},{3,5},{4,2},{5,3},{6,0},{7,1},{8,14},{9,15},{10,... | collective-permute-start | bytes 294920 | tf_op jit(solution)/shard_map/ppermute | solution.py:194
  13.3 0.0 collective-permute-done
  13.3 1.3 %collective-permute-start.6 = (bf16[512,128]{1,0:T(8,128)(2,1)S(1)}, bf16[512,128]{1,0:T(8,128)(2,1)S(1)}, u32[]{:S(2)}, u32[]{:S(2)}) collective-permute-start(bf16[512,128]{1,0:T(8,128)(2,1)S(1)} %pad_maximum_fusion.refs_0_), channel_id=1, source_target_pairs={{0,4},{1,5},{2,6},{3,7},{4,0},{5,1},{6,2},{7,3},{8,12},{9,13},{10,... | collective-permute-start | bytes 393224 | tf_op jit(solution)/shard_map/ppermute | solution.py:194
  14.6 1.5 %collective-permute-start.5 = (bf16[512,128]{1,0:T(8,128)(2,1)S(1)}, bf16[512,128]{1,0:T(8,128)(2,1)S(1)}, u32[]{:S(2)}, u32[]{:S(2)}) collective-permute-start(bf16[512,128]{1,0:T(8,128)(2,1)S(1)} %pad_maximum_fusion.refs_0_), channel_id=1, source_target_pairs={{0,2},{1,3},{2,0},{3,1},{4,6},{5,7},{6,4},{7,5},{8,10},{9,11},{10,... | collective-permute-start | bytes 393224 | tf_op jit(solution)/shard_map/ppermute | solution.py:194
  16.1 0.0 collective-permute-start.4
  16.1 1.0 %collective-permute-done.7 = bf16[384,128]{1,0:T(8,128)(2,1)S(1)} collective-permute-done((bf16[384,128]{1,0:T(8,128)(2,1)S(1)}, bf16[384,128]{1,0:T(8,128)(2,1)S(1)}, u32[]{:S(2)}, u32[]{:S(2)}) %collective-permute-start.7) | collective-permute-done | bytes 98336 | tf_op jit(solution)/shard_map/ppermute | solution.py:194
  17.1 0.1 collective-permute-start.8
  17.2 1.2 %collective-permute-done.6.refs_3_ = bf16[512,128]{1,0:T(8,128)(2,1)S(1)} collective-permute-done((bf16[512,128]{1,0:T(8,128)(2,1)S(1)}, bf16[512,128]{1,0:T(8,128)(2,1)S(1)}, u32[]{:S(2)}, u32[]{:S(2)}) %collective-permute-start.6) | collective-permute-done | bytes 131104 | tf_op jit(solution)/shard_map/ppermute | solution.py:194
  18.4 0.0 collective-permute-start.10
  18.4 1.2 %collective-permute-done.5.refs_2_ = bf16[512,128]{1,0:T(8,128)(2,1)S(1)} collective-permute-done((bf16[512,128]{1,0:T(8,128)(2,1)S(1)}, bf16[512,128]{1,0:T(8,128)(2,1)S(1)}, u32[]{:S(2)}, u32[]{:S(2)}) %collective-permute-start.5) | collective-permute-done | bytes 131104 | tf_op jit(solution)/shard_map/ppermute | solution.py:194
  19.6 0.0 collective-permute-start.9
  19.6 0.0 collective-permute-done.4.refs_1_
  19.6 0.0 collective-permute-done.8.refs_5_
  19.6 0.7 %first_pieces.1 = (bf16[768,512]{1,0:T(8,128)(2,1)S(1)}, f32[512,512]{1,0:T(8,128)S(1)}) custom-call(bf16[512,128]{1,0:T(8,128)(2,1)S(1)} %pad_maximum_fusion.refs_0_, bf16[512,128]{1,0:T(8,128)(2,1)S(1)} %collective-permute-done.4.refs_1_, bf16[512,128]{1,0:T(8,128)(2,1)S(1)} %collective-permute-done.5.refs_2_, ...), custom_call_target="tpu_custom_call" | custom-call | flops 400000000 | tf_op jit(solution)/shard_map/first_pieces/pallas_call | solution.py:223
  20.3 0.0 collective-permute-done.10.refs_7_
  20.3 0.7 %collective-permute-done.9.refs_6_ = bf16[512,128]{1,0:T(8,128)(2,1)S(1)} collective-permute-done((bf16[512,128]{1,0:T(8,128)(2,1)S(1)}, bf16[512,128]{1,0:T(8,128)(2,1)S(1)}, u32[]{:S(2)}, u32[]{:S(2)}) %collective-permute-start.9) | collective-permute-done | bytes 131104 | tf_op jit(solution)/shard_map/ppermute | solution.py:194
  21.0 6.9 %whole_block.1 = bf16[768,1024]{1,0:T(8,128)(2,1)} custom-call(bf16[512,128]{1,0:T(8,128)(2,1)S(1)} %pad_maximum_fusion.refs_0_, bf16[512,128]{1,0:T(8,128)(2,1)S(1)} %collective-permute-done.4.refs_1_, bf16[512,128]{1,0:T(8,128)(2,1)S(1)} %collective-permute-done.5.refs_2_, bf16[512,128]{1,0:T(8,128)(2,1)S(1)} %collective-permute-done.6.refs_3_, ...), custom_call_target="tpu_custom_call" | custom-call | flops 5000000000 | tf_op jit(solution)/shard_map/whole_block/pallas_call | solution.py:232
  (4 shorter events, 0.0 us)
Async XLA Ops:
  0.0 0.9 %copy-start = (bf16[128,4,128]{2,1,0:T(4,128)(2,1)S(1)}, bf16[128,4,128]{2,1,0:T(4,128)(2,1)}, u32[]{:S(2)}) copy-start(bf16[128,4,128]{2,1,0:T(4,128)(2,1)} %param.2) | copy-start | bytes 393220
  1.2 9.5 %collective-permute-start.1 = (bf16[128,128]{1,0:T(8,128)(2,1)S(1)}, bf16[128,128]{1,0:T(8,128)(2,1)S(1)}, u32[]{:S(2)}, u32[]{:S(2)}) collective-permute-start(bf16[128,128]{1,0:T(8,128)(2,1)S(1)} %get-tuple-element.12), channel_id=1, source_target_pairs={{0,8},{8,16},{16,24},{24,0},{1,9},{9,17},{17,25},{25,1},{2,10},{10... | collective-permute-start | bytes 98312 | tf_op jit(solution)/shard_map/ppermute | solution.py:211
  4.3 6.4 %collective-permute-start.2 = (bf16[128,128]{1,0:T(8,128)(2,1)S(1)}, bf16[128,128]{1,0:T(8,128)(2,1)S(1)}, u32[]{:S(2)}, u32[]{:S(2)}) collective-permute-start(bf16[128,128]{1,0:T(8,128)(2,1)S(1)} %get-tuple-element.13), channel_id=1, source_target_pairs={{0,16},{8,24},{16,0},{24,8},{1,17},{9,25},{17,1},{25,9},{2,18},{10... | collective-permute-start | bytes 98312 | tf_op jit(solution)/shard_map/ppermute | solution.py:211
  6.9 3.9 %collective-permute-start.3 = (bf16[128,128]{1,0:T(8,128)(2,1)S(1)}, bf16[128,128]{1,0:T(8,128)(2,1)S(1)}, u32[]{:S(2)}, u32[]{:S(2)}) collective-permute-start(bf16[128,128]{1,0:T(8,128)(2,1)S(1)} %get-tuple-element.14), channel_id=1, source_target_pairs={{0,24},{8,0},{16,8},{24,16},{1,25},{9,1},{17,9},{25,17},{2,26},{10... | collective-permute-start | bytes 98312 | tf_op jit(solution)/shard_map/ppermute | solution.py:211
  8.2 5.1 %collective-permute-start = (bf16[128,128]{1,0:T(8,128)(2,1)S(1)}, bf16[128,128]{1,0:T(8,128)(2,1)S(1)}, u32[]{:S(2)}, u32[]{:S(2)}) collective-permute-start(bf16[128,128]{1,0:T(8,128)(2,1)S(1)} %get-tuple-element.11), channel_id=1, source_target_pairs={{0,6},{1,7},{2,4},{3,5},{4,2},{5,3},{6,0},{7,1},{8,14},{9,15},{10,... | collective-permute-start | bytes 98312 | tf_op jit(solution)/shard_map/ppermute | solution.py:194
  10.8 6.3 %collective-permute-start.7 = (bf16[384,128]{1,0:T(8,128)(2,1)S(1)}, bf16[384,128]{1,0:T(8,128)(2,1)S(1)}, u32[]{:S(2)}, u32[]{:S(2)}) collective-permute-start(bf16[384,128]{1,0:T(8,128)(2,1)S(1)} %pad_maximum_fusion.1), channel_id=1, source_target_pairs={{0,6},{1,7},{2,4},{3,5},{4,2},{5,3},{6,0},{7,1},{8,14},{9,15},{10,... | collective-permute-start | bytes 294920 | tf_op jit(solution)/shard_map/ppermute | solution.py:194
  13.3 5.1 %collective-permute-start.6 = (bf16[512,128]{1,0:T(8,128)(2,1)S(1)}, bf16[512,128]{1,0:T(8,128)(2,1)S(1)}, u32[]{:S(2)}, u32[]{:S(2)}) collective-permute-start(bf16[512,128]{1,0:T(8,128)(2,1)S(1)} %pad_maximum_fusion.refs_0_), channel_id=1, source_target_pairs={{0,4},{1,5},{2,6},{3,7},{4,0},{5,1},{6,2},{7,3},{8,12},{9,13},{10,... | collective-permute-start | bytes 393224 | tf_op jit(solution)/shard_map/ppermute | solution.py:194
  14.6 5.0 %collective-permute-start.5 = (bf16[512,128]{1,0:T(8,128)(2,1)S(1)}, bf16[512,128]{1,0:T(8,128)(2,1)S(1)}, u32[]{:S(2)}, u32[]{:S(2)}) collective-permute-start(bf16[512,128]{1,0:T(8,128)(2,1)S(1)} %pad_maximum_fusion.refs_0_), channel_id=1, source_target_pairs={{0,2},{1,3},{2,0},{3,1},{4,6},{5,7},{6,4},{7,5},{8,10},{9,11},{10,... | collective-permute-start | bytes 393224 | tf_op jit(solution)/shard_map/ppermute | solution.py:194
  16.1 3.5 %collective-permute-start.4 = (bf16[512,128]{1,0:T(8,128)(2,1)S(1)}, bf16[512,128]{1,0:T(8,128)(2,1)S(1)}, u32[]{:S(2)}, u32[]{:S(2)}) collective-permute-start(bf16[512,128]{1,0:T(8,128)(2,1)S(1)} %pad_maximum_fusion.refs_0_), channel_id=1, source_target_pairs={{0,1},{1,0},{2,3},{3,2},{4,5},{5,4},{6,7},{7,6},{8,9},{9,8},{10,11... | collective-permute-start | bytes 393224 | tf_op jit(solution)/shard_map/ppermute | solution.py:194
  17.1 2.5 %collective-permute-start.8 = (bf16[512,128]{1,0:T(8,128)(2,1)S(1)}, bf16[512,128]{1,0:T(8,128)(2,1)S(1)}, u32[]{:S(2)}, u32[]{:S(2)}) collective-permute-start(bf16[512,128]{1,0:T(8,128)(2,1)S(1)} %constant_dynamic-update-slice_fusion.refs_4_), channel_id=1, source_target_pairs={{0,1},{1,0},{2,3},{3,2},{4,5},{5,4},{6,7},{7,6},{8,9},{9,8},{10,11... | collective-permute-start | bytes 393224 | tf_op jit(solution)/shard_map/ppermute | solution.py:194
  18.4 1.8 %collective-permute-start.10 = (bf16[512,128]{1,0:T(8,128)(2,1)S(1)}, bf16[512,128]{1,0:T(8,128)(2,1)S(1)}, u32[]{:S(2)}, u32[]{:S(2)}) collective-permute-start(bf16[512,128]{1,0:T(8,128)(2,1)S(1)} %collective-permute-done.6.refs_3_), channel_id=1, source_target_pairs={{0,1},{1,0},{2,3},{3,2},{4,5},{5,4},{6,7},{7,6},{8,9},{9,8},{10,11... | collective-permute-start | bytes 393224 | tf_op jit(solution)/shard_map/ppermute | solution.py:194
  19.6 1.3 %collective-permute-start.9 = (bf16[512,128]{1,0:T(8,128)(2,1)S(1)}, bf16[512,128]{1,0:T(8,128)(2,1)S(1)}, u32[]{:S(2)}, u32[]{:S(2)}) collective-permute-start(bf16[512,128]{1,0:T(8,128)(2,1)S(1)} %collective-permute-done.5.refs_2_), channel_id=1, source_target_pairs={{0,1},{1,0},{2,3},{3,2},{4,5},{5,4},{6,7},{7,6},{8,9},{9,8},{10,11... | collective-permute-start | bytes 393224 | tf_op jit(solution)/shard_map/ppermute | solution.py:194

commit v11 on v10

v11 whole, which is shorter than its diff:
```python
import functools

import jax
import jax.numpy as jnp
from jax import lax
from jax.experimental import pallas as pl
from jax.experimental.pallas import tpu as pltpu
from jax.sharding import PartitionSpec as P

ITERS = 4
DAMPING = 0.01
WHOLE = pl.BlockSpec(memory_space=pltpu.VMEM)
ANYWHERE = pl.BlockSpec(memory_space=pl.ANY)


def dot(a, b):
    return jnp.dot(a, b, preferred_element_type=jnp.float32)


def gather_block(factor_inputs):
    pieces = jnp.transpose(factor_inputs, (1, 0, 2))
    piece = lax.all_to_all(pieces, "dp", split_axis=0, concat_axis=1, tiled=True)[0]
    return lax.all_gather(piece, "grad", axis=1, tiled=True)


def by_features(columns, tile):
    tokens, width = columns.shape
    covariance = jnp.einsum("tr,tc->rc", columns, columns, preferred_element_type=jnp.float32) * (1.0 / tokens)
    damped = covariance + DAMPING * jnp.eye(width, dtype=jnp.float32)
    scale = 1.0 / jnp.max(jnp.sum(jnp.abs(damped), axis=1))
    image = scale * damped
    result = scale * tile.astype(jnp.float32)
    for step in range(ITERS):
        low = image.astype(jnp.bfloat16)
        result = 2.0 * result - dot(result.astype(jnp.bfloat16), low)
        if step < ITERS - 1:
            image = 2.0 * image - dot(low, low)
    return result


def split_kernel(x_ref, *out_refs):
    replicas, tokens = len(out_refs), out_refs[0].shape[0]
    here = lax.axis_index("dp")
    core = lax.rem(lax.axis_index("grad"), 2)
    fars = (0, 2, 1 + 2 * core, 3 - 2 * core)
    x = x_ref[...]
    rows = lax.broadcasted_iota(jnp.int32, (tokens, tokens * replicas), 0)
    cols = lax.broadcasted_iota(jnp.int32, (tokens, tokens * replicas), 1)
    offset = cols - rows * replicas
    for far, out_ref in zip(fars, out_refs):
        choice = jnp.where(offset == lax.rem(here + far, replicas), 1.0, 0.0).astype(jnp.bfloat16)
        out_ref[...] = dot(choice, x).astype(jnp.bfloat16)


def split_blocks(factor_inputs):
    tokens, blocks, features = factor_inputs.shape
    return pl.pallas_call(
        split_kernel,
        out_shape=[jax.ShapeDtypeStruct((tokens, features), factor_inputs.dtype)] * blocks,
        in_specs=[WHOLE],
        out_specs=[WHOLE] * blocks,
        compiler_params=pltpu.CompilerParams(vmem_limit_bytes=16 * 2**20),
        name="split_blocks",
    )(factor_inputs.reshape(tokens * blocks, features))


def columns_of(same, other):
    tokens = same.shape[0]
    q0, q1, q2, q3 = [slice(at, at + tokens // 4) for at in range(0, tokens, tokens // 4)]
    mine = jnp.concatenate([same[q0, :], same[q1, :], same[q2, :], other[q3, :]], axis=0)
    its = jnp.concatenate([other[q0, :], other[q1, :], same[q3, :], other[q2, :]], axis=0)
    return jnp.concatenate([mine, its], axis=1)


def first_kernel(own, near, across, across_near, got, columns, turned, gram):
    tokens = own.shape[0]
    pairs = [(own, near), (across, across_near), (got.at[:tokens], got.at[tokens:])]
    wide = 2 * own.shape[1]
    for n, (same, other) in enumerate(pairs):
        some = slice(n * wide, (n + 1) * wide)
        value = columns_of(same, other)
        columns[:, some] = value
        turned[some, :] = value.T
    gram[...] = dot(columns[...], turned[...])


def last_kernel(late_ref, x, xt, gram_in, tile_hbm, out_hbm, *refs):
    tile, out, late, late_t, k1, k2, e2, g, z, h, a, k, q, image, mixed, sems = refs
    load = pltpu.make_async_copy(tile_hbm, tile, sems.at[0])
    load.start()
    member = lax.axis_index("grad")
    core = lax.rem(member, 2)
    tokens = x.shape[0]
    half = late.shape[1]
    features = half // 2
    halves = [slice(at, at + half) for at in range(0, tokens, half)]
    blocks = [slice(at, at + half) for at in range(0, x.shape[1], half)]
    chunks = [slice(at, at + 32) for at in range(0, tokens, 32)]
    fars = [0, 6, 2 + 2 * core, 4 - 2 * core]

    def place(far):
        return pl.ds(pl.multiple_of((member ^ far) * features, features), features)

    def chosen(some):
        return jnp.concatenate([tile[:, place(far ^ one)] for far in some for one in (0, 1)], axis=1)

    late[...] = columns_of(late_ref.at[tokens:], late_ref.at[:tokens])
    late_t[...] = late[...].T

    def symmetric(left, right, finish, *refs):
        for n, some in enumerate(halves):
            rows = slice(some.start, tokens)
            product = left(rows, some) if right is None else dot(left[rows, :], right[:, some])
            for r in chunks[some.start // 32 :]:
                values = finish(product[r.start - some.start : r.stop - some.start], r, some)
                for ref, value in zip(refs, values):
                    ref[r, some] = value.astype(jnp.bfloat16)
            for other in halves[n + 1 :]:
                for ref in refs:
                    ref[some, other] = ref[other, some].T

    def gram(rows, some):
        return lax.dot_general(late[rows, :], late[some, :], (((1,), (1,)), ((), ())), preferred_element_type=jnp.float32)

    symmetric(gram, None, lambda product, r, some: [(gram_in[r, some] + product) * (1.0 / tokens)], k1)

    column_sums, row_sums = [0.0] * (len(blocks) + 1), [0.0] * len(blocks)

    def add_sums(n, left, right):
        column = jnp.abs(dot(left, right))
        column_sums[n] = column_sums[n] + jnp.sum(column, axis=0, keepdims=True)
        for i, some in enumerate(blocks[: min(n, column.shape[0] // half)]):
            row_sums[i] = row_sums[i] + column[some, :features] + column[some, features:]

    def move(some):
        moved = dot(chosen(fars[:-1]), xt[:, some]) + dot(chosen(fars[-1:]), late_t[:, some])
        image[:, some] = moved.astype(jnp.bfloat16)

    for n, some in enumerate(blocks):
        add_sums(n, xt[: some.stop, :], x[:, some])
    symmetric(k1, k1, lambda product, r, some: [product], k2)
    add_sums(len(blocks), xt[...], late[...])
    column_sums[-1] = column_sums[-1] + jnp.sum(jnp.abs(dot(late_t[...], late[...])), axis=0, keepdims=True)
    load.wait()
    move(halves[0])

    largest = column_sums[-1]
    for column, row in zip(column_sums[:-1], row_sums):
        largest = jnp.maximum(largest, column + jnp.sum(row.T, axis=0, keepdims=True))
    c = 1.0 / (jnp.max(largest) * (1.0 / tokens) + DAMPING)
    eps = 1.0 - c * DAMPING
    eps2 = eps * eps
    zeta = eps2 * eps2
    eps8 = zeta * zeta
    e2_1, e2_2 = -2.0 * eps * c, c * c
    g_1 = -(1.0 + eps) * c
    g_m = eps2 + (1.0 + eps) * eps + eps
    h_m = zeta + (1.0 + eps2) * eps2 + eps2
    k_m = eps8 + (1.0 + zeta) * zeta + zeta + 1.0 + eps8
    k_z = 1.0 + 3.0 * zeta
    a_m = g_m * h_m
    beta = (1.0 + zeta) * (1.0 + eps8)
    q_m = a_m * k_m + beta * g_m + (1.0 + eps2) * beta
    last = -c * c * (1.0 / tokens)
    q_m = q_m * last
    p = c * (1.0 + eps) * (1.0 + eps2) * beta

    def wide(ref, r, some):
        return ref[r, some].astype(jnp.float32)

    for some in halves:
        for r in chunks:
            first = wide(k1, r, some)
            square = e2_1 * first + e2_2 * wide(k2, r, some)
            e2[r, some] = square.astype(jnp.bfloat16)
            g[r, some] = (square + g_1 * first).astype(jnp.bfloat16)

    def fourth(product, r, some):
        square = wide(e2, r, some)
        value = 2.0 * eps2 * square + product
        return value, value + (1.0 + eps2) * square

    symmetric(e2, e2, fourth, z, h)
    for some in halves[1:]:
        move(some)
    symmetric(z, z, lambda product, r, some: [product + k_z * wide(z, r, some)], k)
    for some in halves:
        product = dot(g[...], h[:, some])
        for r in chunks:
            a[r, some] = (product[r] + g_m * wide(h, r, some) + h_m * wide(g, r, some)).astype(jnp.bfloat16)
    q_k, q_a, q_g = last * a_m, last * k_m, last * beta
    for some in halves:
        product = dot(k[...], a[:, some])
        for r in chunks:
            rest = q_k * wide(k, r, some) + q_a * wide(a, r, some) + q_g * wide(g, r, some)
            q[r, some] = (last * product[r] + rest).astype(jnp.bfloat16)
    for some in halves:
        product = dot(image[...], q[:, some])
        mixed[:, some] = (product + q_m * image[:, some].astype(jnp.float32)).astype(jnp.bfloat16)
    stores = []
    for n, far in enumerate(fars):
        moved = dot(mixed[...], late[...] if n == len(blocks) else x[:, blocks[n]])
        for one in (0, 1):
            here = place(far ^ one)
            kept = p * tile[:, here].astype(jnp.float32)
            out[:, here] = (kept + moved[:, one * features : (one + 1) * features]).astype(jnp.bfloat16)
            store = pltpu.make_async_copy(out.at[:, here], out_hbm.at[:, here], sems.at[1 + len(stores)])
            store.start()
            stores.append(store)
    for store in stores:
        store.wait()


def by_tokens(factor_inputs, tile):
    members, replicas = lax.axis_size("grad"), lax.axis_size("dp")
    rows, width = tile.shape
    features = factor_inputs.shape[2]
    tokens = factor_inputs.shape[0] * replicas

    def shape(*sizes, kind=jnp.bfloat16):
        return jax.ShapeDtypeStruct(sizes, kind)

    def scratch(*sizes):
        return pltpu.VMEM(sizes, jnp.bfloat16)

    def swap(value, *fars):
        return lax.ppermute(value, "grad", [(i, i ^ fars[i % len(fars)]) for i in range(members)])

    part, part_across, mine, given = split_blocks(factor_inputs)
    both = jnp.concatenate([mine, swap(given, 1)], axis=0)
    across = lax.ppermute(part_across, "dp", [(i, (i + 2) % replicas) for i in range(replicas)])
    along = lax.ppermute(
        both,
        ("dp", "grad"),
        [
            (i * members + j, (i + (3 if j % 2 else 1)) % replicas * members + j)
            for i in range(replicas)
            for j in range(members)
        ],
    )
    own = jnp.concatenate([part, across, along], axis=0)
    near = swap(own, 1)
    diagonal = swap(own, 6)
    got = swap(jnp.concatenate([own, near], axis=0), 2, 4)
    diagonal_near = swap(diagonal, 1)
    late = swap(got, 1)
    early = width - 2 * features
    columns, turned, gram = pl.pallas_call(
        first_kernel,
        out_shape=[shape(tokens, early), shape(early, tokens), shape(tokens, tokens, kind=jnp.float32)],
        in_specs=[WHOLE] * 5,
        out_specs=[WHOLE] * 3,
        compiler_params=pltpu.CompilerParams(vmem_limit_bytes=16 * 2**20),
        cost_estimate=pl.CostEstimate(flops=4 * 10**8, bytes_accessed=0, transcendentals=0),
        name="first_chips",
    )(own, near, diagonal, diagonal_near, got)
    return pl.pallas_call(
        last_kernel,
        out_shape=shape(rows, width),
        in_specs=[WHOLE] * 4 + [ANYWHERE],
        out_specs=ANYWHERE,
        scratch_shapes=[scratch(rows, width)] * 2
        + [scratch(tokens, 2 * features), scratch(2 * features, tokens)]
        + [scratch(tokens, tokens)] * 9
        + [scratch(rows, tokens)] * 2
        + [pltpu.SemaphoreType.DMA((1 + members,))],
        compiler_params=pltpu.CompilerParams(vmem_limit_bytes=51 * 2**20),
        cost_estimate=pl.CostEstimate(flops=5 * 10**9, bytes_accessed=0, transcendentals=0),
        name="whole_block",
    )(late, columns, turned, gram, tile)


def local(factor_inputs, gradients):
    features, members = factor_inputs.shape[2], lax.axis_size("grad")
    tokens = factor_inputs.shape[0] * lax.axis_size("dp")
    tile = gradients[0]
    if tokens < features * members and features % 128 == 0 and (members, lax.axis_size("dp")) == (8, 4):
        result = by_tokens(factor_inputs, tile)
    else:
        result = by_features(gather_block(factor_inputs), tile)
    return result.astype(jnp.bfloat16)[None]


def solution(mesh):
    placed = (P("dp", None, "grad"), P("dp", "grad", None))
    return jax.shard_map(
        local, mesh=mesh, in_specs=placed, out_specs=P("dp", "grad", None), check_vma=False
    )
```

time: 28 us -> 33 us (1.18)
  waiting for transfers between devices: 4.17 us -> 15.5 us
  starting transfers between devices: 14.8 us -> 8.8 us
    ppermute x11 -> x8, waiting for transfers between devices: 4.17 us -> 15.5 us  [the longest x6 11 us: swap(): lax.ppermute(value, 'grad', [(i, i ^ fars[i % len(fars)]) for i in range(...]
    ppermute x11 -> x8, starting transfers between devices: 14.8 us -> 8.8 us  [the longest x1 4.1 us: by_tokens(): lax.ppermute(part_across, 'dp', [(i, (i + 2) % replicas) for i in range(r...]
    unnamed x2 -> x4, local copies, waits for them, and re-layouts: 0.9 us -> 0.92 us
  transfers between devices with their start and end apart: 11 -> 8, of which waited for: 5 -> 6; matrix products, arithmetic and copies ran while one was open for 0% -> 0% of each run, Pallas kernels for 2% -> 2%
where the time goes in v11:
time: 33 us; the launch traced here: 32.8 us
  waiting for transfers between devices  15.5 us (47%)
  starting transfers between devices  8.8 us (27%)
  Pallas kernels  7.51 us (23%)
  local copies, waits for them, and re-layouts  0.93 us (3%)
    ppermute x6, waiting for transfers between devices, swap(): lax.ppermute(value, 'grad', [(i, i ^ fars[i % len(fars)]) for i in range(...  11 us
    pallas_call x1, Pallas kernels, by_tokens(): pl.pallas_call(last_kernel, out_shape=shape(rows, width), in_specs=[WHOLE...  6.56 us
    ppermute x1, waiting for transfers between devices, by_tokens(): lax.ppermute(both, ('dp', 'grad'), [(i * members + j, (i + (3 if j % 2 el...  4.47 us
    ppermute x1, starting transfers between devices, by_tokens(): lax.ppermute(part_across, 'dp', [(i, (i + 2) % replicas) for i in range(r...  4.1 us
    ppermute x6, starting transfers between devices, swap(): lax.ppermute(value, 'grad', [(i, i ^ fars[i % len(fars)]) for i in range(...  3.13 us
    ppermute x1, starting transfers between devices, by_tokens(): lax.ppermute(both, ('dp', 'grad'), [(i * members + j, (i + (3 if j % 2 el...  1.58 us
    unnamed x4, local copies, waits for them, and re-layouts  0.92 us
    pallas_call x1, Pallas kernels, by_tokens(): pl.pallas_call(first_kernel, out_shape=[shape(tokens, early), shape(early...  0.67 us
  transfers between devices with their start and end apart: 8, of which 6 were waited for; matrix products, arithmetic and copies ran while one was open for 0% of the time, Pallas kernels for 2%

profile of v11, /device:TPU:0, one launch (start us, length us, event | category | flops | bytes accessed | tf_op | source)
XLA Modules:
  0.0 32.8 jit_solution(14700994635809785826)
XLA Ops:
  0.0 0.0 copy-start
  0.0 0.9 %copy-done = bf16[128,4,128]{2,1,0:T(4,128)(2,1)S(1)} copy-done((bf16[128,4,128]{2,1,0:T(4,128)(2,1)S(1)}, bf16[128,4,128]{2,1,0:T(4,128)(2,1)}, u32[]{:S(2)}) %copy-start) | copy-done | bytes 131096
  0.9 0.3 split_blocks.1
  1.2 4.1 %collective-permute-start = (bf16[128,128]{1,0:T(8,128)(2,1)S(1)}, bf16[128,128]{1,0:T(8,128)(2,1)S(1)}, u32[]{:S(2)}, u32[]{:S(2)}) collective-permute-start(bf16[128,128]{1,0:T(8,128)(2,1)S(1)} %get-tuple-element.13), channel_id=1, source_target_pairs={{0,16},{8,24},{16,0},{24,8},{1,17},{9,25},{17,1},{25,9},{2,18},{10... | collective-permute-start | bytes 98312 | tf_op jit(solution)/shard_map/ppermute | solution.py:231
  5.3 0.0 collective-permute-start.1
  5.3 1.2 %collective-permute-done.1 = bf16[128,128]{1,0:T(8,128)(2,1)S(1)} collective-permute-done((bf16[128,128]{1,0:T(8,128)(2,1)S(1)}, bf16[128,128]{1,0:T(8,128)(2,1)S(1)}, u32[]{:S(2)}, u32[]{:S(2)}) %collective-permute-start.1) | collective-permute-done | bytes 32800 | tf_op jit(solution)/shard_map/ppermute | solution.py:227
  6.5 1.6 %collective-permute-start.2 = (bf16[256,128]{1,0:T(8,128)(2,1)S(1)}, bf16[256,128]{1,0:T(8,128)(2,1)S(1)}, u32[]{:S(2)}, u32[]{:S(2)}) collective-permute-start(bf16[256,128]{1,0:T(8,128)(2,1)S(1)} %pad_maximum_fusion.1), channel_id=1, source_target_pairs={{0,8},{1,25},{2,10},{3,27},{4,12},{5,29},{6,14},{7,31},{8,16},{9,1... | collective-permute-start | bytes 196616 | tf_op jit(solution)/shard_map/ppermute | solution.py:232
  8.1 0.0 collective-permute-done
  8.1 4.5 %collective-permute-done.2 = bf16[256,128]{1,0:T(8,128)(2,1)S(1)} collective-permute-done((bf16[256,128]{1,0:T(8,128)(2,1)S(1)}, bf16[256,128]{1,0:T(8,128)(2,1)S(1)}, u32[]{:S(2)}, u32[]{:S(2)}) %collective-permute-start.2) | collective-permute-done | bytes 65568 | tf_op jit(solution)/shard_map/ppermute | solution.py:232
  12.6 0.1 collective-permute-start.3
  12.7 1.3 %collective-permute-done.3.near = bf16[512,128]{1,0:T(8,128)(2,1)S(1)} collective-permute-done((bf16[512,128]{1,0:T(8,128)(2,1)S(1)}, bf16[512,128]{1,0:T(8,128)(2,1)S(1)}, u32[]{:S(2)}, u32[]{:S(2)}) %collective-permute-start.3) | collective-permute-done | bytes 131104 | tf_op jit(solution)/shard_map/ppermute | solution.py:227
  14.0 1.6 %collective-permute-start.4 = (bf16[1024,128]{1,0:T(8,128)(2,1)S(1)}, bf16[1024,128]{1,0:T(8,128)(2,1)S(1)}, u32[]{:S(2)}, u32[]{:S(2)}) collective-permute-start(bf16[1024,128]{1,0:T(8,128)(2,1)S(1)} %pad_maximum_fusion), channel_id=1, source_target_pairs={{0,2},{1,5},{2,0},{3,7},{4,6},{5,1},{6,4},{7,3},{8,10},{9,13},{10,... | collective-permute-start | bytes 786440 | tf_op jit(solution)/shard_map/ppermute | solution.py:227
  15.6 1.5 %collective-permute-start.6 = (bf16[512,128]{1,0:T(8,128)(2,1)S(1)}, bf16[512,128]{1,0:T(8,128)(2,1)S(1)}, u32[]{:S(2)}, u32[]{:S(2)}) collective-permute-start(bf16[512,128]{1,0:T(8,128)(2,1)S(1)} %constant_dynamic-update-slice_fusion.own), channel_id=1, source_target_pairs={{0,6},{1,7},{2,4},{3,5},{4,2},{5,3},{6,0},{7,1},{8,14},{9,15},{10,... | collective-permute-start | bytes 393224 | tf_op jit(solution)/shard_map/ppermute | solution.py:227
  17.1 4.8 %collective-permute-done.4.got = bf16[1024,128]{1,0:T(8,128)(2,1)S(1)} collective-permute-done((bf16[1024,128]{1,0:T(8,128)(2,1)S(1)}, bf16[1024,128]{1,0:T(8,128)(2,1)S(1)}, u32[]{:S(2)}, u32[]{:S(2)}) %collective-permute-start.4) | collective-permute-done | bytes 262176 | tf_op jit(solution)/shard_map/ppermute | solution.py:227
  21.9 0.0 collective-permute-start.5
  21.9 2.4 %collective-permute-done.6.across = bf16[512,128]{1,0:T(8,128)(2,1)S(1)} collective-permute-done((bf16[512,128]{1,0:T(8,128)(2,1)S(1)}, bf16[512,128]{1,0:T(8,128)(2,1)S(1)}, u32[]{:S(2)}, u32[]{:S(2)}) %collective-permute-start.6) | collective-permute-done | bytes 131104 | tf_op jit(solution)/shard_map/ppermute | solution.py:227
  24.2 0.0 collective-permute-start.7
  24.2 1.3 %collective-permute-done.7.across_near = bf16[512,128]{1,0:T(8,128)(2,1)S(1)} collective-permute-done((bf16[512,128]{1,0:T(8,128)(2,1)S(1)}, bf16[512,128]{1,0:T(8,128)(2,1)S(1)}, u32[]{:S(2)}, u32[]{:S(2)}) %collective-permute-start.7) | collective-permute-done | bytes 131104 | tf_op jit(solution)/shard_map/ppermute | solution.py:227
  25.6 0.7 %first_chips.1 = (bf16[512,768]{1,0:T(8,128)(2,1)S(1)}, bf16[768,512]{1,0:T(8,128)(2,1)S(1)}, f32[512,512]{1,0:T(8,128)S(1)}) custom-call(bf16[512,128]{1,0:T(8,128)(2,1)S(1)} %constant_dynamic-update-slice_fusion.own, bf16[512,128]{1,0:T(8,128)(2,1)S(1)} %collective-permute-done.3.near, bf16[512,128]{1,0:T(8,128)(2,1)S(1)} %collective-permute-done.6.across, ...), custom_call_target="tpu_custom_call" | custom-call | flops 400000000 | tf_op jit(solution)/shard_map/first_chips/pallas_call | solution.py:248
  26.2 0.0 collective-permute-done.5.late_ref
  26.3 6.6 %whole_block.1 = bf16[768,1024]{1,0:T(8,128)(2,1)} custom-call(bf16[1024,128]{1,0:T(8,128)(2,1)S(1)} %collective-permute-done.5.late_ref, bf16[512,768]{1,0:T(8,128)(2,1)S(1)} %get-tuple-element.16.x, bf16[768,512]{1,0:T(8,128)(2,1)S(1)} %get-tuple-element.17.xt, f32[512,512]{1,0:T(8,128)S(1)} %get-tuple-element.18.gram_in, bf16[768,1024]{1,0:T(8,128)(2,1)} %bitcast.4), custom_call_target="tpu_custom_call" | custom-call | flops 5000000000 | tf_op jit(solution)/shard_map/whole_block/pallas_call | solution.py:257
  (5 shorter events, 0.0 us)
Async XLA Ops:
  0.0 0.9 %copy-start = (bf16[128,4,128]{2,1,0:T(4,128)(2,1)S(1)}, bf16[128,4,128]{2,1,0:T(4,128)(2,1)}, u32[]{:S(2)}) copy-start(bf16[128,4,128]{2,1,0:T(4,128)(2,1)} %param.2) | copy-start | bytes 393220
  1.2 6.9 %collective-permute-start = (bf16[128,128]{1,0:T(8,128)(2,1)S(1)}, bf16[128,128]{1,0:T(8,128)(2,1)S(1)}, u32[]{:S(2)}, u32[]{:S(2)}) collective-permute-start(bf16[128,128]{1,0:T(8,128)(2,1)S(1)} %get-tuple-element.13), channel_id=1, source_target_pairs={{0,16},{8,24},{16,0},{24,8},{1,17},{9,25},{17,1},{25,9},{2,18},{10... | collective-permute-start | bytes 98312 | tf_op jit(solution)/shard_map/ppermute | solution.py:231
  5.3 1.2 %collective-permute-start.1 = (bf16[128,128]{1,0:T(8,128)(2,1)S(1)}, bf16[128,128]{1,0:T(8,128)(2,1)S(1)}, u32[]{:S(2)}, u32[]{:S(2)}) collective-permute-start(bf16[128,128]{1,0:T(8,128)(2,1)S(1)} %get-tuple-element.15), channel_id=1, source_target_pairs={{0,1},{1,0},{2,3},{3,2},{4,5},{5,4},{6,7},{7,6},{8,9},{9,8},{10,11... | collective-permute-start | bytes 98312 | tf_op jit(solution)/shard_map/ppermute | solution.py:227
  6.5 6.1 %collective-permute-start.2 = (bf16[256,128]{1,0:T(8,128)(2,1)S(1)}, bf16[256,128]{1,0:T(8,128)(2,1)S(1)}, u32[]{:S(2)}, u32[]{:S(2)}) collective-permute-start(bf16[256,128]{1,0:T(8,128)(2,1)S(1)} %pad_maximum_fusion.1), channel_id=1, source_target_pairs={{0,8},{1,25},{2,10},{3,27},{4,12},{5,29},{6,14},{7,31},{8,16},{9,1... | collective-permute-start | bytes 196616 | tf_op jit(solution)/shard_map/ppermute | solution.py:232
  12.6 1.4 %collective-permute-start.3 = (bf16[512,128]{1,0:T(8,128)(2,1)S(1)}, bf16[512,128]{1,0:T(8,128)(2,1)S(1)}, u32[]{:S(2)}, u32[]{:S(2)}) collective-permute-start(bf16[512,128]{1,0:T(8,128)(2,1)S(1)} %constant_dynamic-update-slice_fusion.own), channel_id=1, source_target_pairs={{0,1},{1,0},{2,3},{3,2},{4,5},{5,4},{6,7},{7,6},{8,9},{9,8},{10,11... | collective-permute-start | bytes 393224 | tf_op jit(solution)/shard_map/ppermute | solution.py:227
  14.0 7.8 %collective-permute-start.4 = (bf16[1024,128]{1,0:T(8,128)(2,1)S(1)}, bf16[1024,128]{1,0:T(8,128)(2,1)S(1)}, u32[]{:S(2)}, u32[]{:S(2)}) collective-permute-start(bf16[1024,128]{1,0:T(8,128)(2,1)S(1)} %pad_maximum_fusion), channel_id=1, source_target_pairs={{0,2},{1,5},{2,0},{3,7},{4,6},{5,1},{6,4},{7,3},{8,10},{9,13},{10,... | collective-permute-start | bytes 786440 | tf_op jit(solution)/shard_map/ppermute | solution.py:227
  15.6 8.6 %collective-permute-start.6 = (bf16[512,128]{1,0:T(8,128)(2,1)S(1)}, bf16[512,128]{1,0:T(8,128)(2,1)S(1)}, u32[]{:S(2)}, u32[]{:S(2)}) collective-permute-start(bf16[512,128]{1,0:T(8,128)(2,1)S(1)} %constant_dynamic-update-slice_fusion.own), channel_id=1, source_target_pairs={{0,6},{1,7},{2,4},{3,5},{4,2},{5,3},{6,0},{7,1},{8,14},{9,15},{10,... | collective-permute-start | bytes 393224 | tf_op jit(solution)/shard_map/ppermute | solution.py:227
  21.9 4.4 %collective-permute-start.5 = (bf16[1024,128]{1,0:T(8,128)(2,1)S(1)}, bf16[1024,128]{1,0:T(8,128)(2,1)S(1)}, u32[]{:S(2)}, u32[]{:S(2)}) collective-permute-start(bf16[1024,128]{1,0:T(8,128)(2,1)S(1)} %collective-permute-done.4.got), channel_id=1, source_target_pairs={{0,1},{1,0},{2,3},{3,2},{4,5},{5,4},{6,7},{7,6},{8,9},{9,8},{10,11... | collective-permute-start | bytes 786440 | tf_op jit(solution)/shard_map/ppermute | solution.py:227
  24.2 1.3 %collective-permute-start.7 = (bf16[512,128]{1,0:T(8,128)(2,1)S(1)}, bf16[512,128]{1,0:T(8,128)(2,1)S(1)}, u32[]{:S(2)}, u32[]{:S(2)}) collective-permute-start(bf16[512,128]{1,0:T(8,128)(2,1)S(1)} %collective-permute-done.6.across), channel_id=1, source_target_pairs={{0,1},{1,0},{2,3},{3,2},{4,5},{5,4},{6,7},{7,6},{8,9},{9,8},{10,11... | collective-permute-start | bytes 393224 | tf_op jit(solution)/shard_map/ppermute | solution.py:227

commit v12 on v11

--- a/solution.py
+++ b/solution.py
@@ -38,11 +38,9 @@
     return result
 
 
-def split_kernel(x_ref, *out_refs):
+def split_kernel(fars, x_ref, *out_refs):
     replicas, tokens = len(out_refs), out_refs[0].shape[0]
     here = lax.axis_index("dp")
-    core = lax.rem(lax.axis_index("grad"), 2)
-    fars = (0, 2, 1 + 2 * core, 3 - 2 * core)
     x = x_ref[...]
     rows = lax.broadcasted_iota(jnp.int32, (tokens, tokens * replicas), 0)
     cols = lax.broadcasted_iota(jnp.int32, (tokens, tokens * replicas), 1)
@@ -52,10 +50,10 @@
         out_ref[...] = dot(choice, x).astype(jnp.bfloat16)
 
 
-def split_blocks(factor_inputs):
+def split_blocks(factor_inputs, fars):
     tokens, blocks, features = factor_inputs.shape
     return pl.pallas_call(
-        split_kernel,
+        functools.partial(split_kernel, fars),
         out_shape=[jax.ShapeDtypeStruct((tokens, features), factor_inputs.dtype)] * blocks,
         in_specs=[WHOLE],
         out_specs=[WHOLE] * blocks,
@@ -64,47 +62,35 @@
     )(factor_inputs.reshape(tokens * blocks, features))
 
 
-def columns_of(same, other):
-    tokens = same.shape[0]
-    q0, q1, q2, q3 = [slice(at, at + tokens // 4) for at in range(0, tokens, tokens // 4)]
-    mine = jnp.concatenate([same[q0, :], same[q1, :], same[q2, :], other[q3, :]], axis=0)
-    its = jnp.concatenate([other[q0, :], other[q1, :], same[q3, :], other[q2, :]], axis=0)
-    return jnp.concatenate([mine, its], axis=1)
-
-
-def first_kernel(own, near, across, across_near, got, columns, turned, gram):
-    tokens = own.shape[0]
-    pairs = [(own, near), (across, across_near), (got.at[:tokens], got.at[tokens:])]
-    wide = 2 * own.shape[1]
-    for n, (same, other) in enumerate(pairs):
-        some = slice(n * wide, (n + 1) * wide)
-        value = columns_of(same, other)
-        columns[:, some] = value
-        turned[some, :] = value.T
+def first_kernel(*refs):
+    *pieces, columns, turned, gram = refs
+    features = pieces[0].shape[1]
+    for n, piece in enumerate(pieces):
+        some = slice(n * features, (n + 1) * features)
+        columns[:, some] = piece[...]
+        turned[some, :] = piece[...].T
     gram[...] = dot(columns[...], turned[...])
 
 
-def last_kernel(late_ref, x, xt, gram_in, tile_hbm, out_hbm, *refs):
+def last_kernel(fars, late0, late1, x, xt, gram_in, tile_hbm, out_hbm, *refs):
     tile, out, late, late_t, k1, k2, e2, g, z, h, a, k, q, image, mixed, sems = refs
     load = pltpu.make_async_copy(tile_hbm, tile, sems.at[0])
     load.start()
     member = lax.axis_index("grad")
-    core = lax.rem(member, 2)
     tokens = x.shape[0]
     half = late.shape[1]
     features = half // 2
     halves = [slice(at, at + half) for at in range(0, tokens, half)]
     blocks = [slice(at, at + half) for at in range(0, x.shape[1], half)]
     chunks = [slice(at, at + 32) for at in range(0, tokens, 32)]
-    fars = [0, 6, 2 + 2 * core, 4 - 2 * core]
 
     def place(far):
         return pl.ds(pl.multiple_of((member ^ far) * features, features), features)
 
     def chosen(some):
-        return jnp.concatenate([tile[:, place(far ^ one)] for far in some for one in (0, 1)], axis=1)
-
-    late[...] = columns_of(late_ref.at[tokens:], late_ref.at[:tokens])
+        return jnp.concatenate([tile[:, place(far)] for far in some], axis=1)
+
+    late[...] = jnp.concatenate([late0[...], late1[...]], axis=1)
     late_t[...] = late[...].T
 
     def symmetric(left, right, finish, *refs):
@@ -133,7 +119,7 @@
             row_sums[i] = row_sums[i] + column[some, :features] + column[some, features:]
 
     def move(some):
-        moved = dot(chosen(fars[:-1]), xt[:, some]) + dot(chosen(fars[-1:]), late_t[:, some])
+        moved = dot(chosen(fars[:-2]), xt[:, some]) + dot(chosen(fars[-2:]), late_t[:, some])
         image[:, some] = moved.astype(jnp.bfloat16)
 
     for n, some in enumerate(blocks):
@@ -198,10 +184,10 @@
         product = dot(image[...], q[:, some])
         mixed[:, some] = (product + q_m * image[:, some].astype(jnp.float32)).astype(jnp.bfloat16)
     stores = []
-    for n, far in enumerate(fars):
+    for n in range(len(blocks) + 1):
         moved = dot(mixed[...], late[...] if n == len(blocks) else x[:, blocks[n]])
         for one in (0, 1):
-            here = place(far ^ one)
+            here = place(fars[2 * n + one])
             kept = p * tile[:, here].astype(jnp.float32)
             out[:, here] = (kept + moved[:, one * features : (one + 1) * features]).astype(jnp.bfloat16)
             store = pltpu.make_async_copy(out.at[:, here], out_hbm.at[:, here], sems.at[1 + len(stores)])
@@ -223,41 +209,35 @@
     def scratch(*sizes):
         return pltpu.VMEM(sizes, jnp.bfloat16)
 
-    def swap(value, *fars):
-        return lax.ppermute(value, "grad", [(i, i ^ fars[i % len(fars)]) for i in range(members)])
-
-    part, part_across, mine, given = split_blocks(factor_inputs)
-    both = jnp.concatenate([mine, swap(given, 1)], axis=0)
-    across = lax.ppermute(part_across, "dp", [(i, (i + 2) % replicas) for i in range(replicas)])
-    along = lax.ppermute(
-        both,
-        ("dp", "grad"),
-        [
-            (i * members + j, (i + (3 if j % 2 else 1)) % replicas * members + j)
-            for i in range(replicas)
-            for j in range(members)
-        ],
-    )
-    own = jnp.concatenate([part, across, along], axis=0)
-    near = swap(own, 1)
-    diagonal = swap(own, 6)
-    got = swap(jnp.concatenate([own, near], axis=0), 2, 4)
-    diagonal_near = swap(diagonal, 1)
-    late = swap(got, 1)
+    def swap(value, far):
+        return lax.ppermute(value, "grad", [(i, i ^ far) for i in range(members)])
+
+    order = (0, 2, 1, 3)
+    parts = dict(zip(order, split_blocks(factor_inputs, order)))
+    for far in order[1:]:
+        parts[far] = lax.ppermute(parts[far], "dp", [(i, (i + far) % replicas) for i in range(replicas)])
+    own = jnp.concatenate([parts[far] for far in order], axis=0)
+    fars = (0, 1, 6, 7, 4, 2, 5, 3)
+    pieces = {0: own}
+    for far in (2, 4, 6):
+        pieces[far] = swap(own, far)
+    for far in (0, 2, 4, 6):
+        pieces[far + 1] = swap(pieces[far], 1)
+    pieces = [pieces[far] for far in fars]
     early = width - 2 * features
     columns, turned, gram = pl.pallas_call(
         first_kernel,
         out_shape=[shape(tokens, early), shape(early, tokens), shape(tokens, tokens, kind=jnp.float32)],
-        in_specs=[WHOLE] * 5,
+        in_specs=[WHOLE] * 6,
         out_specs=[WHOLE] * 3,
         compiler_params=pltpu.CompilerParams(vmem_limit_bytes=16 * 2**20),
         cost_estimate=pl.CostEstimate(flops=4 * 10**8, bytes_accessed=0, transcendentals=0),
-        name="first_chips",
-    )(own, near, diagonal, diagonal_near, got)
+        name="first_pieces",
+    )(*pieces[:6])
     return pl.pallas_call(
-        last_kernel,
+        functools.partial(last_kernel, fars),
         out_shape=shape(rows, width),
-        in_specs=[WHOLE] * 4 + [ANYWHERE],
+        in_specs=[WHOLE] * 5 + [ANYWHERE],
         out_specs=ANYWHERE,
         scratch_shapes=[scratch(rows, width)] * 2
         + [scratch(tokens, 2 * features), scratch(2 * features, tokens)]
@@ -267,7 +247,7 @@
         compiler_params=pltpu.CompilerParams(vmem_limit_bytes=51 * 2**20),
         cost_estimate=pl.CostEstimate(flops=5 * 10**9, bytes_accessed=0, transcendentals=0),
         name="whole_block",
-    )(late, columns, turned, gram, tile)
+    )(*pieces[6:], columns, turned, gram, tile)
 
 
 def local(factor_inputs, gradients):

time: 33 us -> 27.2 us (0.82)
  waiting for transfers between devices: 15.5 us -> 7.09 us
  starting transfers between devices: 8.8 us -> 11.5 us
    ppermute x8 -> x10, waiting for transfers between devices: 15.5 us -> 7.09 us  [the longest x7 5.1 us: swap(): return lax.ppermute(value, 'grad', [(i, i ^ far) for i in range(members)])]
    ppermute x8 -> x10, starting transfers between devices: 8.8 us -> 11.5 us  [the longest x3 7.93 us: by_tokens(): lax.ppermute(parts[far], 'dp', [(i, (i + far) % replicas) for i in range(...]
    unnamed x4 -> x5, local copies, waits for them, and re-layouts: 0.92 us -> 0.92 us
  transfers between devices with their start and end apart: 8 -> 10, of which waited for: 6 -> 6; matrix products, arithmetic and copies ran while one was open for 0% -> 0% of each run, Pallas kernels for 2% -> 2%
where the time goes in v12:
time: 27.2 us; the launch traced here: 27.1 us
  starting transfers between devices  11.5 us (42%)
  Pallas kernels  7.51 us (28%)
  waiting for transfers between devices  7.09 us (26%)
  local copies, waits for them, and re-layouts  0.93 us (3%)
    ppermute x3, starting transfers between devices, by_tokens(): lax.ppermute(parts[far], 'dp', [(i, (i + far) % replicas) for i in range(...  7.93 us
    pallas_call x1, Pallas kernels, by_tokens(): pl.pallas_call(functools.partial(last_kernel, fars), out_shape=shape(rows...  6.55 us
    ppermute x7, waiting for transfers between devices, swap(): return lax.ppermute(value, 'grad', [(i, i ^ far) for i in range(members)])  5.1 us
    ppermute x7, starting transfers between devices, swap(): return lax.ppermute(value, 'grad', [(i, i ^ far) for i in range(members)])  3.59 us
    ppermute x3, waiting for transfers between devices, by_tokens(): lax.ppermute(parts[far], 'dp', [(i, (i + far) % replicas) for i in range(...  1.99 us
    unnamed x5, local copies, waits for them, and re-layouts  0.92 us
    pallas_call x1, Pallas kernels, by_tokens(): pl.pallas_call(first_kernel, out_shape=[shape(tokens, early), shape(early...  0.67 us
  transfers between devices with their start and end apart: 10, of which 6 were waited for; matrix products, arithmetic and copies ran while one was open for 0% of the time, Pallas kernels for 2%

profile of v12, /device:TPU:0, one launch (start us, length us, event | category | flops | bytes accessed | tf_op | source)
XLA Modules:
  0.0 27.1 jit_solution(13694800618248491103)
XLA Ops:
  0.0 0.0 copy-start
  0.0 0.9 %copy-done = bf16[128,4,128]{2,1,0:T(4,128)(2,1)S(1)} copy-done((bf16[128,4,128]{2,1,0:T(4,128)(2,1)S(1)}, bf16[128,4,128]{2,1,0:T(4,128)(2,1)}, u32[]{:S(2)}) %copy-start) | copy-done | bytes 131096
  0.9 0.3 %split_blocks.1 = (bf16[128,128]{1,0:T(8,128)(2,1)S(1)}, bf16[128,128]{1,0:T(8,128)(2,1)S(1)}, bf16[128,128]{1,0:T(8,128)(2,1)S(1)}, bf16[128,128]{1,0:T(8,128)(2,1)S(1)}) custom-call(bf16[512,128]{1,0:T(8,128)(2,1)S(1)} %bitcast.3), custom_call_target="tpu_custom_call" | custom-call | tf_op jit(solution)/shard_map/split_blocks/pallas_call | solution.py:55
  1.2 4.1 %collective-permute-start = (bf16[128,128]{1,0:T(8,128)(2,1)S(1)}, bf16[128,128]{1,0:T(8,128)(2,1)S(1)}, u32[]{:S(2)}, u32[]{:S(2)}) collective-permute-start(bf16[128,128]{1,0:T(8,128)(2,1)S(1)} %get-tuple-element.13), channel_id=1, source_target_pairs={{0,16},{8,24},{16,0},{24,8},{1,17},{9,25},{17,1},{25,9},{2,18},{10... | collective-permute-start | bytes 98312 | tf_op jit(solution)/shard_map/ppermute | solution.py:218
  5.3 1.6 %collective-permute-start.1 = (bf16[128,128]{1,0:T(8,128)(2,1)S(1)}, bf16[128,128]{1,0:T(8,128)(2,1)S(1)}, u32[]{:S(2)}, u32[]{:S(2)}) collective-permute-start(bf16[128,128]{1,0:T(8,128)(2,1)S(1)} %get-tuple-element.14), channel_id=1, source_target_pairs={{0,8},{8,16},{16,24},{24,0},{1,9},{9,17},{17,25},{25,1},{2,10},{10... | collective-permute-start | bytes 98312 | tf_op jit(solution)/shard_map/ppermute | solution.py:218
  6.9 2.2 %collective-permute-start.2 = (bf16[128,128]{1,0:T(8,128)(2,1)S(1)}, bf16[128,128]{1,0:T(8,128)(2,1)S(1)}, u32[]{:S(2)}, u32[]{:S(2)}) collective-permute-start(bf16[128,128]{1,0:T(8,128)(2,1)S(1)} %get-tuple-element.15), channel_id=1, source_target_pairs={{0,24},{8,0},{16,8},{24,16},{1,25},{9,1},{17,9},{25,17},{2,26},{10... | collective-permute-start | bytes 98312 | tf_op jit(solution)/shard_map/ppermute | solution.py:218
  9.1 0.0 collective-permute-done
  9.1 2.0 %collective-permute-done.1 = bf16[128,128]{1,0:T(8,128)(2,1)S(1)} collective-permute-done((bf16[128,128]{1,0:T(8,128)(2,1)S(1)}, bf16[128,128]{1,0:T(8,128)(2,1)S(1)}, u32[]{:S(2)}, u32[]{:S(2)}) %collective-permute-start.1) | collective-permute-done | bytes 32800 | tf_op jit(solution)/shard_map/ppermute | solution.py:218
  11.1 0.0 collective-permute-done.2
  11.2 2.5 %collective-permute-start.8 = (bf16[512,128]{1,0:T(8,128)(2,1)S(1)}, bf16[512,128]{1,0:T(8,128)(2,1)S(1)}, u32[]{:S(2)}, u32[]{:S(2)}) collective-permute-start(bf16[512,128]{1,0:T(8,128)(2,1)S(1)} %constant_dynamic-update-slice_fusion.refs_0_), channel_id=1, source_target_pairs={{0,6},{1,7},{2,4},{3,5},{4,2},{5,3},{6,0},{7,1},{8,14},{9,15},{10,... | collective-permute-start | bytes 393224 | tf_op jit(solution)/shard_map/ppermute | solution.py:213
  13.7 0.5 %collective-permute-start.5 = (bf16[512,128]{1,0:T(8,128)(2,1)S(1)}, bf16[512,128]{1,0:T(8,128)(2,1)S(1)}, u32[]{:S(2)}, u32[]{:S(2)}) collective-permute-start(bf16[512,128]{1,0:T(8,128)(2,1)S(1)} %constant_dynamic-update-slice_fusion.refs_0_), channel_id=1, source_target_pairs={{0,2},{1,3},{2,0},{3,1},{4,6},{5,7},{6,4},{7,5},{8,10},{9,11},{10,... | collective-permute-start | bytes 393224 | tf_op jit(solution)/shard_map/ppermute | solution.py:213
  14.2 0.5 %collective-permute-start.3 = (bf16[512,128]{1,0:T(8,128)(2,1)S(1)}, bf16[512,128]{1,0:T(8,128)(2,1)S(1)}, u32[]{:S(2)}, u32[]{:S(2)}) collective-permute-start(bf16[512,128]{1,0:T(8,128)(2,1)S(1)} %constant_dynamic-update-slice_fusion.refs_0_), channel_id=1, source_target_pairs={{0,4},{1,5},{2,6},{3,7},{4,0},{5,1},{6,2},{7,3},{8,12},{9,13},{10,... | collective-permute-start | bytes 393224 | tf_op jit(solution)/shard_map/ppermute | solution.py:213
  14.7 0.0 collective-permute-start.7
  14.7 2.6 %collective-permute-done.8.refs_2_ = bf16[512,128]{1,0:T(8,128)(2,1)S(1)} collective-permute-done((bf16[512,128]{1,0:T(8,128)(2,1)S(1)}, bf16[512,128]{1,0:T(8,128)(2,1)S(1)}, u32[]{:S(2)}, u32[]{:S(2)}) %collective-permute-start.8) | collective-permute-done | bytes 131104 | tf_op jit(solution)/shard_map/ppermute | solution.py:213
  17.3 0.0 collective-permute-start.9
  17.3 1.3 %collective-permute-done.5.refs_5_ = bf16[512,128]{1,0:T(8,128)(2,1)S(1)} collective-permute-done((bf16[512,128]{1,0:T(8,128)(2,1)S(1)}, bf16[512,128]{1,0:T(8,128)(2,1)S(1)}, u32[]{:S(2)}, u32[]{:S(2)}) %collective-permute-start.5) | collective-permute-done | bytes 131104 | tf_op jit(solution)/shard_map/ppermute | solution.py:213
  18.7 0.0 collective-permute-start.6
  18.7 0.5 %collective-permute-done.3.refs_4_ = bf16[512,128]{1,0:T(8,128)(2,1)S(1)} collective-permute-done((bf16[512,128]{1,0:T(8,128)(2,1)S(1)}, bf16[512,128]{1,0:T(8,128)(2,1)S(1)}, u32[]{:S(2)}, u32[]{:S(2)}) %collective-permute-start.3) | collective-permute-done | bytes 131104 | tf_op jit(solution)/shard_map/ppermute | solution.py:213
  19.2 0.0 collective-permute-start.4
  19.2 0.0 collective-permute-done.7.refs_1_
  19.2 0.0 collective-permute-done.9.refs_3_
  19.2 0.7 %first_pieces.1 = (bf16[512,768]{1,0:T(8,128)(2,1)S(1)}, bf16[768,512]{1,0:T(8,128)(2,1)S(1)}, f32[512,512]{1,0:T(8,128)S(1)}) custom-call(bf16[512,128]{1,0:T(8,128)(2,1)S(1)} %constant_dynamic-update-slice_fusion.refs_0_, bf16[512,128]{1,0:T(8,128)(2,1)S(1)} %collective-permute-done.7.refs_1_, bf16[512,128]{1,0:T(8,128)(2,1)S(1)} %collective-permute-done.8.refs_2_, ...), custom_call_target="tpu_custom_call" | custom-call | flops 400000000 | tf_op jit(solution)/shard_map/first_pieces/pallas_call | solution.py:228
  19.9 0.2 collective-permute-done.6.late1
  20.0 0.5 %collective-permute-done.4.late0 = bf16[512,128]{1,0:T(8,128)(2,1)S(1)} collective-permute-done((bf16[512,128]{1,0:T(8,128)(2,1)S(1)}, bf16[512,128]{1,0:T(8,128)(2,1)S(1)}, u32[]{:S(2)}, u32[]{:S(2)}) %collective-permute-start.4) | collective-permute-done | bytes 131104 | tf_op jit(solution)/shard_map/ppermute | solution.py:213
  20.5 6.6 %whole_block.1 = bf16[768,1024]{1,0:T(8,128)(2,1)} custom-call(bf16[512,128]{1,0:T(8,128)(2,1)S(1)} %collective-permute-done.4.late0, bf16[512,128]{1,0:T(8,128)(2,1)S(1)} %collective-permute-done.6.late1, bf16[512,768]{1,0:T(8,128)(2,1)S(1)} %get-tuple-element.16.x, bf16[768,512]{1,0:T(8,128)(2,1)S(1)} %get-tuple-element.17.xt, ...), custom_call_target="tpu_custom_call" | custom-call | flops 5000000000 | tf_op jit(solution)/shard_map/whole_block/pallas_call | solution.py:237
  (4 shorter events, 0.0 us)
Async XLA Ops:
  0.0 0.9 %copy-start = (bf16[128,4,128]{2,1,0:T(4,128)(2,1)S(1)}, bf16[128,4,128]{2,1,0:T(4,128)(2,1)}, u32[]{:S(2)}) copy-start(bf16[128,4,128]{2,1,0:T(4,128)(2,1)} %param.2) | copy-start | bytes 393220
  1.2 7.9 %collective-permute-start = (bf16[128,128]{1,0:T(8,128)(2,1)S(1)}, bf16[128,128]{1,0:T(8,128)(2,1)S(1)}, u32[]{:S(2)}, u32[]{:S(2)}) collective-permute-start(bf16[128,128]{1,0:T(8,128)(2,1)S(1)} %get-tuple-element.13), channel_id=1, source_target_pairs={{0,16},{8,24},{16,0},{24,8},{1,17},{9,25},{17,1},{25,9},{2,18},{10... | collective-permute-start | bytes 98312 | tf_op jit(solution)/shard_map/ppermute | solution.py:218
  5.3 5.8 %collective-permute-start.1 = (bf16[128,128]{1,0:T(8,128)(2,1)S(1)}, bf16[128,128]{1,0:T(8,128)(2,1)S(1)}, u32[]{:S(2)}, u32[]{:S(2)}) collective-permute-start(bf16[128,128]{1,0:T(8,128)(2,1)S(1)} %get-tuple-element.14), channel_id=1, source_target_pairs={{0,8},{8,16},{16,24},{24,0},{1,9},{9,17},{17,25},{25,1},{2,10},{10... | collective-permute-start | bytes 98312 | tf_op jit(solution)/shard_map/ppermute | solution.py:218
  6.9 4.3 %collective-permute-start.2 = (bf16[128,128]{1,0:T(8,128)(2,1)S(1)}, bf16[128,128]{1,0:T(8,128)(2,1)S(1)}, u32[]{:S(2)}, u32[]{:S(2)}) collective-permute-start(bf16[128,128]{1,0:T(8,128)(2,1)S(1)} %get-tuple-element.15), channel_id=1, source_target_pairs={{0,24},{8,0},{16,8},{24,16},{1,25},{9,1},{17,9},{25,17},{2,26},{10... | collective-permute-start | bytes 98312 | tf_op jit(solution)/shard_map/ppermute | solution.py:218
  11.2 6.2 %collective-permute-start.8 = (bf16[512,128]{1,0:T(8,128)(2,1)S(1)}, bf16[512,128]{1,0:T(8,128)(2,1)S(1)}, u32[]{:S(2)}, u32[]{:S(2)}) collective-permute-start(bf16[512,128]{1,0:T(8,128)(2,1)S(1)} %constant_dynamic-update-slice_fusion.refs_0_), channel_id=1, source_target_pairs={{0,6},{1,7},{2,4},{3,5},{4,2},{5,3},{6,0},{7,1},{8,14},{9,15},{10,... | collective-permute-start | bytes 393224 | tf_op jit(solution)/shard_map/ppermute | solution.py:213
  13.7 5.0 %collective-permute-start.5 = (bf16[512,128]{1,0:T(8,128)(2,1)S(1)}, bf16[512,128]{1,0:T(8,128)(2,1)S(1)}, u32[]{:S(2)}, u32[]{:S(2)}) collective-permute-start(bf16[512,128]{1,0:T(8,128)(2,1)S(1)} %constant_dynamic-update-slice_fusion.refs_0_), channel_id=1, source_target_pairs={{0,2},{1,3},{2,0},{3,1},{4,6},{5,7},{6,4},{7,5},{8,10},{9,11},{10,... | collective-permute-start | bytes 393224 | tf_op jit(solution)/shard_map/ppermute | solution.py:213
  14.2 5.0 %collective-permute-start.3 = (bf16[512,128]{1,0:T(8,128)(2,1)S(1)}, bf16[512,128]{1,0:T(8,128)(2,1)S(1)}, u32[]{:S(2)}, u32[]{:S(2)}) collective-permute-start(bf16[512,128]{1,0:T(8,128)(2,1)S(1)} %constant_dynamic-update-slice_fusion.refs_0_), channel_id=1, source_target_pairs={{0,4},{1,5},{2,6},{3,7},{4,0},{5,1},{6,2},{7,3},{8,12},{9,13},{10,... | collective-permute-start | bytes 393224 | tf_op jit(solution)/shard_map/ppermute | solution.py:213
  14.7 4.5 %collective-permute-start.7 = (bf16[512,128]{1,0:T(8,128)(2,1)S(1)}, bf16[512,128]{1,0:T(8,128)(2,1)S(1)}, u32[]{:S(2)}, u32[]{:S(2)}) collective-permute-start(bf16[512,128]{1,0:T(8,128)(2,1)S(1)} %constant_dynamic-update-slice_fusion.refs_0_), channel_id=1, source_target_pairs={{0,1},{1,0},{2,3},{3,2},{4,5},{5,4},{6,7},{7,6},{8,9},{9,8},{10,11... | collective-permute-start | bytes 393224 | tf_op jit(solution)/shard_map/ppermute | solution.py:213
  17.3 1.9 %collective-permute-start.9 = (bf16[512,128]{1,0:T(8,128)(2,1)S(1)}, bf16[512,128]{1,0:T(8,128)(2,1)S(1)}, u32[]{:S(2)}, u32[]{:S(2)}) collective-permute-start(bf16[512,128]{1,0:T(8,128)(2,1)S(1)} %collective-permute-done.8.refs_2_), channel_id=1, source_target_pairs={{0,1},{1,0},{2,3},{3,2},{4,5},{5,4},{6,7},{7,6},{8,9},{9,8},{10,11... | collective-permute-start | bytes 393224 | tf_op jit(solution)/shard_map/ppermute | solution.py:213
  18.7 1.3 %collective-permute-start.6 = (bf16[512,128]{1,0:T(8,128)(2,1)S(1)}, bf16[512,128]{1,0:T(8,128)(2,1)S(1)}, u32[]{:S(2)}, u32[]{:S(2)}) collective-permute-start(bf16[512,128]{1,0:T(8,128)(2,1)S(1)} %collective-permute-done.5.refs_5_), channel_id=1, source_target_pairs={{0,1},{1,0},{2,3},{3,2},{4,5},{5,4},{6,7},{7,6},{8,9},{9,8},{10,11... | collective-permute-start | bytes 393224 | tf_op jit(solution)/shard_map/ppermute | solution.py:213
  19.2 1.3 %collective-permute-start.4 = (bf16[512,128]{1,0:T(8,128)(2,1)S(1)}, bf16[512,128]{1,0:T(8,128)(2,1)S(1)}, u32[]{:S(2)}, u32[]{:S(2)}) collective-permute-start(bf16[512,128]{1,0:T(8,128)(2,1)S(1)} %collective-permute-done.3.refs_4_), channel_id=1, source_target_pairs={{0,1},{1,0},{2,3},{3,2},{4,5},{5,4},{6,7},{7,6},{8,9},{9,8},{10,11... | collective-permute-start | bytes 393224 | tf_op jit(solution)/shard_map/ppermute | solution.py:213

commit v13 on v12

--- a/solution.py
+++ b/solution.py
@@ -62,26 +62,56 @@
     )(factor_inputs.reshape(tokens * blocks, features))
 
 
-def first_kernel(*refs):
-    *pieces, columns, turned, gram = refs
+def add_sums(sums, earlier_t, columns, columns_t):
+    half = columns.shape[1]
+    mine = jnp.sum(jnp.abs(dot(columns_t, columns)), axis=0, keepdims=True)
+    sums = list(sums)
+    at = 0
+    for before in earlier_t:
+        block = jnp.abs(dot(before, columns))
+        mine = mine + jnp.sum(block, axis=0, keepdims=True)
+        for top in range(0, block.shape[0], half):
+            part = block[top : top + half]
+            part = functools.reduce(jnp.add, [part[:, side : side + 128] for side in range(0, half, 128)])
+            sums[at] = sums[at] + jnp.sum(part.T, axis=0, keepdims=True)
+            at += 1
+    return sums + [mine]
+
+
+def add_kernel(*refs):
+    *refs, columns, turned, gram, sums_out, zeros = refs
+    count = columns.shape[1] // refs[0].shape[1]
+    pieces, before = refs[:count], refs[count:]
     features = pieces[0].shape[1]
     for n, piece in enumerate(pieces):
         some = slice(n * features, (n + 1) * features)
         columns[:, some] = piece[...]
         turned[some, :] = piece[...].T
-    gram[...] = dot(columns[...], turned[...])
-
-
-def last_kernel(fars, late0, late1, x, xt, gram_in, tile_hbm, out_hbm, *refs):
+    product = dot(columns[...], turned[...])
+    sums, earlier = [], []
+    if before:
+        turned_in, gram_in, sums_in = before
+        product = product + gram_in[...]
+        sums, earlier = [sums_in[n : n + 1, :] for n in range(sums_in.shape[0])], [turned_in]
+    gram[...] = product
+    for at in range(0, columns.shape[1], 2 * features):
+        some = slice(at, at + 2 * features)
+        lefts = [ref[...] for ref in earlier] + ([turned[:at, :]] if at else [])
+        sums = add_sums(sums, lefts, columns[:, some], turned[some, :])
+    for n, value in enumerate(sums):
+        sums_out[n : n + 1, :] = value
+    zeros[...] = jnp.zeros_like(zeros)
+
+
+def last_kernel(fars, late0, late1, x0, x1, xt0, xt1, gram_in, sums_in, tile_hbm, out_hbm, *refs):
     tile, out, late, late_t, k1, k2, e2, g, z, h, a, k, q, image, mixed, sems = refs
     load = pltpu.make_async_copy(tile_hbm, tile, sems.at[0])
     load.start()
     member = lax.axis_index("grad")
-    tokens = x.shape[0]
+    tokens = x0.shape[0]
     half = late.shape[1]
     features = half // 2
     halves = [slice(at, at + half) for at in range(0, tokens, half)]
-    blocks = [slice(at, at + half) for at in range(0, x.shape[1], half)]
     chunks = [slice(at, at + 32) for at in range(0, tokens, 32)]
 
     def place(far):
@@ -110,29 +140,21 @@
 
     symmetric(gram, None, lambda product, r, some: [(gram_in[r, some] + product) * (1.0 / tokens)], k1)
 
-    column_sums, row_sums = [0.0] * (len(blocks) + 1), [0.0] * len(blocks)
-
-    def add_sums(n, left, right):
-        column = jnp.abs(dot(left, right))
-        column_sums[n] = column_sums[n] + jnp.sum(column, axis=0, keepdims=True)
-        for i, some in enumerate(blocks[: min(n, column.shape[0] // half)]):
-            row_sums[i] = row_sums[i] + column[some, :features] + column[some, features:]
-
     def move(some):
-        moved = dot(chosen(fars[:-2]), xt[:, some]) + dot(chosen(fars[-2:]), late_t[:, some])
+        moved, at = 0.0, 0
+        for ref in (xt0, xt1, late_t):
+            count = ref.shape[0] // features
+            moved = moved + dot(chosen(fars[at : at + count]), ref[:, some])
+            at += count
         image[:, some] = moved.astype(jnp.bfloat16)
 
-    for n, some in enumerate(blocks):
-        add_sums(n, xt[: some.stop, :], x[:, some])
     symmetric(k1, k1, lambda product, r, some: [product], k2)
-    add_sums(len(blocks), xt[...], late[...])
-    column_sums[-1] = column_sums[-1] + jnp.sum(jnp.abs(dot(late_t[...], late[...])), axis=0, keepdims=True)
+    sums = [sums_in[n : n + 1, :] for n in range(sums_in.shape[0])]
+    sums = add_sums(sums, [xt0[...], xt1[...]], late[...], late_t[...])
     load.wait()
     move(halves[0])
 
-    largest = column_sums[-1]
-    for column, row in zip(column_sums[:-1], row_sums):
-        largest = jnp.maximum(largest, column + jnp.sum(row.T, axis=0, keepdims=True))
+    largest = functools.reduce(jnp.maximum, sums)
     c = 1.0 / (jnp.max(largest) * (1.0 / tokens) + DAMPING)
     eps = 1.0 - c * DAMPING
     eps2 = eps * eps
@@ -184,8 +206,9 @@
         product = dot(image[...], q[:, some])
         mixed[:, some] = (product + q_m * image[:, some].astype(jnp.float32)).astype(jnp.bfloat16)
     stores = []
-    for n in range(len(blocks) + 1):
-        moved = dot(mixed[...], late[...] if n == len(blocks) else x[:, blocks[n]])
+    blocks = [ref[:, at : at + half] for ref in (x0, x1, late) for at in range(0, ref.shape[1], half)]
+    for n, block in enumerate(blocks):
+        moved = dot(mixed[...], block)
         for one in (0, 1):
             here = place(fars[2 * n + one])
             kept = p * tile[:, here].astype(jnp.float32)
@@ -212,32 +235,43 @@
     def swap(value, far):
         return lax.ppermute(value, "grad", [(i, i ^ far) for i in range(members)])
 
-    order = (0, 2, 1, 3)
-    parts = dict(zip(order, split_blocks(factor_inputs, order)))
-    for far in order[1:]:
+    parts = list(split_blocks(factor_inputs, range(replicas)))
+    for far in range(1, replicas):
         parts[far] = lax.ppermute(parts[far], "dp", [(i, (i + far) % replicas) for i in range(replicas)])
-    own = jnp.concatenate([parts[far] for far in order], axis=0)
-    fars = (0, 1, 6, 7, 4, 2, 5, 3)
-    pieces = {0: own}
-    for far in (2, 4, 6):
-        pieces[far] = swap(own, far)
-    for far in (0, 2, 4, 6):
-        pieces[far + 1] = swap(pieces[far], 1)
-    pieces = [pieces[far] for far in fars]
-    early = width - 2 * features
-    columns, turned, gram = pl.pallas_call(
-        first_kernel,
-        out_shape=[shape(tokens, early), shape(early, tokens), shape(tokens, tokens, kind=jnp.float32)],
-        in_specs=[WHOLE] * 6,
-        out_specs=[WHOLE] * 3,
-        compiler_params=pltpu.CompilerParams(vmem_limit_bytes=16 * 2**20),
-        cost_estimate=pl.CostEstimate(flops=4 * 10**8, bytes_accessed=0, transcendentals=0),
-        name="first_pieces",
-    )(*pieces[:6])
+    own = jnp.concatenate(parts, axis=0)
+    here = {0: own, 1: swap(own, 1)}
+    for far in (6, 2, 4):
+        here[far] = swap(own, far)
+    for far in (6, 2):
+        here[far + 1] = swap(here[far], 1)
+
+    def add(name, pieces, *before):
+        wide = len(pieces) * features
+        blocks = wide // (2 * features) + (before[-1].shape[0] if before else 0)
+        return pl.pallas_call(
+            add_kernel,
+            out_shape=[
+                shape(tokens, wide),
+                shape(wide, tokens),
+                shape(tokens, tokens, kind=jnp.float32),
+                shape(blocks, 2 * features, kind=jnp.float32),
+                shape(1, features),
+            ],
+            in_specs=[WHOLE] * (len(pieces) + len(before)),
+            out_specs=[WHOLE] * 5,
+            compiler_params=pltpu.CompilerParams(vmem_limit_bytes=16 * 2**20),
+            cost_estimate=pl.CostEstimate(flops=6 * 10**8, bytes_accessed=0, transcendentals=0),
+            name=name,
+        )(*pieces, *before)
+
+    fars = (0, 1, 6, 2, 7, 4, 3, 5)
+    x0, xt0, gram, sums, zeros = add("first_pieces", [here[far] for far in fars[:4]])
+    here[5] = swap(here[4] + zeros, 1)
+    x1, xt1, gram, sums, _ = add("next_pieces", [here[far] for far in fars[4:6]], xt0, gram, sums)
     return pl.pallas_call(
         functools.partial(last_kernel, fars),
         out_shape=shape(rows, width),
-        in_specs=[WHOLE] * 5 + [ANYWHERE],
+        in_specs=[WHOLE] * 8 + [ANYWHERE],
         out_specs=ANYWHERE,
         scratch_shapes=[scratch(rows, width)] * 2
         + [scratch(tokens, 2 * features), scratch(2 * features, tokens)]
@@ -247,7 +281,7 @@
         compiler_params=pltpu.CompilerParams(vmem_limit_bytes=51 * 2**20),
         cost_estimate=pl.CostEstimate(flops=5 * 10**9, bytes_accessed=0, transcendentals=0),
         name="whole_block",
-    )(*pieces[6:], columns, turned, gram, tile)
+    )(here[3], here[5], x0, x1, xt0, xt1, gram, sums, tile)
 
 
 def local(factor_inputs, gradients):

time: 27.2 us -> 27.9 us (1.026)
  Pallas kernels: 7.51 us -> 8.45 us
  starting transfers between devices: 11.5 us -> 10.6 us
  waiting for transfers between devices: 7.09 us -> 7.71 us
    pallas_call x1 -> x2, Pallas kernels: 0.67 us -> 1.89 us  [add(): pl.pallas_call(add_kernel, out_shape=[shape(tokens, wide), shape(wide, to...]
    ppermute x3, starting transfers between devices: 7.93 us -> 7.01 us  [by_tokens(): lax.ppermute(parts[far], 'dp', [(i, (i + far) % replicas) for i in range(...]
    ppermute x3, waiting for transfers between devices: 1.99 us -> 2.54 us  [by_tokens(): lax.ppermute(parts[far], 'dp', [(i, (i + far) % replicas) for i in range(...]
    pallas_call x1, Pallas kernels: 6.55 us -> 6.27 us  [by_tokens(): pl.pallas_call(functools.partial(last_kernel, fars), out_shape=shape(rows...]
  transfers between devices with their start and end apart: 10 -> 10, of which waited for: 6 -> 6; matrix products, arithmetic and copies ran while one was open for 0% -> 0% of each run, Pallas kernels for 2% -> 7%
where the time goes in v13:
time: 27.9 us; the launch traced here: 27.7 us
  starting transfers between devices  10.6 us (38%)
  Pallas kernels  8.45 us (30%)
  waiting for transfers between devices  7.71 us (28%)
  local copies, waits for them, and re-layouts  0.93 us (3%)
    ppermute x3, starting transfers between devices, by_tokens(): lax.ppermute(parts[far], 'dp', [(i, (i + far) % replicas) for i in range(...  7.01 us
    pallas_call x1, Pallas kernels, by_tokens(): pl.pallas_call(functools.partial(last_kernel, fars), out_shape=shape(rows...  6.27 us
    ppermute x7, waiting for transfers between devices, swap(): return lax.ppermute(value, 'grad', [(i, i ^ far) for i in range(members)])  5.17 us
    ppermute x7, starting transfers between devices, swap(): return lax.ppermute(value, 'grad', [(i, i ^ far) for i in range(members)])  3.57 us
    ppermute x3, waiting for transfers between devices, by_tokens(): lax.ppermute(parts[far], 'dp', [(i, (i + far) % replicas) for i in range(...  2.54 us
    pallas_call x2, Pallas kernels, add(): pl.pallas_call(add_kernel, out_shape=[shape(tokens, wide), shape(wide, to...  1.89 us
    unnamed x5, local copies, waits for them, and re-layouts  0.92 us
  transfers between devices with their start and end apart: 10, of which 6 were waited for; matrix products, arithmetic and copies ran while one was open for 0% of the time, Pallas kernels for 7%

profile of v13, /device:TPU:0, one launch (start us, length us, event | category | flops | bytes accessed | tf_op | source)
XLA Modules:
  0.0 27.7 jit_solution(1576572849032443971)
XLA Ops:
  0.0 0.0 copy-start
  0.0 0.9 %copy-done = bf16[128,4,128]{2,1,0:T(4,128)(2,1)S(1)} copy-done((bf16[128,4,128]{2,1,0:T(4,128)(2,1)S(1)}, bf16[128,4,128]{2,1,0:T(4,128)(2,1)}, u32[]{:S(2)}) %copy-start) | copy-done | bytes 131096
  0.9 0.3 %split_blocks.1 = (bf16[128,128]{1,0:T(8,128)(2,1)S(1)}, bf16[128,128]{1,0:T(8,128)(2,1)S(1)}, bf16[128,128]{1,0:T(8,128)(2,1)S(1)}, bf16[128,128]{1,0:T(8,128)(2,1)S(1)}) custom-call(bf16[512,128]{1,0:T(8,128)(2,1)S(1)} %bitcast.4), custom_call_target="tpu_custom_call" | custom-call | tf_op jit(solution)/shard_map/split_blocks/pallas_call | solution.py:55
  1.2 3.1 %collective-permute-start = (bf16[128,128]{1,0:T(8,128)(2,1)S(1)}, bf16[128,128]{1,0:T(8,128)(2,1)S(1)}, u32[]{:S(2)}, u32[]{:S(2)}) collective-permute-start(bf16[128,128]{1,0:T(8,128)(2,1)S(1)} %get-tuple-element.19), channel_id=1, source_target_pairs={{0,8},{8,16},{16,24},{24,0},{1,9},{9,17},{17,25},{25,1},{2,10},{10... | collective-permute-start | bytes 98312 | tf_op jit(solution)/shard_map/ppermute | solution.py:240
  4.3 2.6 %collective-permute-start.1 = (bf16[128,128]{1,0:T(8,128)(2,1)S(1)}, bf16[128,128]{1,0:T(8,128)(2,1)S(1)}, u32[]{:S(2)}, u32[]{:S(2)}) collective-permute-start(bf16[128,128]{1,0:T(8,128)(2,1)S(1)} %get-tuple-element.20), channel_id=1, source_target_pairs={{0,16},{8,24},{16,0},{24,8},{1,17},{9,25},{17,1},{25,9},{2,18},{10... | collective-permute-start | bytes 98312 | tf_op jit(solution)/shard_map/ppermute | solution.py:240
  6.9 1.3 %collective-permute-start.2 = (bf16[128,128]{1,0:T(8,128)(2,1)S(1)}, bf16[128,128]{1,0:T(8,128)(2,1)S(1)}, u32[]{:S(2)}, u32[]{:S(2)}) collective-permute-start(bf16[128,128]{1,0:T(8,128)(2,1)S(1)} %get-tuple-element.21), channel_id=1, source_target_pairs={{0,24},{8,0},{16,8},{24,16},{1,25},{9,1},{17,9},{25,17},{2,26},{10... | collective-permute-start | bytes 98312 | tf_op jit(solution)/shard_map/ppermute | solution.py:240
  8.2 0.0 collective-permute-done
  8.2 1.2 %collective-permute-done.1 = bf16[128,128]{1,0:T(8,128)(2,1)S(1)} collective-permute-done((bf16[128,128]{1,0:T(8,128)(2,1)S(1)}, bf16[128,128]{1,0:T(8,128)(2,1)S(1)}, u32[]{:S(2)}, u32[]{:S(2)}) %collective-permute-start.1) | collective-permute-done | bytes 32800 | tf_op jit(solution)/shard_map/ppermute | solution.py:240
  9.4 1.3 %collective-permute-done.2 = bf16[128,128]{1,0:T(8,128)(2,1)S(1)} collective-permute-done((bf16[128,128]{1,0:T(8,128)(2,1)S(1)}, bf16[128,128]{1,0:T(8,128)(2,1)S(1)}, u32[]{:S(2)}, u32[]{:S(2)}) %collective-permute-start.2) | collective-permute-done | bytes 32800 | tf_op jit(solution)/shard_map/ppermute | solution.py:240
  10.8 2.4 %collective-permute-start.7 = (bf16[512,128]{1,0:T(8,128)(2,1)S(1)}, bf16[512,128]{1,0:T(8,128)(2,1)S(1)}, u32[]{:S(2)}, u32[]{:S(2)}) collective-permute-start(bf16[512,128]{1,0:T(8,128)(2,1)S(1)} %constant_dynamic-update-slice_fusion.refs_0_), channel_id=1, source_target_pairs={{0,6},{1,7},{2,4},{3,5},{4,2},{5,3},{6,0},{7,1},{8,14},{9,15},{10,... | collective-permute-start | bytes 393224 | tf_op jit(solution)/shard_map/ppermute | solution.py:236
  13.2 0.5 %collective-permute-start.3 = (bf16[512,128]{1,0:T(8,128)(2,1)S(1)}, bf16[512,128]{1,0:T(8,128)(2,1)S(1)}, u32[]{:S(2)}, u32[]{:S(2)}) collective-permute-start(bf16[512,128]{1,0:T(8,128)(2,1)S(1)} %constant_dynamic-update-slice_fusion.refs_0_), channel_id=1, source_target_pairs={{0,2},{1,3},{2,0},{3,1},{4,6},{5,7},{6,4},{7,5},{8,10},{9,11},{10,... | collective-permute-start | bytes 393224 | tf_op jit(solution)/shard_map/ppermute | solution.py:236
  13.8 0.0 collective-permute-start.6
  13.8 0.5 %collective-permute-start.5 = (bf16[512,128]{1,0:T(8,128)(2,1)S(1)}, bf16[512,128]{1,0:T(8,128)(2,1)S(1)}, u32[]{:S(2)}, u32[]{:S(2)}) collective-permute-start(bf16[512,128]{1,0:T(8,128)(2,1)S(1)} %constant_dynamic-update-slice_fusion.refs_0_), channel_id=1, source_target_pairs={{0,4},{1,5},{2,6},{3,7},{4,0},{5,1},{6,2},{7,3},{8,12},{9,13},{10,... | collective-permute-start | bytes 393224 | tf_op jit(solution)/shard_map/ppermute | solution.py:236
  14.3 3.0 %collective-permute-done.7.refs_2_ = bf16[512,128]{1,0:T(8,128)(2,1)S(1)} collective-permute-done((bf16[512,128]{1,0:T(8,128)(2,1)S(1)}, bf16[512,128]{1,0:T(8,128)(2,1)S(1)}, u32[]{:S(2)}, u32[]{:S(2)}) %collective-permute-start.7) | collective-permute-done | bytes 131104 | tf_op jit(solution)/shard_map/ppermute | solution.py:236
  17.2 0.0 collective-permute-start.9
  17.3 1.4 %collective-permute-done.3.refs_3_ = bf16[512,128]{1,0:T(8,128)(2,1)S(1)} collective-permute-done((bf16[512,128]{1,0:T(8,128)(2,1)S(1)}, bf16[512,128]{1,0:T(8,128)(2,1)S(1)}, u32[]{:S(2)}, u32[]{:S(2)}) %collective-permute-start.3) | collective-permute-done | bytes 131104 | tf_op jit(solution)/shard_map/ppermute | solution.py:236
  18.7 0.0 collective-permute-start.4
  18.7 0.0 collective-permute-done.6.refs_1_
  18.7 0.8 %first_pieces.1 = (bf16[512,512]{1,0:T(8,128)(2,1)S(1)}, bf16[512,512]{1,0:T(8,128)(2,1)S(1)}, f32[512,512]{1,0:T(8,128)S(1)}, f32[2,256]{1,0:T(2,128)S(1)}, bf16[1,128]{1,0:T(2,128)(2,1)S(1)}) custom-call(bf16[512,128]{1,0:T(8,128)(2,1)S(1)} %constant_dynamic-update-slice_fusion.refs_0_, bf16[512,128]{1,0:T(8,128)(2,1)S(1)} %collective-permute-done.6.refs_1_, ...), custom_call_target="tpu_custom_call" | custom-call | flops 600000000 | tf_op jit(solution)/shard_map/first_pieces/pallas_call | solution.py:251
  19.5 0.5 %collective-permute-done.5.refs_1_ = bf16[512,128]{1,0:T(8,128)(2,1)S(1)} collective-permute-done((bf16[512,128]{1,0:T(8,128)(2,1)S(1)}, bf16[512,128]{1,0:T(8,128)(2,1)S(1)}, u32[]{:S(2)}, u32[]{:S(2)}) %collective-permute-start.5) | collective-permute-done | bytes 131104 | tf_op jit(solution)/shard_map/ppermute | solution.py:236
  20.0 0.1 collective-permute-start.8
  20.1 0.0 collective-permute-done.9.refs_0_
  20.1 1.1 %next_pieces.1 = (bf16[512,256]{1,0:T(8,128)(2,1)S(1)}, bf16[256,512]{1,0:T(8,128)(2,1)S(1)}, f32[512,512]{1,0:T(8,128)S(1)}, f32[3,256]{1,0:T(4,128)S(1)}, bf16[1,128]{1,0:T(2,128)(2,1)}) custom-call(bf16[512,128]{1,0:T(8,128)(2,1)S(1)} %collective-permute-done.9.refs_0_, bf16[512,128]{1,0:T(8,128)(2,1)S(1)} %collective-permute-done.5.refs_1_, ...), custom_call_target="tpu_custom_call" | custom-call | flops 600000000 | tf_op jit(solution)/shard_map/next_pieces/pallas_call | solution.py:251
  21.2 0.0 collective-permute-done.4.late0
  21.2 0.2 collective-permute-done.8.late1
  21.5 6.3 %whole_block.1 = bf16[768,1024]{1,0:T(8,128)(2,1)} custom-call(bf16[512,128]{1,0:T(8,128)(2,1)S(1)} %collective-permute-done.4.late0, bf16[512,128]{1,0:T(8,128)(2,1)S(1)} %collective-permute-done.8.late1, bf16[512,512]{1,0:T(8,128)(2,1)S(1)} %get-tuple-element.23.x0, bf16[512,256]{1,0:T(8,128)(2,1)S(1)} %get-tuple-element.27.x1, ...), custom_call_target="tpu_custom_call" | custom-call | flops 5000000000 | tf_op jit(solution)/shard_map/whole_block/pallas_call | solution.py:271
  (5 shorter events, 0.0 us)
Async XLA Ops:
  0.0 0.9 %copy-start = (bf16[128,4,128]{2,1,0:T(4,128)(2,1)S(1)}, bf16[128,4,128]{2,1,0:T(4,128)(2,1)}, u32[]{:S(2)}) copy-start(bf16[128,4,128]{2,1,0:T(4,128)(2,1)} %param.2) | copy-start | bytes 393220
  1.2 7.0 %collective-permute-start = (bf16[128,128]{1,0:T(8,128)(2,1)S(1)}, bf16[128,128]{1,0:T(8,128)(2,1)S(1)}, u32[]{:S(2)}, u32[]{:S(2)}) collective-permute-start(bf16[128,128]{1,0:T(8,128)(2,1)S(1)} %get-tuple-element.19), channel_id=1, source_target_pairs={{0,8},{8,16},{16,24},{24,0},{1,9},{9,17},{17,25},{25,1},{2,10},{10... | collective-permute-start | bytes 98312 | tf_op jit(solution)/shard_map/ppermute | solution.py:240
  4.3 5.2 %collective-permute-start.1 = (bf16[128,128]{1,0:T(8,128)(2,1)S(1)}, bf16[128,128]{1,0:T(8,128)(2,1)S(1)}, u32[]{:S(2)}, u32[]{:S(2)}) collective-permute-start(bf16[128,128]{1,0:T(8,128)(2,1)S(1)} %get-tuple-element.20), channel_id=1, source_target_pairs={{0,16},{8,24},{16,0},{24,8},{1,17},{9,25},{17,1},{25,9},{2,18},{10... | collective-permute-start | bytes 98312 | tf_op jit(solution)/shard_map/ppermute | solution.py:240
  6.9 3.9 %collective-permute-start.2 = (bf16[128,128]{1,0:T(8,128)(2,1)S(1)}, bf16[128,128]{1,0:T(8,128)(2,1)S(1)}, u32[]{:S(2)}, u32[]{:S(2)}) collective-permute-start(bf16[128,128]{1,0:T(8,128)(2,1)S(1)} %get-tuple-element.21), channel_id=1, source_target_pairs={{0,24},{8,0},{16,8},{24,16},{1,25},{9,1},{17,9},{25,17},{2,26},{10... | collective-permute-start | bytes 98312 | tf_op jit(solution)/shard_map/ppermute | solution.py:240
  10.8 6.5 %collective-permute-start.7 = (bf16[512,128]{1,0:T(8,128)(2,1)S(1)}, bf16[512,128]{1,0:T(8,128)(2,1)S(1)}, u32[]{:S(2)}, u32[]{:S(2)}) collective-permute-start(bf16[512,128]{1,0:T(8,128)(2,1)S(1)} %constant_dynamic-update-slice_fusion.refs_0_), channel_id=1, source_target_pairs={{0,6},{1,7},{2,4},{3,5},{4,2},{5,3},{6,0},{7,1},{8,14},{9,15},{10,... | collective-permute-start | bytes 393224 | tf_op jit(solution)/shard_map/ppermute | solution.py:236
  13.2 5.4 %collective-permute-start.3 = (bf16[512,128]{1,0:T(8,128)(2,1)S(1)}, bf16[512,128]{1,0:T(8,128)(2,1)S(1)}, u32[]{:S(2)}, u32[]{:S(2)}) collective-permute-start(bf16[512,128]{1,0:T(8,128)(2,1)S(1)} %constant_dynamic-update-slice_fusion.refs_0_), channel_id=1, source_target_pairs={{0,2},{1,3},{2,0},{3,1},{4,6},{5,7},{6,4},{7,5},{8,10},{9,11},{10,... | collective-permute-start | bytes 393224 | tf_op jit(solution)/shard_map/ppermute | solution.py:236
  13.8 4.9 %collective-permute-start.6 = (bf16[512,128]{1,0:T(8,128)(2,1)S(1)}, bf16[512,128]{1,0:T(8,128)(2,1)S(1)}, u32[]{:S(2)}, u32[]{:S(2)}) collective-permute-start(bf16[512,128]{1,0:T(8,128)(2,1)S(1)} %constant_dynamic-update-slice_fusion.refs_0_), channel_id=1, source_target_pairs={{0,1},{1,0},{2,3},{3,2},{4,5},{5,4},{6,7},{7,6},{8,9},{9,8},{10,11... | collective-permute-start | bytes 393224 | tf_op jit(solution)/shard_map/ppermute | solution.py:236
  13.8 6.3 %collective-permute-start.5 = (bf16[512,128]{1,0:T(8,128)(2,1)S(1)}, bf16[512,128]{1,0:T(8,128)(2,1)S(1)}, u32[]{:S(2)}, u32[]{:S(2)}) collective-permute-start(bf16[512,128]{1,0:T(8,128)(2,1)S(1)} %constant_dynamic-update-slice_fusion.refs_0_), channel_id=1, source_target_pairs={{0,4},{1,5},{2,6},{3,7},{4,0},{5,1},{6,2},{7,3},{8,12},{9,13},{10,... | collective-permute-start | bytes 393224 | tf_op jit(solution)/shard_map/ppermute | solution.py:236
  17.2 2.9 %collective-permute-start.9 = (bf16[512,128]{1,0:T(8,128)(2,1)S(1)}, bf16[512,128]{1,0:T(8,128)(2,1)S(1)}, u32[]{:S(2)}, u32[]{:S(2)}) collective-permute-start(bf16[512,128]{1,0:T(8,128)(2,1)S(1)} %collective-permute-done.7.refs_2_), channel_id=1, source_target_pairs={{0,1},{1,0},{2,3},{3,2},{4,5},{5,4},{6,7},{7,6},{8,9},{9,8},{10,11... | collective-permute-start | bytes 393224 | tf_op jit(solution)/shard_map/ppermute | solution.py:236
  18.7 2.5 %collective-permute-start.4 = (bf16[512,128]{1,0:T(8,128)(2,1)S(1)}, bf16[512,128]{1,0:T(8,128)(2,1)S(1)}, u32[]{:S(2)}, u32[]{:S(2)}) collective-permute-start(bf16[512,128]{1,0:T(8,128)(2,1)S(1)} %collective-permute-done.3.refs_3_), channel_id=1, source_target_pairs={{0,1},{1,0},{2,3},{3,2},{4,5},{5,4},{6,7},{7,6},{8,9},{9,8},{10,11... | collective-permute-start | bytes 393224 | tf_op jit(solution)/shard_map/ppermute | solution.py:236
  20.0 1.4 %collective-permute-start.8 = (bf16[512,128]{1,0:T(8,128)(2,1)S(1)}, bf16[512,128]{1,0:T(8,128)(2,1)S(1)}, u32[]{:S(2)}, u32[]{:S(2)}) collective-permute-start(bf16[512,128]{1,0:T(8,128)(2,1)S(1)} %broadcast_add_fusion), channel_id=1, source_target_pairs={{0,1},{1,0},{2,3},{3,2},{4,5},{5,4},{6,7},{7,6},{8,9},{9,8},{10,11... | collective-permute-start | bytes 393224 | tf_op jit(solution)/shard_map/ppermute | solution.py:236

commit v14 on v12

--- a/solution.py
+++ b/solution.py
@@ -9,6 +9,7 @@
 
 ITERS = 4
 DAMPING = 0.01
+LOADS = 8
 WHOLE = pl.BlockSpec(memory_space=pltpu.VMEM)
 ANYWHERE = pl.BlockSpec(memory_space=pl.ANY)
 
@@ -62,26 +63,49 @@
     )(factor_inputs.reshape(tokens * blocks, features))
 
 
-def first_kernel(*refs):
-    *pieces, columns, turned, gram = refs
+def add_sums(sums, before_t, columns, columns_t):
+    half = columns.shape[1]
+    mine = jnp.sum(jnp.abs(dot(columns_t, columns)), axis=0, keepdims=True)
+    sums = list(sums)
+    if before_t is not None:
+        block = jnp.abs(dot(before_t, columns))
+        mine = mine + jnp.sum(block, axis=0, keepdims=True)
+        for n in range(len(sums)):
+            part = block[n * half : (n + 1) * half]
+            part = functools.reduce(jnp.add, [part[:, side : side + 128] for side in range(0, half, 128)])
+            sums[n] = sums[n] + jnp.sum(part.T, axis=0, keepdims=True)
+    return sums + [mine]
+
+
+def add_kernel(*refs):
+    *pieces, columns, turned, gram, sums_out = refs
     features = pieces[0].shape[1]
     for n, piece in enumerate(pieces):
         some = slice(n * features, (n + 1) * features)
         columns[:, some] = piece[...]
         turned[some, :] = piece[...].T
     gram[...] = dot(columns[...], turned[...])
-
-
-def last_kernel(fars, late0, late1, x, xt, gram_in, tile_hbm, out_hbm, *refs):
+    sums = []
+    for at in range(0, columns.shape[1], 2 * features):
+        some = slice(at, at + 2 * features)
+        sums = add_sums(sums, turned[:at, :] if at else None, columns[:, some], turned[some, :])
+    for n, value in enumerate(sums):
+        sums_out[n : n + 1, :] = value
+
+
+def last_kernel(fars, late0, late1, x, xt, gram_in, sums_in, tile_hbm, out_hbm, *refs):
     tile, out, late, late_t, k1, k2, e2, g, z, h, a, k, q, image, mixed, sems = refs
-    load = pltpu.make_async_copy(tile_hbm, tile, sems.at[0])
-    load.start()
+    loads = []
+    step = tile.shape[0] // LOADS
+    for n in range(LOADS):
+        some = pl.ds(n * step, step)
+        loads.append(pltpu.make_async_copy(tile_hbm.at[some, :], tile.at[some, :], sems.at[n]))
+        loads[-1].start()
     member = lax.axis_index("grad")
     tokens = x.shape[0]
     half = late.shape[1]
     features = half // 2
     halves = [slice(at, at + half) for at in range(0, tokens, half)]
-    blocks = [slice(at, at + half) for at in range(0, x.shape[1], half)]
     chunks = [slice(at, at + 32) for at in range(0, tokens, 32)]
 
     def place(far):
@@ -110,29 +134,18 @@
 
     symmetric(gram, None, lambda product, r, some: [(gram_in[r, some] + product) * (1.0 / tokens)], k1)
 
-    column_sums, row_sums = [0.0] * (len(blocks) + 1), [0.0] * len(blocks)
-
-    def add_sums(n, left, right):
-        column = jnp.abs(dot(left, right))
-        column_sums[n] = column_sums[n] + jnp.sum(column, axis=0, keepdims=True)
-        for i, some in enumerate(blocks[: min(n, column.shape[0] // half)]):
-            row_sums[i] = row_sums[i] + column[some, :features] + column[some, features:]
-
     def move(some):
         moved = dot(chosen(fars[:-2]), xt[:, some]) + dot(chosen(fars[-2:]), late_t[:, some])
         image[:, some] = moved.astype(jnp.bfloat16)
 
-    for n, some in enumerate(blocks):
-        add_sums(n, xt[: some.stop, :], x[:, some])
     symmetric(k1, k1, lambda product, r, some: [product], k2)
-    add_sums(len(blocks), xt[...], late[...])
-    column_sums[-1] = column_sums[-1] + jnp.sum(jnp.abs(dot(late_t[...], late[...])), axis=0, keepdims=True)
-    load.wait()
+    sums = [sums_in[n : n + 1, :] for n in range(sums_in.shape[0])]
+    sums = add_sums(sums, xt[...], late[...], late_t[...])
+    for load in loads:
+        load.wait()
     move(halves[0])
 
-    largest = column_sums[-1]
-    for column, row in zip(column_sums[:-1], row_sums):
-        largest = jnp.maximum(largest, column + jnp.sum(row.T, axis=0, keepdims=True))
+    largest = functools.reduce(jnp.maximum, sums)
     c = 1.0 / (jnp.max(largest) * (1.0 / tokens) + DAMPING)
     eps = 1.0 - c * DAMPING
     eps2 = eps * eps
@@ -184,15 +197,20 @@
         product = dot(image[...], q[:, some])
         mixed[:, some] = (product + q_m * image[:, some].astype(jnp.float32)).astype(jnp.bfloat16)
     stores = []
-    for n in range(len(blocks) + 1):
-        moved = dot(mixed[...], late[...] if n == len(blocks) else x[:, blocks[n]])
-        for one in (0, 1):
-            here = place(fars[2 * n + one])
-            kept = p * tile[:, here].astype(jnp.float32)
-            out[:, here] = (kept + moved[:, one * features : (one + 1) * features]).astype(jnp.bfloat16)
-            store = pltpu.make_async_copy(out.at[:, here], out_hbm.at[:, here], sems.at[1 + len(stores)])
-            store.start()
-            stores.append(store)
+    blocks = [x[:, at : at + half] for at in range(0, x.shape[1], half)] + [late[...]]
+    for n, block in enumerate(blocks):
+        moved = dot(mixed[...], block)
+        parts = 3 if n == len(blocks) - 1 else 1
+        step = moved.shape[0] // parts
+        for at in range(0, parts * step, step):
+            r = slice(at, at + step)
+            for one in (0, 1):
+                here = place(fars[2 * n + one])
+                kept = p * tile[r, here].astype(jnp.float32)
+                out[r, here] = (kept + moved[r, one * features : (one + 1) * features]).astype(jnp.bfloat16)
+                store = pltpu.make_async_copy(out.at[r, here], out_hbm.at[r, here], sems.at[LOADS + len(stores)])
+                store.start()
+                stores.append(store)
     for store in stores:
         store.wait()
 
@@ -212,12 +230,11 @@
     def swap(value, far):
         return lax.ppermute(value, "grad", [(i, i ^ far) for i in range(members)])
 
-    order = (0, 2, 1, 3)
-    parts = dict(zip(order, split_blocks(factor_inputs, order)))
-    for far in order[1:]:
+    parts = list(split_blocks(factor_inputs, range(replicas)))
+    for far in range(1, replicas):
         parts[far] = lax.ppermute(parts[far], "dp", [(i, (i + far) % replicas) for i in range(replicas)])
-    own = jnp.concatenate([parts[far] for far in order], axis=0)
-    fars = (0, 1, 6, 7, 4, 2, 5, 3)
+    own = jnp.concatenate(parts, axis=0)
+    fars = (0, 1, 6, 7, 2, 4, 3, 5)
     pieces = {0: own}
     for far in (2, 4, 6):
         pieces[far] = swap(own, far)
@@ -225,29 +242,34 @@
         pieces[far + 1] = swap(pieces[far], 1)
     pieces = [pieces[far] for far in fars]
     early = width - 2 * features
-    columns, turned, gram = pl.pallas_call(
-        first_kernel,
-        out_shape=[shape(tokens, early), shape(early, tokens), shape(tokens, tokens, kind=jnp.float32)],
+    first = pl.pallas_call(
+        add_kernel,
+        out_shape=[
+            shape(tokens, early),
+            shape(early, tokens),
+            shape(tokens, tokens, kind=jnp.float32),
+            shape(early // (2 * features), 2 * features, kind=jnp.float32),
+        ],
         in_specs=[WHOLE] * 6,
-        out_specs=[WHOLE] * 3,
+        out_specs=[WHOLE] * 4,
         compiler_params=pltpu.CompilerParams(vmem_limit_bytes=16 * 2**20),
-        cost_estimate=pl.CostEstimate(flops=4 * 10**8, bytes_accessed=0, transcendentals=0),
+        cost_estimate=pl.CostEstimate(flops=8 * 10**8, bytes_accessed=0, transcendentals=0),
         name="first_pieces",
     )(*pieces[:6])
     return pl.pallas_call(
         functools.partial(last_kernel, fars),
         out_shape=shape(rows, width),
-        in_specs=[WHOLE] * 5 + [ANYWHERE],
+        in_specs=[WHOLE] * 6 + [ANYWHERE],
         out_specs=ANYWHERE,
         scratch_shapes=[scratch(rows, width)] * 2
         + [scratch(tokens, 2 * features), scratch(2 * features, tokens)]
         + [scratch(tokens, tokens)] * 9
         + [scratch(rows, tokens)] * 2
-        + [pltpu.SemaphoreType.DMA((1 + members,))],
+        + [pltpu.SemaphoreType.DMA((LOADS + members + 4,))],
         compiler_params=pltpu.CompilerParams(vmem_limit_bytes=51 * 2**20),
         cost_estimate=pl.CostEstimate(flops=5 * 10**9, bytes_accessed=0, transcendentals=0),
         name="whole_block",
-    )(*pieces[6:], columns, turned, gram, tile)
+    )(*pieces[6:], *first, tile)
 
 
 def local(factor_inputs, gradients):

time: 27.2 us -> 27.4 us (level)
  Pallas kernels: 7.51 us -> 8.27 us
  starting transfers between devices: 11.5 us -> 11 us
    ppermute x3, starting transfers between devices: 7.93 us -> 7.01 us  [by_tokens(): lax.ppermute(parts[far], 'dp', [(i, (i + far) % replicas) for i in range(...]
    ppermute x7, waiting for transfers between devices: 5.1 us -> 4.46 us  [swap(): return lax.ppermute(value, 'grad', [(i, i ^ far) for i in range(members)])]
    ppermute x3, waiting for transfers between devices: 1.99 us -> 2.54 us  [by_tokens(): lax.ppermute(parts[far], 'dp', [(i, (i + far) % replicas) for i in range(...]
    pallas_call x1, Pallas kernels: 0.67 us -> 1.11 us  [by_tokens(): pl.pallas_call(add_kernel, out_shape=[shape(tokens, early), shape(early,...]
    ppermute x7, starting transfers between devices: 3.59 us -> 4 us  [swap(): return lax.ppermute(value, 'grad', [(i, i ^ far) for i in range(members)])]
    pallas_call x1, Pallas kernels: 6.55 us -> 6.87 us  [by_tokens(): pl.pallas_call(functools.partial(last_kernel, fars), out_shape=shape(rows...]
  transfers between devices with their start and end apart: 10 -> 10, of which waited for: 6 -> 4; matrix products, arithmetic and copies ran while one was open for 0% -> 0% of each run, Pallas kernels for 2% -> 4%
where the time goes in v14:
time: 27.4 us; the launch traced here: 27.3 us
  starting transfers between devices  11 us (40%)
  Pallas kernels  8.27 us (30%)
  waiting for transfers between devices  7 us (26%)
  local copies, waits for them, and re-layouts  0.93 us (3%)
    ppermute x3, starting transfers between devices, by_tokens(): lax.ppermute(parts[far], 'dp', [(i, (i + far) % replicas) for i in range(...  7.01 us
    pallas_call x1, Pallas kernels, by_tokens(): pl.pallas_call(functools.partial(last_kernel, fars), out_shape=shape(rows...  6.87 us
    ppermute x7, waiting for transfers between devices, swap(): return lax.ppermute(value, 'grad', [(i, i ^ far) for i in range(members)])  4.46 us
    ppermute x7, starting transfers between devices, swap(): return lax.ppermute(value, 'grad', [(i, i ^ far) for i in range(members)])  4 us
    ppermute x3, waiting for transfers between devices, by_tokens(): lax.ppermute(parts[far], 'dp', [(i, (i + far) % replicas) for i in range(...  2.54 us
    pallas_call x1, Pallas kernels, by_tokens(): pl.pallas_call(add_kernel, out_shape=[shape(tokens, early), shape(early,...  1.11 us
    unnamed x5, local copies, waits for them, and re-layouts  0.92 us
  transfers between devices with their start and end apart: 10, of which 4 were waited for; matrix products, arithmetic and copies ran while one was open for 0% of the time, Pallas kernels for 4%

profile of v14, /device:TPU:0, one launch (start us, length us, event | category | flops | bytes accessed | tf_op | source)
XLA Modules:
  0.0 27.3 jit_solution(12717882279469557000)
XLA Ops:
  0.0 0.0 copy-start
  0.0 0.9 %copy-done = bf16[128,4,128]{2,1,0:T(4,128)(2,1)S(1)} copy-done((bf16[128,4,128]{2,1,0:T(4,128)(2,1)S(1)}, bf16[128,4,128]{2,1,0:T(4,128)(2,1)}, u32[]{:S(2)}) %copy-start) | copy-done | bytes 131096
  0.9 0.3 %split_blocks.1 = (bf16[128,128]{1,0:T(8,128)(2,1)S(1)}, bf16[128,128]{1,0:T(8,128)(2,1)S(1)}, bf16[128,128]{1,0:T(8,128)(2,1)S(1)}, bf16[128,128]{1,0:T(8,128)(2,1)S(1)}) custom-call(bf16[512,128]{1,0:T(8,128)(2,1)S(1)} %bitcast.3), custom_call_target="tpu_custom_call" | custom-call | tf_op jit(solution)/shard_map/split_blocks/pallas_call | solution.py:56
  1.2 3.1 %collective-permute-start = (bf16[128,128]{1,0:T(8,128)(2,1)S(1)}, bf16[128,128]{1,0:T(8,128)(2,1)S(1)}, u32[]{:S(2)}, u32[]{:S(2)}) collective-permute-start(bf16[128,128]{1,0:T(8,128)(2,1)S(1)} %get-tuple-element.14), channel_id=1, source_target_pairs={{0,8},{8,16},{16,24},{24,0},{1,9},{9,17},{17,25},{25,1},{2,10},{10... | collective-permute-start | bytes 98312 | tf_op jit(solution)/shard_map/ppermute | solution.py:235
  4.3 2.6 %collective-permute-start.1 = (bf16[128,128]{1,0:T(8,128)(2,1)S(1)}, bf16[128,128]{1,0:T(8,128)(2,1)S(1)}, u32[]{:S(2)}, u32[]{:S(2)}) collective-permute-start(bf16[128,128]{1,0:T(8,128)(2,1)S(1)} %get-tuple-element.15), channel_id=1, source_target_pairs={{0,16},{8,24},{16,0},{24,8},{1,17},{9,25},{17,1},{25,9},{2,18},{10... | collective-permute-start | bytes 98312 | tf_op jit(solution)/shard_map/ppermute | solution.py:235
  6.9 1.3 %collective-permute-start.2 = (bf16[128,128]{1,0:T(8,128)(2,1)S(1)}, bf16[128,128]{1,0:T(8,128)(2,1)S(1)}, u32[]{:S(2)}, u32[]{:S(2)}) collective-permute-start(bf16[128,128]{1,0:T(8,128)(2,1)S(1)} %get-tuple-element.16), channel_id=1, source_target_pairs={{0,24},{8,0},{16,8},{24,16},{1,25},{9,1},{17,9},{25,17},{2,26},{10... | collective-permute-start | bytes 98312 | tf_op jit(solution)/shard_map/ppermute | solution.py:235
  8.2 0.0 collective-permute-done
  8.2 1.2 %collective-permute-done.1 = bf16[128,128]{1,0:T(8,128)(2,1)S(1)} collective-permute-done((bf16[128,128]{1,0:T(8,128)(2,1)S(1)}, bf16[128,128]{1,0:T(8,128)(2,1)S(1)}, u32[]{:S(2)}, u32[]{:S(2)}) %collective-permute-start.1) | collective-permute-done | bytes 32800 | tf_op jit(solution)/shard_map/ppermute | solution.py:235
  9.4 1.3 %collective-permute-done.2 = bf16[128,128]{1,0:T(8,128)(2,1)S(1)} collective-permute-done((bf16[128,128]{1,0:T(8,128)(2,1)S(1)}, bf16[128,128]{1,0:T(8,128)(2,1)S(1)}, u32[]{:S(2)}, u32[]{:S(2)}) %collective-permute-start.2) | collective-permute-done | bytes 32800 | tf_op jit(solution)/shard_map/ppermute | solution.py:235
  10.8 2.4 %collective-permute-start.8 = (bf16[512,128]{1,0:T(8,128)(2,1)S(1)}, bf16[512,128]{1,0:T(8,128)(2,1)S(1)}, u32[]{:S(2)}, u32[]{:S(2)}) collective-permute-start(bf16[512,128]{1,0:T(8,128)(2,1)S(1)} %constant_dynamic-update-slice_fusion.refs_0_), channel_id=1, source_target_pairs={{0,6},{1,7},{2,4},{3,5},{4,2},{5,3},{6,0},{7,1},{8,14},{9,15},{10,... | collective-permute-start | bytes 393224 | tf_op jit(solution)/shard_map/ppermute | solution.py:231
  13.2 0.5 %collective-permute-start.5 = (bf16[512,128]{1,0:T(8,128)(2,1)S(1)}, bf16[512,128]{1,0:T(8,128)(2,1)S(1)}, u32[]{:S(2)}, u32[]{:S(2)}) collective-permute-start(bf16[512,128]{1,0:T(8,128)(2,1)S(1)} %constant_dynamic-update-slice_fusion.refs_0_), channel_id=1, source_target_pairs={{0,4},{1,5},{2,6},{3,7},{4,0},{5,1},{6,2},{7,3},{8,12},{9,13},{10,... | collective-permute-start | bytes 393224 | tf_op jit(solution)/shard_map/ppermute | solution.py:231
  13.7 0.5 %collective-permute-start.3 = (bf16[512,128]{1,0:T(8,128)(2,1)S(1)}, bf16[512,128]{1,0:T(8,128)(2,1)S(1)}, u32[]{:S(2)}, u32[]{:S(2)}) collective-permute-start(bf16[512,128]{1,0:T(8,128)(2,1)S(1)} %constant_dynamic-update-slice_fusion.refs_0_), channel_id=1, source_target_pairs={{0,2},{1,3},{2,0},{3,1},{4,6},{5,7},{6,4},{7,5},{8,10},{9,11},{10,... | collective-permute-start | bytes 393224 | tf_op jit(solution)/shard_map/ppermute | solution.py:231
  14.3 0.0 collective-permute-start.7
  14.3 3.6 %collective-permute-done.8.refs_2_ = bf16[512,128]{1,0:T(8,128)(2,1)S(1)} collective-permute-done((bf16[512,128]{1,0:T(8,128)(2,1)S(1)}, bf16[512,128]{1,0:T(8,128)(2,1)S(1)}, u32[]{:S(2)}, u32[]{:S(2)}) %collective-permute-start.8) | collective-permute-done | bytes 131104 | tf_op jit(solution)/shard_map/ppermute | solution.py:231
  17.9 0.0 collective-permute-start.9
  17.9 0.9 %collective-permute-done.5.refs_5_ = bf16[512,128]{1,0:T(8,128)(2,1)S(1)} collective-permute-done((bf16[512,128]{1,0:T(8,128)(2,1)S(1)}, bf16[512,128]{1,0:T(8,128)(2,1)S(1)}, u32[]{:S(2)}, u32[]{:S(2)}) %collective-permute-start.5) | collective-permute-done | bytes 131104 | tf_op jit(solution)/shard_map/ppermute | solution.py:231
  18.7 0.0 collective-permute-start.6
  18.7 0.0 collective-permute-done.3.refs_4_
  18.7 0.5 %collective-permute-start.4 = (bf16[512,128]{1,0:T(8,128)(2,1)S(1)}, bf16[512,128]{1,0:T(8,128)(2,1)S(1)}, u32[]{:S(2)}, u32[]{:S(2)}) collective-permute-start(bf16[512,128]{1,0:T(8,128)(2,1)S(1)} %collective-permute-done.3.refs_4_), channel_id=1, source_target_pairs={{0,1},{1,0},{2,3},{3,2},{4,5},{5,4},{6,7},{7,6},{8,9},{9,8},{10,11... | collective-permute-start | bytes 393224 | tf_op jit(solution)/shard_map/ppermute | solution.py:231
  19.2 0.0 collective-permute-done.7.refs_1_
  19.3 0.0 collective-permute-done.9.refs_3_
  19.3 1.1 %first_pieces.1 = (bf16[512,768]{1,0:T(8,128)(2,1)S(1)}, bf16[768,512]{1,0:T(8,128)(2,1)S(1)}, f32[512,512]{1,0:T(8,128)S(1)}, f32[3,256]{1,0:T(4,128)S(1)}) custom-call(bf16[512,128]{1,0:T(8,128)(2,1)S(1)} %constant_dynamic-update-slice_fusion.refs_0_, bf16[512,128]{1,0:T(8,128)(2,1)S(1)} %collective-permute-done.7.refs_1_, ...), custom_call_target="tpu_custom_call" | custom-call | flops 800000000 | tf_op jit(solution)/shard_map/first_pieces/pallas_call | solution.py:245
  20.4 0.0 collective-permute-done.6.late1
  20.4 0.0 collective-permute-done.4.late0
  20.4 6.9 %whole_block.1 = bf16[768,1024]{1,0:T(8,128)(2,1)} custom-call(bf16[512,128]{1,0:T(8,128)(2,1)S(1)} %collective-permute-done.4.late0, bf16[512,128]{1,0:T(8,128)(2,1)S(1)} %collective-permute-done.6.late1, bf16[512,768]{1,0:T(8,128)(2,1)S(1)} %get-tuple-element.17.x, bf16[768,512]{1,0:T(8,128)(2,1)S(1)} %get-tuple-element.18.xt, ...), custom_call_target="tpu_custom_call" | custom-call | flops 5000000000 | tf_op jit(solution)/shard_map/whole_block/pallas_call | solution.py:259
  (4 shorter events, 0.0 us)
Async XLA Ops:
  0.0 0.9 %copy-start = (bf16[128,4,128]{2,1,0:T(4,128)(2,1)S(1)}, bf16[128,4,128]{2,1,0:T(4,128)(2,1)}, u32[]{:S(2)}) copy-start(bf16[128,4,128]{2,1,0:T(4,128)(2,1)} %param.2) | copy-start | bytes 393220
  1.2 7.0 %collective-permute-start = (bf16[128,128]{1,0:T(8,128)(2,1)S(1)}, bf16[128,128]{1,0:T(8,128)(2,1)S(1)}, u32[]{:S(2)}, u32[]{:S(2)}) collective-permute-start(bf16[128,128]{1,0:T(8,128)(2,1)S(1)} %get-tuple-element.14), channel_id=1, source_target_pairs={{0,8},{8,16},{16,24},{24,0},{1,9},{9,17},{17,25},{25,1},{2,10},{10... | collective-permute-start | bytes 98312 | tf_op jit(solution)/shard_map/ppermute | solution.py:235
  4.3 5.2 %collective-permute-start.1 = (bf16[128,128]{1,0:T(8,128)(2,1)S(1)}, bf16[128,128]{1,0:T(8,128)(2,1)S(1)}, u32[]{:S(2)}, u32[]{:S(2)}) collective-permute-start(bf16[128,128]{1,0:T(8,128)(2,1)S(1)} %get-tuple-element.15), channel_id=1, source_target_pairs={{0,16},{8,24},{16,0},{24,8},{1,17},{9,25},{17,1},{25,9},{2,18},{10... | collective-permute-start | bytes 98312 | tf_op jit(solution)/shard_map/ppermute | solution.py:235
  6.9 3.9 %collective-permute-start.2 = (bf16[128,128]{1,0:T(8,128)(2,1)S(1)}, bf16[128,128]{1,0:T(8,128)(2,1)S(1)}, u32[]{:S(2)}, u32[]{:S(2)}) collective-permute-start(bf16[128,128]{1,0:T(8,128)(2,1)S(1)} %get-tuple-element.16), channel_id=1, source_target_pairs={{0,24},{8,0},{16,8},{24,16},{1,25},{9,1},{17,9},{25,17},{2,26},{10... | collective-permute-start | bytes 98312 | tf_op jit(solution)/shard_map/ppermute | solution.py:235
  10.8 7.1 %collective-permute-start.8 = (bf16[512,128]{1,0:T(8,128)(2,1)S(1)}, bf16[512,128]{1,0:T(8,128)(2,1)S(1)}, u32[]{:S(2)}, u32[]{:S(2)}) collective-permute-start(bf16[512,128]{1,0:T(8,128)(2,1)S(1)} %constant_dynamic-update-slice_fusion.refs_0_), channel_id=1, source_target_pairs={{0,6},{1,7},{2,4},{3,5},{4,2},{5,3},{6,0},{7,1},{8,14},{9,15},{10,... | collective-permute-start | bytes 393224 | tf_op jit(solution)/shard_map/ppermute | solution.py:231
  13.2 5.5 %collective-permute-start.5 = (bf16[512,128]{1,0:T(8,128)(2,1)S(1)}, bf16[512,128]{1,0:T(8,128)(2,1)S(1)}, u32[]{:S(2)}, u32[]{:S(2)}) collective-permute-start(bf16[512,128]{1,0:T(8,128)(2,1)S(1)} %constant_dynamic-update-slice_fusion.refs_0_), channel_id=1, source_target_pairs={{0,4},{1,5},{2,6},{3,7},{4,0},{5,1},{6,2},{7,3},{8,12},{9,13},{10,... | collective-permute-start | bytes 393224 | tf_op jit(solution)/shard_map/ppermute | solution.py:231
  13.7 5.0 %collective-permute-start.3 = (bf16[512,128]{1,0:T(8,128)(2,1)S(1)}, bf16[512,128]{1,0:T(8,128)(2,1)S(1)}, u32[]{:S(2)}, u32[]{:S(2)}) collective-permute-start(bf16[512,128]{1,0:T(8,128)(2,1)S(1)} %constant_dynamic-update-slice_fusion.refs_0_), channel_id=1, source_target_pairs={{0,2},{1,3},{2,0},{3,1},{4,6},{5,7},{6,4},{7,5},{8,10},{9,11},{10,... | collective-permute-start | bytes 393224 | tf_op jit(solution)/shard_map/ppermute | solution.py:231
  14.3 5.0 %collective-permute-start.7 = (bf16[512,128]{1,0:T(8,128)(2,1)S(1)}, bf16[512,128]{1,0:T(8,128)(2,1)S(1)}, u32[]{:S(2)}, u32[]{:S(2)}) collective-permute-start(bf16[512,128]{1,0:T(8,128)(2,1)S(1)} %constant_dynamic-update-slice_fusion.refs_0_), channel_id=1, source_target_pairs={{0,1},{1,0},{2,3},{3,2},{4,5},{5,4},{6,7},{7,6},{8,9},{9,8},{10,11... | collective-permute-start | bytes 393224 | tf_op jit(solution)/shard_map/ppermute | solution.py:231
  17.9 1.4 %collective-permute-start.9 = (bf16[512,128]{1,0:T(8,128)(2,1)S(1)}, bf16[512,128]{1,0:T(8,128)(2,1)S(1)}, u32[]{:S(2)}, u32[]{:S(2)}) collective-permute-start(bf16[512,128]{1,0:T(8,128)(2,1)S(1)} %collective-permute-done.8.refs_2_), channel_id=1, source_target_pairs={{0,1},{1,0},{2,3},{3,2},{4,5},{5,4},{6,7},{7,6},{8,9},{9,8},{10,11... | collective-permute-start | bytes 393224 | tf_op jit(solution)/shard_map/ppermute | solution.py:231
  18.7 1.6 %collective-permute-start.6 = (bf16[512,128]{1,0:T(8,128)(2,1)S(1)}, bf16[512,128]{1,0:T(8,128)(2,1)S(1)}, u32[]{:S(2)}, u32[]{:S(2)}) collective-permute-start(bf16[512,128]{1,0:T(8,128)(2,1)S(1)} %collective-permute-done.5.refs_5_), channel_id=1, source_target_pairs={{0,1},{1,0},{2,3},{3,2},{4,5},{5,4},{6,7},{7,6},{8,9},{9,8},{10,11... | collective-permute-start | bytes 393224 | tf_op jit(solution)/shard_map/ppermute | solution.py:231
  18.7 1.6 %collective-permute-start.4 = (bf16[512,128]{1,0:T(8,128)(2,1)S(1)}, bf16[512,128]{1,0:T(8,128)(2,1)S(1)}, u32[]{:S(2)}, u32[]{:S(2)}) collective-permute-start(bf16[512,128]{1,0:T(8,128)(2,1)S(1)} %collective-permute-done.3.refs_4_), channel_id=1, source_target_pairs={{0,1},{1,0},{2,3},{3,2},{4,5},{5,4},{6,7},{7,6},{8,9},{9,8},{10,11... | collective-permute-start | bytes 393224 | tf_op jit(solution)/shard_map/ppermute | solution.py:231

commit v15 on v14

--- a/solution.py
+++ b/solution.py
@@ -9,7 +9,6 @@
 
 ITERS = 4
 DAMPING = 0.01
-LOADS = 8
 WHOLE = pl.BlockSpec(memory_space=pltpu.VMEM)
 ANYWHERE = pl.BlockSpec(memory_space=pl.ANY)
 
@@ -95,12 +94,8 @@
 
 def last_kernel(fars, late0, late1, x, xt, gram_in, sums_in, tile_hbm, out_hbm, *refs):
     tile, out, late, late_t, k1, k2, e2, g, z, h, a, k, q, image, mixed, sems = refs
-    loads = []
-    step = tile.shape[0] // LOADS
-    for n in range(LOADS):
-        some = pl.ds(n * step, step)
-        loads.append(pltpu.make_async_copy(tile_hbm.at[some, :], tile.at[some, :], sems.at[n]))
-        loads[-1].start()
+    load = pltpu.make_async_copy(tile_hbm, tile, sems.at[0])
+    load.start()
     member = lax.axis_index("grad")
     tokens = x.shape[0]
     half = late.shape[1]
@@ -116,6 +111,9 @@
 
     late[...] = jnp.concatenate([late0[...], late1[...]], axis=1)
     late_t[...] = late[...].T
+
+    sums = [sums_in[n : n + 1, :] for n in range(sums_in.shape[0])]
+    largest = functools.reduce(jnp.maximum, add_sums(sums, xt[...], late[...], late_t[...]))
 
     def symmetric(left, right, finish, *refs):
         for n, some in enumerate(halves):
@@ -139,13 +137,6 @@
         image[:, some] = moved.astype(jnp.bfloat16)
 
     symmetric(k1, k1, lambda product, r, some: [product], k2)
-    sums = [sums_in[n : n + 1, :] for n in range(sums_in.shape[0])]
-    sums = add_sums(sums, xt[...], late[...], late_t[...])
-    for load in loads:
-        load.wait()
-    move(halves[0])
-
-    largest = functools.reduce(jnp.maximum, sums)
     c = 1.0 / (jnp.max(largest) * (1.0 / tokens) + DAMPING)
     eps = 1.0 - c * DAMPING
     eps2 = eps * eps
@@ -180,13 +171,15 @@
         return value, value + (1.0 + eps2) * square
 
     symmetric(e2, e2, fourth, z, h)
-    for some in halves[1:]:
-        move(some)
+    load.wait()
+    move(halves[0])
     symmetric(z, z, lambda product, r, some: [product + k_z * wide(z, r, some)], k)
     for some in halves:
         product = dot(g[...], h[:, some])
         for r in chunks:
             a[r, some] = (product[r] + g_m * wide(h, r, some) + h_m * wide(g, r, some)).astype(jnp.bfloat16)
+    for some in halves[1:]:
+        move(some)
     q_k, q_a, q_g = last * a_m, last * k_m, last * beta
     for some in halves:
         product = dot(k[...], a[:, some])
@@ -200,17 +193,13 @@
     blocks = [x[:, at : at + half] for at in range(0, x.shape[1], half)] + [late[...]]
     for n, block in enumerate(blocks):
         moved = dot(mixed[...], block)
-        parts = 3 if n == len(blocks) - 1 else 1
-        step = moved.shape[0] // parts
-        for at in range(0, parts * step, step):
-            r = slice(at, at + step)
-            for one in (0, 1):
-                here = place(fars[2 * n + one])
-                kept = p * tile[r, here].astype(jnp.float32)
-                out[r, here] = (kept + moved[r, one * features : (one + 1) * features]).astype(jnp.bfloat16)
-                store = pltpu.make_async_copy(out.at[r, here], out_hbm.at[r, here], sems.at[LOADS + len(stores)])
-                store.start()
-                stores.append(store)
+        for one in (0, 1):
+            here = place(fars[2 * n + one])
+            kept = p * tile[:, here].astype(jnp.float32)
+            out[:, here] = (kept + moved[:, one * features : (one + 1) * features]).astype(jnp.bfloat16)
+            store = pltpu.make_async_copy(out.at[:, here], out_hbm.at[:, here], sems.at[1 + len(stores)])
+            store.start()
+            stores.append(store)
     for store in stores:
         store.wait()
 
@@ -265,7 +254,7 @@
         + [scratch(tokens, 2 * features), scratch(2 * features, tokens)]
         + [scratch(tokens, tokens)] * 9
         + [scratch(rows, tokens)] * 2
-        + [pltpu.SemaphoreType.DMA((LOADS + members + 4,))],
+        + [pltpu.SemaphoreType.DMA((1 + members,))],
         compiler_params=pltpu.CompilerParams(vmem_limit_bytes=51 * 2**20),
         cost_estimate=pl.CostEstimate(flops=5 * 10**9, bytes_accessed=0, transcendentals=0),
         name="whole_block",

time: 27.4 us -> 27.5 us (level)
  no operation moved by 1% of the time
where the time goes in v15:
time: 27.5 us; the launch traced here: 27.4 us
  starting transfers between devices  11 us (40%)
  Pallas kernels  8.4 us (31%)
  waiting for transfers between devices  7 us (25%)
  local copies, waits for them, and re-layouts  0.93 us (3%)
    ppermute x3, starting transfers between devices, by_tokens(): lax.ppermute(parts[far], 'dp', [(i, (i + far) % replicas) for i in range(...  7.01 us
    pallas_call x1, Pallas kernels, by_tokens(): pl.pallas_call(functools.partial(last_kernel, fars), out_shape=shape(rows...  7 us
    ppermute x7, waiting for transfers between devices, swap(): return lax.ppermute(value, 'grad', [(i, i ^ far) for i in range(members)])  4.46 us
    ppermute x7, starting transfers between devices, swap(): return lax.ppermute(value, 'grad', [(i, i ^ far) for i in range(members)])  4 us
    ppermute x3, waiting for transfers between devices, by_tokens(): lax.ppermute(parts[far], 'dp', [(i, (i + far) % replicas) for i in range(...  2.54 us
    pallas_call x1, Pallas kernels, by_tokens(): pl.pallas_call(add_kernel, out_shape=[shape(tokens, early), shape(early,...  1.11 us
    unnamed x5, local copies, waits for them, and re-layouts  0.92 us
  transfers between devices with their start and end apart: 10, of which 4 were waited for; matrix products, arithmetic and copies ran while one was open for 0% of the time, Pallas kernels for 4%

profile of v15, /device:TPU:0, one launch (start us, length us, event | category | flops | bytes accessed | tf_op | source)
XLA Modules:
  0.0 27.4 jit_solution(248231572185460666)
XLA Ops:
  0.0 0.0 copy-start
  0.0 0.9 %copy-done = bf16[128,4,128]{2,1,0:T(4,128)(2,1)S(1)} copy-done((bf16[128,4,128]{2,1,0:T(4,128)(2,1)S(1)}, bf16[128,4,128]{2,1,0:T(4,128)(2,1)}, u32[]{:S(2)}) %copy-start) | copy-done | bytes 131096
  0.9 0.3 %split_blocks.1 = (bf16[128,128]{1,0:T(8,128)(2,1)S(1)}, bf16[128,128]{1,0:T(8,128)(2,1)S(1)}, bf16[128,128]{1,0:T(8,128)(2,1)S(1)}, bf16[128,128]{1,0:T(8,128)(2,1)S(1)}) custom-call(bf16[512,128]{1,0:T(8,128)(2,1)S(1)} %bitcast.3), custom_call_target="tpu_custom_call" | custom-call | tf_op jit(solution)/shard_map/split_blocks/pallas_call | solution.py:55
  1.2 3.1 %collective-permute-start = (bf16[128,128]{1,0:T(8,128)(2,1)S(1)}, bf16[128,128]{1,0:T(8,128)(2,1)S(1)}, u32[]{:S(2)}, u32[]{:S(2)}) collective-permute-start(bf16[128,128]{1,0:T(8,128)(2,1)S(1)} %get-tuple-element.14), channel_id=1, source_target_pairs={{0,8},{8,16},{16,24},{24,0},{1,9},{9,17},{17,25},{25,1},{2,10},{10... | collective-permute-start | bytes 98312 | tf_op jit(solution)/shard_map/ppermute | solution.py:224
  4.3 2.6 %collective-permute-start.1 = (bf16[128,128]{1,0:T(8,128)(2,1)S(1)}, bf16[128,128]{1,0:T(8,128)(2,1)S(1)}, u32[]{:S(2)}, u32[]{:S(2)}) collective-permute-start(bf16[128,128]{1,0:T(8,128)(2,1)S(1)} %get-tuple-element.15), channel_id=1, source_target_pairs={{0,16},{8,24},{16,0},{24,8},{1,17},{9,25},{17,1},{25,9},{2,18},{10... | collective-permute-start | bytes 98312 | tf_op jit(solution)/shard_map/ppermute | solution.py:224
  6.9 1.3 %collective-permute-start.2 = (bf16[128,128]{1,0:T(8,128)(2,1)S(1)}, bf16[128,128]{1,0:T(8,128)(2,1)S(1)}, u32[]{:S(2)}, u32[]{:S(2)}) collective-permute-start(bf16[128,128]{1,0:T(8,128)(2,1)S(1)} %get-tuple-element.16), channel_id=1, source_target_pairs={{0,24},{8,0},{16,8},{24,16},{1,25},{9,1},{17,9},{25,17},{2,26},{10... | collective-permute-start | bytes 98312 | tf_op jit(solution)/shard_map/ppermute | solution.py:224
  8.2 0.0 collective-permute-done
  8.2 1.2 %collective-permute-done.1 = bf16[128,128]{1,0:T(8,128)(2,1)S(1)} collective-permute-done((bf16[128,128]{1,0:T(8,128)(2,1)S(1)}, bf16[128,128]{1,0:T(8,128)(2,1)S(1)}, u32[]{:S(2)}, u32[]{:S(2)}) %collective-permute-start.1) | collective-permute-done | bytes 32800 | tf_op jit(solution)/shard_map/ppermute | solution.py:224
  9.4 1.3 %collective-permute-done.2 = bf16[128,128]{1,0:T(8,128)(2,1)S(1)} collective-permute-done((bf16[128,128]{1,0:T(8,128)(2,1)S(1)}, bf16[128,128]{1,0:T(8,128)(2,1)S(1)}, u32[]{:S(2)}, u32[]{:S(2)}) %collective-permute-start.2) | collective-permute-done | bytes 32800 | tf_op jit(solution)/shard_map/ppermute | solution.py:224
  10.8 2.4 %collective-permute-start.8 = (bf16[512,128]{1,0:T(8,128)(2,1)S(1)}, bf16[512,128]{1,0:T(8,128)(2,1)S(1)}, u32[]{:S(2)}, u32[]{:S(2)}) collective-permute-start(bf16[512,128]{1,0:T(8,128)(2,1)S(1)} %constant_dynamic-update-slice_fusion.refs_0_), channel_id=1, source_target_pairs={{0,6},{1,7},{2,4},{3,5},{4,2},{5,3},{6,0},{7,1},{8,14},{9,15},{10,... | collective-permute-start | bytes 393224 | tf_op jit(solution)/shard_map/ppermute | solution.py:220
  13.2 0.5 %collective-permute-start.5 = (bf16[512,128]{1,0:T(8,128)(2,1)S(1)}, bf16[512,128]{1,0:T(8,128)(2,1)S(1)}, u32[]{:S(2)}, u32[]{:S(2)}) collective-permute-start(bf16[512,128]{1,0:T(8,128)(2,1)S(1)} %constant_dynamic-update-slice_fusion.refs_0_), channel_id=1, source_target_pairs={{0,4},{1,5},{2,6},{3,7},{4,0},{5,1},{6,2},{7,3},{8,12},{9,13},{10,... | collective-permute-start | bytes 393224 | tf_op jit(solution)/shard_map/ppermute | solution.py:220
  13.7 0.5 %collective-permute-start.3 = (bf16[512,128]{1,0:T(8,128)(2,1)S(1)}, bf16[512,128]{1,0:T(8,128)(2,1)S(1)}, u32[]{:S(2)}, u32[]{:S(2)}) collective-permute-start(bf16[512,128]{1,0:T(8,128)(2,1)S(1)} %constant_dynamic-update-slice_fusion.refs_0_), channel_id=1, source_target_pairs={{0,2},{1,3},{2,0},{3,1},{4,6},{5,7},{6,4},{7,5},{8,10},{9,11},{10,... | collective-permute-start | bytes 393224 | tf_op jit(solution)/shard_map/ppermute | solution.py:220
  14.3 0.0 collective-permute-start.7
  14.3 3.6 %collective-permute-done.8.refs_2_ = bf16[512,128]{1,0:T(8,128)(2,1)S(1)} collective-permute-done((bf16[512,128]{1,0:T(8,128)(2,1)S(1)}, bf16[512,128]{1,0:T(8,128)(2,1)S(1)}, u32[]{:S(2)}, u32[]{:S(2)}) %collective-permute-start.8) | collective-permute-done | bytes 131104 | tf_op jit(solution)/shard_map/ppermute | solution.py:220
  17.9 0.0 collective-permute-start.9
  17.9 0.9 %collective-permute-done.5.refs_5_ = bf16[512,128]{1,0:T(8,128)(2,1)S(1)} collective-permute-done((bf16[512,128]{1,0:T(8,128)(2,1)S(1)}, bf16[512,128]{1,0:T(8,128)(2,1)S(1)}, u32[]{:S(2)}, u32[]{:S(2)}) %collective-permute-start.5) | collective-permute-done | bytes 131104 | tf_op jit(solution)/shard_map/ppermute | solution.py:220
  18.7 0.0 collective-permute-start.6
  18.7 0.0 collective-permute-done.3.refs_4_
  18.7 0.5 %collective-permute-start.4 = (bf16[512,128]{1,0:T(8,128)(2,1)S(1)}, bf16[512,128]{1,0:T(8,128)(2,1)S(1)}, u32[]{:S(2)}, u32[]{:S(2)}) collective-permute-start(bf16[512,128]{1,0:T(8,128)(2,1)S(1)} %collective-permute-done.3.refs_4_), channel_id=1, source_target_pairs={{0,1},{1,0},{2,3},{3,2},{4,5},{5,4},{6,7},{7,6},{8,9},{9,8},{10,11... | collective-permute-start | bytes 393224 | tf_op jit(solution)/shard_map/ppermute | solution.py:220
  19.2 0.0 collective-permute-done.7.refs_1_
  19.3 0.0 collective-permute-done.9.refs_3_
  19.3 1.1 %first_pieces.1 = (bf16[512,768]{1,0:T(8,128)(2,1)S(1)}, bf16[768,512]{1,0:T(8,128)(2,1)S(1)}, f32[512,512]{1,0:T(8,128)S(1)}, f32[3,256]{1,0:T(4,128)S(1)}) custom-call(bf16[512,128]{1,0:T(8,128)(2,1)S(1)} %constant_dynamic-update-slice_fusion.refs_0_, bf16[512,128]{1,0:T(8,128)(2,1)S(1)} %collective-permute-done.7.refs_1_, ...), custom_call_target="tpu_custom_call" | custom-call | flops 800000000 | tf_op jit(solution)/shard_map/first_pieces/pallas_call | solution.py:234
  20.4 0.0 collective-permute-done.6.late1
  20.4 0.0 collective-permute-done.4.late0
  20.4 7.0 %whole_block.1 = bf16[768,1024]{1,0:T(8,128)(2,1)} custom-call(bf16[512,128]{1,0:T(8,128)(2,1)S(1)} %collective-permute-done.4.late0, bf16[512,128]{1,0:T(8,128)(2,1)S(1)} %collective-permute-done.6.late1, bf16[512,768]{1,0:T(8,128)(2,1)S(1)} %get-tuple-element.17.x, bf16[768,512]{1,0:T(8,128)(2,1)S(1)} %get-tuple-element.18.xt, ...), custom_call_target="tpu_custom_call" | custom-call | flops 5000000000 | tf_op jit(solution)/shard_map/whole_block/pallas_call | solution.py:248
  (4 shorter events, 0.0 us)
Async XLA Ops:
  0.0 0.9 %copy-start = (bf16[128,4,128]{2,1,0:T(4,128)(2,1)S(1)}, bf16[128,4,128]{2,1,0:T(4,128)(2,1)}, u32[]{:S(2)}) copy-start(bf16[128,4,128]{2,1,0:T(4,128)(2,1)} %param.2) | copy-start | bytes 393220
  1.2 7.0 %collective-permute-start = (bf16[128,128]{1,0:T(8,128)(2,1)S(1)}, bf16[128,128]{1,0:T(8,128)(2,1)S(1)}, u32[]{:S(2)}, u32[]{:S(2)}) collective-permute-start(bf16[128,128]{1,0:T(8,128)(2,1)S(1)} %get-tuple-element.14), channel_id=1, source_target_pairs={{0,8},{8,16},{16,24},{24,0},{1,9},{9,17},{17,25},{25,1},{2,10},{10... | collective-permute-start | bytes 98312 | tf_op jit(solution)/shard_map/ppermute | solution.py:224
  4.3 5.2 %collective-permute-start.1 = (bf16[128,128]{1,0:T(8,128)(2,1)S(1)}, bf16[128,128]{1,0:T(8,128)(2,1)S(1)}, u32[]{:S(2)}, u32[]{:S(2)}) collective-permute-start(bf16[128,128]{1,0:T(8,128)(2,1)S(1)} %get-tuple-element.15), channel_id=1, source_target_pairs={{0,16},{8,24},{16,0},{24,8},{1,17},{9,25},{17,1},{25,9},{2,18},{10... | collective-permute-start | bytes 98312 | tf_op jit(solution)/shard_map/ppermute | solution.py:224
  6.9 3.9 %collective-permute-start.2 = (bf16[128,128]{1,0:T(8,128)(2,1)S(1)}, bf16[128,128]{1,0:T(8,128)(2,1)S(1)}, u32[]{:S(2)}, u32[]{:S(2)}) collective-permute-start(bf16[128,128]{1,0:T(8,128)(2,1)S(1)} %get-tuple-element.16), channel_id=1, source_target_pairs={{0,24},{8,0},{16,8},{24,16},{1,25},{9,1},{17,9},{25,17},{2,26},{10... | collective-permute-start | bytes 98312 | tf_op jit(solution)/shard_map/ppermute | solution.py:224
  10.8 7.1 %collective-permute-start.8 = (bf16[512,128]{1,0:T(8,128)(2,1)S(1)}, bf16[512,128]{1,0:T(8,128)(2,1)S(1)}, u32[]{:S(2)}, u32[]{:S(2)}) collective-permute-start(bf16[512,128]{1,0:T(8,128)(2,1)S(1)} %constant_dynamic-update-slice_fusion.refs_0_), channel_id=1, source_target_pairs={{0,6},{1,7},{2,4},{3,5},{4,2},{5,3},{6,0},{7,1},{8,14},{9,15},{10,... | collective-permute-start | bytes 393224 | tf_op jit(solution)/shard_map/ppermute | solution.py:220
  13.2 5.5 %collective-permute-start.5 = (bf16[512,128]{1,0:T(8,128)(2,1)S(1)}, bf16[512,128]{1,0:T(8,128)(2,1)S(1)}, u32[]{:S(2)}, u32[]{:S(2)}) collective-permute-start(bf16[512,128]{1,0:T(8,128)(2,1)S(1)} %constant_dynamic-update-slice_fusion.refs_0_), channel_id=1, source_target_pairs={{0,4},{1,5},{2,6},{3,7},{4,0},{5,1},{6,2},{7,3},{8,12},{9,13},{10,... | collective-permute-start | bytes 393224 | tf_op jit(solution)/shard_map/ppermute | solution.py:220
  13.7 5.0 %collective-permute-start.3 = (bf16[512,128]{1,0:T(8,128)(2,1)S(1)}, bf16[512,128]{1,0:T(8,128)(2,1)S(1)}, u32[]{:S(2)}, u32[]{:S(2)}) collective-permute-start(bf16[512,128]{1,0:T(8,128)(2,1)S(1)} %constant_dynamic-update-slice_fusion.refs_0_), channel_id=1, source_target_pairs={{0,2},{1,3},{2,0},{3,1},{4,6},{5,7},{6,4},{7,5},{8,10},{9,11},{10,... | collective-permute-start | bytes 393224 | tf_op jit(solution)/shard_map/ppermute | solution.py:220
  14.3 5.0 %collective-permute-start.7 = (bf16[512,128]{1,0:T(8,128)(2,1)S(1)}, bf16[512,128]{1,0:T(8,128)(2,1)S(1)}, u32[]{:S(2)}, u32[]{:S(2)}) collective-permute-start(bf16[512,128]{1,0:T(8,128)(2,1)S(1)} %constant_dynamic-update-slice_fusion.refs_0_), channel_id=1, source_target_pairs={{0,1},{1,0},{2,3},{3,2},{4,5},{5,4},{6,7},{7,6},{8,9},{9,8},{10,11... | collective-permute-start | bytes 393224 | tf_op jit(solution)/shard_map/ppermute | solution.py:220
  17.9 1.4 %collective-permute-start.9 = (bf16[512,128]{1,0:T(8,128)(2,1)S(1)}, bf16[512,128]{1,0:T(8,128)(2,1)S(1)}, u32[]{:S(2)}, u32[]{:S(2)}) collective-permute-start(bf16[512,128]{1,0:T(8,128)(2,1)S(1)} %collective-permute-done.8.refs_2_), channel_id=1, source_target_pairs={{0,1},{1,0},{2,3},{3,2},{4,5},{5,4},{6,7},{7,6},{8,9},{9,8},{10,11... | collective-permute-start | bytes 393224 | tf_op jit(solution)/shard_map/ppermute | solution.py:220
  18.7 1.6 %collective-permute-start.6 = (bf16[512,128]{1,0:T(8,128)(2,1)S(1)}, bf16[512,128]{1,0:T(8,128)(2,1)S(1)}, u32[]{:S(2)}, u32[]{:S(2)}) collective-permute-start(bf16[512,128]{1,0:T(8,128)(2,1)S(1)} %collective-permute-done.5.refs_5_), channel_id=1, source_target_pairs={{0,1},{1,0},{2,3},{3,2},{4,5},{5,4},{6,7},{7,6},{8,9},{9,8},{10,11... | collective-permute-start | bytes 393224 | tf_op jit(solution)/shard_map/ppermute | solution.py:220
  18.7 1.6 %collective-permute-start.4 = (bf16[512,128]{1,0:T(8,128)(2,1)S(1)}, bf16[512,128]{1,0:T(8,128)(2,1)S(1)}, u32[]{:S(2)}, u32[]{:S(2)}) collective-permute-start(bf16[512,128]{1,0:T(8,128)(2,1)S(1)} %collective-permute-done.3.refs_4_), channel_id=1, source_target_pairs={{0,1},{1,0},{2,3},{3,2},{4,5},{5,4},{6,7},{7,6},{8,9},{9,8},{10,11... | collective-permute-start | bytes 393224 | tf_op jit(solution)/shard_map/ppermute | solution.py:220

commit v16 on v12

--- a/solution.py
+++ b/solution.py
@@ -80,59 +80,49 @@
     tokens = x.shape[0]
     half = late.shape[1]
     features = half // 2
-    halves = [slice(at, at + half) for at in range(0, tokens, half)]
-    blocks = [slice(at, at + half) for at in range(0, x.shape[1], half)]
     chunks = [slice(at, at + 32) for at in range(0, tokens, 32)]
 
     def place(far):
         return pl.ds(pl.multiple_of((member ^ far) * features, features), features)
 
-    def chosen(some):
-        return jnp.concatenate([tile[:, place(far)] for far in some], axis=1)
+    def chosen(some, rows):
+        return jnp.concatenate([tile[rows, place(far)] for far in some], axis=1)
 
     late[...] = jnp.concatenate([late0[...], late1[...]], axis=1)
     late_t[...] = late[...].T
 
-    def symmetric(left, right, finish, *refs):
-        for n, some in enumerate(halves):
-            rows = slice(some.start, tokens)
-            product = left(rows, some) if right is None else dot(left[rows, :], right[:, some])
-            for r in chunks[some.start // 32 :]:
-                values = finish(product[r.start - some.start : r.stop - some.start], r, some)
-                for ref, value in zip(refs, values):
-                    ref[r, some] = value.astype(jnp.bfloat16)
-            for other in halves[n + 1 :]:
-                for ref in refs:
-                    ref[some, other] = ref[other, some].T
-
-    def gram(rows, some):
-        return lax.dot_general(late[rows, :], late[some, :], (((1,), (1,)), ((), ())), preferred_element_type=jnp.float32)
-
-    symmetric(gram, None, lambda product, r, some: [(gram_in[r, some] + product) * (1.0 / tokens)], k1)
-
-    column_sums, row_sums = [0.0] * (len(blocks) + 1), [0.0] * len(blocks)
-
-    def add_sums(n, left, right):
-        column = jnp.abs(dot(left, right))
-        column_sums[n] = column_sums[n] + jnp.sum(column, axis=0, keepdims=True)
-        for i, some in enumerate(blocks[: min(n, column.shape[0] // half)]):
-            row_sums[i] = row_sums[i] + column[some, :features] + column[some, features:]
+    def each(product, finish, *refs):
+        for r in chunks:
+            for ref, value in zip(refs, finish(product[r], r)):
+                ref[r, :] = value.astype(jnp.bfloat16)
+
+    product = lax.dot_general(late[...], late[...], (((1,), (1,)), ((), ())), preferred_element_type=jnp.float32)
+    each(product, lambda product, r: [(gram_in[r, :] + product) * (1.0 / tokens)], k1)
+
+    def sums(column):
+        return jnp.sum(column, axis=0, keepdims=True)
+
+    def turned_sums(column):
+        folded = functools.reduce(jnp.add, [column[:, at : at + 128] for at in range(0, column.shape[1], 128)])
+        return sums(folded.T)
 
     def move(some):
-        moved = dot(chosen(fars[:-2]), xt[:, some]) + dot(chosen(fars[-2:]), late_t[:, some])
-        image[:, some] = moved.astype(jnp.bfloat16)
-
-    for n, some in enumerate(blocks):
-        add_sums(n, xt[: some.stop, :], x[:, some])
-    symmetric(k1, k1, lambda product, r, some: [product], k2)
-    add_sums(len(blocks), xt[...], late[...])
-    column_sums[-1] = column_sums[-1] + jnp.sum(jnp.abs(dot(late_t[...], late[...])), axis=0, keepdims=True)
+        moved = dot(chosen(fars[:-2], some), xt[...]) + dot(chosen(fars[-2:], some), late_t[...])
+        image[some, :] = moved.astype(jnp.bfloat16)
+
+    top, side = xt.shape[0] - half, slice(xt.shape[0] - half, xt.shape[0])
+    first = jnp.abs(dot(xt[:top, :], x[:, :top]))
+    each(dot(k1[...], k1[...]), lambda product, r: [product], k2)
+    ends = jnp.concatenate([x[:, side], late[...]], axis=1)
+    second = jnp.abs(dot(xt[...], ends))
+    third = jnp.abs(dot(late_t[...], ends))
+    tops = sums(first) + turned_sums(second[:top])
     load.wait()
-    move(halves[0])
-
-    largest = column_sums[-1]
-    for column, row in zip(column_sums[:-1], row_sums):
-        largest = jnp.maximum(largest, column + jnp.sum(row.T, axis=0, keepdims=True))
+    rows = tile.shape[0]
+    move(slice(0, rows // 2))
+    sides = sums(second[:, :half]) + sums(third[:, :half])
+    lates = sums(second[:, half:]) + sums(third[:, half:])
+    largest = jnp.maximum(jnp.max(tops, axis=1, keepdims=True), jnp.max(jnp.maximum(sides, lates), axis=1, keepdims=True))
     c = 1.0 / (jnp.max(largest) * (1.0 / tokens) + DAMPING)
     eps = 1.0 - c * DAMPING
     eps2 = eps * eps
@@ -151,45 +141,39 @@
     q_m = q_m * last
     p = c * (1.0 + eps) * (1.0 + eps2) * beta
 
-    def wide(ref, r, some):
-        return ref[r, some].astype(jnp.float32)
-
-    for some in halves:
-        for r in chunks:
-            first = wide(k1, r, some)
-            square = e2_1 * first + e2_2 * wide(k2, r, some)
-            e2[r, some] = square.astype(jnp.bfloat16)
-            g[r, some] = (square + g_1 * first).astype(jnp.bfloat16)
-
-    def fourth(product, r, some):
-        square = wide(e2, r, some)
+    def wide(ref, r):
+        return ref[r, :].astype(jnp.float32)
+
+    for r in chunks:
+        one = wide(k1, r)
+        square = e2_1 * one + e2_2 * wide(k2, r)
+        e2[r, :] = square.astype(jnp.bfloat16)
+        g[r, :] = (square + g_1 * one).astype(jnp.bfloat16)
+
+    def fourth(product, r):
+        square = wide(e2, r)
         value = 2.0 * eps2 * square + product
         return value, value + (1.0 + eps2) * square
 
-    symmetric(e2, e2, fourth, z, h)
-    for some in halves[1:]:
-        move(some)
-    symmetric(z, z, lambda product, r, some: [product + k_z * wide(z, r, some)], k)
-    for some in halves:
-        product = dot(g[...], h[:, some])
-        for r in chunks:
-            a[r, some] = (product[r] + g_m * wide(h, r, some) + h_m * wide(g, r, some)).astype(jnp.bfloat16)
+    each(dot(e2[...], e2[...]), fourth, z, h)
+    move(slice(rows // 2, rows))
+    each(dot(z[...], z[...]), lambda product, r: [product + k_z * wide(z, r)], k)
+    each(dot(g[...], h[...]), lambda product, r: [product + g_m * wide(h, r) + h_m * wide(g, r)], a)
     q_k, q_a, q_g = last * a_m, last * k_m, last * beta
-    for some in halves:
-        product = dot(k[...], a[:, some])
-        for r in chunks:
-            rest = q_k * wide(k, r, some) + q_a * wide(a, r, some) + q_g * wide(g, r, some)
-            q[r, some] = (last * product[r] + rest).astype(jnp.bfloat16)
-    for some in halves:
-        product = dot(image[...], q[:, some])
-        mixed[:, some] = (product + q_m * image[:, some].astype(jnp.float32)).astype(jnp.bfloat16)
+
+    def whole(product, r):
+        return [last * product + q_k * wide(k, r) + q_a * wide(a, r) + q_g * wide(g, r)]
+
+    each(dot(k[...], a[...]), whole, q)
+    product = dot(image[...], q[...])
+    mixed[...] = (product + q_m * image[...].astype(jnp.float32)).astype(jnp.bfloat16)
     stores = []
-    for n in range(len(blocks) + 1):
-        moved = dot(mixed[...], late[...] if n == len(blocks) else x[:, blocks[n]])
-        for one in (0, 1):
-            here = place(fars[2 * n + one])
+    for n, block in enumerate((x[:, :top], ends)):
+        moved = dot(mixed[...], block)
+        for at in range(0, block.shape[1], features):
+            here = place(fars[(n * top + at) // features])
             kept = p * tile[:, here].astype(jnp.float32)
-            out[:, here] = (kept + moved[:, one * features : (one + 1) * features]).astype(jnp.bfloat16)
+            out[:, here] = (kept + moved[:, at : at + features]).astype(jnp.bfloat16)
             store = pltpu.make_async_copy(out.at[:, here], out_hbm.at[:, here], sems.at[1 + len(stores)])
             store.start()
             stores.append(store)
@@ -212,11 +196,10 @@
     def swap(value, far):
         return lax.ppermute(value, "grad", [(i, i ^ far) for i in range(members)])
 
-    order = (0, 2, 1, 3)
-    parts = dict(zip(order, split_blocks(factor_inputs, order)))
-    for far in order[1:]:
+    parts = list(split_blocks(factor_inputs, range(replicas)))
+    for far in range(1, replicas):
         parts[far] = lax.ppermute(parts[far], "dp", [(i, (i + far) % replicas) for i in range(replicas)])
-    own = jnp.concatenate([parts[far] for far in order], axis=0)
+    own = jnp.concatenate(parts, axis=0)
     fars = (0, 1, 6, 7, 4, 2, 5, 3)
     pieces = {0: own}
     for far in (2, 4, 6):

time: 27.2 us -> 27.2 us (level)
  starting transfers between devices: 11.5 us -> 11 us
  Pallas kernels: 7.51 us -> 7.8 us
    ppermute x3, starting transfers between devices: 7.93 us -> 7.01 us  [by_tokens(): lax.ppermute(parts[far], 'dp', [(i, (i + far) % replicas) for i in range(...]
    ppermute x3, waiting for transfers between devices: 1.99 us -> 2.54 us  [by_tokens(): lax.ppermute(parts[far], 'dp', [(i, (i + far) % replicas) for i in range(...]
    ppermute x7, starting transfers between devices: 3.59 us -> 3.95 us  [swap(): return lax.ppermute(value, 'grad', [(i, i ^ far) for i in range(members)])]
    ppermute x7, waiting for transfers between devices: 5.1 us -> 4.8 us  [swap(): return lax.ppermute(value, 'grad', [(i, i ^ far) for i in range(members)])]
    pallas_call x1, Pallas kernels: 6.55 us -> 6.85 us  [by_tokens(): pl.pallas_call(functools.partial(last_kernel, fars), out_shape=shape(rows...]
  transfers between devices with their start and end apart: 10 -> 10, of which waited for: 6 -> 7; matrix products, arithmetic and copies ran while one was open for 0% -> 0% of each run, Pallas kernels for 2% -> 2%
where the time goes in v16:
time: 27.2 us; the launch traced here: 27.1 us
  starting transfers between devices  11 us (40%)
  Pallas kernels  7.8 us (29%)
  waiting for transfers between devices  7.34 us (27%)
  local copies, waits for them, and re-layouts  0.93 us (3%)
    ppermute x3, starting transfers between devices, by_tokens(): lax.ppermute(parts[far], 'dp', [(i, (i + far) % replicas) for i in range(...  7.01 us
    pallas_call x1, Pallas kernels, by_tokens(): pl.pallas_call(functools.partial(last_kernel, fars), out_shape=shape(rows...  6.85 us
    ppermute x7, waiting for transfers between devices, swap(): return lax.ppermute(value, 'grad', [(i, i ^ far) for i in range(members)])  4.8 us
    ppermute x7, starting transfers between devices, swap(): return lax.ppermute(value, 'grad', [(i, i ^ far) for i in range(members)])  3.95 us
    ppermute x3, waiting for transfers between devices, by_tokens(): lax.ppermute(parts[far], 'dp', [(i, (i + far) % replicas) for i in range(...  2.54 us
    unnamed x5, local copies, waits for them, and re-layouts  0.92 us
    pallas_call x1, Pallas kernels, by_tokens(): pl.pallas_call(first_kernel, out_shape=[shape(tokens, early), shape(early...  0.67 us
  transfers between devices with their start and end apart: 10, of which 7 were waited for; matrix products, arithmetic and copies ran while one was open for 0% of the time, Pallas kernels for 2%

profile of v16, /device:TPU:0, one launch (start us, length us, event | category | flops | bytes accessed | tf_op | source)
XLA Modules:
  0.0 27.1 jit_solution(80643725301050719)
XLA Ops:
  0.0 0.0 copy-start
  0.0 0.9 %copy-done = bf16[128,4,128]{2,1,0:T(4,128)(2,1)S(1)} copy-done((bf16[128,4,128]{2,1,0:T(4,128)(2,1)S(1)}, bf16[128,4,128]{2,1,0:T(4,128)(2,1)}, u32[]{:S(2)}) %copy-start) | copy-done | bytes 131096
  0.9 0.3 %split_blocks.1 = (bf16[128,128]{1,0:T(8,128)(2,1)S(1)}, bf16[128,128]{1,0:T(8,128)(2,1)S(1)}, bf16[128,128]{1,0:T(8,128)(2,1)S(1)}, bf16[128,128]{1,0:T(8,128)(2,1)S(1)}) custom-call(bf16[512,128]{1,0:T(8,128)(2,1)S(1)} %bitcast.3), custom_call_target="tpu_custom_call" | custom-call | tf_op jit(solution)/shard_map/split_blocks/pallas_call | solution.py:55
  1.2 3.1 %collective-permute-start = (bf16[128,128]{1,0:T(8,128)(2,1)S(1)}, bf16[128,128]{1,0:T(8,128)(2,1)S(1)}, u32[]{:S(2)}, u32[]{:S(2)}) collective-permute-start(bf16[128,128]{1,0:T(8,128)(2,1)S(1)} %get-tuple-element.13), channel_id=1, source_target_pairs={{0,8},{8,16},{16,24},{24,0},{1,9},{9,17},{17,25},{25,1},{2,10},{10... | collective-permute-start | bytes 98312 | tf_op jit(solution)/shard_map/ppermute | solution.py:201
  4.3 2.6 %collective-permute-start.1 = (bf16[128,128]{1,0:T(8,128)(2,1)S(1)}, bf16[128,128]{1,0:T(8,128)(2,1)S(1)}, u32[]{:S(2)}, u32[]{:S(2)}) collective-permute-start(bf16[128,128]{1,0:T(8,128)(2,1)S(1)} %get-tuple-element.14), channel_id=1, source_target_pairs={{0,16},{8,24},{16,0},{24,8},{1,17},{9,25},{17,1},{25,9},{2,18},{10... | collective-permute-start | bytes 98312 | tf_op jit(solution)/shard_map/ppermute | solution.py:201
  6.9 1.3 %collective-permute-start.2 = (bf16[128,128]{1,0:T(8,128)(2,1)S(1)}, bf16[128,128]{1,0:T(8,128)(2,1)S(1)}, u32[]{:S(2)}, u32[]{:S(2)}) collective-permute-start(bf16[128,128]{1,0:T(8,128)(2,1)S(1)} %get-tuple-element.15), channel_id=1, source_target_pairs={{0,24},{8,0},{16,8},{24,16},{1,25},{9,1},{17,9},{25,17},{2,26},{10... | collective-permute-start | bytes 98312 | tf_op jit(solution)/shard_map/ppermute | solution.py:201
  8.2 0.0 collective-permute-done
  8.2 1.2 %collective-permute-done.1 = bf16[128,128]{1,0:T(8,128)(2,1)S(1)} collective-permute-done((bf16[128,128]{1,0:T(8,128)(2,1)S(1)}, bf16[128,128]{1,0:T(8,128)(2,1)S(1)}, u32[]{:S(2)}, u32[]{:S(2)}) %collective-permute-start.1) | collective-permute-done | bytes 32800 | tf_op jit(solution)/shard_map/ppermute | solution.py:201
  9.4 1.3 %collective-permute-done.2 = bf16[128,128]{1,0:T(8,128)(2,1)S(1)} collective-permute-done((bf16[128,128]{1,0:T(8,128)(2,1)S(1)}, bf16[128,128]{1,0:T(8,128)(2,1)S(1)}, u32[]{:S(2)}, u32[]{:S(2)}) %collective-permute-start.2) | collective-permute-done | bytes 32800 | tf_op jit(solution)/shard_map/ppermute | solution.py:201
  10.8 2.4 %collective-permute-start.8 = (bf16[512,128]{1,0:T(8,128)(2,1)S(1)}, bf16[512,128]{1,0:T(8,128)(2,1)S(1)}, u32[]{:S(2)}, u32[]{:S(2)}) collective-permute-start(bf16[512,128]{1,0:T(8,128)(2,1)S(1)} %constant_dynamic-update-slice_fusion.refs_0_), channel_id=1, source_target_pairs={{0,6},{1,7},{2,4},{3,5},{4,2},{5,3},{6,0},{7,1},{8,14},{9,15},{10,... | collective-permute-start | bytes 393224 | tf_op jit(solution)/shard_map/ppermute | solution.py:197
  13.2 0.5 %collective-permute-start.5 = (bf16[512,128]{1,0:T(8,128)(2,1)S(1)}, bf16[512,128]{1,0:T(8,128)(2,1)S(1)}, u32[]{:S(2)}, u32[]{:S(2)}) collective-permute-start(bf16[512,128]{1,0:T(8,128)(2,1)S(1)} %constant_dynamic-update-slice_fusion.refs_0_), channel_id=1, source_target_pairs={{0,2},{1,3},{2,0},{3,1},{4,6},{5,7},{6,4},{7,5},{8,10},{9,11},{10,... | collective-permute-start | bytes 393224 | tf_op jit(solution)/shard_map/ppermute | solution.py:197
  13.8 0.5 %collective-permute-start.3 = (bf16[512,128]{1,0:T(8,128)(2,1)S(1)}, bf16[512,128]{1,0:T(8,128)(2,1)S(1)}, u32[]{:S(2)}, u32[]{:S(2)}) collective-permute-start(bf16[512,128]{1,0:T(8,128)(2,1)S(1)} %constant_dynamic-update-slice_fusion.refs_0_), channel_id=1, source_target_pairs={{0,4},{1,5},{2,6},{3,7},{4,0},{5,1},{6,2},{7,3},{8,12},{9,13},{10,... | collective-permute-start | bytes 393224 | tf_op jit(solution)/shard_map/ppermute | solution.py:197
  14.3 0.0 collective-permute-start.7
  14.3 3.0 %collective-permute-done.8.refs_2_ = bf16[512,128]{1,0:T(8,128)(2,1)S(1)} collective-permute-done((bf16[512,128]{1,0:T(8,128)(2,1)S(1)}, bf16[512,128]{1,0:T(8,128)(2,1)S(1)}, u32[]{:S(2)}, u32[]{:S(2)}) %collective-permute-start.8) | collective-permute-done | bytes 131104 | tf_op jit(solution)/shard_map/ppermute | solution.py:197
  17.3 0.0 collective-permute-start.9
  17.3 1.3 %collective-permute-done.5.refs_5_ = bf16[512,128]{1,0:T(8,128)(2,1)S(1)} collective-permute-done((bf16[512,128]{1,0:T(8,128)(2,1)S(1)}, bf16[512,128]{1,0:T(8,128)(2,1)S(1)}, u32[]{:S(2)}, u32[]{:S(2)}) %collective-permute-start.5) | collective-permute-done | bytes 131104 | tf_op jit(solution)/shard_map/ppermute | solution.py:197
  18.7 0.0 collective-permute-start.6
  18.7 0.1 collective-permute-done.3.refs_4_
  18.7 0.5 %collective-permute-start.4 = (bf16[512,128]{1,0:T(8,128)(2,1)S(1)}, bf16[512,128]{1,0:T(8,128)(2,1)S(1)}, u32[]{:S(2)}, u32[]{:S(2)}) collective-permute-start(bf16[512,128]{1,0:T(8,128)(2,1)S(1)} %collective-permute-done.3.refs_4_), channel_id=1, source_target_pairs={{0,1},{1,0},{2,3},{3,2},{4,5},{5,4},{6,7},{7,6},{8,9},{9,8},{10,11... | collective-permute-start | bytes 393224 | tf_op jit(solution)/shard_map/ppermute | solution.py:197
  19.2 0.0 collective-permute-done.7.refs_1_
  19.2 0.0 collective-permute-done.9.refs_3_
  19.2 0.7 %first_pieces.1 = (bf16[512,768]{1,0:T(8,128)(2,1)S(1)}, bf16[768,512]{1,0:T(8,128)(2,1)S(1)}, f32[512,512]{1,0:T(8,128)S(1)}) custom-call(bf16[512,128]{1,0:T(8,128)(2,1)S(1)} %constant_dynamic-update-slice_fusion.refs_0_, bf16[512,128]{1,0:T(8,128)(2,1)S(1)} %collective-permute-done.7.refs_1_, bf16[512,128]{1,0:T(8,128)(2,1)S(1)} %collective-permute-done.8.refs_2_, ...), custom_call_target="tpu_custom_call" | custom-call | flops 400000000 | tf_op jit(solution)/shard_map/first_pieces/pallas_call | solution.py:211
  19.9 0.2 collective-permute-done.6.late1
  20.0 0.2 collective-permute-done.4.late0
  20.2 6.9 %whole_block.1 = bf16[768,1024]{1,0:T(8,128)(2,1)} custom-call(bf16[512,128]{1,0:T(8,128)(2,1)S(1)} %collective-permute-done.4.late0, bf16[512,128]{1,0:T(8,128)(2,1)S(1)} %collective-permute-done.6.late1, bf16[512,768]{1,0:T(8,128)(2,1)S(1)} %get-tuple-element.16.x, bf16[768,512]{1,0:T(8,128)(2,1)S(1)} %get-tuple-element.17.xt, ...), custom_call_target="tpu_custom_call" | custom-call | flops 5000000000 | tf_op jit(solution)/shard_map/whole_block/pallas_call | solution.py:220
  (4 shorter events, 0.0 us)
Async XLA Ops:
  0.0 0.9 %copy-start = (bf16[128,4,128]{2,1,0:T(4,128)(2,1)S(1)}, bf16[128,4,128]{2,1,0:T(4,128)(2,1)}, u32[]{:S(2)}) copy-start(bf16[128,4,128]{2,1,0:T(4,128)(2,1)} %param.2) | copy-start | bytes 393220
  1.2 7.0 %collective-permute-start = (bf16[128,128]{1,0:T(8,128)(2,1)S(1)}, bf16[128,128]{1,0:T(8,128)(2,1)S(1)}, u32[]{:S(2)}, u32[]{:S(2)}) collective-permute-start(bf16[128,128]{1,0:T(8,128)(2,1)S(1)} %get-tuple-element.13), channel_id=1, source_target_pairs={{0,8},{8,16},{16,24},{24,0},{1,9},{9,17},{17,25},{25,1},{2,10},{10... | collective-permute-start | bytes 98312 | tf_op jit(solution)/shard_map/ppermute | solution.py:201
  4.3 5.2 %collective-permute-start.1 = (bf16[128,128]{1,0:T(8,128)(2,1)S(1)}, bf16[128,128]{1,0:T(8,128)(2,1)S(1)}, u32[]{:S(2)}, u32[]{:S(2)}) collective-permute-start(bf16[128,128]{1,0:T(8,128)(2,1)S(1)} %get-tuple-element.14), channel_id=1, source_target_pairs={{0,16},{8,24},{16,0},{24,8},{1,17},{9,25},{17,1},{25,9},{2,18},{10... | collective-permute-start | bytes 98312 | tf_op jit(solution)/shard_map/ppermute | solution.py:201
  6.9 3.9 %collective-permute-start.2 = (bf16[128,128]{1,0:T(8,128)(2,1)S(1)}, bf16[128,128]{1,0:T(8,128)(2,1)S(1)}, u32[]{:S(2)}, u32[]{:S(2)}) collective-permute-start(bf16[128,128]{1,0:T(8,128)(2,1)S(1)} %get-tuple-element.15), channel_id=1, source_target_pairs={{0,24},{8,0},{16,8},{24,16},{1,25},{9,1},{17,9},{25,17},{2,26},{10... | collective-permute-start | bytes 98312 | tf_op jit(solution)/shard_map/ppermute | solution.py:201
  10.8 6.5 %collective-permute-start.8 = (bf16[512,128]{1,0:T(8,128)(2,1)S(1)}, bf16[512,128]{1,0:T(8,128)(2,1)S(1)}, u32[]{:S(2)}, u32[]{:S(2)}) collective-permute-start(bf16[512,128]{1,0:T(8,128)(2,1)S(1)} %constant_dynamic-update-slice_fusion.refs_0_), channel_id=1, source_target_pairs={{0,6},{1,7},{2,4},{3,5},{4,2},{5,3},{6,0},{7,1},{8,14},{9,15},{10,... | collective-permute-start | bytes 393224 | tf_op jit(solution)/shard_map/ppermute | solution.py:197
  13.2 5.4 %collective-permute-start.5 = (bf16[512,128]{1,0:T(8,128)(2,1)S(1)}, bf16[512,128]{1,0:T(8,128)(2,1)S(1)}, u32[]{:S(2)}, u32[]{:S(2)}) collective-permute-start(bf16[512,128]{1,0:T(8,128)(2,1)S(1)} %constant_dynamic-update-slice_fusion.refs_0_), channel_id=1, source_target_pairs={{0,2},{1,3},{2,0},{3,1},{4,6},{5,7},{6,4},{7,5},{8,10},{9,11},{10,... | collective-permute-start | bytes 393224 | tf_op jit(solution)/shard_map/ppermute | solution.py:197
  13.8 5.0 %collective-permute-start.3 = (bf16[512,128]{1,0:T(8,128)(2,1)S(1)}, bf16[512,128]{1,0:T(8,128)(2,1)S(1)}, u32[]{:S(2)}, u32[]{:S(2)}) collective-permute-start(bf16[512,128]{1,0:T(8,128)(2,1)S(1)} %constant_dynamic-update-slice_fusion.refs_0_), channel_id=1, source_target_pairs={{0,4},{1,5},{2,6},{3,7},{4,0},{5,1},{6,2},{7,3},{8,12},{9,13},{10,... | collective-permute-start | bytes 393224 | tf_op jit(solution)/shard_map/ppermute | solution.py:197
  14.3 4.9 %collective-permute-start.7 = (bf16[512,128]{1,0:T(8,128)(2,1)S(1)}, bf16[512,128]{1,0:T(8,128)(2,1)S(1)}, u32[]{:S(2)}, u32[]{:S(2)}) collective-permute-start(bf16[512,128]{1,0:T(8,128)(2,1)S(1)} %constant_dynamic-update-slice_fusion.refs_0_), channel_id=1, source_target_pairs={{0,1},{1,0},{2,3},{3,2},{4,5},{5,4},{6,7},{7,6},{8,9},{9,8},{10,11... | collective-permute-start | bytes 393224 | tf_op jit(solution)/shard_map/ppermute | solution.py:197
  17.3 1.9 %collective-permute-start.9 = (bf16[512,128]{1,0:T(8,128)(2,1)S(1)}, bf16[512,128]{1,0:T(8,128)(2,1)S(1)}, u32[]{:S(2)}, u32[]{:S(2)}) collective-permute-start(bf16[512,128]{1,0:T(8,128)(2,1)S(1)} %collective-permute-done.8.refs_2_), channel_id=1, source_target_pairs={{0,1},{1,0},{2,3},{3,2},{4,5},{5,4},{6,7},{7,6},{8,9},{9,8},{10,11... | collective-permute-start | bytes 393224 | tf_op jit(solution)/shard_map/ppermute | solution.py:197
  18.7 1.3 %collective-permute-start.6 = (bf16[512,128]{1,0:T(8,128)(2,1)S(1)}, bf16[512,128]{1,0:T(8,128)(2,1)S(1)}, u32[]{:S(2)}, u32[]{:S(2)}) collective-permute-start(bf16[512,128]{1,0:T(8,128)(2,1)S(1)} %collective-permute-done.5.refs_5_), channel_id=1, source_target_pairs={{0,1},{1,0},{2,3},{3,2},{4,5},{5,4},{6,7},{7,6},{8,9},{9,8},{10,11... | collective-permute-start | bytes 393224 | tf_op jit(solution)/shard_map/ppermute | solution.py:197
  18.7 1.5 %collective-permute-start.4 = (bf16[512,128]{1,0:T(8,128)(2,1)S(1)}, bf16[512,128]{1,0:T(8,128)(2,1)S(1)}, u32[]{:S(2)}, u32[]{:S(2)}) collective-permute-start(bf16[512,128]{1,0:T(8,128)(2,1)S(1)} %collective-permute-done.3.refs_4_), channel_id=1, source_target_pairs={{0,1},{1,0},{2,3},{3,2},{4,5},{5,4},{6,7},{7,6},{8,9},{9,8},{10,11... | collective-permute-start | bytes 393224 | tf_op jit(solution)/shard_map/ppermute | solution.py:197

commit v17 on v16

--- a/solution.py
+++ b/solution.py
@@ -9,6 +9,7 @@
 
 ITERS = 4
 DAMPING = 0.01
+ROWS = (0, 256, 512, 640)
 WHOLE = pl.BlockSpec(memory_space=pltpu.VMEM)
 ANYWHERE = pl.BlockSpec(memory_space=pl.ANY)
 
@@ -73,7 +74,7 @@
 
 
 def last_kernel(fars, late0, late1, x, xt, gram_in, tile_hbm, out_hbm, *refs):
-    tile, out, late, late_t, k1, k2, e2, g, z, h, a, k, q, image, mixed, sems = refs
+    tile, out, late, late_t, k1, k2, e2, g, z, h, a, k, q, image, sems = refs
     load = pltpu.make_async_copy(tile_hbm, tile, sems.at[0])
     load.start()
     member = lax.axis_index("grad")
@@ -165,18 +166,19 @@
         return [last * product + q_k * wide(k, r) + q_a * wide(a, r) + q_g * wide(g, r)]
 
     each(dot(k[...], a[...]), whole, q)
-    product = dot(image[...], q[...])
-    mixed[...] = (product + q_m * image[...].astype(jnp.float32)).astype(jnp.bfloat16)
     stores = []
-    for n, block in enumerate((x[:, :top], ends)):
-        moved = dot(mixed[...], block)
-        for at in range(0, block.shape[1], features):
-            here = place(fars[(n * top + at) // features])
-            kept = p * tile[:, here].astype(jnp.float32)
-            out[:, here] = (kept + moved[:, at : at + features]).astype(jnp.bfloat16)
-            store = pltpu.make_async_copy(out.at[:, here], out_hbm.at[:, here], sems.at[1 + len(stores)])
-            store.start()
-            stores.append(store)
+    for at, stop in zip(ROWS, ROWS[1:] + (rows,)):
+        some = slice(at, stop)
+        mixed = (dot(image[some, :], q[...]) + q_m * image[some, :].astype(jnp.float32)).astype(jnp.bfloat16)
+        for n, block in enumerate((x[:, :top], ends)):
+            moved = dot(mixed, block)
+            for side in range(0, block.shape[1], features):
+                here = place(fars[(n * top + side) // features])
+                kept = p * tile[some, here].astype(jnp.float32)
+                out[some, here] = (kept + moved[:, side : side + features]).astype(jnp.bfloat16)
+        store = pltpu.make_async_copy(out.at[some, :], out_hbm.at[some, :], sems.at[1 + len(stores)])
+        store.start()
+        stores.append(store)
     for store in stores:
         store.wait()
 
@@ -225,8 +227,8 @@
         scratch_shapes=[scratch(rows, width)] * 2
         + [scratch(tokens, 2 * features), scratch(2 * features, tokens)]
         + [scratch(tokens, tokens)] * 9
-        + [scratch(rows, tokens)] * 2
-        + [pltpu.SemaphoreType.DMA((1 + members,))],
+        + [scratch(rows, tokens)]
+        + [pltpu.SemaphoreType.DMA((1 + len(ROWS),))],
         compiler_params=pltpu.CompilerParams(vmem_limit_bytes=51 * 2**20),
         cost_estimate=pl.CostEstimate(flops=5 * 10**9, bytes_accessed=0, transcendentals=0),
         name="whole_block",
@@ -237,7 +239,7 @@
     features, members = factor_inputs.shape[2], lax.axis_size("grad")
     tokens = factor_inputs.shape[0] * lax.axis_size("dp")
     tile = gradients[0]
-    if tokens < features * members and features % 128 == 0 and (members, lax.axis_size("dp")) == (8, 4):
+    if tokens < features * members and features % 128 == 0 and (members, lax.axis_size("dp"), len(tile)) == (8, 4, 768):
         result = by_tokens(factor_inputs, tile)
     else:
         result = by_features(gather_block(factor_inputs), tile)

time: 27.2 us -> 27.4 us (level)
  no operation moved by 1% of the time
where the time goes in v17:
time: 27.4 us; the launch traced here: 27.2 us
  starting transfers between devices  11 us (40%)
  Pallas kernels  7.98 us (29%)
  waiting for transfers between devices  7.34 us (27%)
  local copies, waits for them, and re-layouts  0.93 us (3%)
    pallas_call x1, Pallas kernels, by_tokens(): pl.pallas_call(functools.partial(last_kernel, fars), out_shape=shape(rows...  7.03 us
    ppermute x3, starting transfers between devices, by_tokens(): lax.ppermute(parts[far], 'dp', [(i, (i + far) % replicas) for i in range(...  7.01 us
    ppermute x7, waiting for transfers between devices, swap(): return lax.ppermute(value, 'grad', [(i, i ^ far) for i in range(members)])  4.8 us
    ppermute x7, starting transfers between devices, swap(): return lax.ppermute(value, 'grad', [(i, i ^ far) for i in range(members)])  3.95 us
    ppermute x3, waiting for transfers between devices, by_tokens(): lax.ppermute(parts[far], 'dp', [(i, (i + far) % replicas) for i in range(...  2.54 us
    unnamed x5, local copies, waits for them, and re-layouts  0.92 us
    pallas_call x1, Pallas kernels, by_tokens(): pl.pallas_call(first_kernel, out_shape=[shape(tokens, early), shape(early...  0.67 us
  transfers between devices with their start and end apart: 10, of which 7 were waited for; matrix products, arithmetic and copies ran while one was open for 0% of the time, Pallas kernels for 2%

profile of v17, /device:TPU:0, one launch (start us, length us, event | category | flops | bytes accessed | tf_op | source)
XLA Modules:
  0.0 27.2 jit_solution(1585125951164392410)
XLA Ops:
  0.0 0.0 copy-start
  0.0 0.9 %copy-done = bf16[128,4,128]{2,1,0:T(4,128)(2,1)S(1)} copy-done((bf16[128,4,128]{2,1,0:T(4,128)(2,1)S(1)}, bf16[128,4,128]{2,1,0:T(4,128)(2,1)}, u32[]{:S(2)}) %copy-start) | copy-done | bytes 131096
  0.9 0.3 %split_blocks.1 = (bf16[128,128]{1,0:T(8,128)(2,1)S(1)}, bf16[128,128]{1,0:T(8,128)(2,1)S(1)}, bf16[128,128]{1,0:T(8,128)(2,1)S(1)}, bf16[128,128]{1,0:T(8,128)(2,1)S(1)}) custom-call(bf16[512,128]{1,0:T(8,128)(2,1)S(1)} %bitcast.3), custom_call_target="tpu_custom_call" | custom-call | tf_op jit(solution)/shard_map/split_blocks/pallas_call | solution.py:56
  1.2 3.1 %collective-permute-start = (bf16[128,128]{1,0:T(8,128)(2,1)S(1)}, bf16[128,128]{1,0:T(8,128)(2,1)S(1)}, u32[]{:S(2)}, u32[]{:S(2)}) collective-permute-start(bf16[128,128]{1,0:T(8,128)(2,1)S(1)} %get-tuple-element.13), channel_id=1, source_target_pairs={{0,8},{8,16},{16,24},{24,0},{1,9},{9,17},{17,25},{25,1},{2,10},{10... | collective-permute-start | bytes 98312 | tf_op jit(solution)/shard_map/ppermute | solution.py:203
  4.3 2.6 %collective-permute-start.1 = (bf16[128,128]{1,0:T(8,128)(2,1)S(1)}, bf16[128,128]{1,0:T(8,128)(2,1)S(1)}, u32[]{:S(2)}, u32[]{:S(2)}) collective-permute-start(bf16[128,128]{1,0:T(8,128)(2,1)S(1)} %get-tuple-element.14), channel_id=1, source_target_pairs={{0,16},{8,24},{16,0},{24,8},{1,17},{9,25},{17,1},{25,9},{2,18},{10... | collective-permute-start | bytes 98312 | tf_op jit(solution)/shard_map/ppermute | solution.py:203
  6.9 1.3 %collective-permute-start.2 = (bf16[128,128]{1,0:T(8,128)(2,1)S(1)}, bf16[128,128]{1,0:T(8,128)(2,1)S(1)}, u32[]{:S(2)}, u32[]{:S(2)}) collective-permute-start(bf16[128,128]{1,0:T(8,128)(2,1)S(1)} %get-tuple-element.15), channel_id=1, source_target_pairs={{0,24},{8,0},{16,8},{24,16},{1,25},{9,1},{17,9},{25,17},{2,26},{10... | collective-permute-start | bytes 98312 | tf_op jit(solution)/shard_map/ppermute | solution.py:203
  8.2 0.0 collective-permute-done
  8.2 1.2 %collective-permute-done.1 = bf16[128,128]{1,0:T(8,128)(2,1)S(1)} collective-permute-done((bf16[128,128]{1,0:T(8,128)(2,1)S(1)}, bf16[128,128]{1,0:T(8,128)(2,1)S(1)}, u32[]{:S(2)}, u32[]{:S(2)}) %collective-permute-start.1) | collective-permute-done | bytes 32800 | tf_op jit(solution)/shard_map/ppermute | solution.py:203
  9.4 1.3 %collective-permute-done.2 = bf16[128,128]{1,0:T(8,128)(2,1)S(1)} collective-permute-done((bf16[128,128]{1,0:T(8,128)(2,1)S(1)}, bf16[128,128]{1,0:T(8,128)(2,1)S(1)}, u32[]{:S(2)}, u32[]{:S(2)}) %collective-permute-start.2) | collective-permute-done | bytes 32800 | tf_op jit(solution)/shard_map/ppermute | solution.py:203
  10.8 2.4 %collective-permute-start.8 = (bf16[512,128]{1,0:T(8,128)(2,1)S(1)}, bf16[512,128]{1,0:T(8,128)(2,1)S(1)}, u32[]{:S(2)}, u32[]{:S(2)}) collective-permute-start(bf16[512,128]{1,0:T(8,128)(2,1)S(1)} %constant_dynamic-update-slice_fusion.refs_0_), channel_id=1, source_target_pairs={{0,6},{1,7},{2,4},{3,5},{4,2},{5,3},{6,0},{7,1},{8,14},{9,15},{10,... | collective-permute-start | bytes 393224 | tf_op jit(solution)/shard_map/ppermute | solution.py:199
  13.2 0.5 %collective-permute-start.5 = (bf16[512,128]{1,0:T(8,128)(2,1)S(1)}, bf16[512,128]{1,0:T(8,128)(2,1)S(1)}, u32[]{:S(2)}, u32[]{:S(2)}) collective-permute-start(bf16[512,128]{1,0:T(8,128)(2,1)S(1)} %constant_dynamic-update-slice_fusion.refs_0_), channel_id=1, source_target_pairs={{0,2},{1,3},{2,0},{3,1},{4,6},{5,7},{6,4},{7,5},{8,10},{9,11},{10,... | collective-permute-start | bytes 393224 | tf_op jit(solution)/shard_map/ppermute | solution.py:199
  13.8 0.5 %collective-permute-start.3 = (bf16[512,128]{1,0:T(8,128)(2,1)S(1)}, bf16[512,128]{1,0:T(8,128)(2,1)S(1)}, u32[]{:S(2)}, u32[]{:S(2)}) collective-permute-start(bf16[512,128]{1,0:T(8,128)(2,1)S(1)} %constant_dynamic-update-slice_fusion.refs_0_), channel_id=1, source_target_pairs={{0,4},{1,5},{2,6},{3,7},{4,0},{5,1},{6,2},{7,3},{8,12},{9,13},{10,... | collective-permute-start | bytes 393224 | tf_op jit(solution)/shard_map/ppermute | solution.py:199
  14.3 0.0 collective-permute-start.7
  14.3 3.0 %collective-permute-done.8.refs_2_ = bf16[512,128]{1,0:T(8,128)(2,1)S(1)} collective-permute-done((bf16[512,128]{1,0:T(8,128)(2,1)S(1)}, bf16[512,128]{1,0:T(8,128)(2,1)S(1)}, u32[]{:S(2)}, u32[]{:S(2)}) %collective-permute-start.8) | collective-permute-done | bytes 131104 | tf_op jit(solution)/shard_map/ppermute | solution.py:199
  17.3 0.0 collective-permute-start.9
  17.3 1.3 %collective-permute-done.5.refs_5_ = bf16[512,128]{1,0:T(8,128)(2,1)S(1)} collective-permute-done((bf16[512,128]{1,0:T(8,128)(2,1)S(1)}, bf16[512,128]{1,0:T(8,128)(2,1)S(1)}, u32[]{:S(2)}, u32[]{:S(2)}) %collective-permute-start.5) | collective-permute-done | bytes 131104 | tf_op jit(solution)/shard_map/ppermute | solution.py:199
  18.7 0.0 collective-permute-start.6
  18.7 0.1 collective-permute-done.3.refs_4_
  18.7 0.5 %collective-permute-start.4 = (bf16[512,128]{1,0:T(8,128)(2,1)S(1)}, bf16[512,128]{1,0:T(8,128)(2,1)S(1)}, u32[]{:S(2)}, u32[]{:S(2)}) collective-permute-start(bf16[512,128]{1,0:T(8,128)(2,1)S(1)} %collective-permute-done.3.refs_4_), channel_id=1, source_target_pairs={{0,1},{1,0},{2,3},{3,2},{4,5},{5,4},{6,7},{7,6},{8,9},{9,8},{10,11... | collective-permute-start | bytes 393224 | tf_op jit(solution)/shard_map/ppermute | solution.py:199
  19.2 0.0 collective-permute-done.7.refs_1_
  19.2 0.0 collective-permute-done.9.refs_3_
  19.2 0.7 %first_pieces.1 = (bf16[512,768]{1,0:T(8,128)(2,1)S(1)}, bf16[768,512]{1,0:T(8,128)(2,1)S(1)}, f32[512,512]{1,0:T(8,128)S(1)}) custom-call(bf16[512,128]{1,0:T(8,128)(2,1)S(1)} %constant_dynamic-update-slice_fusion.refs_0_, bf16[512,128]{1,0:T(8,128)(2,1)S(1)} %collective-permute-done.7.refs_1_, bf16[512,128]{1,0:T(8,128)(2,1)S(1)} %collective-permute-done.8.refs_2_, ...), custom_call_target="tpu_custom_call" | custom-call | flops 400000000 | tf_op jit(solution)/shard_map/first_pieces/pallas_call | solution.py:213
  19.9 0.2 collective-permute-done.6.late1
  20.0 0.2 collective-permute-done.4.late0
  20.2 7.0 %whole_block.1 = bf16[768,1024]{1,0:T(8,128)(2,1)} custom-call(bf16[512,128]{1,0:T(8,128)(2,1)S(1)} %collective-permute-done.4.late0, bf16[512,128]{1,0:T(8,128)(2,1)S(1)} %collective-permute-done.6.late1, bf16[512,768]{1,0:T(8,128)(2,1)S(1)} %get-tuple-element.16.x, bf16[768,512]{1,0:T(8,128)(2,1)S(1)} %get-tuple-element.17.xt, ...), custom_call_target="tpu_custom_call" | custom-call | flops 5000000000 | tf_op jit(solution)/shard_map/whole_block/pallas_call | solution.py:222
  (4 shorter events, 0.0 us)
Async XLA Ops:
  0.0 0.9 %copy-start = (bf16[128,4,128]{2,1,0:T(4,128)(2,1)S(1)}, bf16[128,4,128]{2,1,0:T(4,128)(2,1)}, u32[]{:S(2)}) copy-start(bf16[128,4,128]{2,1,0:T(4,128)(2,1)} %param.2) | copy-start | bytes 393220
  1.2 7.0 %collective-permute-start = (bf16[128,128]{1,0:T(8,128)(2,1)S(1)}, bf16[128,128]{1,0:T(8,128)(2,1)S(1)}, u32[]{:S(2)}, u32[]{:S(2)}) collective-permute-start(bf16[128,128]{1,0:T(8,128)(2,1)S(1)} %get-tuple-element.13), channel_id=1, source_target_pairs={{0,8},{8,16},{16,24},{24,0},{1,9},{9,17},{17,25},{25,1},{2,10},{10... | collective-permute-start | bytes 98312 | tf_op jit(solution)/shard_map/ppermute | solution.py:203
  4.3 5.2 %collective-permute-start.1 = (bf16[128,128]{1,0:T(8,128)(2,1)S(1)}, bf16[128,128]{1,0:T(8,128)(2,1)S(1)}, u32[]{:S(2)}, u32[]{:S(2)}) collective-permute-start(bf16[128,128]{1,0:T(8,128)(2,1)S(1)} %get-tuple-element.14), channel_id=1, source_target_pairs={{0,16},{8,24},{16,0},{24,8},{1,17},{9,25},{17,1},{25,9},{2,18},{10... | collective-permute-start | bytes 98312 | tf_op jit(solution)/shard_map/ppermute | solution.py:203
  6.9 3.9 %collective-permute-start.2 = (bf16[128,128]{1,0:T(8,128)(2,1)S(1)}, bf16[128,128]{1,0:T(8,128)(2,1)S(1)}, u32[]{:S(2)}, u32[]{:S(2)}) collective-permute-start(bf16[128,128]{1,0:T(8,128)(2,1)S(1)} %get-tuple-element.15), channel_id=1, source_target_pairs={{0,24},{8,0},{16,8},{24,16},{1,25},{9,1},{17,9},{25,17},{2,26},{10... | collective-permute-start | bytes 98312 | tf_op jit(solution)/shard_map/ppermute | solution.py:203
  10.8 6.5 %collective-permute-start.8 = (bf16[512,128]{1,0:T(8,128)(2,1)S(1)}, bf16[512,128]{1,0:T(8,128)(2,1)S(1)}, u32[]{:S(2)}, u32[]{:S(2)}) collective-permute-start(bf16[512,128]{1,0:T(8,128)(2,1)S(1)} %constant_dynamic-update-slice_fusion.refs_0_), channel_id=1, source_target_pairs={{0,6},{1,7},{2,4},{3,5},{4,2},{5,3},{6,0},{7,1},{8,14},{9,15},{10,... | collective-permute-start | bytes 393224 | tf_op jit(solution)/shard_map/ppermute | solution.py:199
  13.2 5.4 %collective-permute-start.5 = (bf16[512,128]{1,0:T(8,128)(2,1)S(1)}, bf16[512,128]{1,0:T(8,128)(2,1)S(1)}, u32[]{:S(2)}, u32[]{:S(2)}) collective-permute-start(bf16[512,128]{1,0:T(8,128)(2,1)S(1)} %constant_dynamic-update-slice_fusion.refs_0_), channel_id=1, source_target_pairs={{0,2},{1,3},{2,0},{3,1},{4,6},{5,7},{6,4},{7,5},{8,10},{9,11},{10,... | collective-permute-start | bytes 393224 | tf_op jit(solution)/shard_map/ppermute | solution.py:199
  13.8 5.0 %collective-permute-start.3 = (bf16[512,128]{1,0:T(8,128)(2,1)S(1)}, bf16[512,128]{1,0:T(8,128)(2,1)S(1)}, u32[]{:S(2)}, u32[]{:S(2)}) collective-permute-start(bf16[512,128]{1,0:T(8,128)(2,1)S(1)} %constant_dynamic-update-slice_fusion.refs_0_), channel_id=1, source_target_pairs={{0,4},{1,5},{2,6},{3,7},{4,0},{5,1},{6,2},{7,3},{8,12},{9,13},{10,... | collective-permute-start | bytes 393224 | tf_op jit(solution)/shard_map/ppermute | solution.py:199
  14.3 4.9 %collective-permute-start.7 = (bf16[512,128]{1,0:T(8,128)(2,1)S(1)}, bf16[512,128]{1,0:T(8,128)(2,1)S(1)}, u32[]{:S(2)}, u32[]{:S(2)}) collective-permute-start(bf16[512,128]{1,0:T(8,128)(2,1)S(1)} %constant_dynamic-update-slice_fusion.refs_0_), channel_id=1, source_target_pairs={{0,1},{1,0},{2,3},{3,2},{4,5},{5,4},{6,7},{7,6},{8,9},{9,8},{10,11... | collective-permute-start | bytes 393224 | tf_op jit(solution)/shard_map/ppermute | solution.py:199
  17.3 1.9 %collective-permute-start.9 = (bf16[512,128]{1,0:T(8,128)(2,1)S(1)}, bf16[512,128]{1,0:T(8,128)(2,1)S(1)}, u32[]{:S(2)}, u32[]{:S(2)}) collective-permute-start(bf16[512,128]{1,0:T(8,128)(2,1)S(1)} %collective-permute-done.8.refs_2_), channel_id=1, source_target_pairs={{0,1},{1,0},{2,3},{3,2},{4,5},{5,4},{6,7},{7,6},{8,9},{9,8},{10,11... | collective-permute-start | bytes 393224 | tf_op jit(solution)/shard_map/ppermute | solution.py:199
  18.7 1.3 %collective-permute-start.6 = (bf16[512,128]{1,0:T(8,128)(2,1)S(1)}, bf16[512,128]{1,0:T(8,128)(2,1)S(1)}, u32[]{:S(2)}, u32[]{:S(2)}) collective-permute-start(bf16[512,128]{1,0:T(8,128)(2,1)S(1)} %collective-permute-done.5.refs_5_), channel_id=1, source_target_pairs={{0,1},{1,0},{2,3},{3,2},{4,5},{5,4},{6,7},{7,6},{8,9},{9,8},{10,11... | collective-permute-start | bytes 393224 | tf_op jit(solution)/shard_map/ppermute | solution.py:199
  18.7 1.5 %collective-permute-start.4 = (bf16[512,128]{1,0:T(8,128)(2,1)S(1)}, bf16[512,128]{1,0:T(8,128)(2,1)S(1)}, u32[]{:S(2)}, u32[]{:S(2)}) collective-permute-start(bf16[512,128]{1,0:T(8,128)(2,1)S(1)} %collective-permute-done.3.refs_4_), channel_id=1, source_target_pairs={{0,1},{1,0},{2,3},{3,2},{4,5},{5,4},{6,7},{7,6},{8,9},{9,8},{10,11... | collective-permute-start | bytes 393224 | tf_op jit(solution)/shard_map/ppermute | solution.py:199

commit v18 on v12

--- a/solution.py
+++ b/solution.py
@@ -9,6 +9,7 @@
 
 ITERS = 4
 DAMPING = 0.01
+SPLIT_VMEM = 56393728
 WHOLE = pl.BlockSpec(memory_space=pltpu.VMEM)
 ANYWHERE = pl.BlockSpec(memory_space=pl.ANY)
 
@@ -38,16 +39,28 @@
     return result
 
 
-def split_kernel(fars, x_ref, *out_refs):
+def split_kernel(fars, x_hbm, *refs):
+    *out_refs, x, sems = refs
+    count = sems.shape[0]
+    step = x.shape[0] // count
+    loads = [
+        pltpu.make_async_copy(x_hbm.at[pl.ds(n * step, step), :], x.at[pl.ds(n * step, step), :], sems.at[n])
+        for n in range(count)
+    ]
+    for load in loads:
+        load.start()
     replicas, tokens = len(out_refs), out_refs[0].shape[0]
     here = lax.axis_index("dp")
-    x = x_ref[...]
     rows = lax.broadcasted_iota(jnp.int32, (tokens, tokens * replicas), 0)
     cols = lax.broadcasted_iota(jnp.int32, (tokens, tokens * replicas), 1)
     offset = cols - rows * replicas
-    for far, out_ref in zip(fars, out_refs):
-        choice = jnp.where(offset == lax.rem(here + far, replicas), 1.0, 0.0).astype(jnp.bfloat16)
-        out_ref[...] = dot(choice, x).astype(jnp.bfloat16)
+    choices = [
+        jnp.where(offset == lax.rem(here + far, replicas), 1.0, 0.0).astype(jnp.bfloat16) for far in fars
+    ]
+    for load in loads:
+        load.wait()
+    for choice, out_ref in zip(choices, out_refs):
+        out_ref[...] = dot(choice, x[...]).astype(jnp.bfloat16)
 
 
 def split_blocks(factor_inputs, fars):
@@ -55,9 +68,10 @@
     return pl.pallas_call(
         functools.partial(split_kernel, fars),
         out_shape=[jax.ShapeDtypeStruct((tokens, features), factor_inputs.dtype)] * blocks,
-        in_specs=[WHOLE],
+        in_specs=[ANYWHERE],
         out_specs=[WHOLE] * blocks,
-        compiler_params=pltpu.CompilerParams(vmem_limit_bytes=16 * 2**20),
+        scratch_shapes=[pltpu.VMEM((tokens * blocks, features), factor_inputs.dtype), pltpu.SemaphoreType.DMA((2,))],
+        compiler_params=pltpu.CompilerParams(vmem_limit_bytes=SPLIT_VMEM),
         name="split_blocks",
     )(factor_inputs.reshape(tokens * blocks, features))
 
@@ -212,12 +226,11 @@
     def swap(value, far):
         return lax.ppermute(value, "grad", [(i, i ^ far) for i in range(members)])
 
-    order = (0, 2, 1, 3)
-    parts = dict(zip(order, split_blocks(factor_inputs, order)))
-    for far in order[1:]:
+    parts = list(split_blocks(factor_inputs, range(replicas)))
+    for far in range(1, replicas):
         parts[far] = lax.ppermute(parts[far], "dp", [(i, (i + far) % replicas) for i in range(replicas)])
-    own = jnp.concatenate([parts[far] for far in order], axis=0)
-    fars = (0, 1, 6, 7, 4, 2, 5, 3)
+    own = jnp.concatenate(parts, axis=0)
+    fars = (0, 1, 6, 7, 2, 4, 3, 5)
     pieces = {0: own}
     for far in (2, 4, 6):
         pieces[far] = swap(own, far)

time: 27.2 us -> 27 us (level)
  local copies, waits for them, and re-layouts: 0.93 us -> 0.03 us
  Pallas kernels: 7.51 us -> 8.4 us
  starting transfers between devices: 11.5 us -> 11 us
    ppermute x3, starting transfers between devices: 7.93 us -> 7.01 us  [by_tokens(): lax.ppermute(parts[far], 'dp', [(i, (i + far) % replicas) for i in range(...]
    unnamed x5 -> x3, local copies, waits for them, and re-layouts: 0.92 us -> 0.02 us
    pallas_call x1, Pallas kernels: 0.28 us -> 1.18 us  [split_blocks(): pl.pallas_call(functools.partial(split_kernel, fars), out_shape=[jax.Shap...]
    ppermute x3, waiting for transfers between devices: 1.99 us -> 2.54 us  [by_tokens(): lax.ppermute(parts[far], 'dp', [(i, (i + far) % replicas) for i in range(...]
    ppermute x7, starting transfers between devices: 3.59 us -> 4 us  [swap(): return lax.ppermute(value, 'grad', [(i, i ^ far) for i in range(members)])]
    ppermute x7, waiting for transfers between devices: 5.1 us -> 4.8 us  [swap(): return lax.ppermute(value, 'grad', [(i, i ^ far) for i in range(members)])]
where the time goes in v18:
time: 27 us; the launch traced here: 26.8 us
  starting transfers between devices  11 us (41%)
  Pallas kernels  8.4 us (31%)
  waiting for transfers between devices  7.34 us (27%)
    ppermute x3, starting transfers between devices, by_tokens(): lax.ppermute(parts[far], 'dp', [(i, (i + far) % replicas) for i in range(...  7.01 us
    pallas_call x1, Pallas kernels, by_tokens(): pl.pallas_call(functools.partial(last_kernel, fars), out_shape=shape(rows...  6.56 us
    ppermute x7, waiting for transfers between devices, swap(): return lax.ppermute(value, 'grad', [(i, i ^ far) for i in range(members)])  4.8 us
    ppermute x7, starting transfers between devices, swap(): return lax.ppermute(value, 'grad', [(i, i ^ far) for i in range(members)])  4 us
    ppermute x3, waiting for transfers between devices, by_tokens(): lax.ppermute(parts[far], 'dp', [(i, (i + far) % replicas) for i in range(...  2.54 us
    pallas_call x1, Pallas kernels, split_blocks(): pl.pallas_call(functools.partial(split_kernel, fars), out_shape=[jax.Shap...  1.18 us
    pallas_call x1, Pallas kernels, by_tokens(): pl.pallas_call(first_kernel, out_shape=[shape(tokens, early), shape(early...  0.67 us
  transfers between devices with their start and end apart: 10, of which 6 were waited for; matrix products, arithmetic and copies ran while one was open for 0% of the time, Pallas kernels for 2%

profile of v18, /device:TPU:0, one launch (start us, length us, event | category | flops | bytes accessed | tf_op | source)
XLA Modules:
  0.0 26.8 jit_solution(2017206380132381527)
XLA Ops:
  0.0 1.2 %split_blocks.1 = (bf16[128,128]{1,0:T(8,128)(2,1)S(1)}, bf16[128,128]{1,0:T(8,128)(2,1)S(1)}, bf16[128,128]{1,0:T(8,128)(2,1)S(1)}, bf16[128,128]{1,0:T(8,128)(2,1)S(1)}) custom-call(bf16[512,128]{1,0:T(8,128)(2,1)} %bitcast.3), custom_call_target="tpu_custom_call" | custom-call | tf_op jit(solution)/shard_map/split_blocks/pallas_call | solution.py:68
  1.2 3.1 %collective-permute-start = (bf16[128,128]{1,0:T(8,128)(2,1)S(1)}, bf16[128,128]{1,0:T(8,128)(2,1)S(1)}, u32[]{:S(2)}, u32[]{:S(2)}) collective-permute-start(bf16[128,128]{1,0:T(8,128)(2,1)S(1)} %get-tuple-element.13), channel_id=1, source_target_pairs={{0,8},{8,16},{16,24},{24,0},{1,9},{9,17},{17,25},{25,1},{2,10},{10... | collective-permute-start | bytes 98312 | tf_op jit(solution)/shard_map/ppermute | solution.py:231
  4.3 2.6 %collective-permute-start.1 = (bf16[128,128]{1,0:T(8,128)(2,1)S(1)}, bf16[128,128]{1,0:T(8,128)(2,1)S(1)}, u32[]{:S(2)}, u32[]{:S(2)}) collective-permute-start(bf16[128,128]{1,0:T(8,128)(2,1)S(1)} %get-tuple-element.14), channel_id=1, source_target_pairs={{0,16},{8,24},{16,0},{24,8},{1,17},{9,25},{17,1},{25,9},{2,18},{10... | collective-permute-start | bytes 98312 | tf_op jit(solution)/shard_map/ppermute | solution.py:231
  6.9 1.3 %collective-permute-start.2 = (bf16[128,128]{1,0:T(8,128)(2,1)S(1)}, bf16[128,128]{1,0:T(8,128)(2,1)S(1)}, u32[]{:S(2)}, u32[]{:S(2)}) collective-permute-start(bf16[128,128]{1,0:T(8,128)(2,1)S(1)} %get-tuple-element.15), channel_id=1, source_target_pairs={{0,24},{8,0},{16,8},{24,16},{1,25},{9,1},{17,9},{25,17},{2,26},{10... | collective-permute-start | bytes 98312 | tf_op jit(solution)/shard_map/ppermute | solution.py:231
  8.2 0.0 collective-permute-done
  8.2 1.2 %collective-permute-done.1 = bf16[128,128]{1,0:T(8,128)(2,1)S(1)} collective-permute-done((bf16[128,128]{1,0:T(8,128)(2,1)S(1)}, bf16[128,128]{1,0:T(8,128)(2,1)S(1)}, u32[]{:S(2)}, u32[]{:S(2)}) %collective-permute-start.1) | collective-permute-done | bytes 32800 | tf_op jit(solution)/shard_map/ppermute | solution.py:231
  9.4 1.3 %collective-permute-done.2 = bf16[128,128]{1,0:T(8,128)(2,1)S(1)} collective-permute-done((bf16[128,128]{1,0:T(8,128)(2,1)S(1)}, bf16[128,128]{1,0:T(8,128)(2,1)S(1)}, u32[]{:S(2)}, u32[]{:S(2)}) %collective-permute-start.2) | collective-permute-done | bytes 32800 | tf_op jit(solution)/shard_map/ppermute | solution.py:231
  10.8 2.4 %collective-permute-start.8 = (bf16[512,128]{1,0:T(8,128)(2,1)S(1)}, bf16[512,128]{1,0:T(8,128)(2,1)S(1)}, u32[]{:S(2)}, u32[]{:S(2)}) collective-permute-start(bf16[512,128]{1,0:T(8,128)(2,1)S(1)} %constant_dynamic-update-slice_fusion.refs_0_), channel_id=1, source_target_pairs={{0,6},{1,7},{2,4},{3,5},{4,2},{5,3},{6,0},{7,1},{8,14},{9,15},{10,... | collective-permute-start | bytes 393224 | tf_op jit(solution)/shard_map/ppermute | solution.py:227
  13.2 0.5 %collective-permute-start.5 = (bf16[512,128]{1,0:T(8,128)(2,1)S(1)}, bf16[512,128]{1,0:T(8,128)(2,1)S(1)}, u32[]{:S(2)}, u32[]{:S(2)}) collective-permute-start(bf16[512,128]{1,0:T(8,128)(2,1)S(1)} %constant_dynamic-update-slice_fusion.refs_0_), channel_id=1, source_target_pairs={{0,4},{1,5},{2,6},{3,7},{4,0},{5,1},{6,2},{7,3},{8,12},{9,13},{10,... | collective-permute-start | bytes 393224 | tf_op jit(solution)/shard_map/ppermute | solution.py:227
  13.7 0.5 %collective-permute-start.3 = (bf16[512,128]{1,0:T(8,128)(2,1)S(1)}, bf16[512,128]{1,0:T(8,128)(2,1)S(1)}, u32[]{:S(2)}, u32[]{:S(2)}) collective-permute-start(bf16[512,128]{1,0:T(8,128)(2,1)S(1)} %constant_dynamic-update-slice_fusion.refs_0_), channel_id=1, source_target_pairs={{0,2},{1,3},{2,0},{3,1},{4,6},{5,7},{6,4},{7,5},{8,10},{9,11},{10,... | collective-permute-start | bytes 393224 | tf_op jit(solution)/shard_map/ppermute | solution.py:227
  14.3 0.0 collective-permute-start.7
  14.3 3.6 %collective-permute-done.8.refs_2_ = bf16[512,128]{1,0:T(8,128)(2,1)S(1)} collective-permute-done((bf16[512,128]{1,0:T(8,128)(2,1)S(1)}, bf16[512,128]{1,0:T(8,128)(2,1)S(1)}, u32[]{:S(2)}, u32[]{:S(2)}) %collective-permute-start.8) | collective-permute-done | bytes 131104 | tf_op jit(solution)/shard_map/ppermute | solution.py:227
  17.8 0.0 collective-permute-start.9
  17.8 0.9 %collective-permute-done.5.refs_5_ = bf16[512,128]{1,0:T(8,128)(2,1)S(1)} collective-permute-done((bf16[512,128]{1,0:T(8,128)(2,1)S(1)}, bf16[512,128]{1,0:T(8,128)(2,1)S(1)}, u32[]{:S(2)}, u32[]{:S(2)}) %collective-permute-start.5) | collective-permute-done | bytes 131104 | tf_op jit(solution)/shard_map/ppermute | solution.py:227
  18.7 0.0 collective-permute-start.6
  18.7 0.0 collective-permute-done.3.refs_4_
  18.7 0.5 %collective-permute-start.4 = (bf16[512,128]{1,0:T(8,128)(2,1)S(1)}, bf16[512,128]{1,0:T(8,128)(2,1)S(1)}, u32[]{:S(2)}, u32[]{:S(2)}) collective-permute-start(bf16[512,128]{1,0:T(8,128)(2,1)S(1)} %collective-permute-done.3.refs_4_), channel_id=1, source_target_pairs={{0,1},{1,0},{2,3},{3,2},{4,5},{5,4},{6,7},{7,6},{8,9},{9,8},{10,11... | collective-permute-start | bytes 393224 | tf_op jit(solution)/shard_map/ppermute | solution.py:227
  19.2 0.0 collective-permute-done.7.refs_1_
  19.2 0.0 collective-permute-done.9.refs_3_
  19.2 0.7 %first_pieces.1 = (bf16[512,768]{1,0:T(8,128)(2,1)S(1)}, bf16[768,512]{1,0:T(8,128)(2,1)S(1)}, f32[512,512]{1,0:T(8,128)S(1)}) custom-call(bf16[512,128]{1,0:T(8,128)(2,1)S(1)} %constant_dynamic-update-slice_fusion.refs_0_, bf16[512,128]{1,0:T(8,128)(2,1)S(1)} %collective-permute-done.7.refs_1_, bf16[512,128]{1,0:T(8,128)(2,1)S(1)} %collective-permute-done.8.refs_2_, ...), custom_call_target="tpu_custom_call" | custom-call | flops 400000000 | tf_op jit(solution)/shard_map/first_pieces/pallas_call | solution.py:241
  19.9 0.2 collective-permute-done.6.late1
  20.1 0.2 collective-permute-done.4.late0
  20.3 6.6 %whole_block.1 = bf16[768,1024]{1,0:T(8,128)(2,1)} custom-call(bf16[512,128]{1,0:T(8,128)(2,1)S(1)} %collective-permute-done.4.late0, bf16[512,128]{1,0:T(8,128)(2,1)S(1)} %collective-permute-done.6.late1, bf16[512,768]{1,0:T(8,128)(2,1)S(1)} %get-tuple-element.16.x, bf16[768,512]{1,0:T(8,128)(2,1)S(1)} %get-tuple-element.17.xt, ...), custom_call_target="tpu_custom_call" | custom-call | flops 5000000000 | tf_op jit(solution)/shard_map/whole_block/pallas_call | solution.py:250
  (4 shorter events, 0.0 us)
Async XLA Ops:
  1.2 7.0 %collective-permute-start = (bf16[128,128]{1,0:T(8,128)(2,1)S(1)}, bf16[128,128]{1,0:T(8,128)(2,1)S(1)}, u32[]{:S(2)}, u32[]{:S(2)}) collective-permute-start(bf16[128,128]{1,0:T(8,128)(2,1)S(1)} %get-tuple-element.13), channel_id=1, source_target_pairs={{0,8},{8,16},{16,24},{24,0},{1,9},{9,17},{17,25},{25,1},{2,10},{10... | collective-permute-start | bytes 98312 | tf_op jit(solution)/shard_map/ppermute | solution.py:231
  4.3 5.2 %collective-permute-start.1 = (bf16[128,128]{1,0:T(8,128)(2,1)S(1)}, bf16[128,128]{1,0:T(8,128)(2,1)S(1)}, u32[]{:S(2)}, u32[]{:S(2)}) collective-permute-start(bf16[128,128]{1,0:T(8,128)(2,1)S(1)} %get-tuple-element.14), channel_id=1, source_target_pairs={{0,16},{8,24},{16,0},{24,8},{1,17},{9,25},{17,1},{25,9},{2,18},{10... | collective-permute-start | bytes 98312 | tf_op jit(solution)/shard_map/ppermute | solution.py:231
  6.9 3.9 %collective-permute-start.2 = (bf16[128,128]{1,0:T(8,128)(2,1)S(1)}, bf16[128,128]{1,0:T(8,128)(2,1)S(1)}, u32[]{:S(2)}, u32[]{:S(2)}) collective-permute-start(bf16[128,128]{1,0:T(8,128)(2,1)S(1)} %get-tuple-element.15), channel_id=1, source_target_pairs={{0,24},{8,0},{16,8},{24,16},{1,25},{9,1},{17,9},{25,17},{2,26},{10... | collective-permute-start | bytes 98312 | tf_op jit(solution)/shard_map/ppermute | solution.py:231
  10.8 7.1 %collective-permute-start.8 = (bf16[512,128]{1,0:T(8,128)(2,1)S(1)}, bf16[512,128]{1,0:T(8,128)(2,1)S(1)}, u32[]{:S(2)}, u32[]{:S(2)}) collective-permute-start(bf16[512,128]{1,0:T(8,128)(2,1)S(1)} %constant_dynamic-update-slice_fusion.refs_0_), channel_id=1, source_target_pairs={{0,6},{1,7},{2,4},{3,5},{4,2},{5,3},{6,0},{7,1},{8,14},{9,15},{10,... | collective-permute-start | bytes 393224 | tf_op jit(solution)/shard_map/ppermute | solution.py:227
  13.2 5.5 %collective-permute-start.5 = (bf16[512,128]{1,0:T(8,128)(2,1)S(1)}, bf16[512,128]{1,0:T(8,128)(2,1)S(1)}, u32[]{:S(2)}, u32[]{:S(2)}) collective-permute-start(bf16[512,128]{1,0:T(8,128)(2,1)S(1)} %constant_dynamic-update-slice_fusion.refs_0_), channel_id=1, source_target_pairs={{0,4},{1,5},{2,6},{3,7},{4,0},{5,1},{6,2},{7,3},{8,12},{9,13},{10,... | collective-permute-start | bytes 393224 | tf_op jit(solution)/shard_map/ppermute | solution.py:227
  13.7 5.0 %collective-permute-start.3 = (bf16[512,128]{1,0:T(8,128)(2,1)S(1)}, bf16[512,128]{1,0:T(8,128)(2,1)S(1)}, u32[]{:S(2)}, u32[]{:S(2)}) collective-permute-start(bf16[512,128]{1,0:T(8,128)(2,1)S(1)} %constant_dynamic-update-slice_fusion.refs_0_), channel_id=1, source_target_pairs={{0,2},{1,3},{2,0},{3,1},{4,6},{5,7},{6,4},{7,5},{8,10},{9,11},{10,... | collective-permute-start | bytes 393224 | tf_op jit(solution)/shard_map/ppermute | solution.py:227
  14.3 5.0 %collective-permute-start.7 = (bf16[512,128]{1,0:T(8,128)(2,1)S(1)}, bf16[512,128]{1,0:T(8,128)(2,1)S(1)}, u32[]{:S(2)}, u32[]{:S(2)}) collective-permute-start(bf16[512,128]{1,0:T(8,128)(2,1)S(1)} %constant_dynamic-update-slice_fusion.refs_0_), channel_id=1, source_target_pairs={{0,1},{1,0},{2,3},{3,2},{4,5},{5,4},{6,7},{7,6},{8,9},{9,8},{10,11... | collective-permute-start | bytes 393224 | tf_op jit(solution)/shard_map/ppermute | solution.py:227
  17.8 1.4 %collective-permute-start.9 = (bf16[512,128]{1,0:T(8,128)(2,1)S(1)}, bf16[512,128]{1,0:T(8,128)(2,1)S(1)}, u32[]{:S(2)}, u32[]{:S(2)}) collective-permute-start(bf16[512,128]{1,0:T(8,128)(2,1)S(1)} %collective-permute-done.8.refs_2_), channel_id=1, source_target_pairs={{0,1},{1,0},{2,3},{3,2},{4,5},{5,4},{6,7},{7,6},{8,9},{9,8},{10,11... | collective-permute-start | bytes 393224 | tf_op jit(solution)/shard_map/ppermute | solution.py:227
  18.7 1.3 %collective-permute-start.6 = (bf16[512,128]{1,0:T(8,128)(2,1)S(1)}, bf16[512,128]{1,0:T(8,128)(2,1)S(1)}, u32[]{:S(2)}, u32[]{:S(2)}) collective-permute-start(bf16[512,128]{1,0:T(8,128)(2,1)S(1)} %collective-permute-done.5.refs_5_), channel_id=1, source_target_pairs={{0,1},{1,0},{2,3},{3,2},{4,5},{5,4},{6,7},{7,6},{8,9},{9,8},{10,11... | collective-permute-start | bytes 393224 | tf_op jit(solution)/shard_map/ppermute | solution.py:227
  18.7 1.5 %collective-permute-start.4 = (bf16[512,128]{1,0:T(8,128)(2,1)S(1)}, bf16[512,128]{1,0:T(8,128)(2,1)S(1)}, u32[]{:S(2)}, u32[]{:S(2)}) collective-permute-start(bf16[512,128]{1,0:T(8,128)(2,1)S(1)} %collective-permute-done.3.refs_4_), channel_id=1, source_target_pairs={{0,1},{1,0},{2,3},{3,2},{4,5},{5,4},{6,7},{7,6},{8,9},{9,8},{10,11... | collective-permute-start | bytes 393224 | tf_op jit(solution)/shard_map/ppermute | solution.py:227

commit v19 on v12

--- a/solution.py
+++ b/solution.py
@@ -73,7 +73,7 @@
 
 
 def last_kernel(fars, late0, late1, x, xt, gram_in, tile_hbm, out_hbm, *refs):
-    tile, out, late, late_t, k1, k2, e2, g, z, h, a, k, q, image, mixed, sems = refs
+    tile, out, late, late_t, k1, k2, e2, g, z, h, k, image, by_g, by_h, mixed, sems = refs
     load = pltpu.make_async_copy(tile_hbm, tile, sems.at[0])
     load.start()
     member = lax.axis_index("grad")
@@ -128,7 +128,8 @@
     add_sums(len(blocks), xt[...], late[...])
     column_sums[-1] = column_sums[-1] + jnp.sum(jnp.abs(dot(late_t[...], late[...])), axis=0, keepdims=True)
     load.wait()
-    move(halves[0])
+    for some in halves:
+        move(some)
 
     largest = column_sums[-1]
     for column, row in zip(column_sums[:-1], row_sums):
@@ -144,11 +145,8 @@
     h_m = zeta + (1.0 + eps2) * eps2 + eps2
     k_m = eps8 + (1.0 + zeta) * zeta + zeta + 1.0 + eps8
     k_z = 1.0 + 3.0 * zeta
-    a_m = g_m * h_m
     beta = (1.0 + zeta) * (1.0 + eps8)
-    q_m = a_m * k_m + beta * g_m + (1.0 + eps2) * beta
     last = -c * c * (1.0 / tokens)
-    q_m = q_m * last
     p = c * (1.0 + eps) * (1.0 + eps2) * beta
 
     def wide(ref, r, some):
@@ -167,22 +165,19 @@
         return value, value + (1.0 + eps2) * square
 
     symmetric(e2, e2, fourth, z, h)
-    for some in halves[1:]:
-        move(some)
+
+    def apply(left, right, parts, result, scale=None):
+        for some in halves:
+            total = dot(left[...], right[:, some])
+            total = total if scale is None else total * scale
+            for weight, part in parts:
+                total = total + weight * part[:, some].astype(jnp.float32)
+            result[:, some] = total.astype(jnp.bfloat16)
+
+    apply(image, g, [(g_m, image)], by_g)
     symmetric(z, z, lambda product, r, some: [product + k_z * wide(z, r, some)], k)
-    for some in halves:
-        product = dot(g[...], h[:, some])
-        for r in chunks:
-            a[r, some] = (product[r] + g_m * wide(h, r, some) + h_m * wide(g, r, some)).astype(jnp.bfloat16)
-    q_k, q_a, q_g = last * a_m, last * k_m, last * beta
-    for some in halves:
-        product = dot(k[...], a[:, some])
-        for r in chunks:
-            rest = q_k * wide(k, r, some) + q_a * wide(a, r, some) + q_g * wide(g, r, some)
-            q[r, some] = (last * product[r] + rest).astype(jnp.bfloat16)
-    for some in halves:
-        product = dot(image[...], q[:, some])
-        mixed[:, some] = (product + q_m * image[:, some].astype(jnp.float32)).astype(jnp.bfloat16)
+    apply(by_g, h, [(h_m, by_g)], by_h)
+    apply(by_h, k, [(last * (1.0 + eps2) * beta, image), (last * beta, by_g), (last * k_m, by_h)], mixed, last)
     stores = []
     for n in range(len(blocks) + 1):
         moved = dot(mixed[...], late[...] if n == len(blocks) else x[:, blocks[n]])
@@ -212,12 +207,11 @@
     def swap(value, far):
         return lax.ppermute(value, "grad", [(i, i ^ far) for i in range(members)])
 
-    order = (0, 2, 1, 3)
-    parts = dict(zip(order, split_blocks(factor_inputs, order)))
-    for far in order[1:]:
+    parts = list(split_blocks(factor_inputs, range(replicas)))
+    for far in range(1, replicas):
         parts[far] = lax.ppermute(parts[far], "dp", [(i, (i + far) % replicas) for i in range(replicas)])
-    own = jnp.concatenate([parts[far] for far in order], axis=0)
-    fars = (0, 1, 6, 7, 4, 2, 5, 3)
+    own = jnp.concatenate(parts, axis=0)
+    fars = (0, 1, 6, 7, 2, 4, 3, 5)
     pieces = {0: own}
     for far in (2, 4, 6):
         pieces[far] = swap(own, far)
@@ -241,8 +235,8 @@
         out_specs=ANYWHERE,
         scratch_shapes=[scratch(rows, width)] * 2
         + [scratch(tokens, 2 * features), scratch(2 * features, tokens)]
-        + [scratch(tokens, tokens)] * 9
-        + [scratch(rows, tokens)] * 2
+        + [scratch(tokens, tokens)] * 7
+        + [scratch(rows, tokens)] * 4
         + [pltpu.SemaphoreType.DMA((1 + members,))],
         compiler_params=pltpu.CompilerParams(vmem_limit_bytes=51 * 2**20),
         cost_estimate=pl.CostEstimate(flops=5 * 10**9, bytes_accessed=0, transcendentals=0),

time: 27.2 us -> 26.9 us (0.989)
  starting transfers between devices: 11.5 us -> 11 us
    ppermute x3, starting transfers between devices: 7.93 us -> 7.01 us  [by_tokens(): lax.ppermute(parts[far], 'dp', [(i, (i + far) % replicas) for i in range(...]
    ppermute x3, waiting for transfers between devices: 1.99 us -> 2.54 us  [by_tokens(): lax.ppermute(parts[far], 'dp', [(i, (i + far) % replicas) for i in range(...]
    ppermute x7, starting transfers between devices: 3.59 us -> 4 us  [swap(): return lax.ppermute(value, 'grad', [(i, i ^ far) for i in range(members)])]
    ppermute x7, waiting for transfers between devices: 5.1 us -> 4.8 us  [swap(): return lax.ppermute(value, 'grad', [(i, i ^ far) for i in range(members)])]
where the time goes in v19:
time: 26.9 us; the launch traced here: 26.7 us
  starting transfers between devices  11 us (41%)
  Pallas kernels  7.39 us (27%)
  waiting for transfers between devices  7.34 us (27%)
  local copies, waits for them, and re-layouts  0.93 us (3%)
    ppermute x3, starting transfers between devices, by_tokens(): lax.ppermute(parts[far], 'dp', [(i, (i + far) % replicas) for i in range(...  7.01 us
    pallas_call x1, Pallas kernels, by_tokens(): pl.pallas_call(functools.partial(last_kernel, fars), out_shape=shape(rows...  6.44 us
    ppermute x7, waiting for transfers between devices, swap(): return lax.ppermute(value, 'grad', [(i, i ^ far) for i in range(members)])  4.8 us
    ppermute x7, starting transfers between devices, swap(): return lax.ppermute(value, 'grad', [(i, i ^ far) for i in range(members)])  4 us
    ppermute x3, waiting for transfers between devices, by_tokens(): lax.ppermute(parts[far], 'dp', [(i, (i + far) % replicas) for i in range(...  2.54 us
    unnamed x5, local copies, waits for them, and re-layouts  0.92 us
    pallas_call x1, Pallas kernels, by_tokens(): pl.pallas_call(first_kernel, out_shape=[shape(tokens, early), shape(early...  0.67 us
  transfers between devices with their start and end apart: 10, of which 6 were waited for; matrix products, arithmetic and copies ran while one was open for 0% of the time, Pallas kernels for 2%

profile of v19, /device:TPU:0, one launch (start us, length us, event | category | flops | bytes accessed | tf_op | source)
XLA Modules:
  0.0 26.7 jit_solution(12785208478270990715)
XLA Ops:
  0.0 0.0 copy-start
  0.0 0.9 %copy-done = bf16[128,4,128]{2,1,0:T(4,128)(2,1)S(1)} copy-done((bf16[128,4,128]{2,1,0:T(4,128)(2,1)S(1)}, bf16[128,4,128]{2,1,0:T(4,128)(2,1)}, u32[]{:S(2)}) %copy-start) | copy-done | bytes 131096
  0.9 0.3 %split_blocks.1 = (bf16[128,128]{1,0:T(8,128)(2,1)S(1)}, bf16[128,128]{1,0:T(8,128)(2,1)S(1)}, bf16[128,128]{1,0:T(8,128)(2,1)S(1)}, bf16[128,128]{1,0:T(8,128)(2,1)S(1)}) custom-call(bf16[512,128]{1,0:T(8,128)(2,1)S(1)} %bitcast.3), custom_call_target="tpu_custom_call" | custom-call | tf_op jit(solution)/shard_map/split_blocks/pallas_call | solution.py:55
  1.2 3.1 %collective-permute-start = (bf16[128,128]{1,0:T(8,128)(2,1)S(1)}, bf16[128,128]{1,0:T(8,128)(2,1)S(1)}, u32[]{:S(2)}, u32[]{:S(2)}) collective-permute-start(bf16[128,128]{1,0:T(8,128)(2,1)S(1)} %get-tuple-element.13), channel_id=1, source_target_pairs={{0,8},{8,16},{16,24},{24,0},{1,9},{9,17},{17,25},{25,1},{2,10},{10... | collective-permute-start | bytes 98312 | tf_op jit(solution)/shard_map/ppermute | solution.py:212
  4.3 2.6 %collective-permute-start.1 = (bf16[128,128]{1,0:T(8,128)(2,1)S(1)}, bf16[128,128]{1,0:T(8,128)(2,1)S(1)}, u32[]{:S(2)}, u32[]{:S(2)}) collective-permute-start(bf16[128,128]{1,0:T(8,128)(2,1)S(1)} %get-tuple-element.14), channel_id=1, source_target_pairs={{0,16},{8,24},{16,0},{24,8},{1,17},{9,25},{17,1},{25,9},{2,18},{10... | collective-permute-start | bytes 98312 | tf_op jit(solution)/shard_map/ppermute | solution.py:212
  6.9 1.3 %collective-permute-start.2 = (bf16[128,128]{1,0:T(8,128)(2,1)S(1)}, bf16[128,128]{1,0:T(8,128)(2,1)S(1)}, u32[]{:S(2)}, u32[]{:S(2)}) collective-permute-start(bf16[128,128]{1,0:T(8,128)(2,1)S(1)} %get-tuple-element.15), channel_id=1, source_target_pairs={{0,24},{8,0},{16,8},{24,16},{1,25},{9,1},{17,9},{25,17},{2,26},{10... | collective-permute-start | bytes 98312 | tf_op jit(solution)/shard_map/ppermute | solution.py:212
  8.2 0.0 collective-permute-done
  8.2 1.2 %collective-permute-done.1 = bf16[128,128]{1,0:T(8,128)(2,1)S(1)} collective-permute-done((bf16[128,128]{1,0:T(8,128)(2,1)S(1)}, bf16[128,128]{1,0:T(8,128)(2,1)S(1)}, u32[]{:S(2)}, u32[]{:S(2)}) %collective-permute-start.1) | collective-permute-done | bytes 32800 | tf_op jit(solution)/shard_map/ppermute | solution.py:212
  9.4 1.3 %collective-permute-done.2 = bf16[128,128]{1,0:T(8,128)(2,1)S(1)} collective-permute-done((bf16[128,128]{1,0:T(8,128)(2,1)S(1)}, bf16[128,128]{1,0:T(8,128)(2,1)S(1)}, u32[]{:S(2)}, u32[]{:S(2)}) %collective-permute-start.2) | collective-permute-done | bytes 32800 | tf_op jit(solution)/shard_map/ppermute | solution.py:212
  10.8 2.4 %collective-permute-start.8 = (bf16[512,128]{1,0:T(8,128)(2,1)S(1)}, bf16[512,128]{1,0:T(8,128)(2,1)S(1)}, u32[]{:S(2)}, u32[]{:S(2)}) collective-permute-start(bf16[512,128]{1,0:T(8,128)(2,1)S(1)} %constant_dynamic-update-slice_fusion.refs_0_), channel_id=1, source_target_pairs={{0,6},{1,7},{2,4},{3,5},{4,2},{5,3},{6,0},{7,1},{8,14},{9,15},{10,... | collective-permute-start | bytes 393224 | tf_op jit(solution)/shard_map/ppermute | solution.py:208
  13.2 0.5 %collective-permute-start.5 = (bf16[512,128]{1,0:T(8,128)(2,1)S(1)}, bf16[512,128]{1,0:T(8,128)(2,1)S(1)}, u32[]{:S(2)}, u32[]{:S(2)}) collective-permute-start(bf16[512,128]{1,0:T(8,128)(2,1)S(1)} %constant_dynamic-update-slice_fusion.refs_0_), channel_id=1, source_target_pairs={{0,4},{1,5},{2,6},{3,7},{4,0},{5,1},{6,2},{7,3},{8,12},{9,13},{10,... | collective-permute-start | bytes 393224 | tf_op jit(solution)/shard_map/ppermute | solution.py:208
  13.7 0.5 %collective-permute-start.3 = (bf16[512,128]{1,0:T(8,128)(2,1)S(1)}, bf16[512,128]{1,0:T(8,128)(2,1)S(1)}, u32[]{:S(2)}, u32[]{:S(2)}) collective-permute-start(bf16[512,128]{1,0:T(8,128)(2,1)S(1)} %constant_dynamic-update-slice_fusion.refs_0_), channel_id=1, source_target_pairs={{0,2},{1,3},{2,0},{3,1},{4,6},{5,7},{6,4},{7,5},{8,10},{9,11},{10,... | collective-permute-start | bytes 393224 | tf_op jit(solution)/shard_map/ppermute | solution.py:208
  14.3 0.0 collective-permute-start.7
  14.3 3.6 %collective-permute-done.8.refs_2_ = bf16[512,128]{1,0:T(8,128)(2,1)S(1)} collective-permute-done((bf16[512,128]{1,0:T(8,128)(2,1)S(1)}, bf16[512,128]{1,0:T(8,128)(2,1)S(1)}, u32[]{:S(2)}, u32[]{:S(2)}) %collective-permute-start.8) | collective-permute-done | bytes 131104 | tf_op jit(solution)/shard_map/ppermute | solution.py:208
  17.9 0.0 collective-permute-start.9
  17.9 0.9 %collective-permute-done.5.refs_5_ = bf16[512,128]{1,0:T(8,128)(2,1)S(1)} collective-permute-done((bf16[512,128]{1,0:T(8,128)(2,1)S(1)}, bf16[512,128]{1,0:T(8,128)(2,1)S(1)}, u32[]{:S(2)}, u32[]{:S(2)}) %collective-permute-start.5) | collective-permute-done | bytes 131104 | tf_op jit(solution)/shard_map/ppermute | solution.py:208
  18.7 0.0 collective-permute-start.6
  18.7 0.0 collective-permute-done.3.refs_4_
  18.7 0.5 %collective-permute-start.4 = (bf16[512,128]{1,0:T(8,128)(2,1)S(1)}, bf16[512,128]{1,0:T(8,128)(2,1)S(1)}, u32[]{:S(2)}, u32[]{:S(2)}) collective-permute-start(bf16[512,128]{1,0:T(8,128)(2,1)S(1)} %collective-permute-done.3.refs_4_), channel_id=1, source_target_pairs={{0,1},{1,0},{2,3},{3,2},{4,5},{5,4},{6,7},{7,6},{8,9},{9,8},{10,11... | collective-permute-start | bytes 393224 | tf_op jit(solution)/shard_map/ppermute | solution.py:208
  19.2 0.0 collective-permute-done.7.refs_1_
  19.3 0.0 collective-permute-done.9.refs_3_
  19.3 0.7 %first_pieces.1 = (bf16[512,768]{1,0:T(8,128)(2,1)S(1)}, bf16[768,512]{1,0:T(8,128)(2,1)S(1)}, f32[512,512]{1,0:T(8,128)S(1)}) custom-call(bf16[512,128]{1,0:T(8,128)(2,1)S(1)} %constant_dynamic-update-slice_fusion.refs_0_, bf16[512,128]{1,0:T(8,128)(2,1)S(1)} %collective-permute-done.7.refs_1_, bf16[512,128]{1,0:T(8,128)(2,1)S(1)} %collective-permute-done.8.refs_2_, ...), custom_call_target="tpu_custom_call" | custom-call | flops 400000000 | tf_op jit(solution)/shard_map/first_pieces/pallas_call | solution.py:222
  19.9 0.2 collective-permute-done.6.late1
  20.1 0.2 collective-permute-done.4.late0
  20.3 6.4 %whole_block.1 = bf16[768,1024]{1,0:T(8,128)(2,1)} custom-call(bf16[512,128]{1,0:T(8,128)(2,1)S(1)} %collective-permute-done.4.late0, bf16[512,128]{1,0:T(8,128)(2,1)S(1)} %collective-permute-done.6.late1, bf16[512,768]{1,0:T(8,128)(2,1)S(1)} %get-tuple-element.16.x, bf16[768,512]{1,0:T(8,128)(2,1)S(1)} %get-tuple-element.17.xt, ...), custom_call_target="tpu_custom_call" | custom-call | flops 5000000000 | tf_op jit(solution)/shard_map/whole_block/pallas_call | solution.py:231
  (4 shorter events, 0.0 us)
Async XLA Ops:
  0.0 0.9 %copy-start = (bf16[128,4,128]{2,1,0:T(4,128)(2,1)S(1)}, bf16[128,4,128]{2,1,0:T(4,128)(2,1)}, u32[]{:S(2)}) copy-start(bf16[128,4,128]{2,1,0:T(4,128)(2,1)} %param.2) | copy-start | bytes 393220
  1.2 7.0 %collective-permute-start = (bf16[128,128]{1,0:T(8,128)(2,1)S(1)}, bf16[128,128]{1,0:T(8,128)(2,1)S(1)}, u32[]{:S(2)}, u32[]{:S(2)}) collective-permute-start(bf16[128,128]{1,0:T(8,128)(2,1)S(1)} %get-tuple-element.13), channel_id=1, source_target_pairs={{0,8},{8,16},{16,24},{24,0},{1,9},{9,17},{17,25},{25,1},{2,10},{10... | collective-permute-start | bytes 98312 | tf_op jit(solution)/shard_map/ppermute | solution.py:212
  4.3 5.2 %collective-permute-start.1 = (bf16[128,128]{1,0:T(8,128)(2,1)S(1)}, bf16[128,128]{1,0:T(8,128)(2,1)S(1)}, u32[]{:S(2)}, u32[]{:S(2)}) collective-permute-start(bf16[128,128]{1,0:T(8,128)(2,1)S(1)} %get-tuple-element.14), channel_id=1, source_target_pairs={{0,16},{8,24},{16,0},{24,8},{1,17},{9,25},{17,1},{25,9},{2,18},{10... | collective-permute-start | bytes 98312 | tf_op jit(solution)/shard_map/ppermute | solution.py:212
  6.9 3.9 %collective-permute-start.2 = (bf16[128,128]{1,0:T(8,128)(2,1)S(1)}, bf16[128,128]{1,0:T(8,128)(2,1)S(1)}, u32[]{:S(2)}, u32[]{:S(2)}) collective-permute-start(bf16[128,128]{1,0:T(8,128)(2,1)S(1)} %get-tuple-element.15), channel_id=1, source_target_pairs={{0,24},{8,0},{16,8},{24,16},{1,25},{9,1},{17,9},{25,17},{2,26},{10... | collective-permute-start | bytes 98312 | tf_op jit(solution)/shard_map/ppermute | solution.py:212
  10.8 7.1 %collective-permute-start.8 = (bf16[512,128]{1,0:T(8,128)(2,1)S(1)}, bf16[512,128]{1,0:T(8,128)(2,1)S(1)}, u32[]{:S(2)}, u32[]{:S(2)}) collective-permute-start(bf16[512,128]{1,0:T(8,128)(2,1)S(1)} %constant_dynamic-update-slice_fusion.refs_0_), channel_id=1, source_target_pairs={{0,6},{1,7},{2,4},{3,5},{4,2},{5,3},{6,0},{7,1},{8,14},{9,15},{10,... | collective-permute-start | bytes 393224 | tf_op jit(solution)/shard_map/ppermute | solution.py:208
  13.2 5.5 %collective-permute-start.5 = (bf16[512,128]{1,0:T(8,128)(2,1)S(1)}, bf16[512,128]{1,0:T(8,128)(2,1)S(1)}, u32[]{:S(2)}, u32[]{:S(2)}) collective-permute-start(bf16[512,128]{1,0:T(8,128)(2,1)S(1)} %constant_dynamic-update-slice_fusion.refs_0_), channel_id=1, source_target_pairs={{0,4},{1,5},{2,6},{3,7},{4,0},{5,1},{6,2},{7,3},{8,12},{9,13},{10,... | collective-permute-start | bytes 393224 | tf_op jit(solution)/shard_map/ppermute | solution.py:208
  13.7 5.0 %collective-permute-start.3 = (bf16[512,128]{1,0:T(8,128)(2,1)S(1)}, bf16[512,128]{1,0:T(8,128)(2,1)S(1)}, u32[]{:S(2)}, u32[]{:S(2)}) collective-permute-start(bf16[512,128]{1,0:T(8,128)(2,1)S(1)} %constant_dynamic-update-slice_fusion.refs_0_), channel_id=1, source_target_pairs={{0,2},{1,3},{2,0},{3,1},{4,6},{5,7},{6,4},{7,5},{8,10},{9,11},{10,... | collective-permute-start | bytes 393224 | tf_op jit(solution)/shard_map/ppermute | solution.py:208
  14.3 5.0 %collective-permute-start.7 = (bf16[512,128]{1,0:T(8,128)(2,1)S(1)}, bf16[512,128]{1,0:T(8,128)(2,1)S(1)}, u32[]{:S(2)}, u32[]{:S(2)}) collective-permute-start(bf16[512,128]{1,0:T(8,128)(2,1)S(1)} %constant_dynamic-update-slice_fusion.refs_0_), channel_id=1, source_target_pairs={{0,1},{1,0},{2,3},{3,2},{4,5},{5,4},{6,7},{7,6},{8,9},{9,8},{10,11... | collective-permute-start | bytes 393224 | tf_op jit(solution)/shard_map/ppermute | solution.py:208
  17.9 1.4 %collective-permute-start.9 = (bf16[512,128]{1,0:T(8,128)(2,1)S(1)}, bf16[512,128]{1,0:T(8,128)(2,1)S(1)}, u32[]{:S(2)}, u32[]{:S(2)}) collective-permute-start(bf16[512,128]{1,0:T(8,128)(2,1)S(1)} %collective-permute-done.8.refs_2_), channel_id=1, source_target_pairs={{0,1},{1,0},{2,3},{3,2},{4,5},{5,4},{6,7},{7,6},{8,9},{9,8},{10,11... | collective-permute-start | bytes 393224 | tf_op jit(solution)/shard_map/ppermute | solution.py:208
  18.7 1.3 %collective-permute-start.6 = (bf16[512,128]{1,0:T(8,128)(2,1)S(1)}, bf16[512,128]{1,0:T(8,128)(2,1)S(1)}, u32[]{:S(2)}, u32[]{:S(2)}) collective-permute-start(bf16[512,128]{1,0:T(8,128)(2,1)S(1)} %collective-permute-done.5.refs_5_), channel_id=1, source_target_pairs={{0,1},{1,0},{2,3},{3,2},{4,5},{5,4},{6,7},{7,6},{8,9},{9,8},{10,11... | collective-permute-start | bytes 393224 | tf_op jit(solution)/shard_map/ppermute | solution.py:208
  18.7 1.5 %collective-permute-start.4 = (bf16[512,128]{1,0:T(8,128)(2,1)S(1)}, bf16[512,128]{1,0:T(8,128)(2,1)S(1)}, u32[]{:S(2)}, u32[]{:S(2)}) collective-permute-start(bf16[512,128]{1,0:T(8,128)(2,1)S(1)} %collective-permute-done.3.refs_4_), channel_id=1, source_target_pairs={{0,1},{1,0},{2,3},{3,2},{4,5},{5,4},{6,7},{7,6},{8,9},{9,8},{10,11... | collective-permute-start | bytes 393224 | tf_op jit(solution)/shard_map/ppermute | solution.py:208

commit v20 on v19

--- a/solution.py
+++ b/solution.py
@@ -73,7 +73,7 @@
 
 
 def last_kernel(fars, late0, late1, x, xt, gram_in, tile_hbm, out_hbm, *refs):
-    tile, out, late, late_t, k1, k2, e2, g, z, h, k, image, by_g, by_h, mixed, sems = refs
+    tile, out, late, late_t, k1, k2, e2, g, z, h, k, image, by_g, by_h, mixed, *folds, sems = refs
     load = pltpu.make_async_copy(tile_hbm, tile, sems.at[0])
     load.start()
     member = lax.axis_index("grad")
@@ -82,7 +82,11 @@
     features = half // 2
     halves = [slice(at, at + half) for at in range(0, tokens, half)]
     blocks = [slice(at, at + half) for at in range(0, x.shape[1], half)]
-    chunks = [slice(at, at + 32) for at in range(0, tokens, 32)]
+
+    def chunks_of(size):
+        return [slice(at, at + 32) for at in range(0, size, 32)]
+
+    chunks = chunks_of(tokens)
 
     def place(far):
         return pl.ds(pl.multiple_of((member ^ far) * features, features), features)
@@ -110,30 +114,38 @@
 
     symmetric(gram, None, lambda product, r, some: [(gram_in[r, some] + product) * (1.0 / tokens)], k1)
 
-    column_sums, row_sums = [0.0] * (len(blocks) + 1), [0.0] * len(blocks)
+    column_sums = [0.0] * (len(blocks) + 1)
 
     def add_sums(n, left, right):
-        column = jnp.abs(dot(left, right))
-        column_sums[n] = column_sums[n] + jnp.sum(column, axis=0, keepdims=True)
-        for i, some in enumerate(blocks[: min(n, column.shape[0] // half)]):
-            row_sums[i] = row_sums[i] + column[some, :features] + column[some, features:]
+        product = dot(left, right)
+        total = 0.0
+        for r in chunks_of(product.shape[0]):
+            block = jnp.abs(product[r])
+            total = total + block
+            if r.start < n * half:
+                folds[n - 1][r, :] = block[:, :features] + block[:, features:]
+        column_sums[n] = column_sums[n] + jnp.sum(total, axis=0, keepdims=True)
 
     def move(some):
-        moved = dot(chosen(fars[:-2]), xt[:, some]) + dot(chosen(fars[-2:]), late_t[:, some])
-        image[:, some] = moved.astype(jnp.bfloat16)
+        moved, rest = dot(chosen(fars[:-2]), xt[:, some]), dot(chosen(fars[-2:]), late_t[:, some])
+        for r in chunks_of(moved.shape[0]):
+            image[r, some] = (moved[r] + rest[r]).astype(jnp.bfloat16)
 
     for n, some in enumerate(blocks):
         add_sums(n, xt[: some.stop, :], x[:, some])
     symmetric(k1, k1, lambda product, r, some: [product], k2)
     add_sums(len(blocks), xt[...], late[...])
-    column_sums[-1] = column_sums[-1] + jnp.sum(jnp.abs(dot(late_t[...], late[...])), axis=0, keepdims=True)
+    product = dot(late_t[...], late[...])
+    total = functools.reduce(jnp.add, [jnp.abs(product[r]) for r in chunks_of(half)])
+    column_sums[-1] = column_sums[-1] + jnp.sum(total, axis=0, keepdims=True)
     load.wait()
     for some in halves:
         move(some)
 
     largest = column_sums[-1]
-    for column, row in zip(column_sums[:-1], row_sums):
-        largest = jnp.maximum(largest, column + jnp.sum(row.T, axis=0, keepdims=True))
+    for n, (column, some) in enumerate(zip(column_sums[:-1], blocks)):
+        folded = functools.reduce(jnp.add, [fold[some, :] for fold in folds[n:]])
+        largest = jnp.maximum(largest, column + jnp.sum(folded.T, axis=0, keepdims=True))
     c = 1.0 / (jnp.max(largest) * (1.0 / tokens) + DAMPING)
     eps = 1.0 - c * DAMPING
     eps2 = eps * eps
@@ -168,11 +180,12 @@
 
     def apply(left, right, parts, result, scale=None):
         for some in halves:
-            total = dot(left[...], right[:, some])
-            total = total if scale is None else total * scale
-            for weight, part in parts:
-                total = total + weight * part[:, some].astype(jnp.float32)
-            result[:, some] = total.astype(jnp.bfloat16)
+            product = dot(left[...], right[:, some])
+            for r in chunks_of(product.shape[0]):
+                total = product[r] if scale is None else product[r] * scale
+                for weight, part in parts:
+                    total = total + weight * part[r, some].astype(jnp.float32)
+                result[r, some] = total.astype(jnp.bfloat16)
 
     apply(image, g, [(g_m, image)], by_g)
     symmetric(z, z, lambda product, r, some: [product + k_z * wide(z, r, some)], k)
@@ -183,8 +196,9 @@
         moved = dot(mixed[...], late[...] if n == len(blocks) else x[:, blocks[n]])
         for one in (0, 1):
             here = place(fars[2 * n + one])
-            kept = p * tile[:, here].astype(jnp.float32)
-            out[:, here] = (kept + moved[:, one * features : (one + 1) * features]).astype(jnp.bfloat16)
+            part = slice(one * features, (one + 1) * features)
+            for r in chunks_of(moved.shape[0]):
+                out[r, here] = (p * tile[r, here].astype(jnp.float32) + moved[r, part]).astype(jnp.bfloat16)
             store = pltpu.make_async_copy(out.at[:, here], out_hbm.at[:, here], sems.at[1 + len(stores)])
             store.start()
             stores.append(store)
@@ -237,6 +251,7 @@
         + [scratch(tokens, 2 * features), scratch(2 * features, tokens)]
         + [scratch(tokens, tokens)] * 7
         + [scratch(rows, tokens)] * 4
+        + [pltpu.VMEM((2 * features * n, 128), jnp.float32) for n in range(1, members // 2)]
         + [pltpu.SemaphoreType.DMA((1 + members,))],
         compiler_params=pltpu.CompilerParams(vmem_limit_bytes=51 * 2**20),
         cost_estimate=pl.CostEstimate(flops=5 * 10**9, bytes_accessed=0, transcendentals=0),

time: 26.9 us -> 26.9 us (level)
  no operation moved by 1% of the time
where the time goes in v20:
time: 26.9 us; the launch traced here: 26.7 us
  starting transfers between devices  11 us (41%)
  Pallas kernels  7.4 us (28%)
  waiting for transfers between devices  7.34 us (27%)
  local copies, waits for them, and re-layouts  0.93 us (3%)
    ppermute x3, starting transfers between devices, by_tokens(): lax.ppermute(parts[far], 'dp', [(i, (i + far) % replicas) for i in range(...  7.01 us
    pallas_call x1, Pallas kernels, by_tokens(): pl.pallas_call(functools.partial(last_kernel, fars), out_shape=shape(rows...  6.45 us
    ppermute x7, waiting for transfers between devices, swap(): return lax.ppermute(value, 'grad', [(i, i ^ far) for i in range(members)])  4.8 us
    ppermute x7, starting transfers between devices, swap(): return lax.ppermute(value, 'grad', [(i, i ^ far) for i in range(members)])  4 us
    ppermute x3, waiting for transfers between devices, by_tokens(): lax.ppermute(parts[far], 'dp', [(i, (i + far) % replicas) for i in range(...  2.54 us
    unnamed x5, local copies, waits for them, and re-layouts  0.92 us
    pallas_call x1, Pallas kernels, by_tokens(): pl.pallas_call(first_kernel, out_shape=[shape(tokens, early), shape(early...  0.67 us
  transfers between devices with their start and end apart: 10, of which 6 were waited for; matrix products, arithmetic and copies ran while one was open for 0% of the time, Pallas kernels for 2%

profile of v20, /device:TPU:0, one launch (start us, length us, event | category | flops | bytes accessed | tf_op | source)
XLA Modules:
  0.0 26.7 jit_solution(15671633906555629132)
XLA Ops:
  0.0 0.0 copy-start
  0.0 0.9 %copy-done = bf16[128,4,128]{2,1,0:T(4,128)(2,1)S(1)} copy-done((bf16[128,4,128]{2,1,0:T(4,128)(2,1)S(1)}, bf16[128,4,128]{2,1,0:T(4,128)(2,1)}, u32[]{:S(2)}) %copy-start) | copy-done | bytes 131096
  0.9 0.3 %split_blocks.1 = (bf16[128,128]{1,0:T(8,128)(2,1)S(1)}, bf16[128,128]{1,0:T(8,128)(2,1)S(1)}, bf16[128,128]{1,0:T(8,128)(2,1)S(1)}, bf16[128,128]{1,0:T(8,128)(2,1)S(1)}) custom-call(bf16[512,128]{1,0:T(8,128)(2,1)S(1)} %bitcast.3), custom_call_target="tpu_custom_call" | custom-call | tf_op jit(solution)/shard_map/split_blocks/pallas_call | solution.py:55
  1.2 3.1 %collective-permute-start = (bf16[128,128]{1,0:T(8,128)(2,1)S(1)}, bf16[128,128]{1,0:T(8,128)(2,1)S(1)}, u32[]{:S(2)}, u32[]{:S(2)}) collective-permute-start(bf16[128,128]{1,0:T(8,128)(2,1)S(1)} %get-tuple-element.13), channel_id=1, source_target_pairs={{0,8},{8,16},{16,24},{24,0},{1,9},{9,17},{17,25},{25,1},{2,10},{10... | collective-permute-start | bytes 98312 | tf_op jit(solution)/shard_map/ppermute | solution.py:226
  4.3 2.6 %collective-permute-start.1 = (bf16[128,128]{1,0:T(8,128)(2,1)S(1)}, bf16[128,128]{1,0:T(8,128)(2,1)S(1)}, u32[]{:S(2)}, u32[]{:S(2)}) collective-permute-start(bf16[128,128]{1,0:T(8,128)(2,1)S(1)} %get-tuple-element.14), channel_id=1, source_target_pairs={{0,16},{8,24},{16,0},{24,8},{1,17},{9,25},{17,1},{25,9},{2,18},{10... | collective-permute-start | bytes 98312 | tf_op jit(solution)/shard_map/ppermute | solution.py:226
  6.9 1.3 %collective-permute-start.2 = (bf16[128,128]{1,0:T(8,128)(2,1)S(1)}, bf16[128,128]{1,0:T(8,128)(2,1)S(1)}, u32[]{:S(2)}, u32[]{:S(2)}) collective-permute-start(bf16[128,128]{1,0:T(8,128)(2,1)S(1)} %get-tuple-element.15), channel_id=1, source_target_pairs={{0,24},{8,0},{16,8},{24,16},{1,25},{9,1},{17,9},{25,17},{2,26},{10... | collective-permute-start | bytes 98312 | tf_op jit(solution)/shard_map/ppermute | solution.py:226
  8.2 0.0 collective-permute-done
  8.2 1.2 %collective-permute-done.1 = bf16[128,128]{1,0:T(8,128)(2,1)S(1)} collective-permute-done((bf16[128,128]{1,0:T(8,128)(2,1)S(1)}, bf16[128,128]{1,0:T(8,128)(2,1)S(1)}, u32[]{:S(2)}, u32[]{:S(2)}) %collective-permute-start.1) | collective-permute-done | bytes 32800 | tf_op jit(solution)/shard_map/ppermute | solution.py:226
  9.4 1.3 %collective-permute-done.2 = bf16[128,128]{1,0:T(8,128)(2,1)S(1)} collective-permute-done((bf16[128,128]{1,0:T(8,128)(2,1)S(1)}, bf16[128,128]{1,0:T(8,128)(2,1)S(1)}, u32[]{:S(2)}, u32[]{:S(2)}) %collective-permute-start.2) | collective-permute-done | bytes 32800 | tf_op jit(solution)/shard_map/ppermute | solution.py:226
  10.8 2.4 %collective-permute-start.8 = (bf16[512,128]{1,0:T(8,128)(2,1)S(1)}, bf16[512,128]{1,0:T(8,128)(2,1)S(1)}, u32[]{:S(2)}, u32[]{:S(2)}) collective-permute-start(bf16[512,128]{1,0:T(8,128)(2,1)S(1)} %constant_dynamic-update-slice_fusion.refs_0_), channel_id=1, source_target_pairs={{0,6},{1,7},{2,4},{3,5},{4,2},{5,3},{6,0},{7,1},{8,14},{9,15},{10,... | collective-permute-start | bytes 393224 | tf_op jit(solution)/shard_map/ppermute | solution.py:222
  13.2 0.5 %collective-permute-start.5 = (bf16[512,128]{1,0:T(8,128)(2,1)S(1)}, bf16[512,128]{1,0:T(8,128)(2,1)S(1)}, u32[]{:S(2)}, u32[]{:S(2)}) collective-permute-start(bf16[512,128]{1,0:T(8,128)(2,1)S(1)} %constant_dynamic-update-slice_fusion.refs_0_), channel_id=1, source_target_pairs={{0,4},{1,5},{2,6},{3,7},{4,0},{5,1},{6,2},{7,3},{8,12},{9,13},{10,... | collective-permute-start | bytes 393224 | tf_op jit(solution)/shard_map/ppermute | solution.py:222
  13.7 0.5 %collective-permute-start.3 = (bf16[512,128]{1,0:T(8,128)(2,1)S(1)}, bf16[512,128]{1,0:T(8,128)(2,1)S(1)}, u32[]{:S(2)}, u32[]{:S(2)}) collective-permute-start(bf16[512,128]{1,0:T(8,128)(2,1)S(1)} %constant_dynamic-update-slice_fusion.refs_0_), channel_id=1, source_target_pairs={{0,2},{1,3},{2,0},{3,1},{4,6},{5,7},{6,4},{7,5},{8,10},{9,11},{10,... | collective-permute-start | bytes 393224 | tf_op jit(solution)/shard_map/ppermute | solution.py:222
  14.3 0.0 collective-permute-start.7
  14.3 3.6 %collective-permute-done.8.refs_2_ = bf16[512,128]{1,0:T(8,128)(2,1)S(1)} collective-permute-done((bf16[512,128]{1,0:T(8,128)(2,1)S(1)}, bf16[512,128]{1,0:T(8,128)(2,1)S(1)}, u32[]{:S(2)}, u32[]{:S(2)}) %collective-permute-start.8) | collective-permute-done | bytes 131104 | tf_op jit(solution)/shard_map/ppermute | solution.py:222
  17.9 0.0 collective-permute-start.9
  17.9 0.9 %collective-permute-done.5.refs_5_ = bf16[512,128]{1,0:T(8,128)(2,1)S(1)} collective-permute-done((bf16[512,128]{1,0:T(8,128)(2,1)S(1)}, bf16[512,128]{1,0:T(8,128)(2,1)S(1)}, u32[]{:S(2)}, u32[]{:S(2)}) %collective-permute-start.5) | collective-permute-done | bytes 131104 | tf_op jit(solution)/shard_map/ppermute | solution.py:222
  18.7 0.0 collective-permute-start.6
  18.7 0.0 collective-permute-done.3.refs_4_
  18.7 0.5 %collective-permute-start.4 = (bf16[512,128]{1,0:T(8,128)(2,1)S(1)}, bf16[512,128]{1,0:T(8,128)(2,1)S(1)}, u32[]{:S(2)}, u32[]{:S(2)}) collective-permute-start(bf16[512,128]{1,0:T(8,128)(2,1)S(1)} %collective-permute-done.3.refs_4_), channel_id=1, source_target_pairs={{0,1},{1,0},{2,3},{3,2},{4,5},{5,4},{6,7},{7,6},{8,9},{9,8},{10,11... | collective-permute-start | bytes 393224 | tf_op jit(solution)/shard_map/ppermute | solution.py:222
  19.2 0.0 collective-permute-done.7.refs_1_
  19.3 0.0 collective-permute-done.9.refs_3_
  19.3 0.7 %first_pieces.1 = (bf16[512,768]{1,0:T(8,128)(2,1)S(1)}, bf16[768,512]{1,0:T(8,128)(2,1)S(1)}, f32[512,512]{1,0:T(8,128)S(1)}) custom-call(bf16[512,128]{1,0:T(8,128)(2,1)S(1)} %constant_dynamic-update-slice_fusion.refs_0_, bf16[512,128]{1,0:T(8,128)(2,1)S(1)} %collective-permute-done.7.refs_1_, bf16[512,128]{1,0:T(8,128)(2,1)S(1)} %collective-permute-done.8.refs_2_, ...), custom_call_target="tpu_custom_call" | custom-call | flops 400000000 | tf_op jit(solution)/shard_map/first_pieces/pallas_call | solution.py:236
  19.9 0.2 collective-permute-done.6.late1
  20.1 0.2 collective-permute-done.4.late0
  20.3 6.4 %whole_block.1 = bf16[768,1024]{1,0:T(8,128)(2,1)} custom-call(bf16[512,128]{1,0:T(8,128)(2,1)S(1)} %collective-permute-done.4.late0, bf16[512,128]{1,0:T(8,128)(2,1)S(1)} %collective-permute-done.6.late1, bf16[512,768]{1,0:T(8,128)(2,1)S(1)} %get-tuple-element.16.x, bf16[768,512]{1,0:T(8,128)(2,1)S(1)} %get-tuple-element.17.xt, ...), custom_call_target="tpu_custom_call" | custom-call | flops 5000000000 | tf_op jit(solution)/shard_map/whole_block/pallas_call | solution.py:245
  (4 shorter events, 0.0 us)
Async XLA Ops:
  0.0 0.9 %copy-start = (bf16[128,4,128]{2,1,0:T(4,128)(2,1)S(1)}, bf16[128,4,128]{2,1,0:T(4,128)(2,1)}, u32[]{:S(2)}) copy-start(bf16[128,4,128]{2,1,0:T(4,128)(2,1)} %param.2) | copy-start | bytes 393220
  1.2 7.0 %collective-permute-start = (bf16[128,128]{1,0:T(8,128)(2,1)S(1)}, bf16[128,128]{1,0:T(8,128)(2,1)S(1)}, u32[]{:S(2)}, u32[]{:S(2)}) collective-permute-start(bf16[128,128]{1,0:T(8,128)(2,1)S(1)} %get-tuple-element.13), channel_id=1, source_target_pairs={{0,8},{8,16},{16,24},{24,0},{1,9},{9,17},{17,25},{25,1},{2,10},{10... | collective-permute-start | bytes 98312 | tf_op jit(solution)/shard_map/ppermute | solution.py:226
  4.3 5.2 %collective-permute-start.1 = (bf16[128,128]{1,0:T(8,128)(2,1)S(1)}, bf16[128,128]{1,0:T(8,128)(2,1)S(1)}, u32[]{:S(2)}, u32[]{:S(2)}) collective-permute-start(bf16[128,128]{1,0:T(8,128)(2,1)S(1)} %get-tuple-element.14), channel_id=1, source_target_pairs={{0,16},{8,24},{16,0},{24,8},{1,17},{9,25},{17,1},{25,9},{2,18},{10... | collective-permute-start | bytes 98312 | tf_op jit(solution)/shard_map/ppermute | solution.py:226
  6.9 3.9 %collective-permute-start.2 = (bf16[128,128]{1,0:T(8,128)(2,1)S(1)}, bf16[128,128]{1,0:T(8,128)(2,1)S(1)}, u32[]{:S(2)}, u32[]{:S(2)}) collective-permute-start(bf16[128,128]{1,0:T(8,128)(2,1)S(1)} %get-tuple-element.15), channel_id=1, source_target_pairs={{0,24},{8,0},{16,8},{24,16},{1,25},{9,1},{17,9},{25,17},{2,26},{10... | collective-permute-start | bytes 98312 | tf_op jit(solution)/shard_map/ppermute | solution.py:226
  10.8 7.1 %collective-permute-start.8 = (bf16[512,128]{1,0:T(8,128)(2,1)S(1)}, bf16[512,128]{1,0:T(8,128)(2,1)S(1)}, u32[]{:S(2)}, u32[]{:S(2)}) collective-permute-start(bf16[512,128]{1,0:T(8,128)(2,1)S(1)} %constant_dynamic-update-slice_fusion.refs_0_), channel_id=1, source_target_pairs={{0,6},{1,7},{2,4},{3,5},{4,2},{5,3},{6,0},{7,1},{8,14},{9,15},{10,... | collective-permute-start | bytes 393224 | tf_op jit(solution)/shard_map/ppermute | solution.py:222
  13.2 5.5 %collective-permute-start.5 = (bf16[512,128]{1,0:T(8,128)(2,1)S(1)}, bf16[512,128]{1,0:T(8,128)(2,1)S(1)}, u32[]{:S(2)}, u32[]{:S(2)}) collective-permute-start(bf16[512,128]{1,0:T(8,128)(2,1)S(1)} %constant_dynamic-update-slice_fusion.refs_0_), channel_id=1, source_target_pairs={{0,4},{1,5},{2,6},{3,7},{4,0},{5,1},{6,2},{7,3},{8,12},{9,13},{10,... | collective-permute-start | bytes 393224 | tf_op jit(solution)/shard_map/ppermute | solution.py:222
  13.7 5.0 %collective-permute-start.3 = (bf16[512,128]{1,0:T(8,128)(2,1)S(1)}, bf16[512,128]{1,0:T(8,128)(2,1)S(1)}, u32[]{:S(2)}, u32[]{:S(2)}) collective-permute-start(bf16[512,128]{1,0:T(8,128)(2,1)S(1)} %constant_dynamic-update-slice_fusion.refs_0_), channel_id=1, source_target_pairs={{0,2},{1,3},{2,0},{3,1},{4,6},{5,7},{6,4},{7,5},{8,10},{9,11},{10,... | collective-permute-start | bytes 393224 | tf_op jit(solution)/shard_map/ppermute | solution.py:222
  14.3 5.0 %collective-permute-start.7 = (bf16[512,128]{1,0:T(8,128)(2,1)S(1)}, bf16[512,128]{1,0:T(8,128)(2,1)S(1)}, u32[]{:S(2)}, u32[]{:S(2)}) collective-permute-start(bf16[512,128]{1,0:T(8,128)(2,1)S(1)} %constant_dynamic-update-slice_fusion.refs_0_), channel_id=1, source_target_pairs={{0,1},{1,0},{2,3},{3,2},{4,5},{5,4},{6,7},{7,6},{8,9},{9,8},{10,11... | collective-permute-start | bytes 393224 | tf_op jit(solution)/shard_map/ppermute | solution.py:222
  17.9 1.4 %collective-permute-start.9 = (bf16[512,128]{1,0:T(8,128)(2,1)S(1)}, bf16[512,128]{1,0:T(8,128)(2,1)S(1)}, u32[]{:S(2)}, u32[]{:S(2)}) collective-permute-start(bf16[512,128]{1,0:T(8,128)(2,1)S(1)} %collective-permute-done.8.refs_2_), channel_id=1, source_target_pairs={{0,1},{1,0},{2,3},{3,2},{4,5},{5,4},{6,7},{7,6},{8,9},{9,8},{10,11... | collective-permute-start | bytes 393224 | tf_op jit(solution)/shard_map/ppermute | solution.py:222
  18.7 1.3 %collective-permute-start.6 = (bf16[512,128]{1,0:T(8,128)(2,1)S(1)}, bf16[512,128]{1,0:T(8,128)(2,1)S(1)}, u32[]{:S(2)}, u32[]{:S(2)}) collective-permute-start(bf16[512,128]{1,0:T(8,128)(2,1)S(1)} %collective-permute-done.5.refs_5_), channel_id=1, source_target_pairs={{0,1},{1,0},{2,3},{3,2},{4,5},{5,4},{6,7},{7,6},{8,9},{9,8},{10,11... | collective-permute-start | bytes 393224 | tf_op jit(solution)/shard_map/ppermute | solution.py:222
  18.7 1.5 %collective-permute-start.4 = (bf16[512,128]{1,0:T(8,128)(2,1)S(1)}, bf16[512,128]{1,0:T(8,128)(2,1)S(1)}, u32[]{:S(2)}, u32[]{:S(2)}) collective-permute-start(bf16[512,128]{1,0:T(8,128)(2,1)S(1)} %collective-permute-done.3.refs_4_), channel_id=1, source_target_pairs={{0,1},{1,0},{2,3},{3,2},{4,5},{5,4},{6,7},{7,6},{8,9},{9,8},{10,11... | collective-permute-start | bytes 393224 | tf_op jit(solution)/shard_map/ppermute | solution.py:222

commit v21 on v20

--- a/solution.py
+++ b/solution.py
@@ -126,10 +126,10 @@
                 folds[n - 1][r, :] = block[:, :features] + block[:, features:]
         column_sums[n] = column_sums[n] + jnp.sum(total, axis=0, keepdims=True)
 
-    def move(some):
-        moved, rest = dot(chosen(fars[:-2]), xt[:, some]), dot(chosen(fars[-2:]), late_t[:, some])
+    def move():
+        moved, rest = dot(chosen(fars[:-2]), xt[...]), dot(chosen(fars[-2:]), late_t[...])
         for r in chunks_of(moved.shape[0]):
-            image[r, some] = (moved[r] + rest[r]).astype(jnp.bfloat16)
+            image[r, :] = (moved[r] + rest[r]).astype(jnp.bfloat16)
 
     for n, some in enumerate(blocks):
         add_sums(n, xt[: some.stop, :], x[:, some])
@@ -139,8 +139,7 @@
     total = functools.reduce(jnp.add, [jnp.abs(product[r]) for r in chunks_of(half)])
     column_sums[-1] = column_sums[-1] + jnp.sum(total, axis=0, keepdims=True)
     load.wait()
-    for some in halves:
-        move(some)
+    move()
 
     largest = column_sums[-1]
     for n, (column, some) in enumerate(zip(column_sums[:-1], blocks)):
@@ -179,13 +178,12 @@
     symmetric(e2, e2, fourth, z, h)
 
     def apply(left, right, parts, result, scale=None):
-        for some in halves:
-            product = dot(left[...], right[:, some])
-            for r in chunks_of(product.shape[0]):
-                total = product[r] if scale is None else product[r] * scale
-                for weight, part in parts:
-                    total = total + weight * part[r, some].astype(jnp.float32)
-                result[r, some] = total.astype(jnp.bfloat16)
+        product = dot(left[...], right[...])
+        for r in chunks_of(product.shape[0]):
+            total = product[r] if scale is None else product[r] * scale
+            for weight, part in parts:
+                total = total + weight * part[r, :].astype(jnp.float32)
+            result[r, :] = total.astype(jnp.bfloat16)
 
     apply(image, g, [(g_m, image)], by_g)
     symmetric(z, z, lambda product, r, some: [product + k_z * wide(z, r, some)], k)

time: 26.9 us -> 26.9 us (level)
  no operation moved by 1% of the time
where the time goes in v21:
time: 26.9 us; the launch traced here: 26.7 us
  starting transfers between devices  11 us (41%)
  Pallas kernels  7.4 us (28%)
  waiting for transfers between devices  7.34 us (27%)
  local copies, waits for them, and re-layouts  0.93 us (3%)
    ppermute x3, starting transfers between devices, by_tokens(): lax.ppermute(parts[far], 'dp', [(i, (i + far) % replicas) for i in range(...  7.01 us
    pallas_call x1, Pallas kernels, by_tokens(): pl.pallas_call(functools.partial(last_kernel, fars), out_shape=shape(rows...  6.45 us
    ppermute x7, waiting for transfers between devices, swap(): return lax.ppermute(value, 'grad', [(i, i ^ far) for i in range(members)])  4.8 us
    ppermute x7, starting transfers between devices, swap(): return lax.ppermute(value, 'grad', [(i, i ^ far) for i in range(members)])  4 us
    ppermute x3, waiting for transfers between devices, by_tokens(): lax.ppermute(parts[far], 'dp', [(i, (i + far) % replicas) for i in range(...  2.54 us
    unnamed x5, local copies, waits for them, and re-layouts  0.92 us
    pallas_call x1, Pallas kernels, by_tokens(): pl.pallas_call(first_kernel, out_shape=[shape(tokens, early), shape(early...  0.67 us
  transfers between devices with their start and end apart: 10, of which 6 were waited for; matrix products, arithmetic and copies ran while one was open for 0% of the time, Pallas kernels for 2%

profile of v21, /device:TPU:0, one launch (start us, length us, event | category | flops | bytes accessed | tf_op | source)
XLA Modules:
  0.0 26.7 jit_solution(3879532434456628690)
XLA Ops:
  0.0 0.0 copy-start
  0.0 0.9 %copy-done = bf16[128,4,128]{2,1,0:T(4,128)(2,1)S(1)} copy-done((bf16[128,4,128]{2,1,0:T(4,128)(2,1)S(1)}, bf16[128,4,128]{2,1,0:T(4,128)(2,1)}, u32[]{:S(2)}) %copy-start) | copy-done | bytes 131096
  0.9 0.3 %split_blocks.1 = (bf16[128,128]{1,0:T(8,128)(2,1)S(1)}, bf16[128,128]{1,0:T(8,128)(2,1)S(1)}, bf16[128,128]{1,0:T(8,128)(2,1)S(1)}, bf16[128,128]{1,0:T(8,128)(2,1)S(1)}) custom-call(bf16[512,128]{1,0:T(8,128)(2,1)S(1)} %bitcast.3), custom_call_target="tpu_custom_call" | custom-call | tf_op jit(solution)/shard_map/split_blocks/pallas_call | solution.py:55
  1.2 3.1 %collective-permute-start = (bf16[128,128]{1,0:T(8,128)(2,1)S(1)}, bf16[128,128]{1,0:T(8,128)(2,1)S(1)}, u32[]{:S(2)}, u32[]{:S(2)}) collective-permute-start(bf16[128,128]{1,0:T(8,128)(2,1)S(1)} %get-tuple-element.13), channel_id=1, source_target_pairs={{0,8},{8,16},{16,24},{24,0},{1,9},{9,17},{17,25},{25,1},{2,10},{10... | collective-permute-start | bytes 98312 | tf_op jit(solution)/shard_map/ppermute | solution.py:224
  4.3 2.6 %collective-permute-start.1 = (bf16[128,128]{1,0:T(8,128)(2,1)S(1)}, bf16[128,128]{1,0:T(8,128)(2,1)S(1)}, u32[]{:S(2)}, u32[]{:S(2)}) collective-permute-start(bf16[128,128]{1,0:T(8,128)(2,1)S(1)} %get-tuple-element.14), channel_id=1, source_target_pairs={{0,16},{8,24},{16,0},{24,8},{1,17},{9,25},{17,1},{25,9},{2,18},{10... | collective-permute-start | bytes 98312 | tf_op jit(solution)/shard_map/ppermute | solution.py:224
  6.9 1.3 %collective-permute-start.2 = (bf16[128,128]{1,0:T(8,128)(2,1)S(1)}, bf16[128,128]{1,0:T(8,128)(2,1)S(1)}, u32[]{:S(2)}, u32[]{:S(2)}) collective-permute-start(bf16[128,128]{1,0:T(8,128)(2,1)S(1)} %get-tuple-element.15), channel_id=1, source_target_pairs={{0,24},{8,0},{16,8},{24,16},{1,25},{9,1},{17,9},{25,17},{2,26},{10... | collective-permute-start | bytes 98312 | tf_op jit(solution)/shard_map/ppermute | solution.py:224
  8.2 0.0 collective-permute-done
  8.2 1.2 %collective-permute-done.1 = bf16[128,128]{1,0:T(8,128)(2,1)S(1)} collective-permute-done((bf16[128,128]{1,0:T(8,128)(2,1)S(1)}, bf16[128,128]{1,0:T(8,128)(2,1)S(1)}, u32[]{:S(2)}, u32[]{:S(2)}) %collective-permute-start.1) | collective-permute-done | bytes 32800 | tf_op jit(solution)/shard_map/ppermute | solution.py:224
  9.4 1.3 %collective-permute-done.2 = bf16[128,128]{1,0:T(8,128)(2,1)S(1)} collective-permute-done((bf16[128,128]{1,0:T(8,128)(2,1)S(1)}, bf16[128,128]{1,0:T(8,128)(2,1)S(1)}, u32[]{:S(2)}, u32[]{:S(2)}) %collective-permute-start.2) | collective-permute-done | bytes 32800 | tf_op jit(solution)/shard_map/ppermute | solution.py:224
  10.8 2.4 %collective-permute-start.8 = (bf16[512,128]{1,0:T(8,128)(2,1)S(1)}, bf16[512,128]{1,0:T(8,128)(2,1)S(1)}, u32[]{:S(2)}, u32[]{:S(2)}) collective-permute-start(bf16[512,128]{1,0:T(8,128)(2,1)S(1)} %constant_dynamic-update-slice_fusion.refs_0_), channel_id=1, source_target_pairs={{0,6},{1,7},{2,4},{3,5},{4,2},{5,3},{6,0},{7,1},{8,14},{9,15},{10,... | collective-permute-start | bytes 393224 | tf_op jit(solution)/shard_map/ppermute | solution.py:220
  13.2 0.5 %collective-permute-start.5 = (bf16[512,128]{1,0:T(8,128)(2,1)S(1)}, bf16[512,128]{1,0:T(8,128)(2,1)S(1)}, u32[]{:S(2)}, u32[]{:S(2)}) collective-permute-start(bf16[512,128]{1,0:T(8,128)(2,1)S(1)} %constant_dynamic-update-slice_fusion.refs_0_), channel_id=1, source_target_pairs={{0,4},{1,5},{2,6},{3,7},{4,0},{5,1},{6,2},{7,3},{8,12},{9,13},{10,... | collective-permute-start | bytes 393224 | tf_op jit(solution)/shard_map/ppermute | solution.py:220
  13.7 0.5 %collective-permute-start.3 = (bf16[512,128]{1,0:T(8,128)(2,1)S(1)}, bf16[512,128]{1,0:T(8,128)(2,1)S(1)}, u32[]{:S(2)}, u32[]{:S(2)}) collective-permute-start(bf16[512,128]{1,0:T(8,128)(2,1)S(1)} %constant_dynamic-update-slice_fusion.refs_0_), channel_id=1, source_target_pairs={{0,2},{1,3},{2,0},{3,1},{4,6},{5,7},{6,4},{7,5},{8,10},{9,11},{10,... | collective-permute-start | bytes 393224 | tf_op jit(solution)/shard_map/ppermute | solution.py:220
  14.3 0.0 collective-permute-start.7
  14.3 3.6 %collective-permute-done.8.refs_2_ = bf16[512,128]{1,0:T(8,128)(2,1)S(1)} collective-permute-done((bf16[512,128]{1,0:T(8,128)(2,1)S(1)}, bf16[512,128]{1,0:T(8,128)(2,1)S(1)}, u32[]{:S(2)}, u32[]{:S(2)}) %collective-permute-start.8) | collective-permute-done | bytes 131104 | tf_op jit(solution)/shard_map/ppermute | solution.py:220
  17.9 0.0 collective-permute-start.9
  17.9 0.9 %collective-permute-done.5.refs_5_ = bf16[512,128]{1,0:T(8,128)(2,1)S(1)} collective-permute-done((bf16[512,128]{1,0:T(8,128)(2,1)S(1)}, bf16[512,128]{1,0:T(8,128)(2,1)S(1)}, u32[]{:S(2)}, u32[]{:S(2)}) %collective-permute-start.5) | collective-permute-done | bytes 131104 | tf_op jit(solution)/shard_map/ppermute | solution.py:220
  18.7 0.0 collective-permute-start.6
  18.7 0.0 collective-permute-done.3.refs_4_
  18.7 0.5 %collective-permute-start.4 = (bf16[512,128]{1,0:T(8,128)(2,1)S(1)}, bf16[512,128]{1,0:T(8,128)(2,1)S(1)}, u32[]{:S(2)}, u32[]{:S(2)}) collective-permute-start(bf16[512,128]{1,0:T(8,128)(2,1)S(1)} %collective-permute-done.3.refs_4_), channel_id=1, source_target_pairs={{0,1},{1,0},{2,3},{3,2},{4,5},{5,4},{6,7},{7,6},{8,9},{9,8},{10,11... | collective-permute-start | bytes 393224 | tf_op jit(solution)/shard_map/ppermute | solution.py:220
  19.2 0.0 collective-permute-done.7.refs_1_
  19.3 0.0 collective-permute-done.9.refs_3_
  19.3 0.7 %first_pieces.1 = (bf16[512,768]{1,0:T(8,128)(2,1)S(1)}, bf16[768,512]{1,0:T(8,128)(2,1)S(1)}, f32[512,512]{1,0:T(8,128)S(1)}) custom-call(bf16[512,128]{1,0:T(8,128)(2,1)S(1)} %constant_dynamic-update-slice_fusion.refs_0_, bf16[512,128]{1,0:T(8,128)(2,1)S(1)} %collective-permute-done.7.refs_1_, bf16[512,128]{1,0:T(8,128)(2,1)S(1)} %collective-permute-done.8.refs_2_, ...), custom_call_target="tpu_custom_call" | custom-call | flops 400000000 | tf_op jit(solution)/shard_map/first_pieces/pallas_call | solution.py:234
  19.9 0.2 collective-permute-done.6.late1
  20.1 0.2 collective-permute-done.4.late0
  20.3 6.4 %whole_block.1 = bf16[768,1024]{1,0:T(8,128)(2,1)} custom-call(bf16[512,128]{1,0:T(8,128)(2,1)S(1)} %collective-permute-done.4.late0, bf16[512,128]{1,0:T(8,128)(2,1)S(1)} %collective-permute-done.6.late1, bf16[512,768]{1,0:T(8,128)(2,1)S(1)} %get-tuple-element.16.x, bf16[768,512]{1,0:T(8,128)(2,1)S(1)} %get-tuple-element.17.xt, ...), custom_call_target="tpu_custom_call" | custom-call | flops 5000000000 | tf_op jit(solution)/shard_map/whole_block/pallas_call | solution.py:243
  (4 shorter events, 0.0 us)
Async XLA Ops:
  0.0 0.9 %copy-start = (bf16[128,4,128]{2,1,0:T(4,128)(2,1)S(1)}, bf16[128,4,128]{2,1,0:T(4,128)(2,1)}, u32[]{:S(2)}) copy-start(bf16[128,4,128]{2,1,0:T(4,128)(2,1)} %param.2) | copy-start | bytes 393220
  1.2 7.0 %collective-permute-start = (bf16[128,128]{1,0:T(8,128)(2,1)S(1)}, bf16[128,128]{1,0:T(8,128)(2,1)S(1)}, u32[]{:S(2)}, u32[]{:S(2)}) collective-permute-start(bf16[128,128]{1,0:T(8,128)(2,1)S(1)} %get-tuple-element.13), channel_id=1, source_target_pairs={{0,8},{8,16},{16,24},{24,0},{1,9},{9,17},{17,25},{25,1},{2,10},{10... | collective-permute-start | bytes 98312 | tf_op jit(solution)/shard_map/ppermute | solution.py:224
  4.3 5.2 %collective-permute-start.1 = (bf16[128,128]{1,0:T(8,128)(2,1)S(1)}, bf16[128,128]{1,0:T(8,128)(2,1)S(1)}, u32[]{:S(2)}, u32[]{:S(2)}) collective-permute-start(bf16[128,128]{1,0:T(8,128)(2,1)S(1)} %get-tuple-element.14), channel_id=1, source_target_pairs={{0,16},{8,24},{16,0},{24,8},{1,17},{9,25},{17,1},{25,9},{2,18},{10... | collective-permute-start | bytes 98312 | tf_op jit(solution)/shard_map/ppermute | solution.py:224
  6.9 3.9 %collective-permute-start.2 = (bf16[128,128]{1,0:T(8,128)(2,1)S(1)}, bf16[128,128]{1,0:T(8,128)(2,1)S(1)}, u32[]{:S(2)}, u32[]{:S(2)}) collective-permute-start(bf16[128,128]{1,0:T(8,128)(2,1)S(1)} %get-tuple-element.15), channel_id=1, source_target_pairs={{0,24},{8,0},{16,8},{24,16},{1,25},{9,1},{17,9},{25,17},{2,26},{10... | collective-permute-start | bytes 98312 | tf_op jit(solution)/shard_map/ppermute | solution.py:224
  10.8 7.1 %collective-permute-start.8 = (bf16[512,128]{1,0:T(8,128)(2,1)S(1)}, bf16[512,128]{1,0:T(8,128)(2,1)S(1)}, u32[]{:S(2)}, u32[]{:S(2)}) collective-permute-start(bf16[512,128]{1,0:T(8,128)(2,1)S(1)} %constant_dynamic-update-slice_fusion.refs_0_), channel_id=1, source_target_pairs={{0,6},{1,7},{2,4},{3,5},{4,2},{5,3},{6,0},{7,1},{8,14},{9,15},{10,... | collective-permute-start | bytes 393224 | tf_op jit(solution)/shard_map/ppermute | solution.py:220
  13.2 5.5 %collective-permute-start.5 = (bf16[512,128]{1,0:T(8,128)(2,1)S(1)}, bf16[512,128]{1,0:T(8,128)(2,1)S(1)}, u32[]{:S(2)}, u32[]{:S(2)}) collective-permute-start(bf16[512,128]{1,0:T(8,128)(2,1)S(1)} %constant_dynamic-update-slice_fusion.refs_0_), channel_id=1, source_target_pairs={{0,4},{1,5},{2,6},{3,7},{4,0},{5,1},{6,2},{7,3},{8,12},{9,13},{10,... | collective-permute-start | bytes 393224 | tf_op jit(solution)/shard_map/ppermute | solution.py:220
  13.7 5.0 %collective-permute-start.3 = (bf16[512,128]{1,0:T(8,128)(2,1)S(1)}, bf16[512,128]{1,0:T(8,128)(2,1)S(1)}, u32[]{:S(2)}, u32[]{:S(2)}) collective-permute-start(bf16[512,128]{1,0:T(8,128)(2,1)S(1)} %constant_dynamic-update-slice_fusion.refs_0_), channel_id=1, source_target_pairs={{0,2},{1,3},{2,0},{3,1},{4,6},{5,7},{6,4},{7,5},{8,10},{9,11},{10,... | collective-permute-start | bytes 393224 | tf_op jit(solution)/shard_map/ppermute | solution.py:220
  14.3 5.0 %collective-permute-start.7 = (bf16[512,128]{1,0:T(8,128)(2,1)S(1)}, bf16[512,128]{1,0:T(8,128)(2,1)S(1)}, u32[]{:S(2)}, u32[]{:S(2)}) collective-permute-start(bf16[512,128]{1,0:T(8,128)(2,1)S(1)} %constant_dynamic-update-slice_fusion.refs_0_), channel_id=1, source_target_pairs={{0,1},{1,0},{2,3},{3,2},{4,5},{5,4},{6,7},{7,6},{8,9},{9,8},{10,11... | collective-permute-start | bytes 393224 | tf_op jit(solution)/shard_map/ppermute | solution.py:220
  17.9 1.4 %collective-permute-start.9 = (bf16[512,128]{1,0:T(8,128)(2,1)S(1)}, bf16[512,128]{1,0:T(8,128)(2,1)S(1)}, u32[]{:S(2)}, u32[]{:S(2)}) collective-permute-start(bf16[512,128]{1,0:T(8,128)(2,1)S(1)} %collective-permute-done.8.refs_2_), channel_id=1, source_target_pairs={{0,1},{1,0},{2,3},{3,2},{4,5},{5,4},{6,7},{7,6},{8,9},{9,8},{10,11... | collective-permute-start | bytes 393224 | tf_op jit(solution)/shard_map/ppermute | solution.py:220
  18.7 1.3 %collective-permute-start.6 = (bf16[512,128]{1,0:T(8,128)(2,1)S(1)}, bf16[512,128]{1,0:T(8,128)(2,1)S(1)}, u32[]{:S(2)}, u32[]{:S(2)}) collective-permute-start(bf16[512,128]{1,0:T(8,128)(2,1)S(1)} %collective-permute-done.5.refs_5_), channel_id=1, source_target_pairs={{0,1},{1,0},{2,3},{3,2},{4,5},{5,4},{6,7},{7,6},{8,9},{9,8},{10,11... | collective-permute-start | bytes 393224 | tf_op jit(solution)/shard_map/ppermute | solution.py:220
  18.7 1.5 %collective-permute-start.4 = (bf16[512,128]{1,0:T(8,128)(2,1)S(1)}, bf16[512,128]{1,0:T(8,128)(2,1)S(1)}, u32[]{:S(2)}, u32[]{:S(2)}) collective-permute-start(bf16[512,128]{1,0:T(8,128)(2,1)S(1)} %collective-permute-done.3.refs_4_), channel_id=1, source_target_pairs={{0,1},{1,0},{2,3},{3,2},{4,5},{5,4},{6,7},{7,6},{8,9},{9,8},{10,11... | collective-permute-start | bytes 393224 | tf_op jit(solution)/shard_map/ppermute | solution.py:220

commit v22 on v20

--- a/solution.py
+++ b/solution.py
@@ -179,29 +179,41 @@
     symmetric(e2, e2, fourth, z, h)
 
     def apply(left, right, parts, result, scale=None):
-        for some in halves:
-            product = dot(left[...], right[:, some])
-            for r in chunks_of(product.shape[0]):
+        for some in sides:
+            product = dot(left[some, :], right[...])
+            for r in chunks_of(some.stop - some.start):
+                here = slice(some.start + r.start, some.start + r.stop)
                 total = product[r] if scale is None else product[r] * scale
                 for weight, part in parts:
-                    total = total + weight * part[r, some].astype(jnp.float32)
-                result[r, some] = total.astype(jnp.bfloat16)
-
+                    total = total + weight * part[here, :].astype(jnp.float32)
+                result[here, :] = total.astype(jnp.bfloat16)
+
+    rows = tile.shape[0]
+    sides = [slice(0, rows // 2), slice(rows // 2, rows)]
     apply(image, g, [(g_m, image)], by_g)
     symmetric(z, z, lambda product, r, some: [product + k_z * wide(z, r, some)], k)
     apply(by_g, h, [(h_m, by_g)], by_h)
     apply(by_h, k, [(last * (1.0 + eps2) * beta, image), (last * beta, by_g), (last * k_m, by_h)], mixed, last)
     stores = []
-    for n in range(len(blocks) + 1):
-        moved = dot(mixed[...], late[...] if n == len(blocks) else x[:, blocks[n]])
-        for one in (0, 1):
-            here = place(fars[2 * n + one])
-            part = slice(one * features, (one + 1) * features)
-            for r in chunks_of(moved.shape[0]):
-                out[r, here] = (p * tile[r, here].astype(jnp.float32) + moved[r, part]).astype(jnp.bfloat16)
-            store = pltpu.make_async_copy(out.at[:, here], out_hbm.at[:, here], sems.at[1 + len(stores)])
-            store.start()
-            stores.append(store)
+
+    def send(some, here):
+        store = pltpu.make_async_copy(out.at[some, here], out_hbm.at[some, here], sems.at[1 + len(stores)])
+        store.start()
+        stores.append(store)
+
+    for some in sides:
+        for n in range(len(blocks) + 1):
+            moved = dot(mixed[some, :], late[...] if n == len(blocks) else x[:, blocks[n]])
+            for one in (0, 1):
+                here = place(fars[2 * n + one])
+                part = slice(one * features, (one + 1) * features)
+                for r in chunks_of(moved.shape[0]):
+                    at = slice(some.start + r.start, some.start + r.stop)
+                    out[at, here] = (p * tile[at, here].astype(jnp.float32) + moved[r, part]).astype(jnp.bfloat16)
+                if some is sides[-1]:
+                    send(some, here)
+        if some is not sides[-1]:
+            send(some, slice(None))
     for store in stores:
         store.wait()
 
@@ -252,7 +264,7 @@
         + [scratch(tokens, tokens)] * 7
         + [scratch(rows, tokens)] * 4
         + [pltpu.VMEM((2 * features * n, 128), jnp.float32) for n in range(1, members // 2)]
-        + [pltpu.SemaphoreType.DMA((1 + members,))],
+        + [pltpu.SemaphoreType.DMA((2 + members,))],
         compiler_params=pltpu.CompilerParams(vmem_limit_bytes=51 * 2**20),
         cost_estimate=pl.CostEstimate(flops=5 * 10**9, bytes_accessed=0, transcendentals=0),
         name="whole_block",

time: 26.9 us -> 26.9 us (level)
  no operation moved by 1% of the time
where the time goes in v22:
time: 26.9 us; the launch traced here: 26.8 us
  starting transfers between devices  11 us (41%)
  Pallas kernels  7.48 us (28%)
  waiting for transfers between devices  7.34 us (27%)
  local copies, waits for them, and re-layouts  0.93 us (3%)
    ppermute x3, starting transfers between devices, by_tokens(): lax.ppermute(parts[far], 'dp', [(i, (i + far) % replicas) for i in range(...  7.01 us
    pallas_call x1, Pallas kernels, by_tokens(): pl.pallas_call(functools.partial(last_kernel, fars), out_shape=shape(rows...  6.53 us
    ppermute x7, waiting for transfers between devices, swap(): return lax.ppermute(value, 'grad', [(i, i ^ far) for i in range(members)])  4.8 us
    ppermute x7, starting transfers between devices, swap(): return lax.ppermute(value, 'grad', [(i, i ^ far) for i in range(members)])  4 us
    ppermute x3, waiting for transfers between devices, by_tokens(): lax.ppermute(parts[far], 'dp', [(i, (i + far) % replicas) for i in range(...  2.54 us
    unnamed x5, local copies, waits for them, and re-layouts  0.92 us
    pallas_call x1, Pallas kernels, by_tokens(): pl.pallas_call(first_kernel, out_shape=[shape(tokens, early), shape(early...  0.67 us
  transfers between devices with their start and end apart: 10, of which 6 were waited for; matrix products, arithmetic and copies ran while one was open for 0% of the time, Pallas kernels for 2%

profile of v22, /device:TPU:0, one launch (start us, length us, event | category | flops | bytes accessed | tf_op | source)
XLA Modules:
  0.0 26.8 jit_solution(2128112593574211248)
XLA Ops:
  0.0 0.0 copy-start
  0.0 0.9 %copy-done = bf16[128,4,128]{2,1,0:T(4,128)(2,1)S(1)} copy-done((bf16[128,4,128]{2,1,0:T(4,128)(2,1)S(1)}, bf16[128,4,128]{2,1,0:T(4,128)(2,1)}, u32[]{:S(2)}) %copy-start) | copy-done | bytes 131096
  0.9 0.3 %split_blocks.1 = (bf16[128,128]{1,0:T(8,128)(2,1)S(1)}, bf16[128,128]{1,0:T(8,128)(2,1)S(1)}, bf16[128,128]{1,0:T(8,128)(2,1)S(1)}, bf16[128,128]{1,0:T(8,128)(2,1)S(1)}) custom-call(bf16[512,128]{1,0:T(8,128)(2,1)S(1)} %bitcast.3), custom_call_target="tpu_custom_call" | custom-call | tf_op jit(solution)/shard_map/split_blocks/pallas_call | solution.py:55
  1.2 3.1 %collective-permute-start = (bf16[128,128]{1,0:T(8,128)(2,1)S(1)}, bf16[128,128]{1,0:T(8,128)(2,1)S(1)}, u32[]{:S(2)}, u32[]{:S(2)}) collective-permute-start(bf16[128,128]{1,0:T(8,128)(2,1)S(1)} %get-tuple-element.13), channel_id=1, source_target_pairs={{0,8},{8,16},{16,24},{24,0},{1,9},{9,17},{17,25},{25,1},{2,10},{10... | collective-permute-start | bytes 98312 | tf_op jit(solution)/shard_map/ppermute | solution.py:238
  4.3 2.6 %collective-permute-start.1 = (bf16[128,128]{1,0:T(8,128)(2,1)S(1)}, bf16[128,128]{1,0:T(8,128)(2,1)S(1)}, u32[]{:S(2)}, u32[]{:S(2)}) collective-permute-start(bf16[128,128]{1,0:T(8,128)(2,1)S(1)} %get-tuple-element.14), channel_id=1, source_target_pairs={{0,16},{8,24},{16,0},{24,8},{1,17},{9,25},{17,1},{25,9},{2,18},{10... | collective-permute-start | bytes 98312 | tf_op jit(solution)/shard_map/ppermute | solution.py:238
  6.9 1.3 %collective-permute-start.2 = (bf16[128,128]{1,0:T(8,128)(2,1)S(1)}, bf16[128,128]{1,0:T(8,128)(2,1)S(1)}, u32[]{:S(2)}, u32[]{:S(2)}) collective-permute-start(bf16[128,128]{1,0:T(8,128)(2,1)S(1)} %get-tuple-element.15), channel_id=1, source_target_pairs={{0,24},{8,0},{16,8},{24,16},{1,25},{9,1},{17,9},{25,17},{2,26},{10... | collective-permute-start | bytes 98312 | tf_op jit(solution)/shard_map/ppermute | solution.py:238
  8.2 0.0 collective-permute-done
  8.2 1.2 %collective-permute-done.1 = bf16[128,128]{1,0:T(8,128)(2,1)S(1)} collective-permute-done((bf16[128,128]{1,0:T(8,128)(2,1)S(1)}, bf16[128,128]{1,0:T(8,128)(2,1)S(1)}, u32[]{:S(2)}, u32[]{:S(2)}) %collective-permute-start.1) | collective-permute-done | bytes 32800 | tf_op jit(solution)/shard_map/ppermute | solution.py:238
  9.4 1.3 %collective-permute-done.2 = bf16[128,128]{1,0:T(8,128)(2,1)S(1)} collective-permute-done((bf16[128,128]{1,0:T(8,128)(2,1)S(1)}, bf16[128,128]{1,0:T(8,128)(2,1)S(1)}, u32[]{:S(2)}, u32[]{:S(2)}) %collective-permute-start.2) | collective-permute-done | bytes 32800 | tf_op jit(solution)/shard_map/ppermute | solution.py:238
  10.8 2.4 %collective-permute-start.8 = (bf16[512,128]{1,0:T(8,128)(2,1)S(1)}, bf16[512,128]{1,0:T(8,128)(2,1)S(1)}, u32[]{:S(2)}, u32[]{:S(2)}) collective-permute-start(bf16[512,128]{1,0:T(8,128)(2,1)S(1)} %constant_dynamic-update-slice_fusion.refs_0_), channel_id=1, source_target_pairs={{0,6},{1,7},{2,4},{3,5},{4,2},{5,3},{6,0},{7,1},{8,14},{9,15},{10,... | collective-permute-start | bytes 393224 | tf_op jit(solution)/shard_map/ppermute | solution.py:234
  13.2 0.5 %collective-permute-start.5 = (bf16[512,128]{1,0:T(8,128)(2,1)S(1)}, bf16[512,128]{1,0:T(8,128)(2,1)S(1)}, u32[]{:S(2)}, u32[]{:S(2)}) collective-permute-start(bf16[512,128]{1,0:T(8,128)(2,1)S(1)} %constant_dynamic-update-slice_fusion.refs_0_), channel_id=1, source_target_pairs={{0,4},{1,5},{2,6},{3,7},{4,0},{5,1},{6,2},{7,3},{8,12},{9,13},{10,... | collective-permute-start | bytes 393224 | tf_op jit(solution)/shard_map/ppermute | solution.py:234
  13.7 0.5 %collective-permute-start.3 = (bf16[512,128]{1,0:T(8,128)(2,1)S(1)}, bf16[512,128]{1,0:T(8,128)(2,1)S(1)}, u32[]{:S(2)}, u32[]{:S(2)}) collective-permute-start(bf16[512,128]{1,0:T(8,128)(2,1)S(1)} %constant_dynamic-update-slice_fusion.refs_0_), channel_id=1, source_target_pairs={{0,2},{1,3},{2,0},{3,1},{4,6},{5,7},{6,4},{7,5},{8,10},{9,11},{10,... | collective-permute-start | bytes 393224 | tf_op jit(solution)/shard_map/ppermute | solution.py:234
  14.3 0.0 collective-permute-start.7
  14.3 3.6 %collective-permute-done.8.refs_2_ = bf16[512,128]{1,0:T(8,128)(2,1)S(1)} collective-permute-done((bf16[512,128]{1,0:T(8,128)(2,1)S(1)}, bf16[512,128]{1,0:T(8,128)(2,1)S(1)}, u32[]{:S(2)}, u32[]{:S(2)}) %collective-permute-start.8) | collective-permute-done | bytes 131104 | tf_op jit(solution)/shard_map/ppermute | solution.py:234
  17.9 0.0 collective-permute-start.9
  17.9 0.9 %collective-permute-done.5.refs_5_ = bf16[512,128]{1,0:T(8,128)(2,1)S(1)} collective-permute-done((bf16[512,128]{1,0:T(8,128)(2,1)S(1)}, bf16[512,128]{1,0:T(8,128)(2,1)S(1)}, u32[]{:S(2)}, u32[]{:S(2)}) %collective-permute-start.5) | collective-permute-done | bytes 131104 | tf_op jit(solution)/shard_map/ppermute | solution.py:234
  18.7 0.0 collective-permute-start.6
  18.7 0.0 collective-permute-done.3.refs_4_
  18.7 0.5 %collective-permute-start.4 = (bf16[512,128]{1,0:T(8,128)(2,1)S(1)}, bf16[512,128]{1,0:T(8,128)(2,1)S(1)}, u32[]{:S(2)}, u32[]{:S(2)}) collective-permute-start(bf16[512,128]{1,0:T(8,128)(2,1)S(1)} %collective-permute-done.3.refs_4_), channel_id=1, source_target_pairs={{0,1},{1,0},{2,3},{3,2},{4,5},{5,4},{6,7},{7,6},{8,9},{9,8},{10,11... | collective-permute-start | bytes 393224 | tf_op jit(solution)/shard_map/ppermute | solution.py:234
  19.2 0.0 collective-permute-done.7.refs_1_
  19.3 0.0 collective-permute-done.9.refs_3_
  19.3 0.7 %first_pieces.1 = (bf16[512,768]{1,0:T(8,128)(2,1)S(1)}, bf16[768,512]{1,0:T(8,128)(2,1)S(1)}, f32[512,512]{1,0:T(8,128)S(1)}) custom-call(bf16[512,128]{1,0:T(8,128)(2,1)S(1)} %constant_dynamic-update-slice_fusion.refs_0_, bf16[512,128]{1,0:T(8,128)(2,1)S(1)} %collective-permute-done.7.refs_1_, bf16[512,128]{1,0:T(8,128)(2,1)S(1)} %collective-permute-done.8.refs_2_, ...), custom_call_target="tpu_custom_call" | custom-call | flops 400000000 | tf_op jit(solution)/shard_map/first_pieces/pallas_call | solution.py:248
  19.9 0.2 collective-permute-done.6.late1
  20.1 0.2 collective-permute-done.4.late0
  20.3 6.5 %whole_block.1 = bf16[768,1024]{1,0:T(8,128)(2,1)} custom-call(bf16[512,128]{1,0:T(8,128)(2,1)S(1)} %collective-permute-done.4.late0, bf16[512,128]{1,0:T(8,128)(2,1)S(1)} %collective-permute-done.6.late1, bf16[512,768]{1,0:T(8,128)(2,1)S(1)} %get-tuple-element.16.x, bf16[768,512]{1,0:T(8,128)(2,1)S(1)} %get-tuple-element.17.xt, ...), custom_call_target="tpu_custom_call" | custom-call | flops 5000000000 | tf_op jit(solution)/shard_map/whole_block/pallas_call | solution.py:257
  (4 shorter events, 0.0 us)
Async XLA Ops:
  0.0 0.9 %copy-start = (bf16[128,4,128]{2,1,0:T(4,128)(2,1)S(1)}, bf16[128,4,128]{2,1,0:T(4,128)(2,1)}, u32[]{:S(2)}) copy-start(bf16[128,4,128]{2,1,0:T(4,128)(2,1)} %param.2) | copy-start | bytes 393220
  1.2 7.0 %collective-permute-start = (bf16[128,128]{1,0:T(8,128)(2,1)S(1)}, bf16[128,128]{1,0:T(8,128)(2,1)S(1)}, u32[]{:S(2)}, u32[]{:S(2)}) collective-permute-start(bf16[128,128]{1,0:T(8,128)(2,1)S(1)} %get-tuple-element.13), channel_id=1, source_target_pairs={{0,8},{8,16},{16,24},{24,0},{1,9},{9,17},{17,25},{25,1},{2,10},{10... | collective-permute-start | bytes 98312 | tf_op jit(solution)/shard_map/ppermute | solution.py:238
  4.3 5.2 %collective-permute-start.1 = (bf16[128,128]{1,0:T(8,128)(2,1)S(1)}, bf16[128,128]{1,0:T(8,128)(2,1)S(1)}, u32[]{:S(2)}, u32[]{:S(2)}) collective-permute-start(bf16[128,128]{1,0:T(8,128)(2,1)S(1)} %get-tuple-element.14), channel_id=1, source_target_pairs={{0,16},{8,24},{16,0},{24,8},{1,17},{9,25},{17,1},{25,9},{2,18},{10... | collective-permute-start | bytes 98312 | tf_op jit(solution)/shard_map/ppermute | solution.py:238
  6.9 3.9 %collective-permute-start.2 = (bf16[128,128]{1,0:T(8,128)(2,1)S(1)}, bf16[128,128]{1,0:T(8,128)(2,1)S(1)}, u32[]{:S(2)}, u32[]{:S(2)}) collective-permute-start(bf16[128,128]{1,0:T(8,128)(2,1)S(1)} %get-tuple-element.15), channel_id=1, source_target_pairs={{0,24},{8,0},{16,8},{24,16},{1,25},{9,1},{17,9},{25,17},{2,26},{10... | collective-permute-start | bytes 98312 | tf_op jit(solution)/shard_map/ppermute | solution.py:238
  10.8 7.1 %collective-permute-start.8 = (bf16[512,128]{1,0:T(8,128)(2,1)S(1)}, bf16[512,128]{1,0:T(8,128)(2,1)S(1)}, u32[]{:S(2)}, u32[]{:S(2)}) collective-permute-start(bf16[512,128]{1,0:T(8,128)(2,1)S(1)} %constant_dynamic-update-slice_fusion.refs_0_), channel_id=1, source_target_pairs={{0,6},{1,7},{2,4},{3,5},{4,2},{5,3},{6,0},{7,1},{8,14},{9,15},{10,... | collective-permute-start | bytes 393224 | tf_op jit(solution)/shard_map/ppermute | solution.py:234
  13.2 5.5 %collective-permute-start.5 = (bf16[512,128]{1,0:T(8,128)(2,1)S(1)}, bf16[512,128]{1,0:T(8,128)(2,1)S(1)}, u32[]{:S(2)}, u32[]{:S(2)}) collective-permute-start(bf16[512,128]{1,0:T(8,128)(2,1)S(1)} %constant_dynamic-update-slice_fusion.refs_0_), channel_id=1, source_target_pairs={{0,4},{1,5},{2,6},{3,7},{4,0},{5,1},{6,2},{7,3},{8,12},{9,13},{10,... | collective-permute-start | bytes 393224 | tf_op jit(solution)/shard_map/ppermute | solution.py:234
  13.7 5.0 %collective-permute-start.3 = (bf16[512,128]{1,0:T(8,128)(2,1)S(1)}, bf16[512,128]{1,0:T(8,128)(2,1)S(1)}, u32[]{:S(2)}, u32[]{:S(2)}) collective-permute-start(bf16[512,128]{1,0:T(8,128)(2,1)S(1)} %constant_dynamic-update-slice_fusion.refs_0_), channel_id=1, source_target_pairs={{0,2},{1,3},{2,0},{3,1},{4,6},{5,7},{6,4},{7,5},{8,10},{9,11},{10,... | collective-permute-start | bytes 393224 | tf_op jit(solution)/shard_map/ppermute | solution.py:234
  14.3 5.0 %collective-permute-start.7 = (bf16[512,128]{1,0:T(8,128)(2,1)S(1)}, bf16[512,128]{1,0:T(8,128)(2,1)S(1)}, u32[]{:S(2)}, u32[]{:S(2)}) collective-permute-start(bf16[512,128]{1,0:T(8,128)(2,1)S(1)} %constant_dynamic-update-slice_fusion.refs_0_), channel_id=1, source_target_pairs={{0,1},{1,0},{2,3},{3,2},{4,5},{5,4},{6,7},{7,6},{8,9},{9,8},{10,11... | collective-permute-start | bytes 393224 | tf_op jit(solution)/shard_map/ppermute | solution.py:234
  17.9 1.4 %collective-permute-start.9 = (bf16[512,128]{1,0:T(8,128)(2,1)S(1)}, bf16[512,128]{1,0:T(8,128)(2,1)S(1)}, u32[]{:S(2)}, u32[]{:S(2)}) collective-permute-start(bf16[512,128]{1,0:T(8,128)(2,1)S(1)} %collective-permute-done.8.refs_2_), channel_id=1, source_target_pairs={{0,1},{1,0},{2,3},{3,2},{4,5},{5,4},{6,7},{7,6},{8,9},{9,8},{10,11... | collective-permute-start | bytes 393224 | tf_op jit(solution)/shard_map/ppermute | solution.py:234
  18.7 1.3 %collective-permute-start.6 = (bf16[512,128]{1,0:T(8,128)(2,1)S(1)}, bf16[512,128]{1,0:T(8,128)(2,1)S(1)}, u32[]{:S(2)}, u32[]{:S(2)}) collective-permute-start(bf16[512,128]{1,0:T(8,128)(2,1)S(1)} %collective-permute-done.5.refs_5_), channel_id=1, source_target_pairs={{0,1},{1,0},{2,3},{3,2},{4,5},{5,4},{6,7},{7,6},{8,9},{9,8},{10,11... | collective-permute-start | bytes 393224 | tf_op jit(solution)/shard_map/ppermute | solution.py:234
  18.7 1.5 %collective-permute-start.4 = (bf16[512,128]{1,0:T(8,128)(2,1)S(1)}, bf16[512,128]{1,0:T(8,128)(2,1)S(1)}, u32[]{:S(2)}, u32[]{:S(2)}) collective-permute-start(bf16[512,128]{1,0:T(8,128)(2,1)S(1)} %collective-permute-done.3.refs_4_), channel_id=1, source_target_pairs={{0,1},{1,0},{2,3},{3,2},{4,5},{5,4},{6,7},{7,6},{8,9},{9,8},{10,11... | collective-permute-start | bytes 393224 | tf_op jit(solution)/shard_map/ppermute | solution.py:234

commit v23 on v20

--- a/solution.py
+++ b/solution.py
@@ -222,9 +222,9 @@
         return lax.ppermute(value, "grad", [(i, i ^ far) for i in range(members)])
 
     parts = list(split_blocks(factor_inputs, range(replicas)))
-    for far in range(1, replicas):
+    for far in range(replicas - 1, 0, -1):
         parts[far] = lax.ppermute(parts[far], "dp", [(i, (i + far) % replicas) for i in range(replicas)])
-    own = jnp.concatenate(parts, axis=0)
+    own = jnp.concatenate(parts[:1] + parts[:0:-1], axis=0)
     fars = (0, 1, 6, 7, 2, 4, 3, 5)
     pieces = {0: own}
     for far in (2, 4, 6):

time: 26.9 us -> 28.2 us (1.048)
  waiting for transfers between devices: 7.34 us -> 9.58 us
  starting transfers between devices: 11 us -> 10.1 us
    ppermute x3, waiting for transfers between devices: 2.54 us -> 4.68 us  [by_tokens(): lax.ppermute(parts[far], 'dp', [(i, (i + far) % replicas) for i in range(...]
    ppermute x3, starting transfers between devices: 7.01 us -> 6.12 us  [by_tokens(): lax.ppermute(parts[far], 'dp', [(i, (i + far) % replicas) for i in range(...]
  transfers between devices with their start and end apart: 10 -> 10, of which waited for: 6 -> 8; matrix products, arithmetic and copies ran while one was open for 0% -> 0% of each run, Pallas kernels for 2% -> 2%
where the time goes in v23:
time: 28.2 us; the launch traced here: 28 us
  starting transfers between devices  10.1 us (36%)
  waiting for transfers between devices  9.58 us (34%)
  Pallas kernels  7.36 us (26%)
  local copies, waits for them, and re-layouts  0.93 us (3%)
    pallas_call x1, Pallas kernels, by_tokens(): pl.pallas_call(functools.partial(last_kernel, fars), out_shape=shape(rows...  6.41 us
    ppermute x3, starting transfers between devices, by_tokens(): lax.ppermute(parts[far], 'dp', [(i, (i + far) % replicas) for i in range(...  6.12 us
    ppermute x7, waiting for transfers between devices, swap(): return lax.ppermute(value, 'grad', [(i, i ^ far) for i in range(members)])  4.9 us
    ppermute x3, waiting for transfers between devices, by_tokens(): lax.ppermute(parts[far], 'dp', [(i, (i + far) % replicas) for i in range(...  4.68 us
    ppermute x7, starting transfers between devices, swap(): return lax.ppermute(value, 'grad', [(i, i ^ far) for i in range(members)])  4 us
    unnamed x5, local copies, waits for them, and re-layouts  0.92 us
    pallas_call x1, Pallas kernels, by_tokens(): pl.pallas_call(first_kernel, out_shape=[shape(tokens, early), shape(early...  0.66 us
  transfers between devices with their start and end apart: 10, of which 8 were waited for; matrix products, arithmetic and copies ran while one was open for 0% of the time, Pallas kernels for 2%

profile of v23, /device:TPU:0, one launch (start us, length us, event | category | flops | bytes accessed | tf_op | source)
XLA Modules:
  0.0 28.0 jit_solution(12174276252146887584)
XLA Ops:
  0.0 0.0 copy-start
  0.0 0.9 %copy-done = bf16[128,4,128]{2,1,0:T(4,128)(2,1)S(1)} copy-done((bf16[128,4,128]{2,1,0:T(4,128)(2,1)S(1)}, bf16[128,4,128]{2,1,0:T(4,128)(2,1)}, u32[]{:S(2)}) %copy-start) | copy-done | bytes 131096
  0.9 0.3 %split_blocks.1 = (bf16[128,128]{1,0:T(8,128)(2,1)S(1)}, bf16[128,128]{1,0:T(8,128)(2,1)S(1)}, bf16[128,128]{1,0:T(8,128)(2,1)S(1)}, bf16[128,128]{1,0:T(8,128)(2,1)S(1)}) custom-call(bf16[512,128]{1,0:T(8,128)(2,1)S(1)} %bitcast.3), custom_call_target="tpu_custom_call" | custom-call | tf_op jit(solution)/shard_map/split_blocks/pallas_call | solution.py:55
  1.2 5.1 %collective-permute-start = (bf16[128,128]{1,0:T(8,128)(2,1)S(1)}, bf16[128,128]{1,0:T(8,128)(2,1)S(1)}, u32[]{:S(2)}, u32[]{:S(2)}) collective-permute-start(bf16[128,128]{1,0:T(8,128)(2,1)S(1)} %get-tuple-element.13), channel_id=1, source_target_pairs={{0,24},{8,0},{16,8},{24,16},{1,25},{9,1},{17,9},{25,17},{2,26},{10... | collective-permute-start | bytes 98312 | tf_op jit(solution)/shard_map/ppermute | solution.py:226
  6.3 0.0 collective-permute-start.1
  6.3 1.0 %collective-permute-start.2 = (bf16[128,128]{1,0:T(8,128)(2,1)S(1)}, bf16[128,128]{1,0:T(8,128)(2,1)S(1)}, u32[]{:S(2)}, u32[]{:S(2)}) collective-permute-start(bf16[128,128]{1,0:T(8,128)(2,1)S(1)} %get-tuple-element.15), channel_id=1, source_target_pairs={{0,8},{8,16},{16,24},{24,0},{1,9},{9,17},{17,25},{25,1},{2,10},{10... | collective-permute-start | bytes 98312 | tf_op jit(solution)/shard_map/ppermute | solution.py:226
  7.3 0.6 %collective-permute-done = bf16[128,128]{1,0:T(8,128)(2,1)S(1)} collective-permute-done((bf16[128,128]{1,0:T(8,128)(2,1)S(1)}, bf16[128,128]{1,0:T(8,128)(2,1)S(1)}, u32[]{:S(2)}, u32[]{:S(2)}) %collective-permute-start) | collective-permute-done | bytes 32800 | tf_op jit(solution)/shard_map/ppermute | solution.py:226
  7.9 3.2 %collective-permute-done.1 = bf16[128,128]{1,0:T(8,128)(2,1)S(1)} collective-permute-done((bf16[128,128]{1,0:T(8,128)(2,1)S(1)}, bf16[128,128]{1,0:T(8,128)(2,1)S(1)}, u32[]{:S(2)}, u32[]{:S(2)}) %collective-permute-start.1) | collective-permute-done | bytes 32800 | tf_op jit(solution)/shard_map/ppermute | solution.py:226
  11.1 0.9 %collective-permute-done.2 = bf16[128,128]{1,0:T(8,128)(2,1)S(1)} collective-permute-done((bf16[128,128]{1,0:T(8,128)(2,1)S(1)}, bf16[128,128]{1,0:T(8,128)(2,1)S(1)}, u32[]{:S(2)}, u32[]{:S(2)}) %collective-permute-start.2) | collective-permute-done | bytes 32800 | tf_op jit(solution)/shard_map/ppermute | solution.py:226
  12.0 2.4 %collective-permute-start.8 = (bf16[512,128]{1,0:T(8,128)(2,1)S(1)}, bf16[512,128]{1,0:T(8,128)(2,1)S(1)}, u32[]{:S(2)}, u32[]{:S(2)}) collective-permute-start(bf16[512,128]{1,0:T(8,128)(2,1)S(1)} %constant_dynamic-update-slice_fusion.refs_0_), channel_id=1, source_target_pairs={{0,6},{1,7},{2,4},{3,5},{4,2},{5,3},{6,0},{7,1},{8,14},{9,15},{10,... | collective-permute-start | bytes 393224 | tf_op jit(solution)/shard_map/ppermute | solution.py:222
  14.5 0.5 %collective-permute-start.5 = (bf16[512,128]{1,0:T(8,128)(2,1)S(1)}, bf16[512,128]{1,0:T(8,128)(2,1)S(1)}, u32[]{:S(2)}, u32[]{:S(2)}) collective-permute-start(bf16[512,128]{1,0:T(8,128)(2,1)S(1)} %constant_dynamic-update-slice_fusion.refs_0_), channel_id=1, source_target_pairs={{0,4},{1,5},{2,6},{3,7},{4,0},{5,1},{6,2},{7,3},{8,12},{9,13},{10,... | collective-permute-start | bytes 393224 | tf_op jit(solution)/shard_map/ppermute | solution.py:222
  15.0 0.5 %collective-permute-start.3 = (bf16[512,128]{1,0:T(8,128)(2,1)S(1)}, bf16[512,128]{1,0:T(8,128)(2,1)S(1)}, u32[]{:S(2)}, u32[]{:S(2)}) collective-permute-start(bf16[512,128]{1,0:T(8,128)(2,1)S(1)} %constant_dynamic-update-slice_fusion.refs_0_), channel_id=1, source_target_pairs={{0,2},{1,3},{2,0},{3,1},{4,6},{5,7},{6,4},{7,5},{8,10},{9,11},{10,... | collective-permute-start | bytes 393224 | tf_op jit(solution)/shard_map/ppermute | solution.py:222
  15.5 0.0 collective-permute-start.7
  15.5 3.8 %collective-permute-done.8.refs_2_ = bf16[512,128]{1,0:T(8,128)(2,1)S(1)} collective-permute-done((bf16[512,128]{1,0:T(8,128)(2,1)S(1)}, bf16[512,128]{1,0:T(8,128)(2,1)S(1)}, u32[]{:S(2)}, u32[]{:S(2)}) %collective-permute-start.8) | collective-permute-done | bytes 131104 | tf_op jit(solution)/shard_map/ppermute | solution.py:222
  19.3 0.0 collective-permute-start.9
  19.3 0.8 %collective-permute-done.5.refs_5_ = bf16[512,128]{1,0:T(8,128)(2,1)S(1)} collective-permute-done((bf16[512,128]{1,0:T(8,128)(2,1)S(1)}, bf16[512,128]{1,0:T(8,128)(2,1)S(1)}, u32[]{:S(2)}, u32[]{:S(2)}) %collective-permute-start.5) | collective-permute-done | bytes 131104 | tf_op jit(solution)/shard_map/ppermute | solution.py:222
  20.1 0.0 collective-permute-start.6
  20.1 0.0 collective-permute-done.3.refs_4_
  20.1 0.5 %collective-permute-start.4 = (bf16[512,128]{1,0:T(8,128)(2,1)S(1)}, bf16[512,128]{1,0:T(8,128)(2,1)S(1)}, u32[]{:S(2)}, u32[]{:S(2)}) collective-permute-start(bf16[512,128]{1,0:T(8,128)(2,1)S(1)} %collective-permute-done.3.refs_4_), channel_id=1, source_target_pairs={{0,1},{1,0},{2,3},{3,2},{4,5},{5,4},{6,7},{7,6},{8,9},{9,8},{10,11... | collective-permute-start | bytes 393224 | tf_op jit(solution)/shard_map/ppermute | solution.py:222
  20.6 0.0 collective-permute-done.7.refs_1_
  20.6 0.1 collective-permute-done.9.refs_3_
  20.6 0.7 %first_pieces.1 = (bf16[512,768]{1,0:T(8,128)(2,1)S(1)}, bf16[768,512]{1,0:T(8,128)(2,1)S(1)}, f32[512,512]{1,0:T(8,128)S(1)}) custom-call(bf16[512,128]{1,0:T(8,128)(2,1)S(1)} %constant_dynamic-update-slice_fusion.refs_0_, bf16[512,128]{1,0:T(8,128)(2,1)S(1)} %collective-permute-done.7.refs_1_, bf16[512,128]{1,0:T(8,128)(2,1)S(1)} %collective-permute-done.8.refs_2_, ...), custom_call_target="tpu_custom_call" | custom-call | flops 400000000 | tf_op jit(solution)/shard_map/first_pieces/pallas_call | solution.py:236
  21.3 0.1 collective-permute-done.6.late1
  21.4 0.2 collective-permute-done.4.late0
  21.6 6.4 %whole_block.1 = bf16[768,1024]{1,0:T(8,128)(2,1)} custom-call(bf16[512,128]{1,0:T(8,128)(2,1)S(1)} %collective-permute-done.4.late0, bf16[512,128]{1,0:T(8,128)(2,1)S(1)} %collective-permute-done.6.late1, bf16[512,768]{1,0:T(8,128)(2,1)S(1)} %get-tuple-element.16.x, bf16[768,512]{1,0:T(8,128)(2,1)S(1)} %get-tuple-element.17.xt, ...), custom_call_target="tpu_custom_call" | custom-call | flops 5000000000 | tf_op jit(solution)/shard_map/whole_block/pallas_call | solution.py:245
  (4 shorter events, 0.0 us)
Async XLA Ops:
  0.0 0.9 %copy-start = (bf16[128,4,128]{2,1,0:T(4,128)(2,1)S(1)}, bf16[128,4,128]{2,1,0:T(4,128)(2,1)}, u32[]{:S(2)}) copy-start(bf16[128,4,128]{2,1,0:T(4,128)(2,1)} %param.2) | copy-start | bytes 393220
  1.2 6.7 %collective-permute-start = (bf16[128,128]{1,0:T(8,128)(2,1)S(1)}, bf16[128,128]{1,0:T(8,128)(2,1)S(1)}, u32[]{:S(2)}, u32[]{:S(2)}) collective-permute-start(bf16[128,128]{1,0:T(8,128)(2,1)S(1)} %get-tuple-element.13), channel_id=1, source_target_pairs={{0,24},{8,0},{16,8},{24,16},{1,25},{9,1},{17,9},{25,17},{2,26},{10... | collective-permute-start | bytes 98312 | tf_op jit(solution)/shard_map/ppermute | solution.py:226
  6.3 4.8 %collective-permute-start.1 = (bf16[128,128]{1,0:T(8,128)(2,1)S(1)}, bf16[128,128]{1,0:T(8,128)(2,1)S(1)}, u32[]{:S(2)}, u32[]{:S(2)}) collective-permute-start(bf16[128,128]{1,0:T(8,128)(2,1)S(1)} %get-tuple-element.14), channel_id=1, source_target_pairs={{0,16},{8,24},{16,0},{24,8},{1,17},{9,25},{17,1},{25,9},{2,18},{10... | collective-permute-start | bytes 98312 | tf_op jit(solution)/shard_map/ppermute | solution.py:226
  6.3 5.7 %collective-permute-start.2 = (bf16[128,128]{1,0:T(8,128)(2,1)S(1)}, bf16[128,128]{1,0:T(8,128)(2,1)S(1)}, u32[]{:S(2)}, u32[]{:S(2)}) collective-permute-start(bf16[128,128]{1,0:T(8,128)(2,1)S(1)} %get-tuple-element.15), channel_id=1, source_target_pairs={{0,8},{8,16},{16,24},{24,0},{1,9},{9,17},{17,25},{25,1},{2,10},{10... | collective-permute-start | bytes 98312 | tf_op jit(solution)/shard_map/ppermute | solution.py:226
  12.0 7.3 %collective-permute-start.8 = (bf16[512,128]{1,0:T(8,128)(2,1)S(1)}, bf16[512,128]{1,0:T(8,128)(2,1)S(1)}, u32[]{:S(2)}, u32[]{:S(2)}) collective-permute-start(bf16[512,128]{1,0:T(8,128)(2,1)S(1)} %constant_dynamic-update-slice_fusion.refs_0_), channel_id=1, source_target_pairs={{0,6},{1,7},{2,4},{3,5},{4,2},{5,3},{6,0},{7,1},{8,14},{9,15},{10,... | collective-permute-start | bytes 393224 | tf_op jit(solution)/shard_map/ppermute | solution.py:222
  14.5 5.6 %collective-permute-start.5 = (bf16[512,128]{1,0:T(8,128)(2,1)S(1)}, bf16[512,128]{1,0:T(8,128)(2,1)S(1)}, u32[]{:S(2)}, u32[]{:S(2)}) collective-permute-start(bf16[512,128]{1,0:T(8,128)(2,1)S(1)} %constant_dynamic-update-slice_fusion.refs_0_), channel_id=1, source_target_pairs={{0,4},{1,5},{2,6},{3,7},{4,0},{5,1},{6,2},{7,3},{8,12},{9,13},{10,... | collective-permute-start | bytes 393224 | tf_op jit(solution)/shard_map/ppermute | solution.py:222
  15.0 5.1 %collective-permute-start.3 = (bf16[512,128]{1,0:T(8,128)(2,1)S(1)}, bf16[512,128]{1,0:T(8,128)(2,1)S(1)}, u32[]{:S(2)}, u32[]{:S(2)}) collective-permute-start(bf16[512,128]{1,0:T(8,128)(2,1)S(1)} %constant_dynamic-update-slice_fusion.refs_0_), channel_id=1, source_target_pairs={{0,2},{1,3},{2,0},{3,1},{4,6},{5,7},{6,4},{7,5},{8,10},{9,11},{10,... | collective-permute-start | bytes 393224 | tf_op jit(solution)/shard_map/ppermute | solution.py:222
  15.5 5.1 %collective-permute-start.7 = (bf16[512,128]{1,0:T(8,128)(2,1)S(1)}, bf16[512,128]{1,0:T(8,128)(2,1)S(1)}, u32[]{:S(2)}, u32[]{:S(2)}) collective-permute-start(bf16[512,128]{1,0:T(8,128)(2,1)S(1)} %constant_dynamic-update-slice_fusion.refs_0_), channel_id=1, source_target_pairs={{0,1},{1,0},{2,3},{3,2},{4,5},{5,4},{6,7},{7,6},{8,9},{9,8},{10,11... | collective-permute-start | bytes 393224 | tf_op jit(solution)/shard_map/ppermute | solution.py:222
  19.3 1.3 %collective-permute-start.9 = (bf16[512,128]{1,0:T(8,128)(2,1)S(1)}, bf16[512,128]{1,0:T(8,128)(2,1)S(1)}, u32[]{:S(2)}, u32[]{:S(2)}) collective-permute-start(bf16[512,128]{1,0:T(8,128)(2,1)S(1)} %collective-permute-done.8.refs_2_), channel_id=1, source_target_pairs={{0,1},{1,0},{2,3},{3,2},{4,5},{5,4},{6,7},{7,6},{8,9},{9,8},{10,11... | collective-permute-start | bytes 393224 | tf_op jit(solution)/shard_map/ppermute | solution.py:222
  20.1 1.3 %collective-permute-start.6 = (bf16[512,128]{1,0:T(8,128)(2,1)S(1)}, bf16[512,128]{1,0:T(8,128)(2,1)S(1)}, u32[]{:S(2)}, u32[]{:S(2)}) collective-permute-start(bf16[512,128]{1,0:T(8,128)(2,1)S(1)} %collective-permute-done.5.refs_5_), channel_id=1, source_target_pairs={{0,1},{1,0},{2,3},{3,2},{4,5},{5,4},{6,7},{7,6},{8,9},{9,8},{10,11... | collective-permute-start | bytes 393224 | tf_op jit(solution)/shard_map/ppermute | solution.py:222
  20.1 1.5 %collective-permute-start.4 = (bf16[512,128]{1,0:T(8,128)(2,1)S(1)}, bf16[512,128]{1,0:T(8,128)(2,1)S(1)}, u32[]{:S(2)}, u32[]{:S(2)}) collective-permute-start(bf16[512,128]{1,0:T(8,128)(2,1)S(1)} %collective-permute-done.3.refs_4_), channel_id=1, source_target_pairs={{0,1},{1,0},{2,3},{3,2},{4,5},{5,4},{6,7},{7,6},{8,9},{9,8},{10,11... | collective-permute-start | bytes 393224 | tf_op jit(solution)/shard_map/ppermute | solution.py:222

commit v24 on v23

--- a/solution.py
+++ b/solution.py
@@ -222,9 +222,10 @@
         return lax.ppermute(value, "grad", [(i, i ^ far) for i in range(members)])
 
     parts = list(split_blocks(factor_inputs, range(replicas)))
-    for far in range(replicas - 1, 0, -1):
+    order = (0, 1, 3, 2)
+    for far in order[1:]:
         parts[far] = lax.ppermute(parts[far], "dp", [(i, (i + far) % replicas) for i in range(replicas)])
-    own = jnp.concatenate(parts[:1] + parts[:0:-1], axis=0)
+    own = jnp.concatenate([parts[far] for far in order], axis=0)
     fars = (0, 1, 6, 7, 2, 4, 3, 5)
     pieces = {0: own}
     for far in (2, 4, 6):

time: 28.2 us -> 27.4 us (0.972)
  waiting for transfers between devices: 9.58 us -> 8.82 us
    ppermute x3, waiting for transfers between devices: 4.68 us -> 3.84 us  [by_tokens(): lax.ppermute(parts[far], 'dp', [(i, (i + far) % replicas) for i in range(...]
where the time goes in v24:
time: 27.4 us; the launch traced here: 27.3 us
  starting transfers between devices  10.1 us (37%)
  waiting for transfers between devices  8.82 us (32%)
  Pallas kernels  7.36 us (27%)
  local copies, waits for them, and re-layouts  0.93 us (3%)
    pallas_call x1, Pallas kernels, by_tokens(): pl.pallas_call(functools.partial(last_kernel, fars), out_shape=shape(rows...  6.41 us
    ppermute x3, starting transfers between devices, by_tokens(): lax.ppermute(parts[far], 'dp', [(i, (i + far) % replicas) for i in range(...  6.12 us
    ppermute x7, waiting for transfers between devices, swap(): return lax.ppermute(value, 'grad', [(i, i ^ far) for i in range(members)])  4.98 us
    ppermute x7, starting transfers between devices, swap(): return lax.ppermute(value, 'grad', [(i, i ^ far) for i in range(members)])  4 us
    ppermute x3, waiting for transfers between devices, by_tokens(): lax.ppermute(parts[far], 'dp', [(i, (i + far) % replicas) for i in range(...  3.84 us
    unnamed x5, local copies, waits for them, and re-layouts  0.92 us
    pallas_call x1, Pallas kernels, by_tokens(): pl.pallas_call(first_kernel, out_shape=[shape(tokens, early), shape(early...  0.66 us
  transfers between devices with their start and end apart: 10, of which 8 were waited for; matrix products, arithmetic and copies ran while one was open for 0% of the time, Pallas kernels for 2%

profile of v24, /device:TPU:0, one launch (start us, length us, event | category | flops | bytes accessed | tf_op | source)
XLA Modules:
  0.0 27.3 jit_solution(5148094371368712389)
XLA Ops:
  0.0 0.0 copy-start
  0.0 0.9 %copy-done = bf16[128,4,128]{2,1,0:T(4,128)(2,1)S(1)} copy-done((bf16[128,4,128]{2,1,0:T(4,128)(2,1)S(1)}, bf16[128,4,128]{2,1,0:T(4,128)(2,1)}, u32[]{:S(2)}) %copy-start) | copy-done | bytes 131096
  0.9 0.3 %split_blocks.1 = (bf16[128,128]{1,0:T(8,128)(2,1)S(1)}, bf16[128,128]{1,0:T(8,128)(2,1)S(1)}, bf16[128,128]{1,0:T(8,128)(2,1)S(1)}, bf16[128,128]{1,0:T(8,128)(2,1)S(1)}) custom-call(bf16[512,128]{1,0:T(8,128)(2,1)S(1)} %bitcast.3), custom_call_target="tpu_custom_call" | custom-call | tf_op jit(solution)/shard_map/split_blocks/pallas_call | solution.py:55
  1.2 3.1 %collective-permute-start = (bf16[128,128]{1,0:T(8,128)(2,1)S(1)}, bf16[128,128]{1,0:T(8,128)(2,1)S(1)}, u32[]{:S(2)}, u32[]{:S(2)}) collective-permute-start(bf16[128,128]{1,0:T(8,128)(2,1)S(1)} %get-tuple-element.13), channel_id=1, source_target_pairs={{0,8},{8,16},{16,24},{24,0},{1,9},{9,17},{17,25},{25,1},{2,10},{10... | collective-permute-start | bytes 98312 | tf_op jit(solution)/shard_map/ppermute | solution.py:227
  4.3 2.1 %collective-permute-start.1 = (bf16[128,128]{1,0:T(8,128)(2,1)S(1)}, bf16[128,128]{1,0:T(8,128)(2,1)S(1)}, u32[]{:S(2)}, u32[]{:S(2)}) collective-permute-start(bf16[128,128]{1,0:T(8,128)(2,1)S(1)} %get-tuple-element.14), channel_id=1, source_target_pairs={{0,24},{8,0},{16,8},{24,16},{1,25},{9,1},{17,9},{25,17},{2,26},{10... | collective-permute-start | bytes 98312 | tf_op jit(solution)/shard_map/ppermute | solution.py:227
  6.4 0.9 %collective-permute-start.2 = (bf16[128,128]{1,0:T(8,128)(2,1)S(1)}, bf16[128,128]{1,0:T(8,128)(2,1)S(1)}, u32[]{:S(2)}, u32[]{:S(2)}) collective-permute-start(bf16[128,128]{1,0:T(8,128)(2,1)S(1)} %get-tuple-element.15), channel_id=1, source_target_pairs={{0,16},{8,24},{16,0},{24,8},{1,17},{9,25},{17,1},{25,9},{2,18},{10... | collective-permute-start | bytes 98312 | tf_op jit(solution)/shard_map/ppermute | solution.py:227
  7.3 1.0 %collective-permute-done = bf16[128,128]{1,0:T(8,128)(2,1)S(1)} collective-permute-done((bf16[128,128]{1,0:T(8,128)(2,1)S(1)}, bf16[128,128]{1,0:T(8,128)(2,1)S(1)}, u32[]{:S(2)}, u32[]{:S(2)}) %collective-permute-start) | collective-permute-done | bytes 32800 | tf_op jit(solution)/shard_map/ppermute | solution.py:227
  8.3 0.2 collective-permute-done.1
  8.5 2.6 %collective-permute-done.2 = bf16[128,128]{1,0:T(8,128)(2,1)S(1)} collective-permute-done((bf16[128,128]{1,0:T(8,128)(2,1)S(1)}, bf16[128,128]{1,0:T(8,128)(2,1)S(1)}, u32[]{:S(2)}, u32[]{:S(2)}) %collective-permute-start.2) | collective-permute-done | bytes 32800 | tf_op jit(solution)/shard_map/ppermute | solution.py:227
  11.2 2.6 %collective-permute-start.8 = (bf16[512,128]{1,0:T(8,128)(2,1)S(1)}, bf16[512,128]{1,0:T(8,128)(2,1)S(1)}, u32[]{:S(2)}, u32[]{:S(2)}) collective-permute-start(bf16[512,128]{1,0:T(8,128)(2,1)S(1)} %constant_dynamic-update-slice_fusion.refs_0_), channel_id=1, source_target_pairs={{0,6},{1,7},{2,4},{3,5},{4,2},{5,3},{6,0},{7,1},{8,14},{9,15},{10,... | collective-permute-start | bytes 393224 | tf_op jit(solution)/shard_map/ppermute | solution.py:222
  13.8 0.5 %collective-permute-start.5 = (bf16[512,128]{1,0:T(8,128)(2,1)S(1)}, bf16[512,128]{1,0:T(8,128)(2,1)S(1)}, u32[]{:S(2)}, u32[]{:S(2)}) collective-permute-start(bf16[512,128]{1,0:T(8,128)(2,1)S(1)} %constant_dynamic-update-slice_fusion.refs_0_), channel_id=1, source_target_pairs={{0,4},{1,5},{2,6},{3,7},{4,0},{5,1},{6,2},{7,3},{8,12},{9,13},{10,... | collective-permute-start | bytes 393224 | tf_op jit(solution)/shard_map/ppermute | solution.py:222
  14.3 0.4 %collective-permute-start.3 = (bf16[512,128]{1,0:T(8,128)(2,1)S(1)}, bf16[512,128]{1,0:T(8,128)(2,1)S(1)}, u32[]{:S(2)}, u32[]{:S(2)}) collective-permute-start(bf16[512,128]{1,0:T(8,128)(2,1)S(1)} %constant_dynamic-update-slice_fusion.refs_0_), channel_id=1, source_target_pairs={{0,2},{1,3},{2,0},{3,1},{4,6},{5,7},{6,4},{7,5},{8,10},{9,11},{10,... | collective-permute-start | bytes 393224 | tf_op jit(solution)/shard_map/ppermute | solution.py:222
  14.7 0.0 collective-permute-start.7
  14.7 3.9 %collective-permute-done.8.refs_2_ = bf16[512,128]{1,0:T(8,128)(2,1)S(1)} collective-permute-done((bf16[512,128]{1,0:T(8,128)(2,1)S(1)}, bf16[512,128]{1,0:T(8,128)(2,1)S(1)}, u32[]{:S(2)}, u32[]{:S(2)}) %collective-permute-start.8) | collective-permute-done | bytes 131104 | tf_op jit(solution)/shard_map/ppermute | solution.py:222
  18.5 0.0 collective-permute-start.9
  18.5 0.8 %collective-permute-done.5.refs_5_ = bf16[512,128]{1,0:T(8,128)(2,1)S(1)} collective-permute-done((bf16[512,128]{1,0:T(8,128)(2,1)S(1)}, bf16[512,128]{1,0:T(8,128)(2,1)S(1)}, u32[]{:S(2)}, u32[]{:S(2)}) %collective-permute-start.5) | collective-permute-done | bytes 131104 | tf_op jit(solution)/shard_map/ppermute | solution.py:222
  19.3 0.0 collective-permute-start.6
  19.3 0.0 collective-permute-done.3.refs_4_
  19.3 0.5 %collective-permute-start.4 = (bf16[512,128]{1,0:T(8,128)(2,1)S(1)}, bf16[512,128]{1,0:T(8,128)(2,1)S(1)}, u32[]{:S(2)}, u32[]{:S(2)}) collective-permute-start(bf16[512,128]{1,0:T(8,128)(2,1)S(1)} %collective-permute-done.3.refs_4_), channel_id=1, source_target_pairs={{0,1},{1,0},{2,3},{3,2},{4,5},{5,4},{6,7},{7,6},{8,9},{9,8},{10,11... | collective-permute-start | bytes 393224 | tf_op jit(solution)/shard_map/ppermute | solution.py:222
  19.8 0.0 collective-permute-done.7.refs_1_
  19.8 0.1 collective-permute-done.9.refs_3_
  19.9 0.7 %first_pieces.1 = (bf16[512,768]{1,0:T(8,128)(2,1)S(1)}, bf16[768,512]{1,0:T(8,128)(2,1)S(1)}, f32[512,512]{1,0:T(8,128)S(1)}) custom-call(bf16[512,128]{1,0:T(8,128)(2,1)S(1)} %constant_dynamic-update-slice_fusion.refs_0_, bf16[512,128]{1,0:T(8,128)(2,1)S(1)} %collective-permute-done.7.refs_1_, bf16[512,128]{1,0:T(8,128)(2,1)S(1)} %collective-permute-done.8.refs_2_, ...), custom_call_target="tpu_custom_call" | custom-call | flops 400000000 | tf_op jit(solution)/shard_map/first_pieces/pallas_call | solution.py:237
  20.5 0.1 collective-permute-done.6.late1
  20.7 0.2 collective-permute-done.4.late0
  20.8 6.4 %whole_block.1 = bf16[768,1024]{1,0:T(8,128)(2,1)} custom-call(bf16[512,128]{1,0:T(8,128)(2,1)S(1)} %collective-permute-done.4.late0, bf16[512,128]{1,0:T(8,128)(2,1)S(1)} %collective-permute-done.6.late1, bf16[512,768]{1,0:T(8,128)(2,1)S(1)} %get-tuple-element.16.x, bf16[768,512]{1,0:T(8,128)(2,1)S(1)} %get-tuple-element.17.xt, ...), custom_call_target="tpu_custom_call" | custom-call | flops 5000000000 | tf_op jit(solution)/shard_map/whole_block/pallas_call | solution.py:246
  (4 shorter events, 0.0 us)
Async XLA Ops:
  0.0 0.9 %copy-start = (bf16[128,4,128]{2,1,0:T(4,128)(2,1)S(1)}, bf16[128,4,128]{2,1,0:T(4,128)(2,1)}, u32[]{:S(2)}) copy-start(bf16[128,4,128]{2,1,0:T(4,128)(2,1)} %param.2) | copy-start | bytes 393220
  1.2 7.1 %collective-permute-start = (bf16[128,128]{1,0:T(8,128)(2,1)S(1)}, bf16[128,128]{1,0:T(8,128)(2,1)S(1)}, u32[]{:S(2)}, u32[]{:S(2)}) collective-permute-start(bf16[128,128]{1,0:T(8,128)(2,1)S(1)} %get-tuple-element.13), channel_id=1, source_target_pairs={{0,8},{8,16},{16,24},{24,0},{1,9},{9,17},{17,25},{25,1},{2,10},{10... | collective-permute-start | bytes 98312 | tf_op jit(solution)/shard_map/ppermute | solution.py:227
  4.3 4.3 %collective-permute-start.1 = (bf16[128,128]{1,0:T(8,128)(2,1)S(1)}, bf16[128,128]{1,0:T(8,128)(2,1)S(1)}, u32[]{:S(2)}, u32[]{:S(2)}) collective-permute-start(bf16[128,128]{1,0:T(8,128)(2,1)S(1)} %get-tuple-element.14), channel_id=1, source_target_pairs={{0,24},{8,0},{16,8},{24,16},{1,25},{9,1},{17,9},{25,17},{2,26},{10... | collective-permute-start | bytes 98312 | tf_op jit(solution)/shard_map/ppermute | solution.py:227
  6.4 4.8 %collective-permute-start.2 = (bf16[128,128]{1,0:T(8,128)(2,1)S(1)}, bf16[128,128]{1,0:T(8,128)(2,1)S(1)}, u32[]{:S(2)}, u32[]{:S(2)}) collective-permute-start(bf16[128,128]{1,0:T(8,128)(2,1)S(1)} %get-tuple-element.15), channel_id=1, source_target_pairs={{0,16},{8,24},{16,0},{24,8},{1,17},{9,25},{17,1},{25,9},{2,18},{10... | collective-permute-start | bytes 98312 | tf_op jit(solution)/shard_map/ppermute | solution.py:227
  11.2 7.3 %collective-permute-start.8 = (bf16[512,128]{1,0:T(8,128)(2,1)S(1)}, bf16[512,128]{1,0:T(8,128)(2,1)S(1)}, u32[]{:S(2)}, u32[]{:S(2)}) collective-permute-start(bf16[512,128]{1,0:T(8,128)(2,1)S(1)} %constant_dynamic-update-slice_fusion.refs_0_), channel_id=1, source_target_pairs={{0,6},{1,7},{2,4},{3,5},{4,2},{5,3},{6,0},{7,1},{8,14},{9,15},{10,... | collective-permute-start | bytes 393224 | tf_op jit(solution)/shard_map/ppermute | solution.py:222
  13.8 5.5 %collective-permute-start.5 = (bf16[512,128]{1,0:T(8,128)(2,1)S(1)}, bf16[512,128]{1,0:T(8,128)(2,1)S(1)}, u32[]{:S(2)}, u32[]{:S(2)}) collective-permute-start(bf16[512,128]{1,0:T(8,128)(2,1)S(1)} %constant_dynamic-update-slice_fusion.refs_0_), channel_id=1, source_target_pairs={{0,4},{1,5},{2,6},{3,7},{4,0},{5,1},{6,2},{7,3},{8,12},{9,13},{10,... | collective-permute-start | bytes 393224 | tf_op jit(solution)/shard_map/ppermute | solution.py:222
  14.3 5.0 %collective-permute-start.3 = (bf16[512,128]{1,0:T(8,128)(2,1)S(1)}, bf16[512,128]{1,0:T(8,128)(2,1)S(1)}, u32[]{:S(2)}, u32[]{:S(2)}) collective-permute-start(bf16[512,128]{1,0:T(8,128)(2,1)S(1)} %constant_dynamic-update-slice_fusion.refs_0_), channel_id=1, source_target_pairs={{0,2},{1,3},{2,0},{3,1},{4,6},{5,7},{6,4},{7,5},{8,10},{9,11},{10,... | collective-permute-start | bytes 393224 | tf_op jit(solution)/shard_map/ppermute | solution.py:222
  14.7 5.2 %collective-permute-start.7 = (bf16[512,128]{1,0:T(8,128)(2,1)S(1)}, bf16[512,128]{1,0:T(8,128)(2,1)S(1)}, u32[]{:S(2)}, u32[]{:S(2)}) collective-permute-start(bf16[512,128]{1,0:T(8,128)(2,1)S(1)} %constant_dynamic-update-slice_fusion.refs_0_), channel_id=1, source_target_pairs={{0,1},{1,0},{2,3},{3,2},{4,5},{5,4},{6,7},{7,6},{8,9},{9,8},{10,11... | collective-permute-start | bytes 393224 | tf_op jit(solution)/shard_map/ppermute | solution.py:222
  18.5 1.3 %collective-permute-start.9 = (bf16[512,128]{1,0:T(8,128)(2,1)S(1)}, bf16[512,128]{1,0:T(8,128)(2,1)S(1)}, u32[]{:S(2)}, u32[]{:S(2)}) collective-permute-start(bf16[512,128]{1,0:T(8,128)(2,1)S(1)} %collective-permute-done.8.refs_2_), channel_id=1, source_target_pairs={{0,1},{1,0},{2,3},{3,2},{4,5},{5,4},{6,7},{7,6},{8,9},{9,8},{10,11... | collective-permute-start | bytes 393224 | tf_op jit(solution)/shard_map/ppermute | solution.py:222
  19.3 1.3 %collective-permute-start.6 = (bf16[512,128]{1,0:T(8,128)(2,1)S(1)}, bf16[512,128]{1,0:T(8,128)(2,1)S(1)}, u32[]{:S(2)}, u32[]{:S(2)}) collective-permute-start(bf16[512,128]{1,0:T(8,128)(2,1)S(1)} %collective-permute-done.5.refs_5_), channel_id=1, source_target_pairs={{0,1},{1,0},{2,3},{3,2},{4,5},{5,4},{6,7},{7,6},{8,9},{9,8},{10,11... | collective-permute-start | bytes 393224 | tf_op jit(solution)/shard_map/ppermute | solution.py:222
  19.3 1.5 %collective-permute-start.4 = (bf16[512,128]{1,0:T(8,128)(2,1)S(1)}, bf16[512,128]{1,0:T(8,128)(2,1)S(1)}, u32[]{:S(2)}, u32[]{:S(2)}) collective-permute-start(bf16[512,128]{1,0:T(8,128)(2,1)S(1)} %collective-permute-done.3.refs_4_), channel_id=1, source_target_pairs={{0,1},{1,0},{2,3},{3,2},{4,5},{5,4},{6,7},{7,6},{8,9},{9,8},{10,11... | collective-permute-start | bytes 393224 | tf_op jit(solution)/shard_map/ppermute | solution.py:222

commit v25 on v20

--- a/solution.py
+++ b/solution.py
@@ -199,6 +199,11 @@
             part = slice(one * features, (one + 1) * features)
             for r in chunks_of(moved.shape[0]):
                 out[r, here] = (p * tile[r, here].astype(jnp.float32) + moved[r, part]).astype(jnp.bfloat16)
+            if n < 2 and one == 0:
+                continue
+            if n < 2:
+                chip = lax.shift_right_logical(member ^ fars[2 * n], 1)
+                here = pl.ds(pl.multiple_of(chip * half, half), half)
             store = pltpu.make_async_copy(out.at[:, here], out_hbm.at[:, here], sems.at[1 + len(stores)])
             store.start()
             stores.append(store)

time: 26.9 us -> 26.9 us (level)
  no operation moved by 1% of the time
where the time goes in v25:
time: 26.9 us; the launch traced here: 26.7 us
  starting transfers between devices  11 us (41%)
  Pallas kernels  7.41 us (28%)
  waiting for transfers between devices  7.34 us (27%)
  local copies, waits for them, and re-layouts  0.93 us (3%)
    ppermute x3, starting transfers between devices, by_tokens(): lax.ppermute(parts[far], 'dp', [(i, (i + far) % replicas) for i in range(...  7.01 us
    pallas_call x1, Pallas kernels, by_tokens(): pl.pallas_call(functools.partial(last_kernel, fars), out_shape=shape(rows...  6.46 us
    ppermute x7, waiting for transfers between devices, swap(): return lax.ppermute(value, 'grad', [(i, i ^ far) for i in range(members)])  4.8 us
    ppermute x7, starting transfers between devices, swap(): return lax.ppermute(value, 'grad', [(i, i ^ far) for i in range(members)])  4 us
    ppermute x3, waiting for transfers between devices, by_tokens(): lax.ppermute(parts[far], 'dp', [(i, (i + far) % replicas) for i in range(...  2.54 us
    unnamed x5, local copies, waits for them, and re-layouts  0.92 us
    pallas_call x1, Pallas kernels, by_tokens(): pl.pallas_call(first_kernel, out_shape=[shape(tokens, early), shape(early...  0.67 us
  transfers between devices with their start and end apart: 10, of which 6 were waited for; matrix products, arithmetic and copies ran while one was open for 0% of the time, Pallas kernels for 2%

profile of v25, /device:TPU:0, one launch (start us, length us, event | category | flops | bytes accessed | tf_op | source)
XLA Modules:
  0.0 26.7 jit_solution(3763534378430735327)
XLA Ops:
  0.0 0.0 copy-start
  0.0 0.9 %copy-done = bf16[128,4,128]{2,1,0:T(4,128)(2,1)S(1)} copy-done((bf16[128,4,128]{2,1,0:T(4,128)(2,1)S(1)}, bf16[128,4,128]{2,1,0:T(4,128)(2,1)}, u32[]{:S(2)}) %copy-start) | copy-done | bytes 131096
  0.9 0.3 %split_blocks.1 = (bf16[128,128]{1,0:T(8,128)(2,1)S(1)}, bf16[128,128]{1,0:T(8,128)(2,1)S(1)}, bf16[128,128]{1,0:T(8,128)(2,1)S(1)}, bf16[128,128]{1,0:T(8,128)(2,1)S(1)}) custom-call(bf16[512,128]{1,0:T(8,128)(2,1)S(1)} %bitcast.3), custom_call_target="tpu_custom_call" | custom-call | tf_op jit(solution)/shard_map/split_blocks/pallas_call | solution.py:55
  1.2 3.1 %collective-permute-start = (bf16[128,128]{1,0:T(8,128)(2,1)S(1)}, bf16[128,128]{1,0:T(8,128)(2,1)S(1)}, u32[]{:S(2)}, u32[]{:S(2)}) collective-permute-start(bf16[128,128]{1,0:T(8,128)(2,1)S(1)} %get-tuple-element.13), channel_id=1, source_target_pairs={{0,8},{8,16},{16,24},{24,0},{1,9},{9,17},{17,25},{25,1},{2,10},{10... | collective-permute-start | bytes 98312 | tf_op jit(solution)/shard_map/ppermute | solution.py:231
  4.3 2.6 %collective-permute-start.1 = (bf16[128,128]{1,0:T(8,128)(2,1)S(1)}, bf16[128,128]{1,0:T(8,128)(2,1)S(1)}, u32[]{:S(2)}, u32[]{:S(2)}) collective-permute-start(bf16[128,128]{1,0:T(8,128)(2,1)S(1)} %get-tuple-element.14), channel_id=1, source_target_pairs={{0,16},{8,24},{16,0},{24,8},{1,17},{9,25},{17,1},{25,9},{2,18},{10... | collective-permute-start | bytes 98312 | tf_op jit(solution)/shard_map/ppermute | solution.py:231
  6.9 1.3 %collective-permute-start.2 = (bf16[128,128]{1,0:T(8,128)(2,1)S(1)}, bf16[128,128]{1,0:T(8,128)(2,1)S(1)}, u32[]{:S(2)}, u32[]{:S(2)}) collective-permute-start(bf16[128,128]{1,0:T(8,128)(2,1)S(1)} %get-tuple-element.15), channel_id=1, source_target_pairs={{0,24},{8,0},{16,8},{24,16},{1,25},{9,1},{17,9},{25,17},{2,26},{10... | collective-permute-start | bytes 98312 | tf_op jit(solution)/shard_map/ppermute | solution.py:231
  8.2 0.0 collective-permute-done
  8.2 1.2 %collective-permute-done.1 = bf16[128,128]{1,0:T(8,128)(2,1)S(1)} collective-permute-done((bf16[128,128]{1,0:T(8,128)(2,1)S(1)}, bf16[128,128]{1,0:T(8,128)(2,1)S(1)}, u32[]{:S(2)}, u32[]{:S(2)}) %collective-permute-start.1) | collective-permute-done | bytes 32800 | tf_op jit(solution)/shard_map/ppermute | solution.py:231
  9.4 1.3 %collective-permute-done.2 = bf16[128,128]{1,0:T(8,128)(2,1)S(1)} collective-permute-done((bf16[128,128]{1,0:T(8,128)(2,1)S(1)}, bf16[128,128]{1,0:T(8,128)(2,1)S(1)}, u32[]{:S(2)}, u32[]{:S(2)}) %collective-permute-start.2) | collective-permute-done | bytes 32800 | tf_op jit(solution)/shard_map/ppermute | solution.py:231
  10.8 2.4 %collective-permute-start.8 = (bf16[512,128]{1,0:T(8,128)(2,1)S(1)}, bf16[512,128]{1,0:T(8,128)(2,1)S(1)}, u32[]{:S(2)}, u32[]{:S(2)}) collective-permute-start(bf16[512,128]{1,0:T(8,128)(2,1)S(1)} %constant_dynamic-update-slice_fusion.refs_0_), channel_id=1, source_target_pairs={{0,6},{1,7},{2,4},{3,5},{4,2},{5,3},{6,0},{7,1},{8,14},{9,15},{10,... | collective-permute-start | bytes 393224 | tf_op jit(solution)/shard_map/ppermute | solution.py:227
  13.2 0.5 %collective-permute-start.5 = (bf16[512,128]{1,0:T(8,128)(2,1)S(1)}, bf16[512,128]{1,0:T(8,128)(2,1)S(1)}, u32[]{:S(2)}, u32[]{:S(2)}) collective-permute-start(bf16[512,128]{1,0:T(8,128)(2,1)S(1)} %constant_dynamic-update-slice_fusion.refs_0_), channel_id=1, source_target_pairs={{0,4},{1,5},{2,6},{3,7},{4,0},{5,1},{6,2},{7,3},{8,12},{9,13},{10,... | collective-permute-start | bytes 393224 | tf_op jit(solution)/shard_map/ppermute | solution.py:227
  13.7 0.5 %collective-permute-start.3 = (bf16[512,128]{1,0:T(8,128)(2,1)S(1)}, bf16[512,128]{1,0:T(8,128)(2,1)S(1)}, u32[]{:S(2)}, u32[]{:S(2)}) collective-permute-start(bf16[512,128]{1,0:T(8,128)(2,1)S(1)} %constant_dynamic-update-slice_fusion.refs_0_), channel_id=1, source_target_pairs={{0,2},{1,3},{2,0},{3,1},{4,6},{5,7},{6,4},{7,5},{8,10},{9,11},{10,... | collective-permute-start | bytes 393224 | tf_op jit(solution)/shard_map/ppermute | solution.py:227
  14.3 0.0 collective-permute-start.7
  14.3 3.6 %collective-permute-done.8.refs_2_ = bf16[512,128]{1,0:T(8,128)(2,1)S(1)} collective-permute-done((bf16[512,128]{1,0:T(8,128)(2,1)S(1)}, bf16[512,128]{1,0:T(8,128)(2,1)S(1)}, u32[]{:S(2)}, u32[]{:S(2)}) %collective-permute-start.8) | collective-permute-done | bytes 131104 | tf_op jit(solution)/shard_map/ppermute | solution.py:227
  17.9 0.0 collective-permute-start.9
  17.9 0.9 %collective-permute-done.5.refs_5_ = bf16[512,128]{1,0:T(8,128)(2,1)S(1)} collective-permute-done((bf16[512,128]{1,0:T(8,128)(2,1)S(1)}, bf16[512,128]{1,0:T(8,128)(2,1)S(1)}, u32[]{:S(2)}, u32[]{:S(2)}) %collective-permute-start.5) | collective-permute-done | bytes 131104 | tf_op jit(solution)/shard_map/ppermute | solution.py:227
  18.7 0.0 collective-permute-start.6
  18.7 0.0 collective-permute-done.3.refs_4_
  18.7 0.5 %collective-permute-start.4 = (bf16[512,128]{1,0:T(8,128)(2,1)S(1)}, bf16[512,128]{1,0:T(8,128)(2,1)S(1)}, u32[]{:S(2)}, u32[]{:S(2)}) collective-permute-start(bf16[512,128]{1,0:T(8,128)(2,1)S(1)} %collective-permute-done.3.refs_4_), channel_id=1, source_target_pairs={{0,1},{1,0},{2,3},{3,2},{4,5},{5,4},{6,7},{7,6},{8,9},{9,8},{10,11... | collective-permute-start | bytes 393224 | tf_op jit(solution)/shard_map/ppermute | solution.py:227
  19.2 0.0 collective-permute-done.7.refs_1_
  19.3 0.0 collective-permute-done.9.refs_3_
  19.3 0.7 %first_pieces.1 = (bf16[512,768]{1,0:T(8,128)(2,1)S(1)}, bf16[768,512]{1,0:T(8,128)(2,1)S(1)}, f32[512,512]{1,0:T(8,128)S(1)}) custom-call(bf16[512,128]{1,0:T(8,128)(2,1)S(1)} %constant_dynamic-update-slice_fusion.refs_0_, bf16[512,128]{1,0:T(8,128)(2,1)S(1)} %collective-permute-done.7.refs_1_, bf16[512,128]{1,0:T(8,128)(2,1)S(1)} %collective-permute-done.8.refs_2_, ...), custom_call_target="tpu_custom_call" | custom-call | flops 400000000 | tf_op jit(solution)/shard_map/first_pieces/pallas_call | solution.py:241
  19.9 0.2 collective-permute-done.6.late1
  20.1 0.2 collective-permute-done.4.late0
  20.3 6.5 %whole_block.1 = bf16[768,1024]{1,0:T(8,128)(2,1)} custom-call(bf16[512,128]{1,0:T(8,128)(2,1)S(1)} %collective-permute-done.4.late0, bf16[512,128]{1,0:T(8,128)(2,1)S(1)} %collective-permute-done.6.late1, bf16[512,768]{1,0:T(8,128)(2,1)S(1)} %get-tuple-element.16.x, bf16[768,512]{1,0:T(8,128)(2,1)S(1)} %get-tuple-element.17.xt, ...), custom_call_target="tpu_custom_call" | custom-call | flops 5000000000 | tf_op jit(solution)/shard_map/whole_block/pallas_call | solution.py:250
  (4 shorter events, 0.0 us)
Async XLA Ops:
  0.0 0.9 %copy-start = (bf16[128,4,128]{2,1,0:T(4,128)(2,1)S(1)}, bf16[128,4,128]{2,1,0:T(4,128)(2,1)}, u32[]{:S(2)}) copy-start(bf16[128,4,128]{2,1,0:T(4,128)(2,1)} %param.2) | copy-start | bytes 393220
  1.2 7.0 %collective-permute-start = (bf16[128,128]{1,0:T(8,128)(2,1)S(1)}, bf16[128,128]{1,0:T(8,128)(2,1)S(1)}, u32[]{:S(2)}, u32[]{:S(2)}) collective-permute-start(bf16[128,128]{1,0:T(8,128)(2,1)S(1)} %get-tuple-element.13), channel_id=1, source_target_pairs={{0,8},{8,16},{16,24},{24,0},{1,9},{9,17},{17,25},{25,1},{2,10},{10... | collective-permute-start | bytes 98312 | tf_op jit(solution)/shard_map/ppermute | solution.py:231
  4.3 5.2 %collective-permute-start.1 = (bf16[128,128]{1,0:T(8,128)(2,1)S(1)}, bf16[128,128]{1,0:T(8,128)(2,1)S(1)}, u32[]{:S(2)}, u32[]{:S(2)}) collective-permute-start(bf16[128,128]{1,0:T(8,128)(2,1)S(1)} %get-tuple-element.14), channel_id=1, source_target_pairs={{0,16},{8,24},{16,0},{24,8},{1,17},{9,25},{17,1},{25,9},{2,18},{10... | collective-permute-start | bytes 98312 | tf_op jit(solution)/shard_map/ppermute | solution.py:231
  6.9 3.9 %collective-permute-start.2 = (bf16[128,128]{1,0:T(8,128)(2,1)S(1)}, bf16[128,128]{1,0:T(8,128)(2,1)S(1)}, u32[]{:S(2)}, u32[]{:S(2)}) collective-permute-start(bf16[128,128]{1,0:T(8,128)(2,1)S(1)} %get-tuple-element.15), channel_id=1, source_target_pairs={{0,24},{8,0},{16,8},{24,16},{1,25},{9,1},{17,9},{25,17},{2,26},{10... | collective-permute-start | bytes 98312 | tf_op jit(solution)/shard_map/ppermute | solution.py:231
  10.8 7.1 %collective-permute-start.8 = (bf16[512,128]{1,0:T(8,128)(2,1)S(1)}, bf16[512,128]{1,0:T(8,128)(2,1)S(1)}, u32[]{:S(2)}, u32[]{:S(2)}) collective-permute-start(bf16[512,128]{1,0:T(8,128)(2,1)S(1)} %constant_dynamic-update-slice_fusion.refs_0_), channel_id=1, source_target_pairs={{0,6},{1,7},{2,4},{3,5},{4,2},{5,3},{6,0},{7,1},{8,14},{9,15},{10,... | collective-permute-start | bytes 393224 | tf_op jit(solution)/shard_map/ppermute | solution.py:227
  13.2 5.5 %collective-permute-start.5 = (bf16[512,128]{1,0:T(8,128)(2,1)S(1)}, bf16[512,128]{1,0:T(8,128)(2,1)S(1)}, u32[]{:S(2)}, u32[]{:S(2)}) collective-permute-start(bf16[512,128]{1,0:T(8,128)(2,1)S(1)} %constant_dynamic-update-slice_fusion.refs_0_), channel_id=1, source_target_pairs={{0,4},{1,5},{2,6},{3,7},{4,0},{5,1},{6,2},{7,3},{8,12},{9,13},{10,... | collective-permute-start | bytes 393224 | tf_op jit(solution)/shard_map/ppermute | solution.py:227
  13.7 5.0 %collective-permute-start.3 = (bf16[512,128]{1,0:T(8,128)(2,1)S(1)}, bf16[512,128]{1,0:T(8,128)(2,1)S(1)}, u32[]{:S(2)}, u32[]{:S(2)}) collective-permute-start(bf16[512,128]{1,0:T(8,128)(2,1)S(1)} %constant_dynamic-update-slice_fusion.refs_0_), channel_id=1, source_target_pairs={{0,2},{1,3},{2,0},{3,1},{4,6},{5,7},{6,4},{7,5},{8,10},{9,11},{10,... | collective-permute-start | bytes 393224 | tf_op jit(solution)/shard_map/ppermute | solution.py:227
  14.3 5.0 %collective-permute-start.7 = (bf16[512,128]{1,0:T(8,128)(2,1)S(1)}, bf16[512,128]{1,0:T(8,128)(2,1)S(1)}, u32[]{:S(2)}, u32[]{:S(2)}) collective-permute-start(bf16[512,128]{1,0:T(8,128)(2,1)S(1)} %constant_dynamic-update-slice_fusion.refs_0_), channel_id=1, source_target_pairs={{0,1},{1,0},{2,3},{3,2},{4,5},{5,4},{6,7},{7,6},{8,9},{9,8},{10,11... | collective-permute-start | bytes 393224 | tf_op jit(solution)/shard_map/ppermute | solution.py:227
  17.9 1.4 %collective-permute-start.9 = (bf16[512,128]{1,0:T(8,128)(2,1)S(1)}, bf16[512,128]{1,0:T(8,128)(2,1)S(1)}, u32[]{:S(2)}, u32[]{:S(2)}) collective-permute-start(bf16[512,128]{1,0:T(8,128)(2,1)S(1)} %collective-permute-done.8.refs_2_), channel_id=1, source_target_pairs={{0,1},{1,0},{2,3},{3,2},{4,5},{5,4},{6,7},{7,6},{8,9},{9,8},{10,11... | collective-permute-start | bytes 393224 | tf_op jit(solution)/shard_map/ppermute | solution.py:227
  18.7 1.3 %collective-permute-start.6 = (bf16[512,128]{1,0:T(8,128)(2,1)S(1)}, bf16[512,128]{1,0:T(8,128)(2,1)S(1)}, u32[]{:S(2)}, u32[]{:S(2)}) collective-permute-start(bf16[512,128]{1,0:T(8,128)(2,1)S(1)} %collective-permute-done.5.refs_5_), channel_id=1, source_target_pairs={{0,1},{1,0},{2,3},{3,2},{4,5},{5,4},{6,7},{7,6},{8,9},{9,8},{10,11... | collective-permute-start | bytes 393224 | tf_op jit(solution)/shard_map/ppermute | solution.py:227
  18.7 1.5 %collective-permute-start.4 = (bf16[512,128]{1,0:T(8,128)(2,1)S(1)}, bf16[512,128]{1,0:T(8,128)(2,1)S(1)}, u32[]{:S(2)}, u32[]{:S(2)}) collective-permute-start(bf16[512,128]{1,0:T(8,128)(2,1)S(1)} %collective-permute-done.3.refs_4_), channel_id=1, source_target_pairs={{0,1},{1,0},{2,3},{3,2},{4,5},{5,4},{6,7},{7,6},{8,9},{9,8},{10,11... | collective-permute-start | bytes 393224 | tf_op jit(solution)/shard_map/ppermute | solution.py:227

commit v26 on v25

--- a/solution.py
+++ b/solution.py
@@ -188,7 +188,10 @@
                 result[r, some] = total.astype(jnp.bfloat16)
 
     apply(image, g, [(g_m, image)], by_g)
-    symmetric(z, z, lambda product, r, some: [product + k_z * wide(z, r, some)], k)
+    for some in halves:
+        product = dot(z[...], z[:, some])
+        for r in chunks:
+            k[r, some] = (product[r] + k_z * wide(z, r, some)).astype(jnp.bfloat16)
     apply(by_g, h, [(h_m, by_g)], by_h)
     apply(by_h, k, [(last * (1.0 + eps2) * beta, image), (last * beta, by_g), (last * k_m, by_h)], mixed, last)
     stores = []

time: 26.9 us -> 27.1 us (level)
  no operation moved by 1% of the time
where the time goes in v26:
time: 27.1 us; the launch traced here: 27 us
  starting transfers between devices  11 us (41%)
  Pallas kernels  7.67 us (28%)
  waiting for transfers between devices  7.34 us (27%)
  local copies, waits for them, and re-layouts  0.93 us (3%)
    ppermute x3, starting transfers between devices, by_tokens(): lax.ppermute(parts[far], 'dp', [(i, (i + far) % replicas) for i in range(...  7.01 us
    pallas_call x1, Pallas kernels, by_tokens(): pl.pallas_call(functools.partial(last_kernel, fars), out_shape=shape(rows...  6.72 us
    ppermute x7, waiting for transfers between devices, swap(): return lax.ppermute(value, 'grad', [(i, i ^ far) for i in range(members)])  4.8 us
    ppermute x7, starting transfers between devices, swap(): return lax.ppermute(value, 'grad', [(i, i ^ far) for i in range(members)])  4 us
    ppermute x3, waiting for transfers between devices, by_tokens(): lax.ppermute(parts[far], 'dp', [(i, (i + far) % replicas) for i in range(...  2.54 us
    unnamed x5, local copies, waits for them, and re-layouts  0.92 us
    pallas_call x1, Pallas kernels, by_tokens(): pl.pallas_call(first_kernel, out_shape=[shape(tokens, early), shape(early...  0.67 us
  transfers between devices with their start and end apart: 10, of which 6 were waited for; matrix products, arithmetic and copies ran while one was open for 0% of the time, Pallas kernels for 2%

profile of v26, /device:TPU:0, one launch (start us, length us, event | category | flops | bytes accessed | tf_op | source)
XLA Modules:
  0.0 27.0 jit_solution(12400518158048023317)
XLA Ops:
  0.0 0.0 copy-start
  0.0 0.9 %copy-done = bf16[128,4,128]{2,1,0:T(4,128)(2,1)S(1)} copy-done((bf16[128,4,128]{2,1,0:T(4,128)(2,1)S(1)}, bf16[128,4,128]{2,1,0:T(4,128)(2,1)}, u32[]{:S(2)}) %copy-start) | copy-done | bytes 131096
  0.9 0.3 %split_blocks.1 = (bf16[128,128]{1,0:T(8,128)(2,1)S(1)}, bf16[128,128]{1,0:T(8,128)(2,1)S(1)}, bf16[128,128]{1,0:T(8,128)(2,1)S(1)}, bf16[128,128]{1,0:T(8,128)(2,1)S(1)}) custom-call(bf16[512,128]{1,0:T(8,128)(2,1)S(1)} %bitcast.3), custom_call_target="tpu_custom_call" | custom-call | tf_op jit(solution)/shard_map/split_blocks/pallas_call | solution.py:55
  1.2 3.1 %collective-permute-start = (bf16[128,128]{1,0:T(8,128)(2,1)S(1)}, bf16[128,128]{1,0:T(8,128)(2,1)S(1)}, u32[]{:S(2)}, u32[]{:S(2)}) collective-permute-start(bf16[128,128]{1,0:T(8,128)(2,1)S(1)} %get-tuple-element.13), channel_id=1, source_target_pairs={{0,8},{8,16},{16,24},{24,0},{1,9},{9,17},{17,25},{25,1},{2,10},{10... | collective-permute-start | bytes 98312 | tf_op jit(solution)/shard_map/ppermute | solution.py:234
  4.3 2.6 %collective-permute-start.1 = (bf16[128,128]{1,0:T(8,128)(2,1)S(1)}, bf16[128,128]{1,0:T(8,128)(2,1)S(1)}, u32[]{:S(2)}, u32[]{:S(2)}) collective-permute-start(bf16[128,128]{1,0:T(8,128)(2,1)S(1)} %get-tuple-element.14), channel_id=1, source_target_pairs={{0,16},{8,24},{16,0},{24,8},{1,17},{9,25},{17,1},{25,9},{2,18},{10... | collective-permute-start | bytes 98312 | tf_op jit(solution)/shard_map/ppermute | solution.py:234
  6.9 1.3 %collective-permute-start.2 = (bf16[128,128]{1,0:T(8,128)(2,1)S(1)}, bf16[128,128]{1,0:T(8,128)(2,1)S(1)}, u32[]{:S(2)}, u32[]{:S(2)}) collective-permute-start(bf16[128,128]{1,0:T(8,128)(2,1)S(1)} %get-tuple-element.15), channel_id=1, source_target_pairs={{0,24},{8,0},{16,8},{24,16},{1,25},{9,1},{17,9},{25,17},{2,26},{10... | collective-permute-start | bytes 98312 | tf_op jit(solution)/shard_map/ppermute | solution.py:234
  8.2 0.0 collective-permute-done
  8.2 1.2 %collective-permute-done.1 = bf16[128,128]{1,0:T(8,128)(2,1)S(1)} collective-permute-done((bf16[128,128]{1,0:T(8,128)(2,1)S(1)}, bf16[128,128]{1,0:T(8,128)(2,1)S(1)}, u32[]{:S(2)}, u32[]{:S(2)}) %collective-permute-start.1) | collective-permute-done | bytes 32800 | tf_op jit(solution)/shard_map/ppermute | solution.py:234
  9.4 1.3 %collective-permute-done.2 = bf16[128,128]{1,0:T(8,128)(2,1)S(1)} collective-permute-done((bf16[128,128]{1,0:T(8,128)(2,1)S(1)}, bf16[128,128]{1,0:T(8,128)(2,1)S(1)}, u32[]{:S(2)}, u32[]{:S(2)}) %collective-permute-start.2) | collective-permute-done | bytes 32800 | tf_op jit(solution)/shard_map/ppermute | solution.py:234
  10.8 2.4 %collective-permute-start.8 = (bf16[512,128]{1,0:T(8,128)(2,1)S(1)}, bf16[512,128]{1,0:T(8,128)(2,1)S(1)}, u32[]{:S(2)}, u32[]{:S(2)}) collective-permute-start(bf16[512,128]{1,0:T(8,128)(2,1)S(1)} %constant_dynamic-update-slice_fusion.refs_0_), channel_id=1, source_target_pairs={{0,6},{1,7},{2,4},{3,5},{4,2},{5,3},{6,0},{7,1},{8,14},{9,15},{10,... | collective-permute-start | bytes 393224 | tf_op jit(solution)/shard_map/ppermute | solution.py:230
  13.2 0.5 %collective-permute-start.5 = (bf16[512,128]{1,0:T(8,128)(2,1)S(1)}, bf16[512,128]{1,0:T(8,128)(2,1)S(1)}, u32[]{:S(2)}, u32[]{:S(2)}) collective-permute-start(bf16[512,128]{1,0:T(8,128)(2,1)S(1)} %constant_dynamic-update-slice_fusion.refs_0_), channel_id=1, source_target_pairs={{0,4},{1,5},{2,6},{3,7},{4,0},{5,1},{6,2},{7,3},{8,12},{9,13},{10,... | collective-permute-start | bytes 393224 | tf_op jit(solution)/shard_map/ppermute | solution.py:230
  13.7 0.5 %collective-permute-start.3 = (bf16[512,128]{1,0:T(8,128)(2,1)S(1)}, bf16[512,128]{1,0:T(8,128)(2,1)S(1)}, u32[]{:S(2)}, u32[]{:S(2)}) collective-permute-start(bf16[512,128]{1,0:T(8,128)(2,1)S(1)} %constant_dynamic-update-slice_fusion.refs_0_), channel_id=1, source_target_pairs={{0,2},{1,3},{2,0},{3,1},{4,6},{5,7},{6,4},{7,5},{8,10},{9,11},{10,... | collective-permute-start | bytes 393224 | tf_op jit(solution)/shard_map/ppermute | solution.py:230
  14.3 0.0 collective-permute-start.7
  14.3 3.6 %collective-permute-done.8.refs_2_ = bf16[512,128]{1,0:T(8,128)(2,1)S(1)} collective-permute-done((bf16[512,128]{1,0:T(8,128)(2,1)S(1)}, bf16[512,128]{1,0:T(8,128)(2,1)S(1)}, u32[]{:S(2)}, u32[]{:S(2)}) %collective-permute-start.8) | collective-permute-done | bytes 131104 | tf_op jit(solution)/shard_map/ppermute | solution.py:230
  17.9 0.0 collective-permute-start.9
  17.9 0.9 %collective-permute-done.5.refs_5_ = bf16[512,128]{1,0:T(8,128)(2,1)S(1)} collective-permute-done((bf16[512,128]{1,0:T(8,128)(2,1)S(1)}, bf16[512,128]{1,0:T(8,128)(2,1)S(1)}, u32[]{:S(2)}, u32[]{:S(2)}) %collective-permute-start.5) | collective-permute-done | bytes 131104 | tf_op jit(solution)/shard_map/ppermute | solution.py:230
  18.7 0.0 collective-permute-start.6
  18.7 0.0 collective-permute-done.3.refs_4_
  18.7 0.5 %collective-permute-start.4 = (bf16[512,128]{1,0:T(8,128)(2,1)S(1)}, bf16[512,128]{1,0:T(8,128)(2,1)S(1)}, u32[]{:S(2)}, u32[]{:S(2)}) collective-permute-start(bf16[512,128]{1,0:T(8,128)(2,1)S(1)} %collective-permute-done.3.refs_4_), channel_id=1, source_target_pairs={{0,1},{1,0},{2,3},{3,2},{4,5},{5,4},{6,7},{7,6},{8,9},{9,8},{10,11... | collective-permute-start | bytes 393224 | tf_op jit(solution)/shard_map/ppermute | solution.py:230
  19.2 0.0 collective-permute-done.7.refs_1_
  19.3 0.0 collective-permute-done.9.refs_3_
  19.3 0.7 %first_pieces.1 = (bf16[512,768]{1,0:T(8,128)(2,1)S(1)}, bf16[768,512]{1,0:T(8,128)(2,1)S(1)}, f32[512,512]{1,0:T(8,128)S(1)}) custom-call(bf16[512,128]{1,0:T(8,128)(2,1)S(1)} %constant_dynamic-update-slice_fusion.refs_0_, bf16[512,128]{1,0:T(8,128)(2,1)S(1)} %collective-permute-done.7.refs_1_, bf16[512,128]{1,0:T(8,128)(2,1)S(1)} %collective-permute-done.8.refs_2_, ...), custom_call_target="tpu_custom_call" | custom-call | flops 400000000 | tf_op jit(solution)/shard_map/first_pieces/pallas_call | solution.py:244
  19.9 0.2 collective-permute-done.6.late1
  20.1 0.2 collective-permute-done.4.late0
  20.3 6.7 %whole_block.1 = bf16[768,1024]{1,0:T(8,128)(2,1)} custom-call(bf16[512,128]{1,0:T(8,128)(2,1)S(1)} %collective-permute-done.4.late0, bf16[512,128]{1,0:T(8,128)(2,1)S(1)} %collective-permute-done.6.late1, bf16[512,768]{1,0:T(8,128)(2,1)S(1)} %get-tuple-element.16.x, bf16[768,512]{1,0:T(8,128)(2,1)S(1)} %get-tuple-element.17.xt, ...), custom_call_target="tpu_custom_call" | custom-call | flops 5000000000 | tf_op jit(solution)/shard_map/whole_block/pallas_call | solution.py:253
  (4 shorter events, 0.0 us)
Async XLA Ops:
  0.0 0.9 %copy-start = (bf16[128,4,128]{2,1,0:T(4,128)(2,1)S(1)}, bf16[128,4,128]{2,1,0:T(4,128)(2,1)}, u32[]{:S(2)}) copy-start(bf16[128,4,128]{2,1,0:T(4,128)(2,1)} %param.2) | copy-start | bytes 393220
  1.2 7.0 %collective-permute-start = (bf16[128,128]{1,0:T(8,128)(2,1)S(1)}, bf16[128,128]{1,0:T(8,128)(2,1)S(1)}, u32[]{:S(2)}, u32[]{:S(2)}) collective-permute-start(bf16[128,128]{1,0:T(8,128)(2,1)S(1)} %get-tuple-element.13), channel_id=1, source_target_pairs={{0,8},{8,16},{16,24},{24,0},{1,9},{9,17},{17,25},{25,1},{2,10},{10... | collective-permute-start | bytes 98312 | tf_op jit(solution)/shard_map/ppermute | solution.py:234
  4.3 5.2 %collective-permute-start.1 = (bf16[128,128]{1,0:T(8,128)(2,1)S(1)}, bf16[128,128]{1,0:T(8,128)(2,1)S(1)}, u32[]{:S(2)}, u32[]{:S(2)}) collective-permute-start(bf16[128,128]{1,0:T(8,128)(2,1)S(1)} %get-tuple-element.14), channel_id=1, source_target_pairs={{0,16},{8,24},{16,0},{24,8},{1,17},{9,25},{17,1},{25,9},{2,18},{10... | collective-permute-start | bytes 98312 | tf_op jit(solution)/shard_map/ppermute | solution.py:234
  6.9 3.9 %collective-permute-start.2 = (bf16[128,128]{1,0:T(8,128)(2,1)S(1)}, bf16[128,128]{1,0:T(8,128)(2,1)S(1)}, u32[]{:S(2)}, u32[]{:S(2)}) collective-permute-start(bf16[128,128]{1,0:T(8,128)(2,1)S(1)} %get-tuple-element.15), channel_id=1, source_target_pairs={{0,24},{8,0},{16,8},{24,16},{1,25},{9,1},{17,9},{25,17},{2,26},{10... | collective-permute-start | bytes 98312 | tf_op jit(solution)/shard_map/ppermute | solution.py:234
  10.8 7.1 %collective-permute-start.8 = (bf16[512,128]{1,0:T(8,128)(2,1)S(1)}, bf16[512,128]{1,0:T(8,128)(2,1)S(1)}, u32[]{:S(2)}, u32[]{:S(2)}) collective-permute-start(bf16[512,128]{1,0:T(8,128)(2,1)S(1)} %constant_dynamic-update-slice_fusion.refs_0_), channel_id=1, source_target_pairs={{0,6},{1,7},{2,4},{3,5},{4,2},{5,3},{6,0},{7,1},{8,14},{9,15},{10,... | collective-permute-start | bytes 393224 | tf_op jit(solution)/shard_map/ppermute | solution.py:230
  13.2 5.5 %collective-permute-start.5 = (bf16[512,128]{1,0:T(8,128)(2,1)S(1)}, bf16[512,128]{1,0:T(8,128)(2,1)S(1)}, u32[]{:S(2)}, u32[]{:S(2)}) collective-permute-start(bf16[512,128]{1,0:T(8,128)(2,1)S(1)} %constant_dynamic-update-slice_fusion.refs_0_), channel_id=1, source_target_pairs={{0,4},{1,5},{2,6},{3,7},{4,0},{5,1},{6,2},{7,3},{8,12},{9,13},{10,... | collective-permute-start | bytes 393224 | tf_op jit(solution)/shard_map/ppermute | solution.py:230
  13.7 5.0 %collective-permute-start.3 = (bf16[512,128]{1,0:T(8,128)(2,1)S(1)}, bf16[512,128]{1,0:T(8,128)(2,1)S(1)}, u32[]{:S(2)}, u32[]{:S(2)}) collective-permute-start(bf16[512,128]{1,0:T(8,128)(2,1)S(1)} %constant_dynamic-update-slice_fusion.refs_0_), channel_id=1, source_target_pairs={{0,2},{1,3},{2,0},{3,1},{4,6},{5,7},{6,4},{7,5},{8,10},{9,11},{10,... | collective-permute-start | bytes 393224 | tf_op jit(solution)/shard_map/ppermute | solution.py:230
  14.3 5.0 %collective-permute-start.7 = (bf16[512,128]{1,0:T(8,128)(2,1)S(1)}, bf16[512,128]{1,0:T(8,128)(2,1)S(1)}, u32[]{:S(2)}, u32[]{:S(2)}) collective-permute-start(bf16[512,128]{1,0:T(8,128)(2,1)S(1)} %constant_dynamic-update-slice_fusion.refs_0_), channel_id=1, source_target_pairs={{0,1},{1,0},{2,3},{3,2},{4,5},{5,4},{6,7},{7,6},{8,9},{9,8},{10,11... | collective-permute-start | bytes 393224 | tf_op jit(solution)/shard_map/ppermute | solution.py:230
  17.9 1.4 %collective-permute-start.9 = (bf16[512,128]{1,0:T(8,128)(2,1)S(1)}, bf16[512,128]{1,0:T(8,128)(2,1)S(1)}, u32[]{:S(2)}, u32[]{:S(2)}) collective-permute-start(bf16[512,128]{1,0:T(8,128)(2,1)S(1)} %collective-permute-done.8.refs_2_), channel_id=1, source_target_pairs={{0,1},{1,0},{2,3},{3,2},{4,5},{5,4},{6,7},{7,6},{8,9},{9,8},{10,11... | collective-permute-start | bytes 393224 | tf_op jit(solution)/shard_map/ppermute | solution.py:230
  18.7 1.3 %collective-permute-start.6 = (bf16[512,128]{1,0:T(8,128)(2,1)S(1)}, bf16[512,128]{1,0:T(8,128)(2,1)S(1)}, u32[]{:S(2)}, u32[]{:S(2)}) collective-permute-start(bf16[512,128]{1,0:T(8,128)(2,1)S(1)} %collective-permute-done.5.refs_5_), channel_id=1, source_target_pairs={{0,1},{1,0},{2,3},{3,2},{4,5},{5,4},{6,7},{7,6},{8,9},{9,8},{10,11... | collective-permute-start | bytes 393224 | tf_op jit(solution)/shard_map/ppermute | solution.py:230
  18.7 1.5 %collective-permute-start.4 = (bf16[512,128]{1,0:T(8,128)(2,1)S(1)}, bf16[512,128]{1,0:T(8,128)(2,1)S(1)}, u32[]{:S(2)}, u32[]{:S(2)}) collective-permute-start(bf16[512,128]{1,0:T(8,128)(2,1)S(1)} %collective-permute-done.3.refs_4_), channel_id=1, source_target_pairs={{0,1},{1,0},{2,3},{3,2},{4,5},{5,4},{6,7},{7,6},{8,9},{9,8},{10,11... | collective-permute-start | bytes 393224 | tf_op jit(solution)/shard_map/ppermute | solution.py:230
